TPU v7x, 32 devices: a whole 2x2x4 slice. The times are simulated.
32 devices in a mesh: fsdp: 4 (over z), head: 4 (over y, x), tensor: 2 (over core).
Axes of the slice: x: 2, y: 2, z: 4, core: 2. Of those that a mesh axis runs over, the one named last changes fastest.
Arguments:
- tokens: bfloat16 [8192, 2048], P(('fsdp', 'head', 'tensor')), may hold values from -6 to 6
- lengths: int32 [4, 2], P('fsdp'), may hold values from 0 to 2048, as said below
- attention_gain: float32 [2048], replicated, may hold values from 0.5 to 1.5
- query_weight: bfloat16 [2048, 8, 2, 128], P('fsdp', 'head', 'tensor'), may hold values from -0.1875 to 0.1875
- key_weight: bfloat16 [2048, 8, 2, 128], P('fsdp', 'head', 'tensor'), may hold values from -0.1875 to 0.1875
- value_weight: bfloat16 [2048, 8, 256], P('fsdp', 'head', 'tensor'), may hold values from -0.125 to 0.125
- output_weight: bfloat16 [8, 256, 2048], P('head', 'tensor', 'fsdp'), may hold values from -0.125 to 0.125
- lambda_vectors: float32 [8, 4, 128], replicated, may hold values from -0.9 to 0.9
- head_gain: float32 [8, 256], replicated, may hold values from 0.5 to 1.5
- feedforward_gain: float32 [2048], replicated, may hold values from 0.5 to 1.5
- gate_weight: bfloat16 [2048, 5632], P('fsdp', ('head', 'tensor')), may hold values from -0.125 to 0.125
- up_weight: bfloat16 [2048, 5632], P('fsdp', ('head', 'tensor')), may hold values from -0.125 to 0.125
- down_weight: bfloat16 [5632, 2048], P(('head', 'tensor'), 'fsdp'), may hold values from -0.078125 to 0.078125
- cotangent: bfloat16 [8192, 2048], P(('fsdp', 'head', 'tensor')), may hold values from -6 to 6
Outputs:
- block_output: bfloat16 [8192, 2048], P(('fsdp', 'head', 'tensor'))
- tokens_grad: float32 [8192, 2048], P(('fsdp', 'head', 'tensor'))
- attention_gain_grad: float32 [2048], replicated
- query_weight_grad: float32 [2048, 8, 2, 128], P('fsdp', 'head', 'tensor')
- key_weight_grad: float32 [2048, 8, 2, 128], P('fsdp', 'head', 'tensor')
- value_weight_grad: float32 [2048, 8, 256], P('fsdp', 'head', 'tensor')
- output_weight_grad: float32 [8, 256, 2048], P('head', 'tensor', 'fsdp')
- lambda_vectors_grad: float32 [8, 4, 128], replicated
- head_gain_grad: float32 [8, 256], replicated
- feedforward_gain_grad: float32 [2048], replicated
- gate_weight_grad: float32 [2048, 5632], P('fsdp', ('head', 'tensor'))
- up_weight_grad: float32 [2048, 5632], P('fsdp', ('head', 'tensor'))
- down_weight_grad: float32 [5632, 2048], P(('head', 'tensor'), 'fsdp')
Inputs may be any that keep to these rules, and one draw needn't show every extreme that they name: Each row of 2048 slots holds one or two sequences packed from its start, given by its two lengths in order (the second 0 where there is one); every sequence has 512 tokens or more, together they take 5 * 256 slots or more of the row, and the slots after them are padding; some row holds a single sequence of 2048 tokens.
All inputs are finite; a program needn't handle non-finite values.
Results may differ from a plain program's by a relative error of at most 0.019.
Values may be sent and summed in bfloat16 or wider, within the bound.
No kernel may reach another device: no remote copies, remote signals or barrier semaphores. Data moves between devices by JAX's collectives and lax.ppermute only.
A program may use at most 320 MiB of HBM per device.

v0:
```python
import jax
import jax.numpy as jnp
from jax import lax
from jax.sharding import PartitionSpec as P

SLOTS = 2048


lambda_base = 0.2
block_limit = 512


def slot_layout(row_lengths):
    slot_index = jnp.arange(SLOTS, dtype=jnp.int32)
    first_end = row_lengths[:, 0:1]
    second_end = first_end + row_lengths[:, 1:2]
    segment = (slot_index[None, :] >= first_end).astype(jnp.int32) + (
        slot_index[None, :] >= second_end
    ).astype(jnp.int32)
    starts = jnp.where(segment == 0, 0, jnp.where(segment == 1, first_end, second_end))
    return (segment, slot_index[None, :] - starts)


def rope_tables(positions, qk_width):
    half_width = qk_width // 2
    frequency = 10000.0 ** (-jnp.arange(half_width, dtype=jnp.float32) / half_width)
    angles = positions.astype(jnp.float32)[:, None] * frequency[None, :]
    return (jnp.cos(angles), jnp.sin(angles))


def rotate(values, cosine_table, sine_table):
    half_width = values.shape[-1] // 2
    first_half = values[..., :half_width]
    second_half = values[..., half_width:]
    cosine_wide = cosine_table[:, None, :]
    sine_wide = sine_table[:, None, :]
    return jnp.concatenate(
        [
            first_half * cosine_wide - second_half * sine_wide,
            second_half * cosine_wide + first_half * sine_wide,
        ],
        axis=-1,
    )


def rotate_back(grads, cosine_table, sine_table):
    half_width = grads.shape[-1] // 2
    first_half = grads[..., :half_width]
    second_half = grads[..., half_width:]
    cosine_wide = cosine_table[:, None, :]
    sine_wide = sine_table[:, None, :]
    return jnp.concatenate(
        [
            first_half * cosine_wide + second_half * sine_wide,
            second_half * cosine_wide - first_half * sine_wide,
        ],
        axis=-1,
    )


def contract_first(left_side, right_side):
    return lax.dot_general(
        left_side, right_side, (((0,), (0,)), ((), ())), preferred_element_type=jnp.float32
    )


def contract_last(left_side, right_side):
    return lax.dot_general(
        left_side, right_side, (((1,), (1,)), ((), ())), preferred_element_type=jnp.float32
    )


def gather_rows(values):
    return lax.all_gather(values, ("head", "tensor"), axis=0, tiled=True)


def scatter_rows(values):
    return lax.psum_scatter(values, ("head", "tensor"), scatter_dimension=0, tiled=True)


def value_total(partial_value):
    return lax.psum(partial_value, "tensor")


def gather_weights(
    query_weight, key_weight, value_weight, output_weight, gate_weight, up_weight, down_weight
):
    shard_rows = query_weight.shape[0]
    row_parts = (
        lax.all_gather(query_weight.reshape(shard_rows, -1), "fsdp", axis=0, tiled=True),
        lax.all_gather(key_weight.reshape(shard_rows, -1), "fsdp", axis=0, tiled=True),
        lax.all_gather(value_weight.reshape(shard_rows, -1), "fsdp", axis=0, tiled=True),
        lax.all_gather(gate_weight, "fsdp", axis=0, tiled=True),
        lax.all_gather(up_weight, "fsdp", axis=0, tiled=True),
    )
    col_parts = (
        lax.all_gather(
            output_weight.reshape(-1, output_weight.shape[2]), "fsdp", axis=1, tiled=True
        ),
        lax.all_gather(down_weight, "fsdp", axis=1, tiled=True),
    )
    return (row_parts, col_parts)


def block_mask(segment_flat, row_base, block_start, block_stop):
    query_segment = segment_flat[row_base + block_start : row_base + block_stop]
    key_segment = segment_flat[row_base : row_base + block_stop]
    query_slot = jnp.arange(block_start, block_stop, dtype=jnp.int32)
    key_slot = jnp.arange(0, block_stop, dtype=jnp.int32)
    return (query_segment[:, None] == key_segment[None, :]) & (
        key_slot[None, :] <= query_slot[:, None]
    )


def body(
    tokens,
    lengths,
    attention_gain,
    query_weight,
    key_weight,
    value_weight,
    output_weight,
    lambda_vectors,
    head_gain,
    feedforward_gain,
    gate_weight,
    up_weight,
    down_weight,
    cotangent,
):
    rows_here = tokens.shape[0]
    groups = lax.axis_size("head") * lax.axis_size("tensor")
    group_rank = lax.axis_index("head") * lax.axis_size("tensor") + lax.axis_index("tensor")
    map_index = lax.axis_index("tensor")
    group_tokens = rows_here * groups
    heads_here = query_weight.shape[1]
    qk_width = query_weight.shape[3]
    value_half = value_weight.shape[2]
    value_width = value_half * lax.axis_size("tensor")
    block_size = min(block_limit, SLOTS)
    segment, positions = slot_layout(lengths)
    segment_flat = segment.reshape(-1)
    valid_all = (segment_flat < 2).astype(jnp.float32)
    valid_here = lax.dynamic_slice_in_dim(valid_all, group_rank * rows_here, rows_here)[:, None]
    cosine_table, sine_table = rope_tables(positions.reshape(-1), qk_width)
    head_start = lax.axis_index("head") * heads_here
    own_vectors = lax.dynamic_slice_in_dim(lambda_vectors, head_start, heads_here, 0)
    first_exp = jnp.exp(jnp.sum(own_vectors[:, 0] * own_vectors[:, 1], axis=-1))
    second_exp = jnp.exp(jnp.sum(own_vectors[:, 2] * own_vectors[:, 3], axis=-1))
    lambda_value = first_exp - second_exp + lambda_base
    coefficient = jnp.where(map_index == 0, jnp.ones_like(lambda_value), -lambda_value)
    own_gain = lax.dynamic_slice(
        head_gain, (head_start, map_index * value_half), (heads_here, value_half)
    ) * (1.0 - lambda_base)
    row_full, col_full = gather_weights(
        query_weight, key_weight, value_weight, output_weight, gate_weight, up_weight, down_weight
    )
    query_full, key_full, value_full, gate_full, up_full = row_full
    output_full, down_full = col_full
    tokens_wide = tokens.astype(jnp.float32)
    attention_scale = lax.rsqrt(jnp.mean(tokens_wide * tokens_wide, axis=-1, keepdims=True) + 1e-06)
    normed_all = gather_rows((tokens_wide * attention_scale * attention_gain).astype(jnp.bfloat16))
    query_pre = jnp.dot(normed_all, query_full, preferred_element_type=jnp.float32).reshape(
        group_tokens, heads_here, qk_width
    )
    queries = (rotate(query_pre, cosine_table, sine_table) * qk_width ** (-0.5)).astype(
        jnp.bfloat16
    )
    key_pre = jnp.dot(normed_all, key_full, preferred_element_type=jnp.float32).reshape(
        group_tokens, heads_here, qk_width
    )
    keys_all = rotate(key_pre, cosine_table, sine_table).astype(jnp.bfloat16)
    values_own = (
        jnp.dot(normed_all, value_full, preferred_element_type=jnp.float32)
        .astype(jnp.bfloat16)
        .reshape(group_tokens, heads_here, value_half)
    )
    values_all = lax.all_gather(values_own, "tensor", axis=2, tiled=True)
    out_pieces = []
    total_pieces = []
    row_number = 0
    row_base = row_number * SLOTS
    for block_start in range(0, SLOTS, block_size):
        block_stop = block_start + block_size
        allowed = block_mask(segment_flat, row_base, block_start, block_stop)
        query_block = queries[row_base + block_start : row_base + block_stop]
        key_block = keys_all[row_base : row_base + block_stop]
        value_block = values_all[row_base : row_base + block_stop]
        scores = jnp.einsum(
            "qhe,khe->hqk", query_block, key_block, preferred_element_type=jnp.float32
        )
        scores = jnp.where(allowed[None], scores, -1e30)
        row_max = jnp.max(scores, axis=-1, keepdims=True)
        expanded = jnp.exp(scores - row_max)
        row_total = jnp.sum(expanded, axis=-1, keepdims=True)
        probability = (expanded / row_total).astype(jnp.bfloat16)
        out_pieces.append(
            jnp.einsum("hqk,khv->qhv", probability, value_block, preferred_element_type=jnp.float32)
        )
        total_pieces.append(jnp.transpose((row_max + jnp.log(row_total))[:, :, 0]))
    maps_out = jnp.concatenate(out_pieces, axis=0)
    log_total = jnp.concatenate(total_pieces, axis=0)
    mixed_half = lax.psum_scatter(
        maps_out * coefficient[None, :, None], "tensor", scatter_dimension=2, tiled=True
    )
    square_sum = value_total(jnp.sum(mixed_half * mixed_half, axis=-1))
    head_scale = lax.rsqrt(square_sum / value_width + 1e-05)[:, :, None]
    head_out = (
        (mixed_half * head_scale * own_gain[None])
        .astype(jnp.bfloat16)
        .reshape(group_tokens, heads_here * value_half)
    )
    attention_here = scatter_rows(
        jnp.dot(head_out, output_full, preferred_element_type=jnp.float32)
    )
    residual = tokens_wide + attention_here
    ffn_scale = lax.rsqrt(jnp.mean(residual * residual, axis=-1, keepdims=True) + 1e-06)
    ffn_all = gather_rows((residual * ffn_scale * feedforward_gain).astype(jnp.bfloat16))
    gate_pre = jnp.dot(ffn_all, gate_full, preferred_element_type=jnp.float32)
    upward = jnp.dot(ffn_all, up_full, preferred_element_type=jnp.float32)
    sigmoid_gate = jax.nn.sigmoid(gate_pre)
    silu_gate = gate_pre * sigmoid_gate
    hidden = (silu_gate * upward).astype(jnp.bfloat16)
    ffn_here = scatter_rows(jnp.dot(hidden, down_full, preferred_element_type=jnp.float32))
    block_output = (valid_here * (residual + ffn_here)).astype(jnp.bfloat16)
    row_full, col_full = gather_weights(
        query_weight, key_weight, value_weight, output_weight, gate_weight, up_weight, down_weight
    )
    query_full, key_full, value_full, gate_full, up_full = row_full
    output_full, down_full = col_full
    ffn_out_grad = valid_here * cotangent.astype(jnp.float32)
    ffn_grad_all = gather_rows(ffn_out_grad.astype(jnp.bfloat16))
    hidden_grad = contract_last(ffn_grad_all, down_full)
    down_weight_grad = contract_first(hidden, ffn_grad_all)
    gate_grad = (
        hidden_grad * upward * sigmoid_gate * (1.0 + gate_pre * (1.0 - sigmoid_gate))
    ).astype(jnp.bfloat16)
    up_grad = (hidden_grad * silu_gate).astype(jnp.bfloat16)
    ffn_in_grad = scatter_rows(
        contract_last(gate_grad, gate_full) + contract_last(up_grad, up_full)
    )
    gate_weight_grad = contract_first(ffn_all, gate_grad)
    up_weight_grad = contract_first(ffn_all, up_grad)
    feedforward_gain_grad = jnp.sum(ffn_in_grad * residual * ffn_scale, axis=0)
    ffn_gained = ffn_in_grad * feedforward_gain
    residual_grad = (
        ffn_out_grad
        + ffn_scale * ffn_gained
        - residual * ffn_scale**3 * jnp.mean(ffn_gained * residual, axis=-1, keepdims=True)
    )
    attention_grad_all = gather_rows(residual_grad.astype(jnp.bfloat16))
    head_out_grad = contract_last(attention_grad_all, output_full).reshape(
        group_tokens, heads_here, value_half
    )
    output_weight_grad = contract_first(head_out, attention_grad_all)
    head_gain_part = jnp.sum(head_out_grad * mixed_half * head_scale, axis=0) * (1.0 - lambda_base)
    weighted = head_out_grad * own_gain[None]
    inner_sum = value_total(jnp.sum(weighted * mixed_half, axis=-1))
    mixed_grad_half = (
        head_scale * weighted - mixed_half * head_scale**3 * (inner_sum / value_width)[:, :, None]
    )
    mixed_grad = lax.all_gather(
        mixed_grad_half.astype(jnp.bfloat16), "tensor", axis=2, tiled=True
    ).astype(mixed_grad_half.dtype)
    map_grad = (mixed_grad * coefficient[None, :, None]).astype(jnp.bfloat16)
    second_map = jnp.where(map_index == 1, -1.0, 0.0)
    lambda_grad = jnp.sum(mixed_grad * maps_out, axis=(0, 2)) * second_map
    vector_grads = jnp.stack(
        [
            lambda_grad[:, None] * first_exp[:, None] * own_vectors[:, 1],
            lambda_grad[:, None] * first_exp[:, None] * own_vectors[:, 0],
            -lambda_grad[:, None] * second_exp[:, None] * own_vectors[:, 3],
            -lambda_grad[:, None] * second_exp[:, None] * own_vectors[:, 2],
        ],
        axis=1,
    )
    lambda_full = lax.dynamic_update_slice(
        jnp.zeros(lambda_vectors.shape, jnp.float32), vector_grads, (head_start, 0, 0)
    )
    gain_full = lax.dynamic_update_slice(
        jnp.zeros(head_gain.shape, jnp.float32),
        head_gain_part,
        (head_start, map_index * value_half),
    )
    query_pieces = []
    key_grad = jnp.zeros((group_tokens, heads_here, qk_width), jnp.float32)
    value_grad = jnp.zeros((group_tokens, heads_here, value_width), jnp.float32)
    row_number = 0
    row_base = row_number * SLOTS
    for block_start in range(0, SLOTS, block_size):
        block_stop = block_start + block_size
        allowed = block_mask(segment_flat, row_base, block_start, block_stop)
        query_block = queries[row_base + block_start : row_base + block_stop]
        key_block = keys_all[row_base : row_base + block_stop]
        value_block = values_all[row_base : row_base + block_stop]
        grad_block = map_grad[row_base + block_start : row_base + block_stop]
        total_block = jnp.transpose(log_total[row_base + block_start : row_base + block_stop])[
            :, :, None
        ]
        scores = jnp.einsum(
            "qhe,khe->hqk", query_block, key_block, preferred_element_type=jnp.float32
        )
        scores = jnp.where(allowed[None], scores, -1e30)
        probability = jnp.exp(scores - total_block)
        prob_grad = jnp.einsum(
            "qhv,khv->hqk", grad_block, value_block, preferred_element_type=jnp.float32
        )
        value_grad = value_grad.at[row_base : row_base + block_stop].add(
            jnp.einsum(
                "hqk,qhv->khv",
                probability.astype(jnp.bfloat16),
                grad_block,
                preferred_element_type=jnp.float32,
            )
        )
        delta_sum = jnp.sum(probability * prob_grad, axis=-1, keepdims=True)
        score_grad = (probability * (prob_grad - delta_sum)).astype(jnp.bfloat16)
        query_pieces.append(
            jnp.einsum("hqk,khe->qhe", score_grad, key_block, preferred_element_type=jnp.float32)
        )
        key_grad = key_grad.at[row_base : row_base + block_stop].add(
            jnp.einsum("hqk,qhe->khe", score_grad, query_block, preferred_element_type=jnp.float32)
        )
    query_grad = jnp.concatenate(query_pieces, axis=0)
    value_grad_own = lax.psum_scatter(
        value_grad.astype(jnp.bfloat16), "tensor", scatter_dimension=2, tiled=True
    ).reshape(group_tokens, heads_here * value_half)
    query_pre_grad = (
        rotate_back(query_grad * qk_width ** (-0.5), cosine_table, sine_table)
        .astype(jnp.bfloat16)
        .reshape(group_tokens, heads_here * qk_width)
    )
    key_pre_grad = (
        rotate_back(key_grad, cosine_table, sine_table)
        .astype(jnp.bfloat16)
        .reshape(group_tokens, heads_here * qk_width)
    )
    normed_grad = scatter_rows(
        contract_last(query_pre_grad, query_full)
        + contract_last(key_pre_grad, key_full)
        + contract_last(value_grad_own, value_full)
    )
    query_weight_grad = contract_first(normed_all, query_pre_grad)
    key_weight_grad = contract_first(normed_all, key_pre_grad)
    value_weight_grad = contract_first(normed_all, value_grad_own)
    attention_gain_grad = jnp.sum(normed_grad * tokens_wide * attention_scale, axis=0)
    attention_gained = normed_grad * attention_gain
    tokens_grad = (
        residual_grad
        + attention_scale * attention_gained
        - tokens_wide
        * attention_scale**3
        * jnp.mean(attention_gained * tokens_wide, axis=-1, keepdims=True)
    )
    row_grads = (
        lax.psum_scatter(
            query_weight_grad.astype(jnp.bfloat16), "fsdp", scatter_dimension=0, tiled=True
        ).astype(jnp.float32),
        lax.psum_scatter(
            key_weight_grad.astype(jnp.bfloat16), "fsdp", scatter_dimension=0, tiled=True
        ).astype(jnp.float32),
        lax.psum_scatter(
            value_weight_grad.astype(jnp.bfloat16), "fsdp", scatter_dimension=0, tiled=True
        ).astype(jnp.float32),
        lax.psum_scatter(
            gate_weight_grad.astype(jnp.bfloat16), "fsdp", scatter_dimension=0, tiled=True
        ).astype(jnp.float32),
        lax.psum_scatter(
            up_weight_grad.astype(jnp.bfloat16), "fsdp", scatter_dimension=0, tiled=True
        ).astype(jnp.float32),
    )
    col_grads = (
        lax.psum_scatter(
            output_weight_grad.astype(jnp.bfloat16), "fsdp", scatter_dimension=1, tiled=True
        ).astype(jnp.float32),
        lax.psum_scatter(
            down_weight_grad.astype(jnp.bfloat16), "fsdp", scatter_dimension=1, tiled=True
        ).astype(jnp.float32),
    )
    small_sums = lax.psum(
        (attention_gain_grad, feedforward_gain_grad, lambda_full, gain_full),
        ("fsdp", "head", "tensor"),
    )
    return (
        block_output,
        tokens_grad,
        small_sums[0],
        row_grads[0].reshape(query_weight.shape),
        row_grads[1].reshape(key_weight.shape),
        row_grads[2].reshape(value_weight.shape),
        col_grads[0].reshape(output_weight.shape),
        small_sums[2],
        small_sums[3],
        small_sums[1],
        row_grads[3],
        row_grads[4],
        col_grads[1],
    )


def solution(mesh):
    placed = (
        P(("fsdp", "head", "tensor"), None),
        P("fsdp", None),
        P(),
        P("fsdp", "head", "tensor", None),
        P("fsdp", "head", "tensor", None),
        P("fsdp", "head", "tensor"),
        P("head", "tensor", "fsdp"),
        P(),
        P(),
        P(),
        P("fsdp", ("head", "tensor")),
        P("fsdp", ("head", "tensor")),
        P(("head", "tensor"), "fsdp"),
        P(("fsdp", "head", "tensor"), None),
    )
    return jax.shard_map(
        body,
        mesh=mesh,
        in_specs=placed,
        out_specs=(
            P(("fsdp", "head", "tensor"), None),
            P(("fsdp", "head", "tensor"), None),
            P(),
            P("fsdp", "head", "tensor", None),
            P("fsdp", "head", "tensor", None),
            P("fsdp", "head", "tensor"),
            P("head", "tensor", "fsdp"),
            P(),
            P(),
            P(),
            P("fsdp", ("head", "tensor")),
            P("fsdp", ("head", "tensor")),
            P(("head", "tensor"), "fsdp"),
        ),
        check_vma=False,
    )
```

profile of v0, /device:TPU:0, one launch (start us, length us, event | category | flops | bytes accessed | tf_op | source)
XLA Modules:
  0.0 1515.2 jit_solution(9157941047837557775)
XLA Ops:
  20.3 5.3 multiply_cosine_fusion
  29.2 11.6 all-gather.22.cloned.1.call-done
  40.8 56.4 %all-gather.14.cloned.1.call-done = bf16[2048,2048]{1,0:T(8,128)(2,1)} async-done(((bf16[256,2048]{1,0:T(8,128)(2,1)}), bf16[2048,2048]{1,0:T(8,128)(2,1)}) %all-gather.14.cloned.1.call-update) | async-done | bytes 8388624 | tf_op jit(solution)/shard_map/all_gather | solution.py:74
  97.3 6.0 fusion.119
  111.0 16.3 %all-gather.16.cloned.1.call-done = bf16[2048,256]{1,0:T(8,128)(2,1)} async-done(((bf16[512,256]{1,0:T(8,128)(2,1)}), bf16[2048,256]{1,0:T(8,128)(2,1)}) %all-gather.16.cloned.1.call-update) | async-done | bytes 1048592 | tf_op jit(solution)/shard_map/all_gather | solution.py:92
  127.4 7.0 convolution_convert_fusion.7
  134.9 22.0 %all-gather.20.cloned.1.call-done = bf16[2048,256]{1,0:T(8,128)(2,1)} async-done(((bf16[512,256]{1,0:T(8,128)(2,1)}), bf16[2048,256]{1,0:T(8,128)(2,1)}) %all-gather.20.cloned.1.call-update) | async-done | bytes 1048592 | tf_op jit(solution)/shard_map/all_gather | solution.py:90
  156.8 6.0 fusion.118
  170.8 4.8 subtract_convert_fusion.3
  206.7 10.2 reduce-scatter.14.cloned.1.call-done
  224.1 23.7 %all-gather.24.cloned.1.call-done = bf16[256,2048]{1,0:T(8,128)(2,1)} async-done(((bf16[256,512]{1,0:T(8,128)(2,1)}), bf16[256,2048]{1,0:T(8,128)(2,1)}) %all-gather.24.cloned.1.call-update) | async-done | bytes 1048592 | tf_op jit(solution)/shard_map/all_gather | solution.py:97
  247.8 9.4 fusion.120
  258.2 114.6 %reduce-scatter.16.cloned.1.call-done = f32[256,2048]{1,0:T(8,128)} async-done(((f32[2048,2048]{1,0:T(8,128)}), f32[256,2048]{1,0:T(8,128)}) %reduce-scatter.16.cloned.1.call-update) | async-done | bytes 2097168 | tf_op jit(solution)/shard_map/reduce_scatter | solution.py:78
  380.1 53.6 %all-gather.30.cloned.1.call-done = bf16[2048,704]{0,1:T(8,128)(2,1)} async-done(((bf16[512,704]{0,1:T(8,128)(2,1)}), bf16[2048,704]{0,1:T(8,128)(2,1)}) %all-gather.30.cloned.1.call-update) | async-done | bytes 2883600 | tf_op jit(solution)/shard_map/all_gather | solution.py:94
  433.6 55.6 %all-gather.26.cloned.1.call-done = bf16[2048,2048]{1,0:T(8,128)(2,1)} async-done(((bf16[256,2048]{1,0:T(8,128)(2,1)}), bf16[2048,2048]{1,0:T(8,128)(2,1)}) %all-gather.26.cloned.1.call-update) | async-done | bytes 8388624 | tf_op jit(solution)/shard_map/all_gather | solution.py:74
  489.3 11.1 fusion.122
  500.4 49.7 %all-gather.28.cloned.1.call-done = bf16[2048,704]{0,1:T(8,128)(2,1)} async-done(((bf16[512,704]{0,1:T(8,128)(2,1)}), bf16[2048,704]{0,1:T(8,128)(2,1)}) %all-gather.28.cloned.1.call-update) | async-done | bytes 2883600 | tf_op jit(solution)/shard_map/all_gather | solution.py:93
  550.1 11.0 fusion.121
  561.1 48.4 %all-gather.32.cloned.1.call-done = bf16[704,2048]{1,0:T(8,128)(2,1)} async-done(((bf16[704,512]{1,0:T(8,128)(2,1)}), bf16[704,2048]{1,0:T(8,128)(2,1)}) %all-gather.32.cloned.1.call-update) | async-done | bytes 2883600 | tf_op jit(solution)/shard_map/all_gather | solution.py:100
  609.5 55.8 %all-gather.34.cloned.1.call-done = bf16[2048,2048]{1,0:T(8,128)(2,1)} async-done(((bf16[256,2048]{1,0:T(8,128)(2,1)}), bf16[2048,2048]{1,0:T(8,128)(2,1)}) %all-gather.34.cloned.1.call-update) | async-done | bytes 8388624 | tf_op jit(solution)/shard_map/all_gather | solution.py:74
  665.3 15.3 %multiply_convert_fusion.2 = (bf16[2048,704]{0,1:T(8,128)(2,1)S(1)}, bf16[2048,704]{0,1:T(8,128)(2,1)S(1)}, bf16[2048,704]{0,1:T(8,128)(2,1)}) fusion(f32[2048,704]{0,1:T(8,128)} %fusion.121, f32[2048,704]{0,1:T(8,128)} %fusion.122, bf16[2048,2048]{1,0:T(8,128)(2,1)} %all-gather.34.cloned.1.call-done, bf16[704,2048]{1,0:T(8,128)(2,1)} %all-gather.32.cloned.1.call-done), kind=kOutput, calls=%fused_computation.14 | convolution fusion | flops 5927206912 | bytes 31457280 | tf_op jit(solution)/shard_map/dot_general | solution.py:68
  680.5 10.7 fusion.124
  691.2 13.7 convolution_add_fusion
  705.0 14.3 fusion.123
  719.4 101.7 %reduce-scatter.20.cloned.1.call-done = f32[256,2048]{1,0:T(8,128)} async-done(((f32[2048,2048]{1,0:T(8,128)}), f32[256,2048]{1,0:T(8,128)}) %reduce-scatter.20.cloned.1.call-update) | async-done | bytes 2097168 | tf_op jit(solution)/shard_map/reduce_scatter | solution.py:78
  824.5 116.4 %reduce-scatter.18.cloned.1.call-done = f32[256,2048]{1,0:T(8,128)} async-done(((f32[2048,2048]{1,0:T(8,128)}), f32[256,2048]{1,0:T(8,128)}) %reduce-scatter.18.cloned.1.call-update) | async-done | bytes 2097168 | tf_op jit(solution)/shard_map/reduce_scatter | solution.py:78
  940.9 5.7 fusion.113
  946.9 54.3 %all-gather.36.cloned.1.call-done = bf16[2048,2048]{1,0:T(8,128)(2,1)} async-done(((bf16[256,2048]{1,0:T(8,128)(2,1)}), bf16[2048,2048]{1,0:T(8,128)(2,1)}) %all-gather.36.cloned.1.call-update) | async-done | bytes 8388624 | tf_op jit(solution)/shard_map/all_gather | solution.py:74
  1001.2 6.1 fusion.125
  1016.5 10.6 all-gather.38.cloned.1.call-done
  1042.4 10.6 convolution_convert_fusion.2
  1053.1 10.5 convolution_convert_fusion
  1063.7 10.6 convolution_convert_fusion.1
  1075.5 6.8 convolution_convert_fusion.3
  1102.8 4.5 multiply_reduce_fusion
  1118.5 7.4 convolution_convert_fusion.6
  1127.7 7.0 convolution_convert_fusion.5
  1134.8 9.4 fusion.127
  1144.2 7.2 convolution_convert_fusion.4
  1151.5 9.5 fusion.126
  1161.0 18.9 %add_add_fusion = f32[2048,2048]{1,0:T(8,128)} fusion(f32[2048,2048]{1,0:T(8,128)} %fusion.126, f32[2048,2048]{1,0:T(8,128)} %fusion.127, bf16[2048,256]{0,1:T(8,128)(2,1)} %bitcast.164, bf16[2048,256]{1,0:T(8,128)(2,1)S(1)} %copy-done.44), kind=kOutput, calls=%fused_computation | convolution fusion | flops 2155872256 | bytes 52428800 | tf_op jit(solution)/shard_map/dot_general | solution.py:68
  1184.9 44.5 %reduce-scatter.34.cloned.1.call-done = bf16[512,704]{0,1:T(8,128)(2,1)} async-done(((bf16[2048,704]{0,1:T(8,128)(2,1)}), bf16[512,704]{0,1:T(8,128)(2,1)}) %reduce-scatter.34.cloned.1.call-update) | async-done | bytes 720912 | tf_op jit(solution)/shard_map/reduce_scatter | solution.py:365
  1231.8 26.9 %reduce-scatter.32.cloned.1.call-done = bf16[256,512]{1,0:T(8,128)(2,1)} async-done(((bf16[256,2048]{1,0:T(8,128)(2,1)}), bf16[256,512]{1,0:T(8,128)(2,1)}) %reduce-scatter.32.cloned.1.call-update) | async-done | bytes 262160 | tf_op jit(solution)/shard_map/reduce_scatter | solution.py:373
  1261.5 26.0 %reduce-scatter.26.cloned.1.call-done = bf16[512,256]{1,0:T(8,128)(2,1)} async-done(((bf16[2048,256]{1,0:T(8,128)(2,1)}), bf16[512,256]{1,0:T(8,128)(2,1)}) %reduce-scatter.26.cloned.1.call-update) | async-done | bytes 262160 | tf_op jit(solution)/shard_map/reduce_scatter | solution.py:356
  1289.5 26.0 %reduce-scatter.28.cloned.1.call-done = bf16[512,256]{1,0:T(8,128)(2,1)} async-done(((bf16[2048,256]{1,0:T(8,128)(2,1)}), bf16[512,256]{1,0:T(8,128)(2,1)}) %reduce-scatter.28.cloned.1.call-update) | async-done | bytes 262160 | tf_op jit(solution)/shard_map/reduce_scatter | solution.py:359
  1317.5 26.2 %reduce-scatter.30.cloned.1.call-done = bf16[512,256]{1,0:T(8,128)(2,1)} async-done(((bf16[2048,256]{1,0:T(8,128)(2,1)}), bf16[512,256]{1,0:T(8,128)(2,1)}) %reduce-scatter.30.cloned.1.call-update) | async-done | bytes 262160 | tf_op jit(solution)/shard_map/reduce_scatter | solution.py:362
  1345.7 116.1 %reduce-scatter.24.cloned.1.call-done = f32[256,2048]{1,0:T(8,128)} async-done(((f32[2048,2048]{1,0:T(8,128)}), f32[256,2048]{1,0:T(8,128)}) %reduce-scatter.24.cloned.1.call-update) | async-done | bytes 2097168 | tf_op jit(solution)/shard_map/reduce_scatter | solution.py:78
  1463.9 40.4 %all-reduce.2 = (f32[2048]{0:T(1024)}, f32[8,4,128]{2,1,0:T(4,128)}, f32[8,256]{1,0:T(8,128)}, f32[2048]{0:T(1024)}) all-reduce(f32[2048]{0:T(1024)S(1)} %get-tuple-element.153, f32[8,4,128]{2,1,0:T(4,128)S(1)} %maximum_dynamic-update-slice_fusion, ...), channel_id=1, replica_groups=mesh['fsdp'=4,'head'=4,'tensor'=2] {'fsdp','head','tensor'}, use_global_device_ids=true, to_apply=%region_29.30 | all-reduce | flops 10240 | bytes 81920 | tf_op jit(solution)/shard_map/psum | solution.py:380
  (329 shorter events, 162.4 us)
Async XLA Ops:
  7.2 33.6 %all-gather.22.cloned.1.call-start = ((), (), s32[]{:S(2)}) async-start(), calls=%async_computation.17 | async-start | bytes 1310720 | tf_op jit(solution)/shard_map/all_gather | solution.py:91
  9.0 88.2 %all-gather.14.cloned.1.call-start = ((), (), s32[]{:S(2)}) async-start(), calls=%async_computation.13 | async-start | bytes 9437184 | tf_op jit(solution)/shard_map/all_gather | solution.py:74
  11.1 14.5 copy-start.52
  13.7 113.7 %all-gather.16.cloned.1.call-start = ((), (), s32[]{:S(2)}) async-start(), calls=%async_computation.14 | async-start | bytes 1310720 | tf_op jit(solution)/shard_map/all_gather | solution.py:92
  14.5 142.3 %all-gather.20.cloned.1.call-start = ((), (), s32[]{:S(2)}) async-start(), calls=%async_computation.16 | async-start | bytes 1310720 | tf_op jit(solution)/shard_map/all_gather | solution.py:90
  15.3 174.6 %all-gather.18.cloned.1.call-start = ((), (), s32[]{:S(2)}) async-start(), calls=%async_computation.15 | async-start | bytes 3145728 | tf_op jit(solution)/shard_map/all_gather | solution.py:178
  25.6 145.2 %copy-start.25 = (f32[2048,64]{1,0:T(8,128)}, f32[2048,64]{1,0:T(8,128)S(1)}, u32[]{:S(2)}) copy-start(f32[2048,64]{1,0:T(8,128)S(1)} %get-tuple-element.197) | copy-start | bytes 1572868
  27.2 165.5 %copy-start.17 = (pred[512,1024]{1,0:T(8,128)(4,1)}, pred[512,1024]{1,0:T(8,128)(4,1)S(1)}, u32[]{:S(2)}) copy-start(pred[512,1024]{1,0:T(8,128)(4,1)S(1)} %fusion.46) | copy-start | bytes 1572868
  134.3 82.5 %reduce-scatter.14.cloned.1.call-start = ((), (), s32[]{:S(2)}) async-start(), calls=%async_computation.18 | async-start | bytes 6291456 | tf_op jit(solution)/shard_map/reduce_scatter | solution.py:203
  178.1 11.8 copy-start.49
  205.1 42.7 %all-gather.24.cloned.1.call-start = ((), (), s32[]{:S(2)}) async-start(), calls=%async_computation.19 | async-start | bytes 1310720 | tf_op jit(solution)/shard_map/all_gather | solution.py:97
  205.9 167.0 %reduce-scatter.16.cloned.1.call-start = ((), (), s32[]{:S(2)}) async-start(), calls=%async_computation.20 | async-start | bytes 18874368 | tf_op jit(solution)/shard_map/reduce_scatter | solution.py:78
  224.1 33.2 %copy-start.37 = (bf16[2048,2,128]{0,2,1:T(8,128)(2,1)}, bf16[2048,2,128]{0,2,1:T(8,128)(2,1)S(1)}, u32[]{:S(2)}) copy-start(bf16[2048,2,128]{0,2,1:T(8,128)(2,1)S(1)} %multiply_convert_fusion.9) | copy-start | bytes 3145732
  257.2 115.6 %copy-start.15 = (bf16[256,2048]{1,0:T(8,128)(2,1)S(1)}, bf16[256,2048]{1,0:T(8,128)(2,1)}, u32[]{:S(2)}) copy-start(bf16[256,2048]{1,0:T(8,128)(2,1)} %param.34) | copy-start | bytes 3145732
  257.2 118.9 %copy-start.47 = (f32[2048]{0:T(1024)S(1)}, f32[2048]{0:T(1024)}, u32[]{:S(2)}) copy-start(f32[2048]{0:T(1024)} %param.43) | copy-start | bytes 24580
  257.2 176.4 %all-gather.30.cloned.1.call-start = ((), (), s32[]{:S(2)}) async-start(), calls=%async_computation.23 | async-start | bytes 3604480 | tf_op jit(solution)/shard_map/all_gather | solution.py:94
  258.0 231.3 %all-gather.26.cloned.1.call-start = ((), (), s32[]{:S(2)}) async-start(), calls=%async_computation.21 | async-start | bytes 9437184 | tf_op jit(solution)/shard_map/all_gather | solution.py:74
  377.3 172.8 %all-gather.28.cloned.1.call-start = ((), (), s32[]{:S(2)}) async-start(), calls=%async_computation.22 | async-start | bytes 3604480 | tf_op jit(solution)/shard_map/all_gather | solution.py:93
  378.1 231.4 %all-gather.32.cloned.1.call-start = ((), (), s32[]{:S(2)}) async-start(), calls=%async_computation.24 | async-start | bytes 3604480 | tf_op jit(solution)/shard_map/all_gather | solution.py:100
  378.7 286.6 %all-gather.34.cloned.1.call-start = ((), (), s32[]{:S(2)}) async-start(), calls=%async_computation.26 | async-start | bytes 9437184 | tf_op jit(solution)/shard_map/all_gather | solution.py:74
  380.0 441.1 %reduce-scatter.20.cloned.1.call-start = ((), (), s32[]{:S(2)}) async-start(), calls=%async_computation.27 | async-start | bytes 18874368 | tf_op jit(solution)/shard_map/reduce_scatter | solution.py:78
  665.3 15.3 %copy-start.65 = (bf16[2048,704]{0,1:T(8,128)(2,1)S(1)}, bf16[2048,704]{0,1:T(8,128)(2,1)}, u32[]{:S(2)}) copy-start(bf16[2048,704]{0,1:T(8,128)(2,1)} %all-gather.28.cloned.1.call-done) | copy-start | bytes 8650756
  680.5 10.7 copy-start.67
  680.5 10.7 copy-start.66
  680.5 10.7 copy-start.64
  705.0 236.0 %reduce-scatter.18.cloned.1.call-start = ((), (), s32[]{:S(2)}) async-start(), calls=%async_computation.25 | async-start | bytes 18874368 | tf_op jit(solution)/shard_map/reduce_scatter | solution.py:78
  719.3 281.8 %all-gather.36.cloned.1.call-start = ((), (), s32[]{:S(2)}) async-start(), calls=%async_computation.28 | async-start | bytes 9437184 | tf_op jit(solution)/shard_map/all_gather | solution.py:74
  946.6 80.4 %all-gather.38.cloned.1.call-start = ((), (), s32[]{:S(2)}) async-start(), calls=%async_computation.29 | async-start | bytes 3145728 | tf_op jit(solution)/shard_map/all_gather | solution.py:262
  1012.3 14.8 copy-start.33
  1016.3 127.9 %reduce-scatter.22.cloned.1.call-start = ((), (), s32[]{:S(2)}) async-start(), calls=%async_computation.30 | async-start | bytes 3145728 | tf_op jit(solution)/shard_map/reduce_scatter | solution.py:325
  1016.5 14.6 copy-start.31
  1042.1 137.9 %reduce-scatter.38.cloned.1.call-start = ((), (), s32[]{:S(2)}) async-start(), calls=%async_computation.38 | async-start | bytes 3604480 | tf_op jit(solution)/shard_map/reduce_scatter | solution.py:376
  1053.0 129.4 %reduce-scatter.36.cloned.1.call-start = ((), (), s32[]{:S(2)}) async-start(), calls=%async_computation.37 | async-start | bytes 3604480 | tf_op jit(solution)/shard_map/reduce_scatter | solution.py:368
  1063.6 165.7 %reduce-scatter.34.cloned.1.call-start = ((), (), s32[]{:S(2)}) async-start(), calls=%async_computation.36 | async-start | bytes 3604480 | tf_op jit(solution)/shard_map/reduce_scatter | solution.py:365
  1074.3 184.4 %reduce-scatter.32.cloned.1.call-start = ((), (), s32[]{:S(2)}) async-start(), calls=%async_computation.35 | async-start | bytes 1310720 | tf_op jit(solution)/shard_map/reduce_scatter | solution.py:373
  1082.3 205.2 %reduce-scatter.26.cloned.1.call-start = ((), (), s32[]{:S(2)}) async-start(), calls=%async_computation.32 | async-start | bytes 1310720 | tf_op jit(solution)/shard_map/reduce_scatter | solution.py:356
  1125.9 189.5 %reduce-scatter.28.cloned.1.call-start = ((), (), s32[]{:S(2)}) async-start(), calls=%async_computation.33 | async-start | bytes 1310720 | tf_op jit(solution)/shard_map/reduce_scatter | solution.py:359
  1134.8 208.9 %reduce-scatter.30.cloned.1.call-start = ((), (), s32[]{:S(2)}) async-start(), calls=%async_computation.34 | async-start | bytes 1310720 | tf_op jit(solution)/shard_map/reduce_scatter | solution.py:362
  1151.5 310.3 %reduce-scatter.24.cloned.1.call-start = ((), (), s32[]{:S(2)}) async-start(), calls=%async_computation.31 | async-start | bytes 18874368 | tf_op jit(solution)/shard_map/reduce_scatter | solution.py:78
  1180.0 51.8 %copy-start.61 = (f32[2,128]{1,0:T(2,128)S(1)}, f32[2,128]{1,0:T(2,128)}, u32[]{:S(2)}) copy-start(f32[2,128]{1,0:T(2,128)} %get-tuple-element.155) | copy-start | bytes 3076
  1182.4 78.1 %copy-start.57 = (f32[2]{0:T(128)S(1)}, f32[2]{0:T(128)}, u32[]{:S(2)}) copy-start(f32[2]{0:T(128)} %copy-done.56) | copy-start | bytes 28
  1182.4 78.1 %copy-start.59 = (f32[2]{0:T(128)S(1)}, f32[2]{0:T(128)}, u32[]{:S(2)}) copy-start(f32[2]{0:T(128)} %copy-done.58) | copy-start | bytes 28
  1182.4 78.1 %copy-start.62 = (f32[2]{0:T(128)S(1)}, f32[2]{0:T(128)}, u32[]{:S(2)}) copy-start(f32[2]{0:T(128)} %get-tuple-element.179) | copy-start | bytes 28
  1184.9 276.9 %copy-start.16 = (bf16[256,2048]{1,0:T(8,128)(2,1)S(1)}, bf16[256,2048]{1,0:T(8,128)(2,1)}, u32[]{:S(2)}) copy-start(bf16[256,2048]{1,0:T(8,128)(2,1)} %param.34) | copy-start | bytes 3145732
  1184.9 276.9 %copy-start.48 = (f32[2048]{0:T(1024)S(1)}, f32[2048]{0:T(1024)}, u32[]{:S(2)}) copy-start(f32[2048]{0:T(1024)} %param.36) | copy-start | bytes 24580
  1184.9 276.9 %copy-start.53 = (f32[256]{0:T(256)S(1)}, f32[256]{0:T(256)}, u32[]{:S(2)}) copy-start(f32[256]{0:T(256)} %copy-done.52) | copy-start | bytes 3076
  1260.5 203.4 %copy-start.51 = (f32[2048]{0:T(1024)S(1)}, f32[2048]{0:T(1024)}, u32[]{:S(2)}) copy-start(f32[2048]{0:T(1024)} %get-tuple-element.151) | copy-start | bytes 24580
  1260.5 243.8 %copy-start.60 = (f32[256]{0:T(256)S(1)}, f32[256]{0:T(256)}, u32[]{:S(2)}) copy-start(f32[256]{0:T(256)} %get-tuple-element.203) | copy-start | bytes 3076
  (58 other events, 222.8 us)
Sparse Core Ops, SparseCore 0:
  10.2 30.6 all-gather.21
  43.3 53.9 all-gather.13
  99.4 27.9 all-gather.15
  129.4 27.4 all-gather.19
  158.8 10.0 all-gather.17
  205.2 11.6 reduce-scatter.13
  218.5 29.2 all-gather.23
  257.4 115.4 reduce-scatter.15
  374.5 59.1 all-gather.29
  436.1 53.1 all-gather.25
  490.9 59.1 all-gather.27
  551.6 57.8 all-gather.31
  612.1 53.1 all-gather.33
  705.1 115.9 reduce-scatter.19
  824.9 115.9 reduce-scatter.17
  946.8 54.3 all-gather.35
  1016.4 10.5 all-gather.37
  1042.2 10.7 reduce-scatter.21
  1055.3 57.3 reduce-scatter.37
  1114.9 56.0 reduce-scatter.35
  1173.3 56.0 reduce-scatter.33
  1231.6 26.9 reduce-scatter.31
  1261.6 25.7 reduce-scatter.25
  1289.6 25.7 reduce-scatter.27
  1317.8 25.7 reduce-scatter.29
  1347.1 114.6 reduce-scatter.23
where the time goes:
time: 1520 us
  waiting for transfers between devices  1070 us (70%)
  matrix products  255 us (17%)
  other arithmetic  84.2 us (6%)
  blocking collectives  47.3 us (3%)
  local copies, waits for them, and re-layouts  40.2 us (3%)
  between operations  16.9 us (1%)
    reduce_scatter x4, waiting for transfers between devices, scatter_rows(): lax.psum_scatter(values, ('head', 'tensor'), scatter_dimension=0, tiled=T...  449 us
    all_gather x4, waiting for transfers between devices, gather_rows(): return lax.all_gather(values, ('head', 'tensor'), axis=0, tiled=True)  222 us
    dot_general x7, matrix products, contract_last(): lax.dot_general(left_side, right_side, (((1,), (1,)), ((), ())), preferre...  83.6 us
    dot_general x7, matrix products, contract_first(): lax.dot_general(left_side, right_side, (((0,), (0,)), ((), ())), preferre...  60.2 us
    all_gather x1, waiting for transfers between devices, gather_weights(): lax.all_gather(up_weight, 'fsdp', axis=0, tiled=True)  53.6 us
    all_gather x1, waiting for transfers between devices, gather_weights(): lax.all_gather(gate_weight, 'fsdp', axis=0, tiled=True)  49.7 us
    all_gather x1, waiting for transfers between devices, gather_weights(): lax.all_gather(down_weight, 'fsdp', axis=1, tiled=True)  48.4 us
    reduce_scatter x1, waiting for transfers between devices, body(): lax.psum_scatter(gate_weight_grad.astype(jnp.bfloat16), 'fsdp', scatter_d...  44.5 us
  transfers between devices with their start and end apart: 26, of which 22 were waited for; matrix products, arithmetic and copies ran while one was open for 18% of the time, Pallas kernels for 0%

commit v1 on v0

v1 whole, which is shorter than its diff:
```python
import jax
import jax.numpy as jnp
from jax import lax
from jax.sharding import PartitionSpec as P

lambda_base = 0.2
attention_block = 512
low = jnp.bfloat16


def contract(left_side, right_side, left_dim, right_dim):
    return lax.dot_general(
        left_side,
        right_side,
        (((left_dim,), (right_dim,)), ((), ())),
        preferred_element_type=jnp.float32,
    )


def swap(values, axis, mask):
    size = lax.axis_size(axis)
    return lax.ppermute(values, axis, [(place, place ^ mask) for place in range(size)])


def shift(values, axis, step):
    size = lax.axis_size(axis)
    return lax.ppermute(values, axis, [(place, (place + step) % size) for place in range(size)])


def fsdp_gather(own):
    size = lax.axis_size("fsdp")
    shards = [own] + [None] * (size - 1)
    up, down = own, own
    for step in range(1, size // 2 + 1):
        up = shift(up, "fsdp", 1)
        shards[size - step] = up
        if step <= size - 1 - size // 2:
            down = shift(down, "fsdp", -1)
            shards[step] = down
    return shards


def fsdp_reduce(partial):
    size = lax.axis_size("fsdp")
    up_steps = size // 2
    down_steps = size - 1 - up_steps
    total = partial[0]
    carry = partial[up_steps].astype(low)
    for left in range(up_steps - 1, -1, -1):
        carry = shift(carry, "fsdp", 1).astype(jnp.float32)
        if left:
            carry = (carry + partial[left]).astype(low)
    total = total + carry
    if down_steps:
        carry = partial[size - down_steps].astype(low)
        for left in range(down_steps - 1, -1, -1):
            carry = shift(carry, "fsdp", -1).astype(jnp.float32)
            if left:
                carry = (carry + partial[size - left]).astype(low)
        total = total + carry
    return total


def group_gather(own):
    half = own.shape[0] // 2
    first = swap(own, "head", 1)
    second = swap(own, "head", 2)
    third_low = swap(second[:half], "head", 1)
    third_high = swap(first[half:], "head", 2)
    return jnp.concatenate([own, first, second, third_low, third_high], axis=0)


def group_reduce(partial, rows):
    half = rows // 2
    own, first, second, third = (partial[place * rows : (place + 1) * rows] for place in range(4))
    to_first = swap(third[:half].astype(low), "head", 1)
    to_second = swap(third[half:].astype(low), "head", 2)
    second = jnp.concatenate(
        [second[:half] + to_first.astype(jnp.float32), second[half:]], axis=0
    ).astype(low)
    first = jnp.concatenate(
        [first[:half], first[half:] + to_second.astype(jnp.float32)], axis=0
    ).astype(low)
    from_first = swap(first, "head", 1)
    from_second = swap(second, "head", 2)
    return own + from_first.astype(jnp.float32) + from_second.astype(jnp.float32)


def total_over_all(values):
    for axis in ("tensor", "head", "fsdp"):
        mask = 1
        while mask < lax.axis_size(axis):
            values = values + swap(values, axis, mask)
            mask *= 2
    return values


def rolled(values, start):
    twice = jnp.concatenate([values, values], axis=-1)
    return lax.dynamic_slice_in_dim(twice, start, values.shape[-1], values.ndim - 1)


def slot_layout(lengths, slots):
    first_end = lengths[0, 0]
    second_end = first_end + lengths[0, 1]
    segment = (slots >= first_end).astype(jnp.int32) + (slots >= second_end).astype(jnp.int32)
    start = jnp.where(segment == 0, 0, jnp.where(segment == 1, first_end, second_end))
    return segment, slots - start


def swap_halves(values):
    half = values.shape[1] // 2
    return jnp.concatenate([values[:, half:], values[:, :half]], axis=1)


def body(
    tokens,
    lengths,
    attention_gain,
    query_weight,
    key_weight,
    value_weight,
    output_weight,
    lambda_vectors,
    head_gain,
    feedforward_gain,
    gate_weight,
    up_weight,
    down_weight,
    cotangent,
):
    rows, width = tokens.shape
    fsdp_index = lax.axis_index("fsdp")
    head_index = lax.axis_index("head")
    core = lax.axis_index("tensor")
    shard = query_weight.shape[0]
    qk_width = query_weight.shape[3]
    value_half = value_weight.shape[2]
    value_width = 2 * value_half
    slots = rows * 8
    scale = qk_width ** (-0.5)
    column_start = fsdp_index * shard

    own_slots = (
        (jnp.arange(4, dtype=jnp.int32) ^ head_index)[:, None] * (2 * rows)
        + core * rows
        + jnp.arange(rows, dtype=jnp.int32)[None, :]
    ).reshape(-1)
    segment_own, position_own = slot_layout(lengths, own_slots)
    valid = (segment_own[:rows] < 2).astype(jnp.float32)[:, None]
    half_width = qk_width // 2
    frequency = 10000.0 ** (-jnp.arange(half_width, dtype=jnp.float32) / half_width)
    angles = position_own.astype(jnp.float32)[:, None] * frequency[None, :]
    cosine = jnp.cos(angles)
    sine = jnp.sin(angles)
    cosine = jnp.concatenate([cosine, cosine], axis=1)
    sine = jnp.concatenate([-sine, sine], axis=1)

    own_head = head_index * 2 + core
    vectors = lax.dynamic_slice_in_dim(lambda_vectors, own_head, 1, 0)[0]
    first_exp = jnp.exp(jnp.sum(vectors[0] * vectors[1]))
    second_exp = jnp.exp(jnp.sum(vectors[2] * vectors[3]))
    lambda_value = first_exp - second_exp + lambda_base
    own_coefficient = jnp.where(core == 0, 1.0, -lambda_value)
    other_coefficient = jnp.where(core == 0, -lambda_value, 1.0)
    gain_own = rolled(
        lax.dynamic_slice_in_dim(head_gain, own_head, 1, 0), core * value_half
    ) * (1.0 - lambda_base)

    tokens_wide = rolled(tokens, column_start).astype(jnp.float32)
    attention_gain = rolled(attention_gain, column_start)
    feedforward_gain = rolled(feedforward_gain, column_start)
    attention_scale = lax.rsqrt(jnp.mean(tokens_wide * tokens_wide, axis=-1, keepdims=True) + 1e-06)
    normed = group_gather((tokens_wide * attention_scale * attention_gain).astype(low))

    def by_head(weight, axis):
        return jnp.where(core == 0, weight, jnp.flip(weight, axis))

    mine = [
        by_head(weight, 1).reshape(shard, 2, -1)
        for weight in (query_weight, key_weight, value_weight)
    ]
    qkv_local = jnp.concatenate(
        [part[:, place] for place in range(2) for part in mine], axis=1
    )
    qkv_own = fsdp_gather(qkv_local)
    qkv_other = [swap(part, "tensor", 1) for part in qkv_own]
    third = 3 * qk_width

    def qkv_columns(own, other):
        pieces = [
            source[:, start + place * qk_width : start + (place + 1) * qk_width]
            for sources in (((own, 0), (other, third)), ((other, 0), (own, third)))
            for place in range(3)
            for source, start in sources
        ]
        return jnp.concatenate(pieces, axis=1)

    qkv_all = jnp.concatenate(
        [qkv_columns(own, other) for own, other in zip(qkv_own, qkv_other)], axis=0
    )

    output_local = by_head(output_weight, 0).reshape(2 * value_half, -1)
    output_own = fsdp_gather(output_local)
    output_other = [swap(part, "tensor", 1) for part in output_own]
    output_own = jnp.concatenate(output_own, axis=1)
    output_other = jnp.concatenate(output_other, axis=1)
    output_all = jnp.concatenate(
        [
            output_own[:value_half],
            output_other[value_half:],
            output_other[:value_half],
            output_own[value_half:],
        ],
        axis=0,
    )

    def hidden_rows(local):
        own = fsdp_gather(local)
        other = [swap(part, "tensor", 1) for part in own]
        return jnp.concatenate(
            [jnp.concatenate(own, axis=1), jnp.concatenate(other, axis=1)], axis=0
        )

    gate_all = hidden_rows(jnp.transpose(gate_weight))
    up_all = hidden_rows(jnp.transpose(up_weight))
    down_all = hidden_rows(down_weight)
    units = down_weight.shape[0]

    qkv = contract(normed, qkv_all, 1, 0)

    def rotate(part):
        return part * cosine + swap_halves(part) * sine

    def rotate_back(part):
        return part * cosine - swap_halves(part) * sine

    def finish(block):
        columns = [
            block[:, place * qk_width : (place + 1) * qk_width] for place in range(6)
        ]
        return jnp.concatenate(
            [
                rotate(columns[0]) * scale,
                rotate(columns[1]) * scale,
                rotate(columns[2]),
                rotate(columns[3]),
                columns[4],
                columns[5],
            ],
            axis=1,
        ).astype(low)

    head_columns = 2 * third
    qkv_kept = finish(qkv[:, :head_columns])
    qkv_received = swap(finish(qkv[:, head_columns:]), "tensor", 1)

    block_order = jnp.arange(8, dtype=jnp.int32)
    place_of = ((block_order & 1) ^ core) * 4 + ((block_order >> 1) ^ head_index)

    def in_order(kept, received):
        both = jnp.concatenate([kept, received], axis=0).reshape(8, rows, -1)
        return jnp.take(both, place_of, axis=0).reshape(slots, -1)

    slot_of_place = jnp.zeros((8,), jnp.int32).at[place_of].set(block_order)

    def by_place(ordered):
        both = jnp.take(ordered.reshape(8, rows, -1), slot_of_place, axis=0)
        return both[:4].reshape(slots // 2, -1), both[4:].reshape(slots // 2, -1)

    qkv_head = in_order(qkv_kept, qkv_received)
    queries = jnp.stack([qkv_head[:, :qk_width], qkv_head[:, qk_width : 2 * qk_width]])
    keys = jnp.stack(
        [qkv_head[:, 2 * qk_width : 3 * qk_width], qkv_head[:, 3 * qk_width : 4 * qk_width]]
    )
    values = qkv_head[:, 4 * qk_width :]
    segment, _ = slot_layout(lengths, jnp.arange(slots, dtype=jnp.int32))

    def allowed(start, stop):
        query_slot = jnp.arange(start, stop, dtype=jnp.int32)
        key_slot = jnp.arange(stop, dtype=jnp.int32)
        return (segment[start:stop, None] == segment[None, :stop]) & (
            key_slot[None, :] <= query_slot[:, None]
        )

    out_pieces, total_pieces = [], []
    for start in range(0, slots, attention_block):
        stop = start + attention_block
        scores = jnp.einsum(
            "mqe,mke->mqk",
            queries[:, start:stop],
            keys[:, :stop],
            preferred_element_type=jnp.float32,
        )
        scores = jnp.where(allowed(start, stop)[None], scores, -1e30)
        row_max = jnp.max(scores, axis=-1, keepdims=True)
        expanded = jnp.exp(scores - row_max)
        row_total = jnp.sum(expanded, axis=-1, keepdims=True)
        probability = (expanded / row_total).astype(low)
        out_pieces.append(
            jnp.einsum(
                "mqk,kv->mqv", probability, values[:stop], preferred_element_type=jnp.float32
            )
        )
        total_pieces.append(row_max + jnp.log(row_total))
    maps_out = jnp.concatenate(out_pieces, axis=1)
    log_total = jnp.concatenate(total_pieces, axis=1)
    mixed = maps_out[0] * own_coefficient + maps_out[1] * other_coefficient
    head_scale = lax.rsqrt(jnp.mean(mixed * mixed, axis=-1, keepdims=True) + 1e-05)
    head_out_kept, head_out_sent = by_place((mixed * head_scale * gain_own).astype(low))
    head_out = jnp.concatenate([head_out_kept, swap(head_out_sent, "tensor", 1)], axis=1)

    residual = tokens_wide + group_reduce(contract(head_out, output_all, 1, 0), rows)
    ffn_scale = lax.rsqrt(jnp.mean(residual * residual, axis=-1, keepdims=True) + 1e-06)
    ffn_in = group_gather((residual * ffn_scale * feedforward_gain).astype(low))
    ffn_out_grad = valid * rolled(cotangent, column_start).astype(jnp.float32)
    ffn_out_grad_all = group_gather(ffn_out_grad.astype(low))
    gate_pre = contract(gate_all, ffn_in, 1, 1)
    upward = contract(up_all, ffn_in, 1, 1)
    sigmoid_gate = jax.nn.sigmoid(gate_pre)
    silu_gate = gate_pre * sigmoid_gate
    hidden = (silu_gate * upward).astype(low)
    ffn_here = group_reduce(contract(hidden, down_all, 0, 0), rows)
    block_output = (valid * (residual + ffn_here)).astype(low)

    def shared(partial_all):
        own, other = partial_all[: partial_all.shape[0] // 2], partial_all[partial_all.shape[0] // 2 :]
        total = own + swap(other.astype(low), "tensor", 1).astype(jnp.float32)
        return fsdp_reduce(
            [total[:, start : start + shard] for start in range(0, width, shard)]
        )

    hidden_grad = contract(down_all, ffn_out_grad_all, 1, 1)
    down_grad = shared(contract(hidden, ffn_out_grad_all, 1, 0))
    gate_grad = (
        hidden_grad * upward * sigmoid_gate * (1.0 + gate_pre * (1.0 - sigmoid_gate))
    ).astype(low)
    up_grad = (hidden_grad * silu_gate).astype(low)
    ffn_in_grad = group_reduce(
        contract(gate_grad, gate_all, 0, 0) + contract(up_grad, up_all, 0, 0), rows
    )
    gate_weight_grad = jnp.transpose(shared(contract(gate_grad, ffn_in, 1, 0)))
    up_weight_grad = jnp.transpose(shared(contract(up_grad, ffn_in, 1, 0)))
    feedforward_gain_grad = jnp.sum(ffn_in_grad * residual * ffn_scale, axis=0)
    ffn_gained = ffn_in_grad * feedforward_gain
    residual_grad = (
        ffn_out_grad
        + ffn_scale * ffn_gained
        - residual * ffn_scale**3 * jnp.mean(ffn_gained * residual, axis=-1, keepdims=True)
    )

    attention_out_grad = group_gather(residual_grad.astype(low))
    head_out_grad_all = contract(attention_out_grad, output_all, 1, 1)
    head_out_grad = in_order(
        head_out_grad_all[:, :value_width].astype(low),
        swap(head_out_grad_all[:, value_width:].astype(low), "tensor", 1),
    ).astype(jnp.float32)
    output_grad = contract(head_out, attention_out_grad, 0, 0)
    output_grad = shared(
        jnp.concatenate(
            [
                output_grad[:value_half],
                output_grad[3 * value_half :],
                output_grad[2 * value_half : 3 * value_half],
                output_grad[value_half : 2 * value_half],
            ],
            axis=0,
        )
    )
    head_gain_part = jnp.sum(head_out_grad * mixed * head_scale, axis=0, keepdims=True) * (
        1.0 - lambda_base
    )
    weighted = head_out_grad * gain_own
    mixed_grad = head_scale * weighted - mixed * head_scale**3 * jnp.mean(
        weighted * mixed, axis=-1, keepdims=True
    )
    second_map = jnp.where(core == 1, maps_out[0], maps_out[1])
    lambda_grad = -jnp.sum(mixed_grad * second_map)
    vector_grads = lambda_grad * jnp.stack(
        [
            first_exp * vectors[1],
            first_exp * vectors[0],
            -second_exp * vectors[3],
            -second_exp * vectors[2],
        ]
    )
    map_grad = jnp.stack([mixed_grad * own_coefficient, mixed_grad * other_coefficient]).astype(low)
    query_pieces = []
    key_grad = jnp.zeros((2, slots, qk_width), jnp.float32)
    value_grad = jnp.zeros((slots, value_width), jnp.float32)
    for start in range(0, slots, attention_block):
        stop = start + attention_block
        scores = jnp.einsum(
            "mqe,mke->mqk",
            queries[:, start:stop],
            keys[:, :stop],
            preferred_element_type=jnp.float32,
        )
        scores = jnp.where(allowed(start, stop)[None], scores, -1e30)
        probability = jnp.exp(scores - log_total[:, start:stop])
        prob_grad = jnp.einsum(
            "mqv,kv->mqk",
            map_grad[:, start:stop],
            values[:stop],
            preferred_element_type=jnp.float32,
        )
        value_grad = value_grad.at[:stop].add(
            jnp.einsum(
                "mqk,mqv->kv",
                probability.astype(low),
                map_grad[:, start:stop],
                preferred_element_type=jnp.float32,
            )
        )
        delta_sum = jnp.sum(probability * prob_grad, axis=-1, keepdims=True)
        score_grad = (probability * (prob_grad - delta_sum)).astype(low)
        query_pieces.append(
            jnp.einsum("mqk,mke->mqe", score_grad, keys[:, :stop], preferred_element_type=jnp.float32)
        )
        key_grad = key_grad.at[:, :stop].add(
            jnp.einsum(
                "mqk,mqe->mke",
                score_grad,
                queries[:, start:stop],
                preferred_element_type=jnp.float32,
            )
        )
    query_grad = jnp.concatenate(query_pieces, axis=1)
    segment_all, position_all = slot_layout(lengths, jnp.arange(slots, dtype=jnp.int32))
    angles = position_all.astype(jnp.float32)[:, None] * frequency[None, :]
    cosine = jnp.concatenate([jnp.cos(angles)] * 2, axis=1)
    sine = jnp.concatenate([-jnp.sin(angles), jnp.sin(angles)], axis=1)
    qkv_grad = jnp.concatenate(
        [
            rotate_back(query_grad[0] * scale),
            rotate_back(query_grad[1] * scale),
            rotate_back(key_grad[0]),
            rotate_back(key_grad[1]),
            value_grad,
        ],
        axis=1,
    ).astype(low)
    qkv_grad_kept, qkv_grad_sent = by_place(qkv_grad)
    qkv_grad = jnp.concatenate([qkv_grad_kept, swap(qkv_grad_sent, "tensor", 1)], axis=1)

    normed_partial = contract(qkv_grad, qkv_all, 1, 1)
    attention_gain_part = jnp.sum(normed_partial * normed.astype(jnp.float32), axis=0)
    back = width - column_start
    attention_gain_grad = total_over_all(rolled(attention_gain_part / attention_gain, back))
    normed_grad = group_reduce(normed_partial, rows)
    qkv_weight_grad = contract(normed, qkv_grad, 0, 0)
    columns = [
        qkv_weight_grad[:, place * qk_width : (place + 1) * qk_width] for place in range(12)
    ]
    own_terms = jnp.concatenate([columns[k] for k in (0, 2, 4, 7, 9, 11)], axis=1)
    other_terms = jnp.concatenate([columns[k] for k in (6, 8, 10, 1, 3, 5)], axis=1)
    own_terms = own_terms + swap(other_terms.astype(low), "tensor", 1).astype(jnp.float32)
    qkv_weight_grad = fsdp_reduce(
        [own_terms[start : start + shard] for start in range(0, width, shard)]
    ).reshape(shard, 2, 3, qk_width)
    qkv_weight_grad = by_head(qkv_weight_grad, 1)
    output_grad = by_head(output_grad.reshape(2, value_half, -1), 0)

    attention_gained = normed_grad * attention_gain
    tokens_grad = (
        residual_grad
        + attention_scale * attention_gained
        - tokens_wide
        * attention_scale**3
        * jnp.mean(attention_gained * tokens_wide, axis=-1, keepdims=True)
    )

    lambda_full = lax.dynamic_update_slice(
        jnp.zeros(lambda_vectors.shape, jnp.float32), vector_grads[None], (own_head, 0, 0)
    )
    gain_full = lax.dynamic_update_slice(
        jnp.zeros(head_gain.shape, jnp.float32),
        rolled(head_gain_part, core * value_half),
        (own_head, 0),
    )
    small = total_over_all(
        jnp.concatenate(
            [
                rolled(feedforward_gain_grad, back),
                lambda_full.reshape(-1),
                gain_full.reshape(-1),
            ]
        )
    )
    feedforward_gain_grad = small[:width]
    lambda_grads = small[width : width + lambda_full.size].reshape(lambda_full.shape)
    gain_grads = small[width + lambda_full.size :].reshape(gain_full.shape)
    return (
        rolled(block_output, back),
        rolled(tokens_grad, back),
        attention_gain_grad,
        qkv_weight_grad[:, :, 0].reshape(query_weight.shape),
        qkv_weight_grad[:, :, 1].reshape(key_weight.shape),
        qkv_weight_grad[:, :, 2].reshape(value_weight.shape),
        output_grad.reshape(output_weight.shape),
        lambda_grads,
        gain_grads,
        feedforward_gain_grad,
        gate_weight_grad,
        up_weight_grad,
        down_grad,
    )


def solution(mesh):
    placed = (
        P(("fsdp", "head", "tensor"), None),
        P("fsdp", None),
        P(),
        P("fsdp", "head", "tensor", None),
        P("fsdp", "head", "tensor", None),
        P("fsdp", "head", "tensor"),
        P("head", "tensor", "fsdp"),
        P(),
        P(),
        P(),
        P("fsdp", ("head", "tensor")),
        P("fsdp", ("head", "tensor")),
        P(("head", "tensor"), "fsdp"),
        P(("fsdp", "head", "tensor"), None),
    )
    return jax.shard_map(
        body,
        mesh=mesh,
        in_specs=placed,
        out_specs=(
            P(("fsdp", "head", "tensor"), None),
            P(("fsdp", "head", "tensor"), None),
            P(),
            P("fsdp", "head", "tensor", None),
            P("fsdp", "head", "tensor", None),
            P("fsdp", "head", "tensor"),
            P("head", "tensor", "fsdp"),
            P(),
            P(),
            P(),
            P("fsdp", ("head", "tensor")),
            P("fsdp", ("head", "tensor")),
            P(("head", "tensor"), "fsdp"),
        ),
        check_vma=False,
    )
```

time: 1520 us -> 952 us (0.63)
  waiting for transfers between devices: 1070 us -> 275 us
  starting transfers between devices: 2.13 us -> 120 us
  local copies, waits for them, and re-layouts: 40.2 us -> 157 us
  other arithmetic: 84.2 us -> 141 us
  blocking collectives: 47.3 us -> 0 us
    reduce_scatter x13 -> x0, waiting for transfers between devices: 609 us -> none  [the longest x4 449 us: scatter_rows(): lax.psum_scatter(values, ('head', 'tensor'), scatter_dimension=0, tiled=T...]
    all_gather x13 -> x0, waiting for transfers between devices: 458 us -> none  [the longest x4 222 us: gather_rows(): return lax.all_gather(values, ('head', 'tensor'), axis=0, tiled=True)]
    ppermute x0 -> x101, waiting for transfers between devices: none -> 275 us  [the longest x30 168 us: shift(): lax.ppermute(values, axis, [(place, (place + step) % size) for place in r...]
    ppermute x0 -> x101, starting transfers between devices: none -> 120 us  [the longest x30 74.1 us: shift(): lax.ppermute(values, axis, [(place, (place + step) % size) for place in r...]
    psum x3 -> x0, blocking collectives: 47.3 us -> none  [the longest x1 40.4 us: body(): lax.psum((attention_gain_grad, feedforward_gain_grad, lambda_full, gain_f...]
    slice x6 -> x38, local copies, waits for them, and re-layouts: 3.53 us -> 45 us  [the longest x3 9.15 us: shared(): partial_all[partial_all.shape[0] // 2:]]
    unnamed x167 -> x415, local copies, waits for them, and re-layouts: 27.8 us -> 62.2 us
    unnamed x6 -> x19, other arithmetic: 0.01 us -> 25.6 us
  transfers between devices with their start and end apart: 26 -> 101, of which waited for: 22 -> 36; matrix products, arithmetic and copies ran while one was open for 18% -> 44% of each run, Pallas kernels for 0% -> 0%
where the time goes in v1:
time: 952 us; the launch traced here: 943 us
  waiting for transfers between devices  275 us (29%)
  matrix products  243 us (26%)
  local copies, waits for them, and re-layouts  157 us (16%)
  other arithmetic  141 us (15%)
  starting transfers between devices  120 us (13%)
    dot_general x15, matrix products, contract(): lax.dot_general(left_side, right_side, (((left_dim,), (right_dim,)), ((),...  198 us
    ppermute x30, waiting for transfers between devices, shift(): lax.ppermute(values, axis, [(place, (place + step) % size) for place in r...  168 us
    ppermute x71, waiting for transfers between devices, swap(): lax.ppermute(values, axis, [(place, place ^ mask) for place in range(size)])  107 us
    ppermute x30, starting transfers between devices, shift(): lax.ppermute(values, axis, [(place, (place + step) % size) for place in r...  74.1 us
    unnamed x415, local copies, waits for them, and re-layouts  62.2 us
    ppermute x71, starting transfers between devices, swap(): lax.ppermute(values, axis, [(place, place ^ mask) for place in range(size)])  45.4 us
    another operation x11, other arithmetic  28.4 us
    unnamed x19, other arithmetic  25.6 us
  transfers between devices with their start and end apart: 101, of which 36 were waited for; matrix products, arithmetic and copies ran while one was open for 44% of the time, Pallas kernels for 0%

profile of v1, /device:TPU:0, one launch (start us, length us, event | category | flops | bytes accessed | tf_op | source)
XLA Modules:
  0.0 942.7 jit_solution(963722923282336669)
XLA Ops:
  40.8 13.4 %collective-permute-start.13 = (bf16[256,512]{1,0:T(8,128)(2,1)}, bf16[256,512]{1,0:T(8,128)(2,1)}, u32[]{:S(2)}, u32[]{:S(2)}) collective-permute-start(bf16[256,512]{1,0:T(8,128)(2,1)} %bitcast.25), channel_id=1, source_target_pairs={{0,24},{8,0},{16,8},{24,16},{1,25},{9,1},{17,9},{25,17},{2,26},{10... | collective-permute-start | bytes 786440 | tf_op jit(solution)/shard_map/ppermute | solution.py:27
  63.1 7.5 collective-permute-done.2
  78.7 14.4 %collective-permute-done.8 = bf16[512,768]{1,0:T(8,128)(2,1)S(1)} collective-permute-done((bf16[512,768]{1,0:T(8,128)(2,1)}, bf16[512,768]{1,0:T(8,128)(2,1)S(1)}, u32[]{:S(2)}, u32[]{:S(2)}) %collective-permute-start.8) | collective-permute-done | bytes 786464 | tf_op jit(solution)/shard_map/ppermute | solution.py:27
  108.0 9.5 %fusion.265 = (bf16[1024,1536]{1,0:T(8,128)(2,1)}, f32[1024,1536]{1,0:T(8,128)S(1)}) fusion(bf16[1024,2048]{1,0:T(8,128)(2,1)S(1)} %constant_dynamic-update-slice_fusion, bf16[512,1536]{1,0:T(8,128)(2,1)S(1)} %constant_dynamic-update-slice_fusion.47, bf16[512,1536]{1,0:T(8,128)(2,1)} %constant_dynamic-update-slice_fusion.35, ...), kind=kOutput, calls=%fused_computation.577 | convolution fusion | flops 6469189632 | bytes 19922944 | tf_op jit(solution)/shard_map/dot_general | solution.py:12
  132.6 6.9 collective-permute-done.15
  147.6 4.3 gather_fusion
  189.3 5.8 fusion.153
  197.9 4.2 collective-permute-done.20
  217.5 21.1 %collective-permute-done.56 = bf16[128,2048]{1,0:T(8,128)(2,1)S(1)} collective-permute-done((bf16[128,2048]{1,0:T(8,128)(2,1)S(1)}, bf16[128,2048]{1,0:T(8,128)(2,1)S(1)}, u32[]{:S(2)}, u32[]{:S(2)}) %collective-permute-start.56) | collective-permute-done | bytes 524320 | tf_op jit(solution)/shard_map/ppermute | solution.py:22
  239.4 4.5 collective-permute-done.44
  254.5 19.0 %fusion.227 = f32[1408,1024]{1,0:T(8,128)} fusion(bf16[1024,2048]{1,0:T(8,128)(2,1)} %constant_dynamic-update-slice_fusion.68, bf16[704,512]{1,0:T(8,128)(2,1)} %copy-done.147, bf16[704,512]{1,0:T(8,128)(2,1)} %copy-done.149, bf16[704,512]{1,0:T(8,128)(2,1)} %copy-done.148, bf16[704,512]{1,0:T(8,128)(2,1)} %copy-done.146, ...), kind=kOutput, calls=%fused_computation.543 | convolution fusion | flops 5951717376 | bytes 15728640 | tf_op jit(solution)/shard_map/dot_general | solution.py:12
  287.7 8.1 collective-permute-done.25
  295.7 15.3 %collective-permute-done.37 = bf16[704,512]{1,0:T(8,128)(2,1)S(1)} collective-permute-done((bf16[704,512]{1,0:T(8,128)(2,1)}, bf16[704,512]{1,0:T(8,128)(2,1)S(1)}, u32[]{:S(2)}, u32[]{:S(2)}) %collective-permute-start.37) | collective-permute-done | bytes 720928 | tf_op jit(solution)/shard_map/ppermute | solution.py:27
  311.1 12.9 %collective-permute-start.26 = (bf16[704,512]{1,0:T(8,128)(2,1)S(1)}, bf16[704,512]{1,0:T(8,128)(2,1)}, u32[]{:S(2)}, u32[]{:S(2)}) collective-permute-start(bf16[704,512]{1,0:T(8,128)(2,1)S(1)} %collective-permute-done.25), channel_id=1, source_target_pairs={{0,8},{8,16},{16,24},{24,0},{1,9},{9,17},{17,25},{25,1},{2,10},{10... | collective-permute-start | bytes 2162696 | tf_op jit(solution)/shard_map/ppermute | solution.py:27
  327.7 13.1 %collective-permute-done.26 = bf16[704,512]{1,0:T(8,128)(2,1)} collective-permute-done((bf16[704,512]{1,0:T(8,128)(2,1)S(1)}, bf16[704,512]{1,0:T(8,128)(2,1)}, u32[]{:S(2)}, u32[]{:S(2)}) %collective-permute-start.26) | collective-permute-done | bytes 720928 | tf_op jit(solution)/shard_map/ppermute | solution.py:27
  340.9 17.2 %fusion.230 = f32[1408,1024]{1,0:T(8,128)} fusion(bf16[1024,2048]{1,0:T(8,128)(2,1)} %constant_dynamic-update-slice_fusion.63, bf16[704,512]{1,0:T(8,128)(2,1)} %copy-done.152, bf16[704,512]{1,0:T(8,128)(2,1)} %collective-permute-done.40, bf16[704,512]{1,0:T(8,128)(2,1)} %copy-done.154, bf16[704,512]{1,0:T(8,128)(2,1)} %collective-permute-done.38, ...), kind=kOutput, calls=%fused_computation.546 | convolution fusion | flops 5951717376 | bytes 15728640 | tf_op jit(solution)/shard_map/dot_general | solution.py:12
  358.1 25.1 %multiply_convert_fusion.3 = (bf16[1408,1024]{1,0:T(8,128)(2,1)}, bf16[1408,1024]{1,0:T(8,128)(2,1)}, bf16[1408,1024]{1,0:T(8,128)(2,1)}) fusion(f32[1408,1024]{1,0:T(8,128)} %fusion.227, f32[1408,1024]{1,0:T(8,128)} %fusion.230, bf16[1024,2048]{1,0:T(8,128)(2,1)S(1)} %copy-done.89, bf16[704,512]{1,0:T(8,128)(2,1)} %collective-permute-done.30, ...), kind=kOutput, calls=%fused_computation.30 | convolution fusion | flops 5973344256 | bytes 30146560 | tf_op jit(solution)/shard_map/dot_general | solution.py:12
  383.3 10.9 %fusion.272 = f32[1408,2048]{1,0:T(8,128)} fusion(bf16[1408,1024]{1,0:T(8,128)(2,1)} %get-tuple-element.192, bf16[1024,2048]{1,0:T(8,128)(2,1)S(1)} %copy-done.89), kind=kOutput, calls=%fused_computation.584 | convolution fusion | flops 5905580032 | bytes 18612224 | tf_op jit(solution)/shard_map/dot_general | solution.py:12
  394.2 27.6 %fusion.229 = f32[1024,2048]{1,0:T(8,128)} fusion(bf16[1408,1024]{1,0:T(8,128)(2,1)S(1)} %copy-done.156, bf16[704,512]{1,0:T(8,128)(2,1)S(1)} %copy-done.153, bf16[704,512]{1,0:T(8,128)(2,1)} %collective-permute-done.40, bf16[704,512]{1,0:T(8,128)(2,1)S(1)} %copy-done.155, bf16[704,512]{1,0:T(8,128)(2,1)} %collective-permute-done.38, ...), kind=kOutput, calls=%fused_computation.545 | convolution fusion | flops 5951717376 | bytes 17039360 | tf_op jit(solution)/shard_map/dot_general | solution.py:12
  421.8 22.7 %fusion.267 = (bf16[1024,2048]{1,0:T(8,128)(2,1)}, f32[1024,2048]{1,0:T(8,128)}) fusion(f32[1024,2048]{1,0:T(8,128)} %fusion.229, bf16[1408,1024]{1,0:T(8,128)(2,1)} %get-tuple-element.192, bf16[704,512]{1,0:T(8,128)(2,1)} %collective-permute-done.30, bf16[704,512]{1,0:T(8,128)(2,1)} %collective-permute-done.29, ...), kind=kOutput, calls=%fused_computation.579 | convolution fusion | flops 5955911680 | bytes 29622272 | tf_op jit(solution)/shard_map/dot_general | solution.py:12
  447.9 17.4 %fusion.268 = (bf16[1024,2048]{1,0:T(8,128)(2,1)}, f32[1024,2048]{1,0:T(8,128)}) fusion(bf16[1408,1024]{1,0:T(8,128)(2,1)} %get-tuple-element.194, bf16[704,512]{1,0:T(8,128)(2,1)} %copy-done.147, bf16[704,512]{1,0:T(8,128)(2,1)} %copy-done.149, bf16[704,512]{1,0:T(8,128)(2,1)} %copy-done.148, bf16[704,512]{1,0:T(8,128)(2,1)} %copy-done.146, ...), kind=kOutput, calls=%fused_computation.580 | convolution fusion | flops 5953814528 | bytes 21233664 | tf_op jit(solution)/shard_map/dot_general | solution.py:12
  469.6 4.6 slice.1791
  477.6 4.4 collective-permute-done.49
  487.2 8.3 fusion.273
  497.7 6.8 collective-permute-done.60
  505.9 19.9 %collective-permute-done.52 = bf16[256,2048]{1,0:T(8,128)(2,1)S(1)} collective-permute-done((bf16[256,2048]{1,0:T(8,128)(2,1)S(1)}, bf16[256,2048]{1,0:T(8,128)(2,1)S(1)}, u32[]{:S(2)}, u32[]{:S(2)}) %collective-permute-start.52) | collective-permute-done | bytes 1048608 | tf_op jit(solution)/shard_map/ppermute | solution.py:22
  534.7 8.0 fusion.274
  547.3 10.2 %collective-permute-done.62 = bf16[256,2048]{1,0:T(8,128)(2,1)S(1)} collective-permute-done((bf16[256,2048]{1,0:T(8,128)(2,1)S(1)}, bf16[256,2048]{1,0:T(8,128)(2,1)S(1)}, u32[]{:S(2)}, u32[]{:S(2)}) %collective-permute-start.62) | collective-permute-done | bytes 1048608 | tf_op jit(solution)/shard_map/ppermute | solution.py:22
  561.2 4.7 fusion.233
  570.0 4.7 fusion.232
  576.0 3.8 collective-permute-start.96
  579.8 6.3 fusion.231
  599.8 4.5 collective-permute-done.90
  606.7 28.5 %collective-permute-done.94 = bf16[704,512]{1,0:T(8,128)(2,1)S(1)} collective-permute-done((bf16[704,512]{1,0:T(8,128)(2,1)}, bf16[704,512]{1,0:T(8,128)(2,1)S(1)}, u32[]{:S(2)}, u32[]{:S(2)}) %collective-permute-start.94) | collective-permute-done | bytes 720928 | tf_op jit(solution)/shard_map/ppermute | solution.py:27
  636.3 10.5 %collective-permute-done.98 = bf16[704,512]{1,0:T(8,128)(2,1)S(1)} collective-permute-done((bf16[704,512]{1,0:T(8,128)(2,1)S(1)}, bf16[704,512]{1,0:T(8,128)(2,1)S(1)}, u32[]{:S(2)}, u32[]{:S(2)}) %collective-permute-start.98) | collective-permute-done | bytes 720928 | tf_op jit(solution)/shard_map/ppermute | solution.py:27
  663.5 4.0 multiply_reduce_fusion.1
  723.9 4.1 fusion.125
  767.1 3.8 collective-permute-start.83
  770.9 6.4 collective-permute-done.95
  777.3 13.1 %collective-permute-start.81 = (bf16[256,512]{1,0:T(8,128)(2,1)S(1)}, bf16[256,512]{1,0:T(8,128)(2,1)S(1)}, u32[]{:S(2)}, u32[]{:S(2)}) collective-permute-start(bf16[256,512]{1,0:T(8,128)(2,1)S(1)} %get-tuple-element.276), channel_id=1, source_target_pairs={{0,8},{8,16},{16,24},{24,0},{1,9},{9,17},{17,25},{25,1},{2,10},{10... | collective-permute-start | bytes 786440 | tf_op jit(solution)/shard_map/ppermute | solution.py:27
  793.4 23.0 %collective-permute-done.81 = bf16[256,512]{1,0:T(8,128)(2,1)S(1)} collective-permute-done((bf16[256,512]{1,0:T(8,128)(2,1)S(1)}, bf16[256,512]{1,0:T(8,128)(2,1)S(1)}, u32[]{:S(2)}, u32[]{:S(2)}) %collective-permute-start.81) | collective-permute-done | bytes 262176 | tf_op jit(solution)/shard_map/ppermute | solution.py:27
  819.4 5.3 collective-permute-done.82
  826.0 13.7 %multiply_reduce_fusion = (f32[2048]{0:T(1024)S(1)}, bf16[1024,2048]{1,0:T(8,128)(2,1)}, f32[1024,2048]{1,0:T(8,128)}) fusion(bf16[1024,2048]{1,0:T(8,128)(2,1)} %copy-done.93, bf16[512,1536]{1,0:T(8,128)(2,1)} %copy-done.122, bf16[512,1536]{1,0:T(8,128)(2,1)} %constant_dynamic-update-slice_fusion.35, bf16[512,1536]{1,0:T(8,128)(2,1)} %copy-done.121, ...), kind=kOutput, calls=%fused_computation.5 | convolution fusion | flops 6482294784 | bytes 26222592 | tf_op jit(solution)/shard_map/dot_general | solution.py:12
  843.3 11.2 %fusion.269 = (bf16[2048,1536]{0,1:T(8,128)(2,1)S(1)}, f32[2048,1536]{0,1:T(8,128)}) fusion(bf16[1024,2048]{1,0:T(8,128)(2,1)S(1)} %copy-done.94, bf16[1024,768]{1,0:T(8,128)(2,1)} %copy-done.139, bf16[1024,768]{1,0:T(8,128)(2,1)S(1)} %bitcast.238), kind=kOutput, calls=%fused_computation.581 | convolution fusion | flops 6451888128 | bytes 26214400 | tf_op jit(solution)/shard_map/dot_general | solution.py:12
  882.6 11.5 %collective-permute-done.70 = bf16[256,2048]{1,0:T(8,128)(2,1)S(1)} collective-permute-done((bf16[256,2048]{1,0:T(8,128)(2,1)S(1)}, bf16[256,2048]{1,0:T(8,128)(2,1)S(1)}, u32[]{:S(2)}, u32[]{:S(2)}) %collective-permute-start.70) | collective-permute-done | bytes 1048608 | tf_op jit(solution)/shard_map/ppermute | solution.py:22
  906.2 13.4 %collective-permute-done.79 = bf16[512,768]{0,1:T(8,128)(2,1)S(1)} collective-permute-done((bf16[512,768]{0,1:T(8,128)(2,1)S(1)}, bf16[512,768]{0,1:T(8,128)(2,1)S(1)}, u32[]{:S(2)}, u32[]{:S(2)}) %collective-permute-start.79) | collective-permute-done | bytes 786464 | tf_op jit(solution)/shard_map/ppermute | solution.py:27
  919.6 13.0 %collective-permute-done.78 = bf16[512,768]{0,1:T(8,128)(2,1)S(1)} collective-permute-done((bf16[512,768]{0,1:T(8,128)(2,1)S(1)}, bf16[512,768]{0,1:T(8,128)(2,1)S(1)}, u32[]{:S(2)}, u32[]{:S(2)}) %collective-permute-start.78) | collective-permute-done | bytes 786464 | tf_op jit(solution)/shard_map/ppermute | solution.py:27
  933.7 7.2 rev.27
  (824 shorter events, 399.2 us)
Async XLA Ops:
  6.4 52.3 %collective-permute-start = (bf16[256,2048]{1,0:T(8,128)(2,1)}, bf16[256,2048]{1,0:T(8,128)(2,1)}, u32[]{:S(2)}, u32[]{:S(2)}) collective-permute-start(bf16[256,2048]{1,0:T(8,128)(2,1)} %get-tuple-element.189), channel_id=1, source_target_pairs={{0,2},{2,0},{4,6},{6,4},{1,3},{3,1},{5,7},{7,5},{8,10},{10,8},{12,... | collective-permute-start | bytes 3145736 | tf_op jit(solution)/shard_map/ppermute | solution.py:22
  9.3 45.8 %collective-permute-start.1 = (bf16[256,2048]{1,0:T(8,128)(2,1)}, bf16[256,2048]{1,0:T(8,128)(2,1)}, u32[]{:S(2)}, u32[]{:S(2)}) collective-permute-start(bf16[256,2048]{1,0:T(8,128)(2,1)} %get-tuple-element.189), channel_id=1, source_target_pairs={{0,4},{2,6},{4,0},{6,2},{1,5},{3,7},{5,1},{7,3},{8,12},{10,14},{12... | collective-permute-start | bytes 3145736 | tf_op jit(solution)/shard_map/ppermute | solution.py:22
  16.8 40.3 %collective-permute-start.5 = (bf16[512,768]{1,0:T(8,128)(2,1)}, bf16[512,768]{1,0:T(8,128)(2,1)}, u32[]{:S(2)}, u32[]{:S(2)}) collective-permute-start(bf16[512,768]{1,0:T(8,128)(2,1)} %constant_dynamic-update-slice_fusion.5), channel_id=1, source_target_pairs={{0,24},{8,0},{16,8},{24,16},{1,25},{9,1},{17,9},{25,17},{2,26},{10... | collective-permute-start | bytes 2359304 | tf_op jit(solution)/shard_map/ppermute | solution.py:27
  33.6 95.6 %collective-permute-start.14 = (bf16[256,512]{1,0:T(8,128)(2,1)}, bf16[256,512]{1,0:T(8,128)(2,1)}, u32[]{:S(2)}, u32[]{:S(2)}) collective-permute-start(bf16[256,512]{1,0:T(8,128)(2,1)} %bitcast.25), channel_id=1, source_target_pairs={{0,8},{8,16},{16,24},{24,0},{1,9},{9,17},{17,25},{25,1},{2,10},{10... | collective-permute-start | bytes 786440 | tf_op jit(solution)/shard_map/ppermute | solution.py:27
  40.8 90.5 %collective-permute-start.13 = (bf16[256,512]{1,0:T(8,128)(2,1)}, bf16[256,512]{1,0:T(8,128)(2,1)}, u32[]{:S(2)}, u32[]{:S(2)}) collective-permute-start(bf16[256,512]{1,0:T(8,128)(2,1)} %bitcast.25), channel_id=1, source_target_pairs={{0,24},{8,0},{16,8},{24,16},{1,25},{9,1},{17,9},{25,17},{2,26},{10... | collective-permute-start | bytes 786440 | tf_op jit(solution)/shard_map/ppermute | solution.py:27
  70.7 61.2 %collective-permute-start.16 = (bf16[256,512]{1,0:T(8,128)(2,1)}, bf16[256,512]{1,0:T(8,128)(2,1)S(1)}, u32[]{:S(2)}, u32[]{:S(2)}) collective-permute-start(bf16[256,512]{1,0:T(8,128)(2,1)} %bitcast.25), channel_id=1, source_target_pairs={{0,1},{1,0},{2,3},{3,2},{4,5},{5,4},{6,7},{7,6},{8,9},{9,8},{10,11... | collective-permute-start | bytes 786440 | tf_op jit(solution)/shard_map/ppermute | solution.py:22
  93.1 112.7 %collective-permute-start.53 = (bf16[256,2048]{1,0:T(8,128)(2,1)}, bf16[256,2048]{1,0:T(8,128)(2,1)}, u32[]{:S(2)}, u32[]{:S(2)}) collective-permute-start(bf16[256,2048]{1,0:T(8,128)(2,1)} %get-tuple-element.177), channel_id=1, source_target_pairs={{0,2},{2,0},{4,6},{6,4},{1,3},{3,1},{5,7},{7,5},{8,10},{10,8},{12,... | collective-permute-start | bytes 3145736 | tf_op jit(solution)/shard_map/ppermute | solution.py:22
  131.3 63.7 %collective-permute-start.54 = (bf16[256,2048]{1,0:T(8,128)(2,1)}, bf16[256,2048]{1,0:T(8,128)(2,1)}, u32[]{:S(2)}, u32[]{:S(2)}) collective-permute-start(bf16[256,2048]{1,0:T(8,128)(2,1)} %get-tuple-element.177), channel_id=1, source_target_pairs={{0,4},{2,6},{4,0},{6,2},{1,5},{3,7},{5,1},{7,3},{8,12},{10,14},{12... | collective-permute-start | bytes 3145736 | tf_op jit(solution)/shard_map/ppermute | solution.py:22
  141.9 67.9 %collective-permute-start.43 = (bf16[704,512]{1,0:T(8,128)(2,1)}, bf16[704,512]{1,0:T(8,128)(2,1)}, u32[]{:S(2)}, u32[]{:S(2)}) collective-permute-start(bf16[704,512]{1,0:T(8,128)(2,1)} %param.50), channel_id=1, source_target_pairs={{0,8},{8,16},{16,24},{24,0},{1,9},{9,17},{17,25},{25,1},{2,10},{10... | collective-permute-start | bytes 2162696 | tf_op jit(solution)/shard_map/ppermute | solution.py:27
  142.6 40.4 %collective-permute-start.19 = (bf16[256,512]{1,0:T(8,128)(2,1)}, bf16[256,512]{1,0:T(8,128)(2,1)S(1)}, u32[]{:S(2)}, u32[]{:S(2)}) collective-permute-start(bf16[256,512]{1,0:T(8,128)(2,1)} %collective-permute-done.14), channel_id=1, source_target_pairs={{0,1},{1,0},{2,3},{3,2},{4,5},{5,4},{6,7},{7,6},{8,9},{9,8},{10,11... | collective-permute-start | bytes 786440 | tf_op jit(solution)/shard_map/ppermute | solution.py:22
  203.5 40.5 %collective-permute-start.23 = (bf16[256,2048]{1,0:T(8,128)(2,1)S(1)}, bf16[256,2048]{1,0:T(8,128)(2,1)S(1)}, u32[]{:S(2)}, u32[]{:S(2)}) collective-permute-start(bf16[256,2048]{1,0:T(8,128)(2,1)S(1)} %pad_maximum_fusion.14), channel_id=1, source_target_pairs={{0,4},{2,6},{4,0},{6,2},{1,5},{3,7},{5,1},{7,3},{8,12},{10,14},{12... | collective-permute-start | bytes 3145736 | tf_op jit(solution)/shard_map/ppermute | solution.py:22
  205.2 39.3 %collective-permute-start.21 = (bf16[256,2048]{1,0:T(8,128)(2,1)S(1)}, bf16[256,2048]{1,0:T(8,128)(2,1)S(1)}, u32[]{:S(2)}, u32[]{:S(2)}) collective-permute-start(bf16[256,2048]{1,0:T(8,128)(2,1)S(1)} %pad_maximum_fusion.13), channel_id=1, source_target_pairs={{0,2},{2,0},{4,6},{6,4},{1,3},{3,1},{5,7},{7,5},{8,10},{10,8},{12,... | collective-permute-start | bytes 3145736 | tf_op jit(solution)/shard_map/ppermute | solution.py:22
  207.0 31.6 %collective-permute-start.56 = (bf16[128,2048]{1,0:T(8,128)(2,1)S(1)}, bf16[128,2048]{1,0:T(8,128)(2,1)S(1)}, u32[]{:S(2)}, u32[]{:S(2)}) collective-permute-start(bf16[128,2048]{1,0:T(8,128)(2,1)S(1)} %slice.1332), channel_id=1, source_target_pairs={{0,4},{2,6},{4,0},{6,2},{1,5},{3,7},{5,1},{7,3},{8,12},{10,14},{12... | collective-permute-start | bytes 1572872 | tf_op jit(solution)/shard_map/ppermute | solution.py:22
  209.7 29.6 %collective-permute-start.42 = (bf16[704,512]{1,0:T(8,128)(2,1)S(1)}, bf16[704,512]{1,0:T(8,128)(2,1)S(1)}, u32[]{:S(2)}, u32[]{:S(2)}) collective-permute-start(bf16[704,512]{1,0:T(8,128)(2,1)S(1)} %copy-done.142), channel_id=1, source_target_pairs={{0,24},{8,0},{16,8},{24,16},{1,25},{9,1},{17,9},{25,17},{2,26},{10... | collective-permute-start | bytes 2162696 | tf_op jit(solution)/shard_map/ppermute | solution.py:27
  214.3 29.6 %collective-permute-start.44 = (bf16[704,512]{1,0:T(8,128)(2,1)}, bf16[704,512]{1,0:T(8,128)(2,1)S(1)}, u32[]{:S(2)}, u32[]{:S(2)}) collective-permute-start(bf16[704,512]{1,0:T(8,128)(2,1)} %collective-permute-done.43), channel_id=1, source_target_pairs={{0,8},{8,16},{16,24},{24,0},{1,9},{9,17},{17,25},{25,1},{2,10},{10... | collective-permute-start | bytes 2162696 | tf_op jit(solution)/shard_map/ppermute | solution.py:27
  239.4 35.3 %collective-permute-start.36 = (bf16[704,512]{1,0:T(8,128)(2,1)S(1)}, bf16[704,512]{1,0:T(8,128)(2,1)}, u32[]{:S(2)}, u32[]{:S(2)}) collective-permute-start(bf16[704,512]{1,0:T(8,128)(2,1)S(1)} %bitcast.258), channel_id=1, source_target_pairs={{0,8},{8,16},{16,24},{24,0},{1,9},{9,17},{17,25},{25,1},{2,10},{10... | collective-permute-start | bytes 2162696 | tf_op jit(solution)/shard_map/ppermute | solution.py:27
  247.9 33.3 %collective-permute-start.35 = (bf16[704,512]{1,0:T(8,128)(2,1)S(1)}, bf16[704,512]{1,0:T(8,128)(2,1)}, u32[]{:S(2)}, u32[]{:S(2)}) collective-permute-start(bf16[704,512]{1,0:T(8,128)(2,1)S(1)} %bitcast.259), channel_id=1, source_target_pairs={{0,24},{8,0},{16,8},{24,16},{1,25},{9,1},{17,9},{25,17},{2,26},{10... | collective-permute-start | bytes 2162696 | tf_op jit(solution)/shard_map/ppermute | solution.py:27
  250.5 34.5 %collective-permute-start.38 = (bf16[704,512]{1,0:T(8,128)(2,1)S(1)}, bf16[704,512]{1,0:T(8,128)(2,1)}, u32[]{:S(2)}, u32[]{:S(2)}) collective-permute-start(bf16[704,512]{1,0:T(8,128)(2,1)S(1)} %bitcast.260), channel_id=1, source_target_pairs={{0,1},{1,0},{2,3},{3,2},{4,5},{5,4},{6,7},{7,6},{8,9},{9,8},{10,11... | collective-permute-start | bytes 2162696 | tf_op jit(solution)/shard_map/ppermute | solution.py:22
  278.2 32.9 %collective-permute-start.37 = (bf16[704,512]{1,0:T(8,128)(2,1)}, bf16[704,512]{1,0:T(8,128)(2,1)S(1)}, u32[]{:S(2)}, u32[]{:S(2)}) collective-permute-start(bf16[704,512]{1,0:T(8,128)(2,1)} %collective-permute-done.36), channel_id=1, source_target_pairs={{0,8},{8,16},{16,24},{24,0},{1,9},{9,17},{17,25},{25,1},{2,10},{10... | collective-permute-start | bytes 2162696 | tf_op jit(solution)/shard_map/ppermute | solution.py:27
  279.8 31.3 %collective-permute-start.33 = (bf16[128,2048]{1,0:T(8,128)(2,1)S(1)}, bf16[128,2048]{1,0:T(8,128)(2,1)S(1)}, u32[]{:S(2)}, u32[]{:S(2)}) collective-permute-start(bf16[128,2048]{1,0:T(8,128)(2,1)S(1)} %slice.1322), channel_id=1, source_target_pairs={{0,2},{2,0},{4,6},{6,4},{1,3},{3,1},{5,7},{7,5},{8,10},{10,8},{12,... | collective-permute-start | bytes 1572872 | tf_op jit(solution)/shard_map/ppermute | solution.py:22
  281.2 42.7 %collective-permute-start.34 = (bf16[128,2048]{1,0:T(8,128)(2,1)S(1)}, bf16[128,2048]{1,0:T(8,128)(2,1)S(1)}, u32[]{:S(2)}, u32[]{:S(2)}) collective-permute-start(bf16[128,2048]{1,0:T(8,128)(2,1)S(1)} %slice.1323), channel_id=1, source_target_pairs={{0,4},{2,6},{4,0},{6,2},{1,5},{3,7},{5,1},{7,3},{8,12},{10,14},{12... | collective-permute-start | bytes 1572872 | tf_op jit(solution)/shard_map/ppermute | solution.py:22
  285.0 41.9 %collective-permute-start.24 = (bf16[704,512]{1,0:T(8,128)(2,1)S(1)}, bf16[704,512]{1,0:T(8,128)(2,1)}, u32[]{:S(2)}, u32[]{:S(2)}) collective-permute-start(bf16[704,512]{1,0:T(8,128)(2,1)S(1)} %bitcast.264), channel_id=1, source_target_pairs={{0,24},{8,0},{16,8},{24,16},{1,25},{9,1},{17,9},{25,17},{2,26},{10... | collective-permute-start | bytes 2162696 | tf_op jit(solution)/shard_map/ppermute | solution.py:27
  295.7 31.5 %collective-permute-start.41 = (bf16[704,512]{1,0:T(8,128)(2,1)}, bf16[704,512]{1,0:T(8,128)(2,1)S(1)}, u32[]{:S(2)}, u32[]{:S(2)}) collective-permute-start(bf16[704,512]{1,0:T(8,128)(2,1)} %collective-permute-done.36), channel_id=1, source_target_pairs={{0,1},{1,0},{2,3},{3,2},{4,5},{5,4},{6,7},{7,6},{8,9},{9,8},{10,11... | collective-permute-start | bytes 2162696 | tf_op jit(solution)/shard_map/ppermute | solution.py:22
  311.1 29.8 %collective-permute-start.26 = (bf16[704,512]{1,0:T(8,128)(2,1)S(1)}, bf16[704,512]{1,0:T(8,128)(2,1)}, u32[]{:S(2)}, u32[]{:S(2)}) collective-permute-start(bf16[704,512]{1,0:T(8,128)(2,1)S(1)} %collective-permute-done.25), channel_id=1, source_target_pairs={{0,8},{8,16},{16,24},{24,0},{1,9},{9,17},{17,25},{25,1},{2,10},{10... | collective-permute-start | bytes 2162696 | tf_op jit(solution)/shard_map/ppermute | solution.py:27
  326.9 31.2 %collective-permute-start.27 = (bf16[704,512]{1,0:T(8,128)(2,1)S(1)}, bf16[704,512]{1,0:T(8,128)(2,1)}, u32[]{:S(2)}, u32[]{:S(2)}) collective-permute-start(bf16[704,512]{1,0:T(8,128)(2,1)S(1)} %bitcast.265), channel_id=1, source_target_pairs={{0,1},{1,0},{2,3},{3,2},{4,5},{5,4},{6,7},{7,6},{8,9},{9,8},{10,11... | collective-permute-start | bytes 2162696 | tf_op jit(solution)/shard_map/ppermute | solution.py:22
  327.2 30.9 %collective-permute-start.30 = (bf16[704,512]{1,0:T(8,128)(2,1)S(1)}, bf16[704,512]{1,0:T(8,128)(2,1)}, u32[]{:S(2)}, u32[]{:S(2)}) collective-permute-start(bf16[704,512]{1,0:T(8,128)(2,1)S(1)} %collective-permute-done.25), channel_id=1, source_target_pairs={{0,1},{1,0},{2,3},{3,2},{4,5},{5,4},{6,7},{7,6},{8,9},{9,8},{10,11... | collective-permute-start | bytes 2162696 | tf_op jit(solution)/shard_map/ppermute | solution.py:22
  327.4 30.7 %collective-permute-start.28 = (bf16[704,512]{1,0:T(8,128)(2,1)}, bf16[704,512]{1,0:T(8,128)(2,1)}, u32[]{:S(2)}, u32[]{:S(2)}) collective-permute-start(bf16[704,512]{1,0:T(8,128)(2,1)} %collective-permute-done.24), channel_id=1, source_target_pairs={{0,1},{1,0},{2,3},{3,2},{4,5},{5,4},{6,7},{7,6},{8,9},{9,8},{10,11... | collective-permute-start | bytes 2162696 | tf_op jit(solution)/shard_map/ppermute | solution.py:22
  474.2 87.0 %collective-permute-start.89 = (bf16[704,2048]{1,0:T(8,128)(2,1)}, bf16[704,2048]{1,0:T(8,128)(2,1)}, u32[]{:S(2)}, u32[]{:S(2)}) collective-permute-start(bf16[704,2048]{1,0:T(8,128)(2,1)} %slice.1791), channel_id=1, source_target_pairs={{0,1},{1,0},{2,3},{3,2},{4,5},{5,4},{6,7},{7,6},{8,9},{9,8},{10,11... | collective-permute-start | bytes 8650760 | tf_op jit(solution)/shard_map/ppermute | solution.py:22
  485.4 40.5 %collective-permute-start.52 = (bf16[256,2048]{1,0:T(8,128)(2,1)S(1)}, bf16[256,2048]{1,0:T(8,128)(2,1)S(1)}, u32[]{:S(2)}, u32[]{:S(2)}) collective-permute-start(bf16[256,2048]{1,0:T(8,128)(2,1)S(1)} %pad_maximum_fusion.16), channel_id=1, source_target_pairs={{0,4},{2,6},{4,0},{6,2},{1,5},{3,7},{5,1},{7,3},{8,12},{10,14},{12... | collective-permute-start | bytes 3145736 | tf_op jit(solution)/shard_map/ppermute | solution.py:22
  486.2 40.9 %collective-permute-start.50 = (bf16[256,2048]{1,0:T(8,128)(2,1)S(1)}, bf16[256,2048]{1,0:T(8,128)(2,1)S(1)}, u32[]{:S(2)}, u32[]{:S(2)}) collective-permute-start(bf16[256,2048]{1,0:T(8,128)(2,1)S(1)} %pad_maximum_fusion.15), channel_id=1, source_target_pairs={{0,2},{2,0},{4,6},{6,4},{1,3},{3,1},{5,7},{7,5},{8,10},{10,8},{12,... | collective-permute-start | bytes 3145736 | tf_op jit(solution)/shard_map/ppermute | solution.py:22
  504.5 65.3 %collective-permute-start.93 = (bf16[704,2048]{1,0:T(8,128)(2,1)}, bf16[704,2048]{1,0:T(8,128)(2,1)}, u32[]{:S(2)}, u32[]{:S(2)}) collective-permute-start(bf16[704,2048]{1,0:T(8,128)(2,1)} %slice.1790), channel_id=1, source_target_pairs={{0,1},{1,0},{2,3},{3,2},{4,5},{5,4},{6,7},{7,6},{8,9},{9,8},{10,11... | collective-permute-start | bytes 8650760 | tf_op jit(solution)/shard_map/ppermute | solution.py:22
  545.0 30.9 %collective-permute-start.97 = (bf16[704,2048]{1,0:T(8,128)(2,1)}, bf16[704,2048]{1,0:T(8,128)(2,1)}, u32[]{:S(2)}, u32[]{:S(2)}) collective-permute-start(bf16[704,2048]{1,0:T(8,128)(2,1)} %slice.1789), channel_id=1, source_target_pairs={{0,1},{1,0},{2,3},{3,2},{4,5},{5,4},{6,7},{7,6},{8,9},{9,8},{10,11... | collective-permute-start | bytes 8650760 | tf_op jit(solution)/shard_map/ppermute | solution.py:22
  558.4 31.3 %collective-permute-start.63 = (bf16[128,2048]{1,0:T(8,128)(2,1)}, bf16[128,2048]{1,0:T(8,128)(2,1)}, u32[]{:S(2)}, u32[]{:S(2)}) collective-permute-start(bf16[128,2048]{1,0:T(8,128)(2,1)} %slice.1340), channel_id=1, source_target_pairs={{0,2},{2,0},{4,6},{6,4},{1,3},{3,1},{5,7},{7,5},{8,10},{10,8},{12,... | collective-permute-start | bytes 1572872 | tf_op jit(solution)/shard_map/ppermute | solution.py:22
  560.3 30.4 %collective-permute-start.64 = (bf16[128,2048]{1,0:T(8,128)(2,1)}, bf16[128,2048]{1,0:T(8,128)(2,1)}, u32[]{:S(2)}, u32[]{:S(2)}) collective-permute-start(bf16[128,2048]{1,0:T(8,128)(2,1)} %slice.1341), channel_id=1, source_target_pairs={{0,4},{2,6},{4,0},{6,2},{1,5},{3,7},{5,1},{7,3},{8,12},{10,14},{12... | collective-permute-start | bytes 1572872 | tf_op jit(solution)/shard_map/ppermute | solution.py:22
  567.0 194.2 %collective-permute-start.92 = (bf16[704,512]{1,0:T(8,128)(2,1)}, bf16[704,512]{1,0:T(8,128)(2,1)}, u32[]{:S(2)}, u32[]{:S(2)}) collective-permute-start(bf16[704,512]{1,0:T(8,128)(2,1)} %get-tuple-element.261), channel_id=1, source_target_pairs={{0,24},{8,0},{16,8},{24,16},{1,25},{9,1},{17,9},{25,17},{2,26},{10... | collective-permute-start | bytes 2162696 | tf_op jit(solution)/shard_map/ppermute | solution.py:27
  569.8 34.6 %collective-permute-start.90 = (bf16[704,512]{1,0:T(8,128)(2,1)S(1)}, bf16[704,512]{1,0:T(8,128)(2,1)}, u32[]{:S(2)}, u32[]{:S(2)}) collective-permute-start(bf16[704,512]{1,0:T(8,128)(2,1)S(1)} %get-tuple-element.260), channel_id=1, source_target_pairs={{0,8},{8,16},{16,24},{24,0},{1,9},{9,17},{17,25},{25,1},{2,10},{10... | collective-permute-start | bytes 2162696 | tf_op jit(solution)/shard_map/ppermute | solution.py:27
  576.0 191.2 %collective-permute-start.96 = (bf16[704,512]{1,0:T(8,128)(2,1)}, bf16[704,512]{1,0:T(8,128)(2,1)}, u32[]{:S(2)}, u32[]{:S(2)}) collective-permute-start(bf16[704,512]{1,0:T(8,128)(2,1)} %get-tuple-element.259), channel_id=1, source_target_pairs={{0,24},{8,0},{16,8},{24,16},{1,25},{9,1},{17,9},{25,17},{2,26},{10... | collective-permute-start | bytes 2162696 | tf_op jit(solution)/shard_map/ppermute | solution.py:27
  589.7 45.4 %collective-permute-start.94 = (bf16[704,512]{1,0:T(8,128)(2,1)}, bf16[704,512]{1,0:T(8,128)(2,1)S(1)}, u32[]{:S(2)}, u32[]{:S(2)}) collective-permute-start(bf16[704,512]{1,0:T(8,128)(2,1)} %get-tuple-element.258), channel_id=1, source_target_pairs={{0,8},{8,16},{16,24},{24,0},{1,9},{9,17},{17,25},{25,1},{2,10},{10... | collective-permute-start | bytes 2162696 | tf_op jit(solution)/shard_map/ppermute | solution.py:27
  590.8 56.0 %collective-permute-start.98 = (bf16[704,512]{1,0:T(8,128)(2,1)S(1)}, bf16[704,512]{1,0:T(8,128)(2,1)S(1)}, u32[]{:S(2)}, u32[]{:S(2)}) collective-permute-start(bf16[704,512]{1,0:T(8,128)(2,1)S(1)} %get-tuple-element.256), channel_id=1, source_target_pairs={{0,8},{8,16},{16,24},{24,0},{1,9},{9,17},{17,25},{25,1},{2,10},{10... | collective-permute-start | bytes 2162696 | tf_op jit(solution)/shard_map/ppermute | solution.py:27
  604.4 43.9 %collective-permute-start.65 = (bf16[1024,256]{1,0:T(8,128)(2,1)S(1)}, bf16[1024,256]{1,0:T(8,128)(2,1)S(1)}, u32[]{:S(2)}, u32[]{:S(2)}) collective-permute-start(bf16[1024,256]{1,0:T(8,128)(2,1)S(1)} %get-tuple-element.287), channel_id=1, source_target_pairs={{0,1},{1,0},{2,3},{3,2},{4,5},{5,4},{6,7},{7,6},{8,9},{9,8},{10,11... | collective-permute-start | bytes 1572872 | tf_op jit(solution)/shard_map/ppermute | solution.py:22
  635.1 124.3 %collective-permute-start.80 = (bf16[256,2048]{1,0:T(8,128)(2,1)}, bf16[256,2048]{1,0:T(8,128)(2,1)}, u32[]{:S(2)}, u32[]{:S(2)}) collective-permute-start(bf16[256,2048]{1,0:T(8,128)(2,1)} %pad_maximum_fusion.24), channel_id=1, source_target_pairs={{0,1},{1,0},{2,3},{3,2},{4,5},{5,4},{6,7},{7,6},{8,9},{9,8},{10,11... | collective-permute-start | bytes 3145736 | tf_op jit(solution)/shard_map/ppermute | solution.py:22
  646.8 117.2 %collective-permute-start.91 = (bf16[704,512]{1,0:T(8,128)(2,1)}, bf16[704,512]{1,0:T(8,128)(2,1)}, u32[]{:S(2)}, u32[]{:S(2)}) collective-permute-start(bf16[704,512]{1,0:T(8,128)(2,1)} %fusion.75), channel_id=1, source_target_pairs={{0,8},{8,16},{16,24},{24,0},{1,9},{9,17},{17,25},{25,1},{2,10},{10... | collective-permute-start | bytes 2162696 | tf_op jit(solution)/shard_map/ppermute | solution.py:27
  759.4 65.4 %collective-permute-start.66 = (bf16[1024,768]{1,0:T(8,128)(2,1)}, bf16[1024,768]{1,0:T(8,128)(2,1)S(1)}, u32[]{:S(2)}, u32[]{:S(2)}) collective-permute-start(bf16[1024,768]{1,0:T(8,128)(2,1)} %bitcast.239), channel_id=1, source_target_pairs={{0,1},{1,0},{2,3},{3,2},{4,5},{5,4},{6,7},{7,6},{8,9},{9,8},{10,11... | collective-permute-start | bytes 4718600 | tf_op jit(solution)/shard_map/ppermute | solution.py:22
  761.2 55.3 %collective-permute-start.100 = (bf16[704,512]{1,0:T(8,128)(2,1)S(1)}, bf16[704,512]{1,0:T(8,128)(2,1)S(1)}, u32[]{:S(2)}, u32[]{:S(2)}) collective-permute-start(bf16[704,512]{1,0:T(8,128)(2,1)S(1)} %copy-done.86), channel_id=1, source_target_pairs={{0,24},{8,0},{16,8},{24,16},{1,25},{9,1},{17,9},{25,17},{2,26},{10... | collective-permute-start | bytes 2162696 | tf_op jit(solution)/shard_map/ppermute | solution.py:27
  764.0 52.6 %collective-permute-start.99 = (bf16[704,512]{1,0:T(8,128)(2,1)S(1)}, bf16[704,512]{1,0:T(8,128)(2,1)S(1)}, u32[]{:S(2)}, u32[]{:S(2)}) collective-permute-start(bf16[704,512]{1,0:T(8,128)(2,1)S(1)} %copy-done.87), channel_id=1, source_target_pairs={{0,8},{8,16},{16,24},{24,0},{1,9},{9,17},{17,25},{25,1},{2,10},{10... | collective-permute-start | bytes 2162696 | tf_op jit(solution)/shard_map/ppermute | solution.py:27
  767.1 52.3 %collective-permute-start.83 = (bf16[256,512]{1,0:T(8,128)(2,1)S(1)}, bf16[256,512]{1,0:T(8,128)(2,1)S(1)}, u32[]{:S(2)}, u32[]{:S(2)}) collective-permute-start(bf16[256,512]{1,0:T(8,128)(2,1)S(1)} %get-tuple-element.277), channel_id=1, source_target_pairs={{0,24},{8,0},{16,8},{24,16},{1,25},{9,1},{17,9},{25,17},{2,26},{10... | collective-permute-start | bytes 786440 | tf_op jit(solution)/shard_map/ppermute | solution.py:27
  777.3 39.0 %collective-permute-start.81 = (bf16[256,512]{1,0:T(8,128)(2,1)S(1)}, bf16[256,512]{1,0:T(8,128)(2,1)S(1)}, u32[]{:S(2)}, u32[]{:S(2)}) collective-permute-start(bf16[256,512]{1,0:T(8,128)(2,1)S(1)} %get-tuple-element.276), channel_id=1, source_target_pairs={{0,8},{8,16},{16,24},{24,0},{1,9},{9,17},{17,25},{25,1},{2,10},{10... | collective-permute-start | bytes 786440 | tf_op jit(solution)/shard_map/ppermute | solution.py:27
  901.9 30.7 %collective-permute-start.78 = (bf16[512,768]{0,1:T(8,128)(2,1)S(1)}, bf16[512,768]{0,1:T(8,128)(2,1)S(1)}, u32[]{:S(2)}, u32[]{:S(2)}) collective-permute-start(bf16[512,768]{0,1:T(8,128)(2,1)S(1)} %fusion.68), channel_id=1, source_target_pairs={{0,8},{8,16},{16,24},{24,0},{1,9},{9,17},{17,25},{25,1},{2,10},{10... | collective-permute-start | bytes 2359304 | tf_op jit(solution)/shard_map/ppermute | solution.py:27
  (221 other events, 3802.4 us)

commit v2 on v1

v2 whole, which is shorter than its diff:
```python
import functools

import jax
import jax.numpy as jnp
from jax import lax
from jax.experimental import pallas as pl
from jax.experimental.pallas import tpu as pltpu
from jax.sharding import PartitionSpec as P

lambda_base = 0.2
tile = 512
low = jnp.bfloat16


def contract(left_side, right_side, left_dim, right_dim):
    return lax.dot_general(
        left_side,
        right_side,
        (((left_dim,), (right_dim,)), ((), ())),
        preferred_element_type=jnp.float32,
    )


def after(values, *others):
    return lax.optimization_barrier((values, *others))[0]


def swap(values, axis, mask):
    size = lax.axis_size(axis)
    return lax.ppermute(values, axis, [(place, place ^ mask) for place in range(size)])


def shift(values, axis, step):
    size = lax.axis_size(axis)
    return lax.ppermute(values, axis, [(place, (place + step) % size) for place in range(size)])


class Line:
    def __init__(self):
        self.arrived = []

    def send(self, values, step):
        if len(self.arrived) > 1:
            values = after(values, self.arrived[-2])
        values = shift(values, "fsdp", step)
        self.arrived.append(values)
        return values

    def gather(self, own):
        size = lax.axis_size("fsdp")
        shards = [own] + [None] * (size - 1)
        up, down = own, own
        for step in range(1, size // 2 + 1):
            up = self.send(up, 1)
            shards[size - step] = up
            if step <= size - 1 - size // 2:
                down = self.send(down, -1)
                shards[step] = down
        return shards

    def reduce(self, partial):
        size = lax.axis_size("fsdp")
        up_steps = size // 2
        down_steps = size - 1 - up_steps
        up = down = None
        for step in range(up_steps):
            term = partial[up_steps - step]
            up = self.send(term if up is None else add_low(term, up), 1)
            if step < down_steps:
                term = partial[size - down_steps + step]
                down = self.send(term if down is None else add_low(term, down), -1)
        total = partial[0].astype(jnp.float32) + up.astype(jnp.float32)
        return total if down is None else total + down.astype(jnp.float32)


def add_low(left_side, right_side):
    return (left_side.astype(jnp.float32) + right_side.astype(jnp.float32)).astype(low)


def group_gather(own):
    half = own.shape[0] // 2
    first = swap(own, "head", 1)
    second = swap(own, "head", 2)
    third_low = swap(second[:half], "head", 1)
    third_high = swap(first[half:], "head", 2)
    return jnp.concatenate([own, first, second, third_low, third_high], axis=0)


def group_reduce(nearer, third):
    rows = third.shape[0]
    half = rows // 2
    own, first, second = (nearer[place * rows : (place + 1) * rows] for place in range(3))
    to_first = swap(third[:half].astype(low), "head", 1)
    to_second = swap(third[half:].astype(low), "head", 2)
    second = jnp.concatenate(
        [add_low(second[:half], to_first), second[half:].astype(low)], axis=0
    )
    first = jnp.concatenate(
        [first[:half].astype(low), add_low(first[half:], to_second)], axis=0
    )
    from_first = swap(first, "head", 1)
    from_second = swap(second, "head", 2)
    return (
        own.astype(jnp.float32) + from_first.astype(jnp.float32) + from_second.astype(jnp.float32)
    )


def total_over_all(values):
    for axis in ("tensor", "head", "fsdp"):
        mask = 1
        while mask < lax.axis_size(axis):
            values = values + swap(values, axis, mask)
            mask *= 2
    return values


def rolled(values, start):
    twice = jnp.concatenate([values, values], axis=-1)
    return lax.dynamic_slice_in_dim(twice, start, values.shape[-1], values.ndim - 1)


def slot_layout(lengths, slots):
    first_end = lengths[0, 0]
    second_end = first_end + lengths[0, 1]
    segment = (slots >= first_end).astype(jnp.int32) + (slots >= second_end).astype(jnp.int32)
    start = jnp.where(segment == 0, 0, jnp.where(segment == 1, first_end, second_end))
    return segment, slots - start


def swap_halves(values):
    half = values.shape[1] // 2
    return jnp.concatenate([values[:, half:], values[:, :half]], axis=1)


def place_of(block, head_index, core):
    return ((block & 1) ^ core) * 4 + ((block >> 1) ^ head_index)


def row_starts(slots, first_end, second_end):
    return jnp.where(slots >= second_end, second_end, jnp.where(slots >= first_end, first_end, 0))


def attention_forward_kernel(
    ints, floats, kept, received, gain, head_out, ordered, outs, log_totals
):
    head_index, core, first_end, second_end = (ints[place] for place in range(4))
    rows = kept.shape[0] // 4
    slots = 8 * rows
    width = gain.shape[1]
    e = width // 2
    for part, other in ((kept, 0), (received, 1)):
        for j in range(4):
            block = (head_index ^ j) * 2 + (core ^ other)
            at = pl.ds(pl.multiple_of(block * rows, rows), rows)
            for m in range(2):
                for kind in range(3):
                    to, source = (2 * kind + m) * e, (3 * m + kind) * e
                    ordered[at, to : to + e] = part[
                        j * rows : (j + 1) * rows, source : source + e
                    ]
    for start in range(0, slots, tile):
        stop = start + tile
        row = start + lax.broadcasted_iota(jnp.int32, (tile, 1), 0)
        begin = row_starts(row, first_end, second_end)
        value = ordered[:stop, 4 * e :]
        results = []
        for m in range(2):
            scores = contract(
                ordered[start:stop, m * e : (m + 1) * e],
                ordered[:stop, (2 + m) * e : (3 + m) * e],
                1,
                1,
            )
            column = lax.broadcasted_iota(jnp.int32, (tile, stop), 1)
            scores = jnp.where((column >= begin) & (column <= row), scores, -1e30)
            row_max = jnp.max(scores, axis=1, keepdims=True)
            expanded = jnp.exp(scores - row_max)
            row_total = jnp.sum(expanded, axis=1, keepdims=True)
            result = contract(expanded.astype(low), value, 1, 0) / row_total
            outs[m, start:stop, :] = result
            results.append(result)
            wide = jnp.broadcast_to(row_max + jnp.log(row_total), (tile, 128))
            log_totals[m : m + 1, start:stop] = jnp.transpose(wide)[:1]
        mixed = results[0] * floats[0] + results[1] * floats[1]
        scale = lax.rsqrt(jnp.mean(mixed * mixed, axis=1, keepdims=True) + 1e-05)
        normed = (mixed * scale * gain[...]).astype(low)
        for piece in range(tile // rows):
            place = place_of(start // rows + piece, head_index, core)
            head_out[pl.ds(pl.multiple_of(place * rows, rows), rows), :] = normed[
                piece * rows : (piece + 1) * rows
            ]


def attention_forward(ints, floats, kept, received, gain):
    rows = kept.shape[0] // 4
    slots = 8 * rows
    width = gain.shape[1]
    vmem = pl.BlockSpec(memory_space=pltpu.VMEM)
    smem = pl.BlockSpec(memory_space=pltpu.SMEM)
    return pl.pallas_call(
        attention_forward_kernel,
        in_specs=[smem, smem, vmem, vmem, vmem],
        out_specs=[vmem] * 4,
        out_shape=[
            jax.ShapeDtypeStruct((slots, width), low),
            jax.ShapeDtypeStruct((slots, 3 * width), low),
            jax.ShapeDtypeStruct((2, slots, width), jnp.float32),
            jax.ShapeDtypeStruct((2, slots), jnp.float32),
        ],
        compiler_params=pltpu.CompilerParams(vmem_limit_bytes=40 * 2**20),
        cost_estimate=pl.CostEstimate(
            flops=20 * 10**9, bytes_accessed=16 * 2**20, transcendentals=6 * 10**6
        ),
        name="attention_forward",
    )(ints, floats, kept, received, gain)


def attention_backward_kernel(
    ints,
    floats,
    ordered,
    grads_kept,
    grads_received,
    outs,
    log_totals,
    gain,
    cosine,
    sine,
    qkv_grad,
    gain_grad,
    lambda_grad,
    map_grads,
    deltas,
    query_grads,
    key_grads,
    value_grads,
):
    head_index, core, first_end, second_end = (ints[place] for place in range(4))
    rows = grads_kept.shape[0] // 4
    slots = 8 * rows
    width = gain.shape[1]
    e = width // 2
    gain_total = jnp.zeros((1, width), jnp.float32)
    lambda_total = jnp.zeros((1, width), jnp.float32)
    for part, other in ((grads_kept, 0), (grads_received, 1)):
        for j in range(4):
            block = (head_index ^ j) * 2 + (core ^ other)
            at = pl.ds(pl.multiple_of(block * rows, rows), rows)
            grad = part[j * rows : (j + 1) * rows, :].astype(jnp.float32)
            first, second = outs[0, at, :], outs[1, at, :]
            mixed = first * floats[0] + second * floats[1]
            scale = lax.rsqrt(jnp.mean(mixed * mixed, axis=1, keepdims=True) + 1e-05)
            gain_total += jnp.sum(grad * (mixed * scale), axis=0, keepdims=True)
            weighted = grad * gain[...]
            inner = jnp.mean(weighted * mixed, axis=1, keepdims=True)
            mixed_grad = scale * weighted - mixed * (scale * scale * scale * inner)
            lambda_total += jnp.sum(
                mixed_grad * jnp.where(core == 1, first, second), axis=0, keepdims=True
            )
            for m, out in ((0, first), (1, second)):
                map_grad = (mixed_grad * floats[m]).astype(low)
                map_grads[m, at, :] = map_grad
                delta = jnp.sum(map_grad.astype(jnp.float32) * out, axis=1, keepdims=True)
                deltas[m, :, at] = jnp.transpose(jnp.broadcast_to(delta, (rows, 128)))[:8]
    gain_grad[...] = gain_total * (1.0 - lambda_base)
    lambda_grad[...] = lambda_total
    query_grads[...] = jnp.zeros_like(query_grads)

    def pair(key_start, query_start, diagonal):
        at_keys = pl.ds(key_start, tile)
        at_queries = pl.ds(query_start, tile)
        column = query_start + lax.broadcasted_iota(jnp.int32, (1, tile), 1)
        begin = row_starts(column, first_end, second_end)
        row = key_start + lax.broadcasted_iota(jnp.int32, (tile, tile), 0)
        allowed = row >= begin
        if diagonal:
            allowed = allowed & (row <= column)
        value = ordered[at_keys, 4 * e :]
        for m in range(2):
            query = ordered[at_queries, m * e : (m + 1) * e]
            key = ordered[at_keys, (2 + m) * e : (3 + m) * e]
            map_grad = map_grads[m, at_queries, :]
            scores = contract(key, query, 1, 1)
            probability = jnp.where(
                allowed, jnp.exp(scores - log_totals[m : m + 1, at_queries]), 0.0
            )
            prob_grad = contract(value, map_grad, 1, 1)
            score_grad = (probability * (prob_grad - deltas[m, 0:1, at_queries])).astype(low)
            value_term = contract(probability.astype(low), map_grad, 1, 0)
            key_term = contract(score_grad, query, 1, 0)
            query_grads[m, at_queries, :] += contract(score_grad, key, 0, 0)
            if diagonal:
                key_grads[m, at_keys, :] = key_term
                if m == 0:
                    value_grads[at_keys, :] = value_term
                else:
                    value_grads[at_keys, :] += value_term
            else:
                key_grads[m, at_keys, :] += key_term
                value_grads[at_keys, :] += value_term

    for key_start in range(0, slots, tile):
        pair(key_start, key_start, True)

        def step(at, carry, key_start=key_start):
            pair(key_start, pl.multiple_of(at * tile, tile), False)
            return carry

        lax.fori_loop(key_start // tile + 1, slots // tile, step, 0)

    def turn_back(values, at):
        return values * cosine[at, :] - pltpu.roll(values, e // 2, 1) * sine[at, :]

    for block in range(8):
        at = slice(block * rows, (block + 1) * rows)
        to = pl.ds(pl.multiple_of(place_of(block, head_index, core) * rows, rows), rows)
        for m in range(2):
            first = 3 * m * e
            qkv_grad[to, first : first + e] = (
                turn_back(query_grads[m, at, :], at) * e ** (-0.5)
            ).astype(low)
            qkv_grad[to, first + e : first + 2 * e] = turn_back(key_grads[m, at, :], at).astype(
                low
            )
            qkv_grad[to, first + 2 * e : first + 3 * e] = value_grads[
                at, m * e : (m + 1) * e
            ].astype(low)


def attention_backward(
    ints, floats, ordered, grads_kept, grads_received, outs, log_totals, gain, cosine, sine
):
    slots, width = outs.shape[1:]
    vmem = pl.BlockSpec(memory_space=pltpu.VMEM)
    smem = pl.BlockSpec(memory_space=pltpu.SMEM)
    return pl.pallas_call(
        attention_backward_kernel,
        in_specs=[smem, smem] + [vmem] * 8,
        out_specs=[vmem] * 3,
        out_shape=[
            jax.ShapeDtypeStruct((slots, 3 * width), low),
            jax.ShapeDtypeStruct((1, width), jnp.float32),
            jax.ShapeDtypeStruct((1, width), jnp.float32),
        ],
        scratch_shapes=[
            pltpu.VMEM((2, slots, width), low),
            pltpu.VMEM((2, 8, slots), jnp.float32),
            pltpu.VMEM((2, slots, width // 2), jnp.float32),
            pltpu.VMEM((2, slots, width // 2), jnp.float32),
            pltpu.VMEM((slots, width), jnp.float32),
        ],
        compiler_params=pltpu.CompilerParams(vmem_limit_bytes=48 * 2**20),
        cost_estimate=pl.CostEstimate(
            flops=40 * 10**9, bytes_accessed=24 * 2**20, transcendentals=6 * 10**6
        ),
        name="attention_backward",
    )(ints, floats, ordered, grads_kept, grads_received, outs, log_totals, gain, cosine, sine)


def gate_kernel(inputs, gate, up, hidden, gate_factor, up_factor):
    gate_pre = contract(gate[...], inputs[...], 1, 1)
    upward = contract(up[...], inputs[...], 1, 1)
    sigmoid = 1.0 / (1.0 + jnp.exp(-gate_pre))
    silu = gate_pre * sigmoid
    hidden[...] = (silu * upward).astype(low)
    gate_factor[...] = (upward * (sigmoid * (1.0 + gate_pre * (1.0 - sigmoid)))).astype(low)
    up_factor[...] = silu.astype(low)


def gate_units(inputs, gate, up):
    slots, width = inputs.shape
    units = gate.shape[0]
    block = slots // 4
    whole = pl.BlockSpec((units, width), lambda i: (0, 0))
    across = pl.BlockSpec((units, block), lambda i: (0, i))
    return pl.pallas_call(
        gate_kernel,
        grid=(4,),
        in_specs=[pl.BlockSpec((block, width), lambda i: (i, 0)), whole, whole],
        out_specs=[across] * 3,
        out_shape=[jax.ShapeDtypeStruct((units, slots), low)] * 3,
        compiler_params=pltpu.CompilerParams(vmem_limit_bytes=40 * 2**20),
        cost_estimate=pl.CostEstimate(
            flops=4 * slots * width * units,
            bytes_accessed=16 * 2**20,
            transcendentals=units * slots,
        ),
        name="gate_units",
    )(inputs, gate, up)


def gate_grad_kernel(grads, down, gate_factor, up_factor, gate_grad, up_grad):
    hidden_grad = contract(down[...], grads[...], 1, 1)
    gate_grad[...] = (hidden_grad * gate_factor[...].astype(jnp.float32)).astype(low)
    up_grad[...] = (hidden_grad * up_factor[...].astype(jnp.float32)).astype(low)


def gate_grads(grads, down, gate_factor, up_factor):
    slots, width = grads.shape
    units = down.shape[0]
    block = slots // 4
    across = pl.BlockSpec((units, block), lambda i: (0, i))
    return pl.pallas_call(
        gate_grad_kernel,
        grid=(4,),
        in_specs=[
            pl.BlockSpec((block, width), lambda i: (i, 0)),
            pl.BlockSpec((units, width), lambda i: (0, 0)),
            across,
            across,
        ],
        out_specs=[across] * 2,
        out_shape=[jax.ShapeDtypeStruct((units, slots), low)] * 2,
        compiler_params=pltpu.CompilerParams(vmem_limit_bytes=40 * 2**20),
        cost_estimate=pl.CostEstimate(
            flops=2 * slots * width * units, bytes_accessed=16 * 2**20, transcendentals=0
        ),
        name="gate_grads",
    )(grads, down, gate_factor, up_factor)


def sum_kernel(terms, *refs):
    out = refs[-1]
    total = contract(refs[0][...], refs[terms][...], 0, 0)
    for place in range(1, terms):
        total += contract(refs[place][...], refs[terms + place][...], 0, 0)
    out[...] = total.astype(out.dtype)


def sum_over_units(factors, weights, first, count, rows):
    units, width = weights[0].shape
    terms = len(factors)
    return pl.pallas_call(
        functools.partial(sum_kernel, terms),
        grid=(count,),
        in_specs=[pl.BlockSpec((units, rows), lambda i: (0, first + i))] * terms
        + [pl.BlockSpec((units, width), lambda i: (0, 0))] * terms,
        out_specs=pl.BlockSpec((rows, width), lambda i: (i, 0)),
        out_shape=jax.ShapeDtypeStruct((count * rows, width), low),
        compiler_params=pltpu.CompilerParams(vmem_limit_bytes=48 * 2**20),
        cost_estimate=pl.CostEstimate(
            flops=2 * count * rows * width * units * terms,
            bytes_accessed=terms * 4 * 2**20,
            transcendentals=0,
        ),
        name="sum_over_units",
    )(*factors, *weights)


def body(
    tokens,
    lengths,
    attention_gain,
    query_weight,
    key_weight,
    value_weight,
    output_weight,
    lambda_vectors,
    head_gain,
    feedforward_gain,
    gate_weight,
    up_weight,
    down_weight,
    cotangent,
):
    rows, width = tokens.shape
    fsdp_index = lax.axis_index("fsdp")
    head_index = lax.axis_index("head")
    core = lax.axis_index("tensor")
    shard = query_weight.shape[0]
    qk_width = query_weight.shape[3]
    value_half = value_weight.shape[2]
    slots = rows * 8
    half_slots = slots // 2
    scale = qk_width ** (-0.5)
    column_start = fsdp_index * shard
    back = width - column_start

    def in_order(mine, other):
        return jnp.where(core == 0, mine, other), jnp.where(core == 0, other, mine)

    tokens_wide = rolled(tokens, column_start).astype(jnp.float32)
    attention_gain = rolled(attention_gain, column_start)
    feedforward_gain = rolled(feedforward_gain, column_start)
    attention_scale = lax.rsqrt(jnp.mean(tokens_wide * tokens_wide, axis=-1, keepdims=True) + 1e-06)
    normed = group_gather((tokens_wide * attention_scale * attention_gain).astype(low))

    third = 3 * qk_width
    heads = [
        jnp.concatenate(
            [
                weight[:, place].reshape(shard, -1)
                for weight in (query_weight, key_weight, value_weight)
            ],
            axis=1,
        )
        for place in range(2)
    ]
    line = Line()
    qkv_own = jnp.concatenate(line.gather(jnp.concatenate(in_order(*heads), axis=1)), axis=0)
    qkv_other = swap(qkv_own, "tensor", 1)
    output_own = jnp.concatenate(
        line.gather(jnp.concatenate(in_order(output_weight[0], output_weight[1]), axis=0)), axis=1
    )
    output_all = jnp.concatenate([output_own, swap(output_own, "tensor", 1)], axis=0)

    def both_cores(local):
        own = jnp.concatenate(line.gather(local), axis=1)
        return own, swap(own, "tensor", 1)

    gate_own, gate_other = both_cores(jnp.transpose(gate_weight))
    up_own, up_other = both_cores(jnp.transpose(up_weight))
    down_own, down_other = both_cores(down_weight)

    own_slots = (
        (jnp.arange(4, dtype=jnp.int32) ^ head_index)[:, None] * (2 * rows)
        + core * rows
        + jnp.arange(rows, dtype=jnp.int32)[None, :]
    ).reshape(-1)
    segment_own, position_own = slot_layout(lengths, own_slots)
    valid = (segment_own[:rows] < 2).astype(jnp.float32)[:, None]
    half_width = qk_width // 2
    frequency = 10000.0 ** (-jnp.arange(half_width, dtype=jnp.float32) / half_width)

    def turn_tables(positions):
        angles = positions.astype(jnp.float32)[:, None] * frequency[None, :]
        cosine, sine = jnp.cos(angles), jnp.sin(angles)
        return jnp.concatenate([cosine, cosine], axis=1), jnp.concatenate([-sine, sine], axis=1)

    cosine, sine = turn_tables(position_own)
    cosine_all, sine_all = turn_tables(
        slot_layout(lengths, jnp.arange(slots, dtype=jnp.int32))[1]
    )
    own_head = head_index * 2 + core
    vectors = lax.dynamic_slice_in_dim(lambda_vectors, own_head, 1, 0)[0]
    first_exp = jnp.exp(jnp.sum(vectors[0] * vectors[1]))
    second_exp = jnp.exp(jnp.sum(vectors[2] * vectors[3]))
    lambda_value = first_exp - second_exp + lambda_base
    floats = jnp.stack(in_order(1.0, -lambda_value))
    ints = jnp.stack([head_index, core, lengths[0, 0], lengths[0, 0] + lengths[0, 1]])
    gain_own = rolled(
        lax.dynamic_slice_in_dim(head_gain, own_head, 1, 0), core * value_half
    ) * (1.0 - lambda_base)

    from_own = contract(normed, qkv_own, 1, 0)
    from_other = contract(normed, qkv_other, 1, 0)

    def rotate(part):
        return part * cosine + swap_halves(part) * sine

    def finish(block):
        return [
            rotate(block[:, :qk_width]) * scale,
            rotate(block[:, qk_width : 2 * qk_width]),
            block[:, 2 * qk_width :],
        ]

    qkv_kept = jnp.concatenate(
        finish(from_own[:, :third]) + finish(from_other[:, third:]), axis=1
    ).astype(low)
    qkv_sent = jnp.concatenate(
        finish(from_other[:, :third]) + finish(from_own[:, third:]), axis=1
    ).astype(low)
    head_out_both, ordered, outs, log_totals = attention_forward(
        ints, floats, qkv_kept, swap(qkv_sent, "tensor", 1), gain_own
    )
    kept, received = head_out_both[:half_slots], swap(head_out_both[half_slots:], "tensor", 1)
    head_out = jnp.concatenate(
        [
            kept[:, :value_half],
            received[:, value_half:],
            received[:, :value_half],
            kept[:, value_half:],
        ],
        axis=1,
    )

    ffn_out_grad = valid * rolled(cotangent, column_start).astype(jnp.float32)
    ffn_out_grad_all = group_gather(after(ffn_out_grad.astype(low), normed))
    third_out = contract(head_out[3 * rows :], output_all, 1, 0).astype(low)
    nearer_out = contract(after(head_out, third_out)[: 3 * rows], output_all, 1, 0)
    residual = tokens_wide + group_reduce(nearer_out, after(third_out, ffn_out_grad_all))
    ffn_scale = lax.rsqrt(jnp.mean(residual * residual, axis=-1, keepdims=True) + 1e-06)
    ffn_in = group_gather((residual * ffn_scale * feedforward_gain).astype(low))
    hidden_own, gate_factor_own, up_factor_own = gate_units(ffn_in, gate_own, up_own)
    hidden_other, gate_factor_other, up_factor_other = gate_units(ffn_in, gate_other, up_other)

    def weight_grad(own_side, other_side, right_side, left_dim):
        other = contract(other_side, right_side, left_dim, 0).astype(low)
        other = swap(other, "tensor", 1)
        total = add_low(contract(own_side, right_side, left_dim, 0), other)
        return [total[:, start : start + shard] for start in range(0, width, shard)]

    down_terms = weight_grad(hidden_own, hidden_other, ffn_out_grad_all, 1)
    down_grad = line.reduce(down_terms)
    gate_grad_own, up_grad_own = gate_grads(
        ffn_out_grad_all, down_own, gate_factor_own, up_factor_own
    )
    gate_grad_other, up_grad_other = gate_grads(
        ffn_out_grad_all, down_other, gate_factor_other, up_factor_other
    )
    factors = [gate_grad_own, up_grad_own, gate_grad_other, up_grad_other]
    weights = [gate_own, up_own, gate_other, up_other]
    third_grad = sum_over_units(factors, weights, 3, 1, rows)
    nearer_grad = sum_over_units([after(factors[0], third_grad)] + factors[1:], weights, 0, 3, rows)
    ffn_in_grad = group_reduce(nearer_grad, third_grad)
    gate_weight_grad = jnp.transpose(
        line.reduce(weight_grad(after(gate_grad_own, nearer_grad), gate_grad_other, ffn_in, 1))
    )
    up_weight_grad = jnp.transpose(
        line.reduce(weight_grad(after(up_grad_own, nearer_grad), up_grad_other, ffn_in, 1))
    )
    feedforward_gain_part = jnp.sum(ffn_in_grad * residual * ffn_scale, axis=0)
    ffn_gained = ffn_in_grad * feedforward_gain
    residual_grad = (
        ffn_out_grad
        + ffn_scale * ffn_gained
        - residual * ffn_scale**3 * jnp.mean(ffn_gained * residual, axis=-1, keepdims=True)
    )

    attention_out_grad = group_gather(residual_grad.astype(low))
    head_out_grad = contract(attention_out_grad, output_all, 1, 1).astype(low)
    pieces = [
        head_out_grad[:, place * value_half : (place + 1) * value_half] for place in range(4)
    ]
    qkv_grad_both, head_gain_part, lambda_part = attention_backward(
        ints,
        floats,
        ordered,
        jnp.concatenate([pieces[0], pieces[3]], axis=1),
        swap(jnp.concatenate([pieces[2], pieces[1]], axis=1), "tensor", 1),
        outs,
        log_totals,
        gain_own,
        cosine_all,
        sine_all,
    )
    output_terms = contract(head_out, attention_out_grad, 0, 0)
    output_other_part = swap(output_terms[2 * value_half :].astype(low), "tensor", 1)
    output_terms = add_low(output_terms[: 2 * value_half], output_other_part)
    output_grad = line.reduce(
        [output_terms[:, start : start + shard] for start in range(0, width, shard)]
    )

    ffn_out = sum_over_units(
        [after(hidden_own, attention_out_grad), hidden_other], [down_own, down_other], 0, 4, rows
    )
    ffn_here = group_reduce(ffn_out[: 3 * rows], ffn_out[3 * rows :])
    block_output = (valid * (residual + ffn_here)).astype(low)

    kept, received = qkv_grad_both[:half_slots], swap(qkv_grad_both[half_slots:], "tensor", 1)
    grad_own = jnp.concatenate([kept[:, :third], received[:, third:]], axis=1)
    grad_other = jnp.concatenate([received[:, :third], kept[:, third:]], axis=1)
    other_terms = swap(contract(normed, grad_other, 0, 0).astype(low), "tensor", 1)
    own_terms = add_low(contract(normed, grad_own, 0, 0), other_terms)
    qkv_weight_grad = line.reduce(
        [own_terms[start : start + shard] for start in range(0, width, shard)]
    )
    qkv_weight_grad = jnp.stack(
        in_order(qkv_weight_grad[:, :third], qkv_weight_grad[:, third:]), axis=1
    )
    output_grad = jnp.stack(in_order(output_grad[:value_half], output_grad[value_half:]))
    normed_terms = contract(
        jnp.concatenate([grad_own, grad_other], axis=1),
        jnp.concatenate([qkv_own, qkv_other], axis=1),
        1,
        1,
    )
    normed_grad = group_reduce(normed_terms[: 3 * rows], after(normed_terms[3 * rows :], ffn_here))
    attention_gain_part = jnp.sum(normed_terms * normed.astype(jnp.float32), axis=0)
    attention_gained = normed_grad * attention_gain
    tokens_grad = (
        residual_grad
        + attention_scale * attention_gained
        - tokens_wide
        * attention_scale**3
        * jnp.mean(attention_gained * tokens_wide, axis=-1, keepdims=True)
    )

    lambda_grad = -jnp.sum(lambda_part)
    vector_grads = lambda_grad * jnp.stack(
        [
            first_exp * vectors[1],
            first_exp * vectors[0],
            -second_exp * vectors[3],
            -second_exp * vectors[2],
        ]
    )
    lambda_full = lax.dynamic_update_slice(
        jnp.zeros(lambda_vectors.shape, jnp.float32), vector_grads[None], (own_head, 0, 0)
    )
    gain_full = lax.dynamic_update_slice(
        jnp.zeros(head_gain.shape, jnp.float32),
        rolled(head_gain_part, core * value_half),
        (own_head, 0),
    )
    small = total_over_all(
        jnp.concatenate(
            [
                rolled(attention_gain_part / attention_gain, back),
                rolled(feedforward_gain_part, back),
                lambda_full.reshape(-1),
                gain_full.reshape(-1),
            ]
        )
    )
    lambda_end = 2 * width + lambda_full.size
    return (
        rolled(block_output, back),
        rolled(tokens_grad, back),
        small[:width],
        qkv_weight_grad[:, :, :qk_width].reshape(query_weight.shape),
        qkv_weight_grad[:, :, qk_width : 2 * qk_width].reshape(key_weight.shape),
        qkv_weight_grad[:, :, 2 * qk_width :].reshape(value_weight.shape),
        output_grad.reshape(output_weight.shape),
        small[2 * width : lambda_end].reshape(lambda_full.shape),
        small[lambda_end:].reshape(gain_full.shape),
        small[width : 2 * width],
        gate_weight_grad,
        up_weight_grad,
        down_grad,
    )


def solution(mesh):
    placed = (
        P(("fsdp", "head", "tensor"), None),
        P("fsdp", None),
        P(),
        P("fsdp", "head", "tensor", None),
        P("fsdp", "head", "tensor", None),
        P("fsdp", "head", "tensor"),
        P("head", "tensor", "fsdp"),
        P(),
        P(),
        P(),
        P("fsdp", ("head", "tensor")),
        P("fsdp", ("head", "tensor")),
        P(("head", "tensor"), "fsdp"),
        P(("fsdp", "head", "tensor"), None),
    )
    return jax.shard_map(
        body,
        mesh=mesh,
        in_specs=placed,
        out_specs=(
            P(("fsdp", "head", "tensor"), None),
            P(("fsdp", "head", "tensor"), None),
            P(),
            P("fsdp", "head", "tensor", None),
            P("fsdp", "head", "tensor", None),
            P("fsdp", "head", "tensor"),
            P("head", "tensor", "fsdp"),
            P(),
            P(),
            P(),
            P("fsdp", ("head", "tensor")),
            P("fsdp", ("head", "tensor")),
            P(("head", "tensor"), "fsdp"),
        ),
        check_vma=False,
    )
```

time: 952 us -> 689 us (0.72)
  matrix products: 243 us -> 81.3 us
  Pallas kernels: 0 us -> 105 us
  local copies, waits for them, and re-layouts: 157 us -> 79.8 us
  other arithmetic: 141 us -> 70.6 us
  waiting for transfers between devices: 275 us -> 246 us
  starting transfers between devices: 120 us -> 94.4 us
    dot_general x15, matrix products: 198 us -> 81.3 us  [contract(): lax.dot_general(left_side, right_side, (((left_dim,), (right_dim,)), ((),...]
    pallas_call x0 -> x9, Pallas kernels: none -> 105 us  [the longest x3 35.4 us: sum_over_units(): pl.pallas_call(functools.partial(sum_kernel, terms), grid=(count,), in_sp...]
    dot_general x24 -> x0, matrix products: 44.7 us -> none  [the longest x4 11.8 us: body(): jnp.einsum('mqv,kv->mqk', map_grad[:, start:stop], values[:stop], preferr...]
    unnamed x415 -> x186, local copies, waits for them, and re-layouts: 62.2 us -> 31.7 us
    ppermute x71 -> x51, waiting for transfers between devices: 107 us -> 77 us  [swap(): lax.ppermute(values, axis, [(place, place ^ mask) for place in range(size)])]
    another operation x13 -> x6, other arithmetic: 28.5 us -> 1.88 us  [the longest x2 0.87 us: body(): jnp.stack(in_order(output_grad[:value_half], output_grad[value_half:]))]
    ppermute x30, starting transfers between devices: 74.1 us -> 53.1 us  [shift(): lax.ppermute(values, axis, [(place, (place + step) % size) for place in r...]
    concatenate x14 -> x3, local copies, waits for them, and re-layouts: 18.4 us -> 1.14 us  [the longest x1 0.95 us: both_cores(): own = jnp.concatenate(line.gather(local), axis=1)]
  transfers between devices with their start and end apart: 101 -> 81, of which waited for: 36 -> 30; matrix products, arithmetic and copies ran while one was open for 44% -> 31% of each run, Pallas kernels for 0% -> 13%
where the time goes in v2:
time: 689 us; the launch traced here: 683 us
  waiting for transfers between devices  246 us (36%)
  Pallas kernels  105 us (15%)
  starting transfers between devices  94.4 us (14%)
  matrix products  81.3 us (12%)
  local copies, waits for them, and re-layouts  79.8 us (12%)
  other arithmetic  70.6 us (10%)
    ppermute x30, waiting for transfers between devices, shift(): lax.ppermute(values, axis, [(place, (place + step) % size) for place in r...  169 us
    dot_general x15, matrix products, contract(): lax.dot_general(left_side, right_side, (((left_dim,), (right_dim,)), ((),...  81.3 us
    ppermute x51, waiting for transfers between devices, swap(): lax.ppermute(values, axis, [(place, place ^ mask) for place in range(size)])  77 us
    ppermute x30, starting transfers between devices, shift(): lax.ppermute(values, axis, [(place, (place + step) % size) for place in r...  53.1 us
    ppermute x51, starting transfers between devices, swap(): lax.ppermute(values, axis, [(place, place ^ mask) for place in range(size)])  41.3 us
    pallas_call x3, Pallas kernels, sum_over_units(): pl.pallas_call(functools.partial(sum_kernel, terms), grid=(count,), in_sp...  35.4 us
    unnamed x186, local copies, waits for them, and re-layouts  31.7 us
    pallas_call x1, Pallas kernels, attention_backward(): pl.pallas_call(attention_backward_kernel, in_specs=[smem, smem] + [vmem]...  24.5 us
  transfers between devices with their start and end apart: 81, of which 30 were waited for; matrix products, arithmetic and copies ran while one was open for 31% of the time, Pallas kernels for 13%

profile of v2, /device:TPU:0, one launch (start us, length us, event | category | flops | bytes accessed | tf_op | source)
XLA Modules:
  0.0 683.1 jit_solution(7094900354790358036)
XLA Ops:
  6.7 5.0 collective-permute-start.4
  21.5 25.1 %collective-permute-done.5 = bf16[512,768]{1,0:T(8,128)(2,1)} collective-permute-done((bf16[512,768]{1,0:T(8,128)(2,1)}, bf16[512,768]{1,0:T(8,128)(2,1)}, u32[]{:S(2)}, u32[]{:S(2)}) %collective-permute-start.5) | collective-permute-done | bytes 786464 | tf_op jit(solution)/shard_map/ppermute | solution.py:35
  51.3 15.8 %collective-permute-done.6 = bf16[512,768]{1,0:T(8,128)(2,1)S(1)} collective-permute-done((bf16[512,768]{1,0:T(8,128)(2,1)}, bf16[512,768]{1,0:T(8,128)(2,1)S(1)}, u32[]{:S(2)}, u32[]{:S(2)}) %collective-permute-start.6) | collective-permute-done | bytes 786464 | tf_op jit(solution)/shard_map/ppermute | solution.py:35
  67.1 5.5 pad_maximum_fusion
  79.5 7.3 %collective-permute-done.11 = bf16[256,512]{1,0:T(8,128)(2,1)} collective-permute-done((bf16[256,512]{1,0:T(8,128)(2,1)}, bf16[256,512]{1,0:T(8,128)(2,1)}, u32[]{:S(2)}, u32[]{:S(2)}) %collective-permute-start.11) | collective-permute-done | bytes 262176 | tf_op jit(solution)/shard_map/ppermute | solution.py:35
  105.4 3.5 collective-permute-start.10
  108.9 6.1 fusion.122
  115.8 3.5 collective-permute-done.10
  119.5 5.3 fusion.121
  130.2 7.3 %collective-permute-done.27 = bf16[704,512]{1,0:T(8,128)(2,1)S(1)} collective-permute-done((bf16[704,512]{1,0:T(8,128)(2,1)S(1)}, bf16[704,512]{1,0:T(8,128)(2,1)S(1)}, u32[]{:S(2)}, u32[]{:S(2)}) %collective-permute-start.27) | collective-permute-done | bytes 720928 | tf_op jit(solution)/shard_map/ppermute | solution.py:35
  141.7 11.1 %attention_forward.1 = (bf16[2048,256]{1,0:T(8,128)(2,1)S(1)}, bf16[2048,768]{1,0:T(8,128)(2,1)S(1)}, f32[2,2048,256]{2,1,0:T(8,128)S(1)}, f32[2,2048]{1,0:T(2,128)S(1)}) custom-call(s32[4]{0:T(128)S(1)} %pad_add_fusion.ints, f32[2]{0:T(128)S(1)} %pad_maximum_fusion.27.floats, bf16[1024,768]{1,0:T(8,128)(2,1)S(1)} %slice_dynamic-update-slice_fusion.2.kept, ...), custom_call_target="tpu_custom_call" | custom-call | flops 20000000000 | bytes 16777216 | tf_op jit(solution)/shard_map/attention_forward/pallas_call | solution.py:200
  152.8 11.6 %slice.548 = bf16[1024,256]{1,0:T(8,128)(2,1)S(1)} slice(bf16[2048,256]{1,0:T(8,128)(2,1)S(1)} %get-tuple-element.67), slice={[1024:2048], [0:256]} | slice | bytes 1048576 | tf_op jit(solution)/shard_map/slice | solution.py:567
  164.7 5.2 collective-permute-done.28
  175.8 6.4 fusion.123
  182.2 3.5 collective-permute-done.18
  193.5 16.2 %collective-permute-done.31 = bf16[704,512]{1,0:T(8,128)(2,1)S(1)} collective-permute-done((bf16[704,512]{1,0:T(8,128)(2,1)S(1)}, bf16[704,512]{1,0:T(8,128)(2,1)S(1)}, u32[]{:S(2)}, u32[]{:S(2)}) %collective-permute-start.31) | collective-permute-done | bytes 720928 | tf_op jit(solution)/shard_map/ppermute | solution.py:35
  209.7 15.3 %collective-permute-done.33 = bf16[704,512]{1,0:T(8,128)(2,1)S(1)} collective-permute-done((bf16[704,512]{1,0:T(8,128)(2,1)S(1)}, bf16[704,512]{1,0:T(8,128)(2,1)S(1)}, u32[]{:S(2)}, u32[]{:S(2)}) %collective-permute-start.33) | collective-permute-done | bytes 720928 | tf_op jit(solution)/shard_map/ppermute | solution.py:35
  225.1 12.7 %collective-permute-start.34 = (bf16[704,512]{1,0:T(8,128)(2,1)S(1)}, bf16[704,512]{1,0:T(8,128)(2,1)S(1)}, u32[]{:S(2)}, u32[]{:S(2)}) collective-permute-start(bf16[704,512]{1,0:T(8,128)(2,1)S(1)} %collective-permute-done.33), channel_id=1, source_target_pairs={{0,8},{8,16},{16,24},{24,0},{1,9},{9,17},{17,25},{25,1},{2,10},{10... | collective-permute-start | bytes 2162696 | tf_op jit(solution)/shard_map/ppermute | solution.py:35
  243.8 7.9 %collective-permute-done.34 = bf16[704,512]{1,0:T(8,128)(2,1)S(1)} collective-permute-done((bf16[704,512]{1,0:T(8,128)(2,1)S(1)}, bf16[704,512]{1,0:T(8,128)(2,1)S(1)}, u32[]{:S(2)}, u32[]{:S(2)}) %collective-permute-start.34) | collective-permute-done | bytes 720928 | tf_op jit(solution)/shard_map/ppermute | solution.py:35
  253.6 3.7 fusion.70
  262.7 7.3 %collective-permute-done.22 = bf16[256,2048]{1,0:T(8,128)(2,1)} collective-permute-done((bf16[256,2048]{1,0:T(8,128)(2,1)}, bf16[256,2048]{1,0:T(8,128)(2,1)}, u32[]{:S(2)}, u32[]{:S(2)}) %collective-permute-start.22) | collective-permute-done | bytes 1048608 | tf_op jit(solution)/shard_map/ppermute | solution.py:30
  276.0 4.9 collective-permute-done.24
  287.4 10.0 %gate_units.2 = (bf16[704,1024]{1,0:T(8,128)(2,1)S(1)}, bf16[704,1024]{1,0:T(8,128)(2,1)S(1)}, bf16[704,1024]{1,0:T(8,128)(2,1)S(1)}) custom-call(bf16[1024,2048]{1,0:T(8,128)(2,1)S(1)} %copy-done.7, bf16[704,2048]{1,0:T(8,128)(2,1)S(1)} %pad_maximum_fusion.1.gate.refs_4_, bf16[704,2048]{1,0:T(8,128)(2,1)} %pad_maximum_fusion.2.up.refs_5_), custom_call_target="tpu_custom_call" | custom-call | flops 5905580032 | bytes 16777216 | tf_op jit(solution)/shard_map/gate_units/pallas_call | solution.py:376
  298.5 6.3 gate_grads.2
  307.1 10.9 %gate_units.3 = (bf16[704,1024]{1,0:T(8,128)(2,1)S(1)}, bf16[704,1024]{1,0:T(8,128)(2,1)S(1)}, bf16[704,1024]{1,0:T(8,128)(2,1)S(1)}) custom-call(bf16[1024,2048]{1,0:T(8,128)(2,1)S(1)} %copy-done.8, bf16[704,2048]{1,0:T(8,128)(2,1)} %collective-permute-done.36.gate.refs_6_, bf16[704,2048]{1,0:T(8,128)(2,1)} %collective-permute-done.37.up.refs_7_), custom_call_target="tpu_custom_call" | custom-call | flops 5905580032 | bytes 16777216 | tf_op jit(solution)/shard_map/gate_units/pallas_call | solution.py:376
  318.0 7.1 %gate_grads.3 = (bf16[704,1024]{1,0:T(8,128)(2,1)S(1)}, bf16[704,1024]{1,0:T(8,128)(2,1)S(1)}) custom-call(bf16[1024,2048]{1,0:T(8,128)(2,1)S(1)} %copy-done.12, bf16[704,2048]{1,0:T(8,128)(2,1)} %collective-permute-done.35.down.refs_3_, bf16[704,1024]{1,0:T(8,128)(2,1)S(1)} %get-tuple-element.88.gate_factor, bf16[704,1024]{1,0:T(8,128)(2,1)S(1)} %get-tuple-element.89.up_factor), custom_call_target="tpu_custom_call" | custom-call | flops 2952790016 | bytes 16777216 | tf_op jit(solution)/shard_map/gate_grads/pallas_call | solution.py:403
  326.2 8.0 %sum_over_units.3 = bf16[256,2048]{1,0:T(8,128)(2,1)S(1)} custom-call(bf16[704,1024]{1,0:T(8,128)(2,1)S(1)} %get-tuple-element.103.refs_0_, bf16[704,1024]{1,0:T(8,128)(2,1)S(1)} %get-tuple-element.102.refs_1_, bf16[704,1024]{1,0:T(8,128)(2,1)S(1)} %get-tuple-element.90.refs_2_, bf16[704,1024]{1,0:T(8,128)(2,1)} %copy-done.3, bf16[704,2048]{1,0:T(8,128)(2,1)} %copy-done.2, ...), custom_call_target="tpu_custom_call" | custom-call | flops 2952790016 | bytes 16777216 | tf_op jit(solution)/shard_map/sum_over_units/pallas_call | solution.py:433
  336.3 16.1 %sum_over_units.4 = bf16[768,2048]{1,0:T(8,128)(2,1)} custom-call(bf16[704,1024]{1,0:T(8,128)(2,1)S(1)} %get-tuple-element.103.refs_0_, bf16[704,1024]{1,0:T(8,128)(2,1)S(1)} %get-tuple-element.102.refs_1_, bf16[704,1024]{1,0:T(8,128)(2,1)S(1)} %get-tuple-element.90.refs_2_, bf16[704,1024]{1,0:T(8,128)(2,1)S(1)} %copy-done.4, bf16[704,2048]{1,0:T(8,128)(2,1)} %copy-done.2, ...), custom_call_target="tpu_custom_call" | custom-call | flops 8858370048 | bytes 16777216 | tf_op jit(solution)/shard_map/sum_over_units/pallas_call | solution.py:433
  361.2 4.6 convolution_convert_fusion.1
  366.3 12.5 %collective-permute-done.41 = bf16[256,2048]{1,0:T(8,128)(2,1)S(1)} collective-permute-done((bf16[256,2048]{1,0:T(8,128)(2,1)S(1)}, bf16[256,2048]{1,0:T(8,128)(2,1)S(1)}, u32[]{:S(2)}, u32[]{:S(2)}) %collective-permute-start.41) | collective-permute-done | bytes 1048608 | tf_op jit(solution)/shard_map/ppermute | solution.py:30
  385.9 3.5 convolution_convert_fusion.2
  389.6 16.5 %collective-permute-done.43 = bf16[256,2048]{1,0:T(8,128)(2,1)S(1)} collective-permute-done((bf16[256,2048]{1,0:T(8,128)(2,1)S(1)}, bf16[256,2048]{1,0:T(8,128)(2,1)S(1)}, u32[]{:S(2)}, u32[]{:S(2)}) %collective-permute-start.43) | collective-permute-done | bytes 1048608 | tf_op jit(solution)/shard_map/ppermute | solution.py:30
  412.4 4.7 add_convert_fusion.1
  433.3 11.3 %sum_over_units.5 = bf16[1024,2048]{1,0:T(8,128)(2,1)} custom-call(bf16[704,1024]{1,0:T(8,128)(2,1)S(1)} %copy-done.14, bf16[704,1024]{1,0:T(8,128)(2,1)S(1)} %copy-done.16, bf16[704,2048]{1,0:T(8,128)(2,1)} %constant_dynamic-update-slice_fusion.15.down.refs_2_, bf16[704,2048]{1,0:T(8,128)(2,1)} %collective-permute-done.35.down.refs_3_), custom_call_target="tpu_custom_call" | custom-call | flops 5905580032 | bytes 8388608 | tf_op jit(solution)/shard_map/sum_over_units/pallas_call | solution.py:433
  447.2 5.0 convolution_convert_fusion.5
  452.4 4.6 fusion.94
  468.7 24.5 %attention_backward.1 = (bf16[2048,768]{1,0:T(8,128)(2,1)}, f32[1,256]{1,0:T(1,128)S(1)}, f32[1,256]{1,0:T(1,128)S(1)}) custom-call(s32[4]{0:T(128)S(1)} %pad_add_fusion.ints, f32[2]{0:T(128)S(1)} %pad_maximum_fusion.27.floats, bf16[2048,768]{1,0:T(8,128)(2,1)} %copy-done.18, bf16[1024,256]{1,0:T(8,128)(2,1)S(1)} %pad_maximum_fusion.20.grads_kept, ...), custom_call_target="tpu_custom_call" | custom-call | flops 40000000000 | bytes 25165824 | tf_op jit(solution)/shard_map/attention_backward/pallas_call | solution.py:336
  507.3 3.7 collective-permute-start.68
  515.1 18.8 %multiply_reduce_fusion = (f32[2048]{0:T(1024)S(1)}, bf16[1024,2048]{1,0:T(8,128)(2,1)}, f32[1024,2048]{1,0:T(8,128)}) fusion(bf16[1024,2048]{1,0:T(8,128)(2,1)} %constant_dynamic-update-slice_fusion, bf16[2048,768]{1,0:T(8,128)(2,1)} %collective-permute-done.7, bf16[512,768]{1,0:T(8,128)(2,1)} %collective-permute-done.5, bf16[512,768]{1,0:T(8,128)(2,1)S(1)} %copy-done.51, ...), kind=kOutput, calls=%fused_computation | convolution fusion | flops 6501169152 | bytes 26222592 | tf_op jit(solution)/shard_map/dot_general | solution.py:16
  538.6 6.2 collective-permute-start.77
  549.0 4.9 convolution_convert_fusion
  555.7 20.7 %collective-permute-done.59 = f32[10240]{0:T(1024)S(1)} collective-permute-done((f32[10240]{0:T(1024)S(1)}, f32[10240]{0:T(1024)S(1)}, u32[]{:S(2)}, u32[]{:S(2)}) %collective-permute-start.59) | collective-permute-done | bytes 40992 | tf_op jit(solution)/shard_map/ppermute | solution.py:30
  599.4 12.4 %collective-permute-done.70 = bf16[704,512]{1,0:T(8,128)(2,1)S(1)} collective-permute-done((bf16[704,512]{1,0:T(8,128)(2,1)S(1)}, bf16[704,512]{1,0:T(8,128)(2,1)S(1)}, u32[]{:S(2)}, u32[]{:S(2)}) %collective-permute-start.70) | collective-permute-done | bytes 720928 | tf_op jit(solution)/shard_map/ppermute | solution.py:35
  620.1 5.4 add_convert_fusion
  627.8 3.4 collective-permute-start.80
  631.2 16.8 %collective-permute-done.72 = bf16[512,768]{1,0:T(8,128)(2,1)S(1)} collective-permute-done((bf16[512,768]{1,0:T(8,128)(2,1)S(1)}, bf16[512,768]{1,0:T(8,128)(2,1)S(1)}, u32[]{:S(2)}, u32[]{:S(2)}) %collective-permute-start.72) | collective-permute-done | bytes 786464 | tf_op jit(solution)/shard_map/ppermute | solution.py:35
  650.8 13.8 %collective-permute-done.80 = bf16[512,768]{1,0:T(8,128)(2,1)S(1)} collective-permute-done((bf16[512,768]{1,0:T(8,128)(2,1)S(1)}, bf16[512,768]{1,0:T(8,128)(2,1)S(1)}, u32[]{:S(2)}, u32[]{:S(2)}) %collective-permute-start.80) | collective-permute-done | bytes 786464 | tf_op jit(solution)/shard_map/ppermute | solution.py:35
  664.6 13.9 %collective-permute-done.73 = bf16[512,768]{1,0:T(8,128)(2,1)S(1)} collective-permute-done((bf16[512,768]{1,0:T(8,128)(2,1)S(1)}, bf16[512,768]{1,0:T(8,128)(2,1)S(1)}, u32[]{:S(2)}, u32[]{:S(2)}) %collective-permute-start.73) | collective-permute-done | bytes 786464 | tf_op jit(solution)/shard_map/ppermute | solution.py:35
  (466 shorter events, 221.2 us)
Async XLA Ops:
  6.7 44.6 %collective-permute-start.4 = (bf16[512,768]{1,0:T(8,128)(2,1)}, bf16[512,768]{1,0:T(8,128)(2,1)}, u32[]{:S(2)}, u32[]{:S(2)}) collective-permute-start(bf16[512,768]{1,0:T(8,128)(2,1)} %pad_maximum_fusion.16), channel_id=1, source_target_pairs={{0,24},{8,0},{16,8},{24,16},{1,25},{9,1},{17,9},{25,17},{2,26},{10... | collective-permute-start | bytes 2359304 | tf_op jit(solution)/shard_map/ppermute | solution.py:35
  11.8 34.9 %collective-permute-start.5 = (bf16[512,768]{1,0:T(8,128)(2,1)}, bf16[512,768]{1,0:T(8,128)(2,1)}, u32[]{:S(2)}, u32[]{:S(2)}) collective-permute-start(bf16[512,768]{1,0:T(8,128)(2,1)} %pad_maximum_fusion.16), channel_id=1, source_target_pairs={{0,8},{8,16},{16,24},{24,0},{1,9},{9,17},{17,25},{25,1},{2,10},{10... | collective-permute-start | bytes 2359304 | tf_op jit(solution)/shard_map/ppermute | solution.py:35
  15.2 71.6 %collective-permute-start = (bf16[256,2048]{1,0:T(8,128)(2,1)}, bf16[256,2048]{1,0:T(8,128)(2,1)}, u32[]{:S(2)}, u32[]{:S(2)}) collective-permute-start(bf16[256,2048]{1,0:T(8,128)(2,1)} %get-tuple-element.148), channel_id=1, source_target_pairs={{0,2},{2,0},{4,6},{6,4},{1,3},{3,1},{5,7},{7,5},{8,10},{10,8},{12,... | collective-permute-start | bytes 3145736 | tf_op jit(solution)/shard_map/ppermute | solution.py:30
  16.7 59.4 %collective-permute-start.1 = (bf16[256,2048]{1,0:T(8,128)(2,1)}, bf16[256,2048]{1,0:T(8,128)(2,1)}, u32[]{:S(2)}, u32[]{:S(2)}) collective-permute-start(bf16[256,2048]{1,0:T(8,128)(2,1)} %get-tuple-element.148), channel_id=1, source_target_pairs={{0,4},{2,6},{4,0},{6,2},{1,5},{3,7},{5,1},{7,3},{8,12},{10,14},{12... | collective-permute-start | bytes 3145736 | tf_op jit(solution)/shard_map/ppermute | solution.py:30
  72.5 47.0 %collective-permute-start.7 = (bf16[2048,768]{1,0:T(8,128)(2,1)}, bf16[2048,768]{1,0:T(8,128)(2,1)}, u32[]{:S(2)}, u32[]{:S(2)}) collective-permute-start(bf16[2048,768]{1,0:T(8,128)(2,1)} %pad_maximum_fusion), channel_id=1, source_target_pairs={{0,1},{1,0},{2,3},{3,2},{4,5},{5,4},{6,7},{7,6},{8,9},{9,8},{10,11... | collective-permute-start | bytes 9437192 | tf_op jit(solution)/shard_map/ppermute | solution.py:30
  96.8 32.8 %collective-permute-start.26 = (bf16[704,512]{1,0:T(8,128)(2,1)S(1)}, bf16[704,512]{1,0:T(8,128)(2,1)S(1)}, u32[]{:S(2)}, u32[]{:S(2)}) collective-permute-start(bf16[704,512]{1,0:T(8,128)(2,1)S(1)} %bitcast.71), channel_id=1, source_target_pairs={{0,24},{8,0},{16,8},{24,16},{1,25},{9,1},{17,9},{25,17},{2,26},{10... | collective-permute-start | bytes 2162696 | tf_op jit(solution)/shard_map/ppermute | solution.py:35
  102.4 36.0 %collective-permute-start.14 = (bf16[256,2048]{1,0:T(8,128)(2,1)S(1)}, bf16[256,2048]{1,0:T(8,128)(2,1)S(1)}, u32[]{:S(2)}, u32[]{:S(2)}) collective-permute-start(bf16[256,2048]{1,0:T(8,128)(2,1)S(1)} %fusion.30), channel_id=1, source_target_pairs={{0,2},{2,0},{4,6},{6,4},{1,3},{3,1},{5,7},{7,5},{8,10},{10,8},{12,... | collective-permute-start | bytes 3145736 | tf_op jit(solution)/shard_map/ppermute | solution.py:30
  103.9 33.6 %collective-permute-start.15 = (bf16[256,2048]{1,0:T(8,128)(2,1)S(1)}, bf16[256,2048]{1,0:T(8,128)(2,1)S(1)}, u32[]{:S(2)}, u32[]{:S(2)}) collective-permute-start(bf16[256,2048]{1,0:T(8,128)(2,1)S(1)} %fusion.30), channel_id=1, source_target_pairs={{0,4},{2,6},{4,0},{6,2},{1,5},{3,7},{5,1},{7,3},{8,12},{10,14},{12... | collective-permute-start | bytes 3145736 | tf_op jit(solution)/shard_map/ppermute | solution.py:30
  129.6 41.5 %collective-permute-start.13 = (bf16[256,2048]{1,0:T(8,128)(2,1)S(1)}, bf16[256,2048]{1,0:T(8,128)(2,1)}, u32[]{:S(2)}, u32[]{:S(2)}) collective-permute-start(bf16[256,2048]{1,0:T(8,128)(2,1)S(1)} %pad_maximum_fusion.5), channel_id=1, source_target_pairs={{0,1},{1,0},{2,3},{3,2},{4,5},{5,4},{6,7},{7,6},{8,9},{9,8},{10,11... | collective-permute-start | bytes 3145736 | tf_op jit(solution)/shard_map/ppermute | solution.py:30
  137.4 51.2 %collective-permute-start.30 = (bf16[704,512]{1,0:T(8,128)(2,1)S(1)}, bf16[704,512]{1,0:T(8,128)(2,1)S(1)}, u32[]{:S(2)}, u32[]{:S(2)}) collective-permute-start(bf16[704,512]{1,0:T(8,128)(2,1)S(1)} %bitcast.74), channel_id=1, source_target_pairs={{0,8},{8,16},{16,24},{24,0},{1,9},{9,17},{17,25},{25,1},{2,10},{10... | collective-permute-start | bytes 2162696 | tf_op jit(solution)/shard_map/ppermute | solution.py:35
  137.4 32.5 %collective-permute-start.28 = (bf16[704,512]{1,0:T(8,128)(2,1)S(1)}, bf16[704,512]{1,0:T(8,128)(2,1)S(1)}, u32[]{:S(2)}, u32[]{:S(2)}) collective-permute-start(bf16[704,512]{1,0:T(8,128)(2,1)S(1)} %collective-permute-done.27), channel_id=1, source_target_pairs={{0,8},{8,16},{16,24},{24,0},{1,9},{9,17},{17,25},{25,1},{2,10},{10... | collective-permute-start | bytes 2162696 | tf_op jit(solution)/shard_map/ppermute | solution.py:35
  138.4 26.0 %collective-permute-start.16 = (bf16[128,2048]{1,0:T(8,128)(2,1)S(1)}, bf16[128,2048]{1,0:T(8,128)(2,1)S(1)}, u32[]{:S(2)}, u32[]{:S(2)}) collective-permute-start(bf16[128,2048]{1,0:T(8,128)(2,1)S(1)} %slice.671), channel_id=1, source_target_pairs={{0,2},{2,0},{4,6},{6,4},{1,3},{3,1},{5,7},{7,5},{8,10},{10,8},{12,... | collective-permute-start | bytes 1572872 | tf_op jit(solution)/shard_map/ppermute | solution.py:30
  141.2 23.4 %collective-permute-start.17 = (bf16[128,2048]{1,0:T(8,128)(2,1)S(1)}, bf16[128,2048]{1,0:T(8,128)(2,1)S(1)}, u32[]{:S(2)}, u32[]{:S(2)}) collective-permute-start(bf16[128,2048]{1,0:T(8,128)(2,1)S(1)} %slice.672), channel_id=1, source_target_pairs={{0,4},{2,6},{4,0},{6,2},{1,5},{3,7},{5,1},{7,3},{8,12},{10,14},{12... | collective-permute-start | bytes 1572872 | tf_op jit(solution)/shard_map/ppermute | solution.py:30
  186.6 51.2 %collective-permute-start.21 = (bf16[256,2048]{1,0:T(8,128)(2,1)S(1)}, bf16[256,2048]{1,0:T(8,128)(2,1)S(1)}, u32[]{:S(2)}, u32[]{:S(2)}) collective-permute-start(bf16[256,2048]{1,0:T(8,128)(2,1)S(1)} %pad_maximum_fusion.7), channel_id=1, source_target_pairs={{0,4},{2,6},{4,0},{6,2},{1,5},{3,7},{5,1},{7,3},{8,12},{10,14},{12... | collective-permute-start | bytes 3145736 | tf_op jit(solution)/shard_map/ppermute | solution.py:30
  188.0 49.8 %collective-permute-start.19 = (bf16[256,2048]{1,0:T(8,128)(2,1)S(1)}, bf16[256,2048]{1,0:T(8,128)(2,1)S(1)}, u32[]{:S(2)}, u32[]{:S(2)}) collective-permute-start(bf16[256,2048]{1,0:T(8,128)(2,1)S(1)} %pad_maximum_fusion.6), channel_id=1, source_target_pairs={{0,2},{2,0},{4,6},{6,4},{1,3},{3,1},{5,7},{7,5},{8,10},{10,8},{12,... | collective-permute-start | bytes 3145736 | tf_op jit(solution)/shard_map/ppermute | solution.py:30
  190.1 35.0 %collective-permute-start.33 = (bf16[704,512]{1,0:T(8,128)(2,1)S(1)}, bf16[704,512]{1,0:T(8,128)(2,1)S(1)}, u32[]{:S(2)}, u32[]{:S(2)}) collective-permute-start(bf16[704,512]{1,0:T(8,128)(2,1)S(1)} %copy-done.58), channel_id=1, source_target_pairs={{0,8},{8,16},{16,24},{24,0},{1,9},{9,17},{17,25},{25,1},{2,10},{10... | collective-permute-start | bytes 2162696 | tf_op jit(solution)/shard_map/ppermute | solution.py:35
  193.4 111.4 %collective-permute-start.36 = (bf16[704,2048]{1,0:T(8,128)(2,1)S(1)}, bf16[704,2048]{1,0:T(8,128)(2,1)}, u32[]{:S(2)}, u32[]{:S(2)}) collective-permute-start(bf16[704,2048]{1,0:T(8,128)(2,1)S(1)} %pad_maximum_fusion.1.gate.refs_4_), channel_id=1, source_target_pairs={{0,1},{1,0},{2,3},{3,2},{4,5},{5,4},{6,7},{7,6},{8,9},{9,8},{10,11... | collective-permute-start | bytes 8650760 | tf_op jit(solution)/shard_map/ppermute | solution.py:30
  209.7 33.1 %collective-permute-start.32 = (bf16[704,512]{1,0:T(8,128)(2,1)S(1)}, bf16[704,512]{1,0:T(8,128)(2,1)S(1)}, u32[]{:S(2)}, u32[]{:S(2)}) collective-permute-start(bf16[704,512]{1,0:T(8,128)(2,1)S(1)} %copy-done.58), channel_id=1, source_target_pairs={{0,24},{8,0},{16,8},{24,16},{1,25},{9,1},{17,9},{25,17},{2,26},{10... | collective-permute-start | bytes 2162696 | tf_op jit(solution)/shard_map/ppermute | solution.py:35
  225.1 26.6 %collective-permute-start.34 = (bf16[704,512]{1,0:T(8,128)(2,1)S(1)}, bf16[704,512]{1,0:T(8,128)(2,1)S(1)}, u32[]{:S(2)}, u32[]{:S(2)}) collective-permute-start(bf16[704,512]{1,0:T(8,128)(2,1)S(1)} %collective-permute-done.33), channel_id=1, source_target_pairs={{0,8},{8,16},{16,24},{24,0},{1,9},{9,17},{17,25},{25,1},{2,10},{10... | collective-permute-start | bytes 2162696 | tf_op jit(solution)/shard_map/ppermute | solution.py:35
  242.8 62.0 %collective-permute-start.37 = (bf16[704,2048]{1,0:T(8,128)(2,1)}, bf16[704,2048]{1,0:T(8,128)(2,1)}, u32[]{:S(2)}, u32[]{:S(2)}) collective-permute-start(bf16[704,2048]{1,0:T(8,128)(2,1)} %pad_maximum_fusion.2.up.refs_5_), channel_id=1, source_target_pairs={{0,1},{1,0},{2,3},{3,2},{4,5},{5,4},{6,7},{7,6},{8,9},{9,8},{10,11... | collective-permute-start | bytes 8650760 | tf_op jit(solution)/shard_map/ppermute | solution.py:30
  243.8 26.3 %collective-permute-start.22 = (bf16[256,2048]{1,0:T(8,128)(2,1)}, bf16[256,2048]{1,0:T(8,128)(2,1)}, u32[]{:S(2)}, u32[]{:S(2)}) collective-permute-start(bf16[256,2048]{1,0:T(8,128)(2,1)} %get-tuple-element.142), channel_id=1, source_target_pairs={{0,2},{2,0},{4,6},{6,4},{1,3},{3,1},{5,7},{7,5},{8,10},{10,8},{12,... | collective-permute-start | bytes 3145736 | tf_op jit(solution)/shard_map/ppermute | solution.py:30
  253.6 64.4 %collective-permute-start.35 = (bf16[704,2048]{1,0:T(8,128)(2,1)}, bf16[704,2048]{1,0:T(8,128)(2,1)}, u32[]{:S(2)}, u32[]{:S(2)}) collective-permute-start(bf16[704,2048]{1,0:T(8,128)(2,1)} %constant_dynamic-update-slice_fusion.15.down.refs_2_), channel_id=1, source_target_pairs={{0,1},{1,0},{2,3},{3,2},{4,5},{5,4},{6,7},{7,6},{8,9},{9,8},{10,11... | collective-permute-start | bytes 8650760 | tf_op jit(solution)/shard_map/ppermute | solution.py:30
  355.4 23.4 %collective-permute-start.41 = (bf16[256,2048]{1,0:T(8,128)(2,1)S(1)}, bf16[256,2048]{1,0:T(8,128)(2,1)S(1)}, u32[]{:S(2)}, u32[]{:S(2)}) collective-permute-start(bf16[256,2048]{1,0:T(8,128)(2,1)S(1)} %pad_maximum_fusion.9), channel_id=1, source_target_pairs={{0,4},{2,6},{4,0},{6,2},{1,5},{3,7},{5,1},{7,3},{8,12},{10,14},{12... | collective-permute-start | bytes 3145736 | tf_op jit(solution)/shard_map/ppermute | solution.py:30
  356.2 23.1 %collective-permute-start.39 = (bf16[256,2048]{1,0:T(8,128)(2,1)S(1)}, bf16[256,2048]{1,0:T(8,128)(2,1)S(1)}, u32[]{:S(2)}, u32[]{:S(2)}) collective-permute-start(bf16[256,2048]{1,0:T(8,128)(2,1)S(1)} %pad_maximum_fusion.8), channel_id=1, source_target_pairs={{0,2},{2,0},{4,6},{6,4},{1,3},{3,1},{5,7},{7,5},{8,10},{10,8},{12,... | collective-permute-start | bytes 3145736 | tf_op jit(solution)/shard_map/ppermute | solution.py:30
  361.1 57.3 %collective-permute-start.63 = (bf16[704,2048]{1,0:T(8,128)(2,1)S(1)}, bf16[704,2048]{1,0:T(8,128)(2,1)S(1)}, u32[]{:S(2)}, u32[]{:S(2)}) collective-permute-start(bf16[704,2048]{1,0:T(8,128)(2,1)S(1)} %convolution_convert_fusion.3), channel_id=1, source_target_pairs={{0,1},{1,0},{2,3},{3,2},{4,5},{5,4},{6,7},{7,6},{8,9},{9,8},{10,11... | collective-permute-start | bytes 8650760 | tf_op jit(solution)/shard_map/ppermute | solution.py:30
  365.8 46.5 %collective-permute-start.65 = (bf16[704,2048]{1,0:T(8,128)(2,1)}, bf16[704,2048]{1,0:T(8,128)(2,1)}, u32[]{:S(2)}, u32[]{:S(2)}) collective-permute-start(bf16[704,2048]{1,0:T(8,128)(2,1)} %convolution_convert_fusion.1), channel_id=1, source_target_pairs={{0,1},{1,0},{2,3},{3,2},{4,5},{5,4},{6,7},{7,6},{8,9},{9,8},{10,11... | collective-permute-start | bytes 8650760 | tf_op jit(solution)/shard_map/ppermute | solution.py:30
  383.4 25.2 %collective-permute-start.42 = (bf16[256,2048]{1,0:T(8,128)(2,1)S(1)}, bf16[256,2048]{1,0:T(8,128)(2,1)S(1)}, u32[]{:S(2)}, u32[]{:S(2)}) collective-permute-start(bf16[256,2048]{1,0:T(8,128)(2,1)S(1)} %get-tuple-element.139), channel_id=1, source_target_pairs={{0,2},{2,0},{4,6},{6,4},{1,3},{3,1},{5,7},{7,5},{8,10},{10,8},{12,... | collective-permute-start | bytes 3145736 | tf_op jit(solution)/shard_map/ppermute | solution.py:30
  389.4 36.7 %collective-permute-start.64 = (bf16[704,2048]{1,0:T(8,128)(2,1)S(1)}, bf16[704,2048]{1,0:T(8,128)(2,1)S(1)}, u32[]{:S(2)}, u32[]{:S(2)}) collective-permute-start(bf16[704,2048]{1,0:T(8,128)(2,1)S(1)} %convolution_convert_fusion.2), channel_id=1, source_target_pairs={{0,1},{1,0},{2,3},{3,2},{4,5},{5,4},{6,7},{7,6},{8,9},{9,8},{10,11... | collective-permute-start | bytes 8650760 | tf_op jit(solution)/shard_map/ppermute | solution.py:30
  406.1 25.4 %collective-permute-start.44 = (bf16[128,2048]{1,0:T(8,128)(2,1)S(1)}, bf16[128,2048]{1,0:T(8,128)(2,1)S(1)}, u32[]{:S(2)}, u32[]{:S(2)}) collective-permute-start(bf16[128,2048]{1,0:T(8,128)(2,1)S(1)} %slice.684), channel_id=1, source_target_pairs={{0,2},{2,0},{4,6},{6,4},{1,3},{3,1},{5,7},{7,5},{8,10},{10,8},{12,... | collective-permute-start | bytes 1572872 | tf_op jit(solution)/shard_map/ppermute | solution.py:30
  408.7 23.8 %collective-permute-start.45 = (bf16[128,2048]{1,0:T(8,128)(2,1)S(1)}, bf16[128,2048]{1,0:T(8,128)(2,1)S(1)}, u32[]{:S(2)}, u32[]{:S(2)}) collective-permute-start(bf16[128,2048]{1,0:T(8,128)(2,1)S(1)} %slice.685), channel_id=1, source_target_pairs={{0,4},{2,6},{4,0},{6,2},{1,5},{3,7},{5,1},{7,3},{8,12},{10,14},{12... | collective-permute-start | bytes 1572872 | tf_op jit(solution)/shard_map/ppermute | solution.py:30
  418.4 40.9 %collective-permute-start.74 = (bf16[704,512]{1,0:T(8,128)(2,1)}, bf16[704,512]{1,0:T(8,128)(2,1)S(1)}, u32[]{:S(2)}, u32[]{:S(2)}) collective-permute-start(bf16[704,512]{1,0:T(8,128)(2,1)} %get-tuple-element.112), channel_id=1, source_target_pairs={{0,24},{8,0},{16,8},{24,16},{1,25},{9,1},{17,9},{25,17},{2,26},{10... | collective-permute-start | bytes 2162696 | tf_op jit(solution)/shard_map/ppermute | solution.py:35
  418.4 41.0 %collective-permute-start.66 = (bf16[704,512]{1,0:T(8,128)(2,1)}, bf16[704,512]{1,0:T(8,128)(2,1)}, u32[]{:S(2)}, u32[]{:S(2)}) collective-permute-start(bf16[704,512]{1,0:T(8,128)(2,1)} %get-tuple-element.104), channel_id=1, source_target_pairs={{0,8},{8,16},{16,24},{24,0},{1,9},{9,17},{17,25},{25,1},{2,10},{10... | collective-permute-start | bytes 2162696 | tf_op jit(solution)/shard_map/ppermute | solution.py:35
  459.4 40.4 %collective-permute-start.62 = (bf16[256,2048]{1,0:T(8,128)(2,1)}, bf16[256,2048]{1,0:T(8,128)(2,1)}, u32[]{:S(2)}, u32[]{:S(2)}) collective-permute-start(bf16[256,2048]{1,0:T(8,128)(2,1)} %slice.902), channel_id=1, source_target_pairs={{0,1},{1,0},{2,3},{3,2},{4,5},{5,4},{6,7},{7,6},{8,9},{9,8},{10,11... | collective-permute-start | bytes 3145736 | tf_op jit(solution)/shard_map/ppermute | solution.py:30
  459.5 45.3 %collective-permute-start.75 = (bf16[704,512]{1,0:T(8,128)(2,1)}, bf16[704,512]{1,0:T(8,128)(2,1)}, u32[]{:S(2)}, u32[]{:S(2)}) collective-permute-start(bf16[704,512]{1,0:T(8,128)(2,1)} %get-tuple-element.113), channel_id=1, source_target_pairs={{0,8},{8,16},{16,24},{24,0},{1,9},{9,17},{17,25},{25,1},{2,10},{10... | collective-permute-start | bytes 2162696 | tf_op jit(solution)/shard_map/ppermute | solution.py:35
  464.0 43.3 %collective-permute-start.67 = (bf16[704,512]{1,0:T(8,128)(2,1)}, bf16[704,512]{1,0:T(8,128)(2,1)}, u32[]{:S(2)}, u32[]{:S(2)}) collective-permute-start(bf16[704,512]{1,0:T(8,128)(2,1)} %add_convert_fusion.7), channel_id=1, source_target_pairs={{0,8},{8,16},{16,24},{24,0},{1,9},{9,17},{17,25},{25,1},{2,10},{10... | collective-permute-start | bytes 2162696 | tf_op jit(solution)/shard_map/ppermute | solution.py:35
  467.3 66.8 %collective-permute-start.49 = (bf16[256,2048]{1,0:T(8,128)(2,1)}, bf16[256,2048]{1,0:T(8,128)(2,1)}, u32[]{:S(2)}, u32[]{:S(2)}) collective-permute-start(bf16[256,2048]{1,0:T(8,128)(2,1)} %pad_maximum_fusion.11), channel_id=1, source_target_pairs={{0,4},{2,6},{4,0},{6,2},{1,5},{3,7},{5,1},{7,3},{8,12},{10,14},{12... | collective-permute-start | bytes 3145736 | tf_op jit(solution)/shard_map/ppermute | solution.py:30
  499.8 34.4 %collective-permute-start.47 = (bf16[256,2048]{1,0:T(8,128)(2,1)}, bf16[256,2048]{1,0:T(8,128)(2,1)}, u32[]{:S(2)}, u32[]{:S(2)}) collective-permute-start(bf16[256,2048]{1,0:T(8,128)(2,1)} %pad_maximum_fusion.10), channel_id=1, source_target_pairs={{0,2},{2,0},{4,6},{6,4},{1,3},{3,1},{5,7},{7,5},{8,10},{10,8},{12,... | collective-permute-start | bytes 3145736 | tf_op jit(solution)/shard_map/ppermute | solution.py:30
  507.1 31.5 %collective-permute-start.76 = (bf16[704,512]{1,0:T(8,128)(2,1)}, bf16[704,512]{1,0:T(8,128)(2,1)}, u32[]{:S(2)}, u32[]{:S(2)}) collective-permute-start(bf16[704,512]{1,0:T(8,128)(2,1)} %add_convert_fusion.5), channel_id=1, source_target_pairs={{0,8},{8,16},{16,24},{24,0},{1,9},{9,17},{17,25},{25,1},{2,10},{10... | collective-permute-start | bytes 2162696 | tf_op jit(solution)/shard_map/ppermute | solution.py:35
  507.3 37.5 %collective-permute-start.68 = (bf16[704,512]{1,0:T(8,128)(2,1)}, bf16[704,512]{1,0:T(8,128)(2,1)}, u32[]{:S(2)}, u32[]{:S(2)}) collective-permute-start(bf16[704,512]{1,0:T(8,128)(2,1)} %get-tuple-element.106), channel_id=1, source_target_pairs={{0,24},{8,0},{16,8},{24,16},{1,25},{9,1},{17,9},{25,17},{2,26},{10... | collective-permute-start | bytes 2162696 | tf_op jit(solution)/shard_map/ppermute | solution.py:35
  538.6 46.6 %collective-permute-start.77 = (bf16[704,512]{1,0:T(8,128)(2,1)}, bf16[704,512]{1,0:T(8,128)(2,1)S(1)}, u32[]{:S(2)}, u32[]{:S(2)}) collective-permute-start(bf16[704,512]{1,0:T(8,128)(2,1)} %get-tuple-element.115), channel_id=1, source_target_pairs={{0,24},{8,0},{16,8},{24,16},{1,25},{9,1},{17,9},{25,17},{2,26},{10... | collective-permute-start | bytes 2162696 | tf_op jit(solution)/shard_map/ppermute | solution.py:35
  544.8 42.6 %collective-permute-start.69 = (bf16[704,512]{1,0:T(8,128)(2,1)}, bf16[704,512]{1,0:T(8,128)(2,1)S(1)}, u32[]{:S(2)}, u32[]{:S(2)}) collective-permute-start(bf16[704,512]{1,0:T(8,128)(2,1)} %get-tuple-element.107), channel_id=1, source_target_pairs={{0,8},{8,16},{16,24},{24,0},{1,9},{9,17},{17,25},{25,1},{2,10},{10... | collective-permute-start | bytes 2162696 | tf_op jit(solution)/shard_map/ppermute | solution.py:35
  548.9 27.5 %collective-permute-start.59 = (f32[10240]{0:T(1024)S(1)}, f32[10240]{0:T(1024)S(1)}, u32[]{:S(2)}, u32[]{:S(2)}) collective-permute-start(f32[10240]{0:T(1024)S(1)} %add.308), channel_id=1, source_target_pairs={{0,8},{8,0},{16,24},{24,16},{1,9},{9,1},{17,25},{25,17},{2,10},{10... | collective-permute-start | bytes 122888 | tf_op jit(solution)/shard_map/ppermute | solution.py:30
  555.6 64.4 %collective-permute-start.61 = (bf16[2048,768]{1,0:T(8,128)(2,1)}, bf16[2048,768]{1,0:T(8,128)(2,1)}, u32[]{:S(2)}, u32[]{:S(2)}) collective-permute-start(bf16[2048,768]{1,0:T(8,128)(2,1)} %convolution_convert_fusion), channel_id=1, source_target_pairs={{0,1},{1,0},{2,3},{3,2},{4,5},{5,4},{6,7},{7,6},{8,9},{9,8},{10,11... | collective-permute-start | bytes 9437192 | tf_op jit(solution)/shard_map/ppermute | solution.py:30
  588.8 23.0 %collective-permute-start.70 = (bf16[704,512]{1,0:T(8,128)(2,1)S(1)}, bf16[704,512]{1,0:T(8,128)(2,1)S(1)}, u32[]{:S(2)}, u32[]{:S(2)}) collective-permute-start(bf16[704,512]{1,0:T(8,128)(2,1)S(1)} %add_convert_fusion.6), channel_id=1, source_target_pairs={{0,8},{8,16},{16,24},{24,0},{1,9},{9,17},{17,25},{25,1},{2,10},{10... | collective-permute-start | bytes 2162696 | tf_op jit(solution)/shard_map/ppermute | solution.py:35
  595.1 32.0 %collective-permute-start.55 = (bf16[256,2048]{1,0:T(8,128)(2,1)S(1)}, bf16[256,2048]{1,0:T(8,128)(2,1)S(1)}, u32[]{:S(2)}, u32[]{:S(2)}) collective-permute-start(bf16[256,2048]{1,0:T(8,128)(2,1)S(1)} %pad_maximum_fusion.15), channel_id=1, source_target_pairs={{0,4},{2,6},{4,0},{6,2},{1,5},{3,7},{5,1},{7,3},{8,12},{10,14},{12... | collective-permute-start | bytes 3145736 | tf_op jit(solution)/shard_map/ppermute | solution.py:30
  595.9 31.2 %collective-permute-start.53 = (bf16[256,2048]{1,0:T(8,128)(2,1)S(1)}, bf16[256,2048]{1,0:T(8,128)(2,1)S(1)}, u32[]{:S(2)}, u32[]{:S(2)}) collective-permute-start(bf16[256,2048]{1,0:T(8,128)(2,1)S(1)} %pad_maximum_fusion.14), channel_id=1, source_target_pairs={{0,2},{2,0},{4,6},{6,4},{1,3},{3,1},{5,7},{7,5},{8,10},{10,8},{12,... | collective-permute-start | bytes 3145736 | tf_op jit(solution)/shard_map/ppermute | solution.py:30
  627.8 36.9 %collective-permute-start.80 = (bf16[512,768]{1,0:T(8,128)(2,1)S(1)}, bf16[512,768]{1,0:T(8,128)(2,1)S(1)}, u32[]{:S(2)}, u32[]{:S(2)}) collective-permute-start(bf16[512,768]{1,0:T(8,128)(2,1)S(1)} %get-tuple-element.118), channel_id=1, source_target_pairs={{0,24},{8,0},{16,8},{24,16},{1,25},{9,1},{17,9},{25,17},{2,26},{10... | collective-permute-start | bytes 2359304 | tf_op jit(solution)/shard_map/ppermute | solution.py:35
  648.2 30.3 %collective-permute-start.73 = (bf16[512,768]{1,0:T(8,128)(2,1)S(1)}, bf16[512,768]{1,0:T(8,128)(2,1)S(1)}, u32[]{:S(2)}, u32[]{:S(2)}) collective-permute-start(bf16[512,768]{1,0:T(8,128)(2,1)S(1)} %add_convert_fusion.4), channel_id=1, source_target_pairs={{0,8},{8,16},{16,24},{24,0},{1,9},{9,17},{17,25},{25,1},{2,10},{10... | collective-permute-start | bytes 2359304 | tf_op jit(solution)/shard_map/ppermute | solution.py:35
  (115 other events, 1551.3 us)

commit v3 on v2

v3 whole, which is shorter than its diff:
```python
import functools

import jax
import jax.numpy as jnp
from jax import lax
from jax.experimental import pallas as pl
from jax.experimental.pallas import tpu as pltpu
from jax.sharding import PartitionSpec as P

lambda_base = 0.2
tile = 512
cost_share = 0.4
low = jnp.bfloat16


def contract(left_side, right_side, left_dim, right_dim):
    return lax.dot_general(
        left_side,
        right_side,
        (((left_dim,), (right_dim,)), ((), ())),
        preferred_element_type=jnp.float32,
    )


def after(values, *others):
    if not others:
        return values
    return lax.optimization_barrier((values, *others))[0]


def swap(values, axis, mask):
    size = lax.axis_size(axis)
    return lax.ppermute(values, axis, [(place, place ^ mask) for place in range(size)])


def fsdp_gather(own, axis, *others):
    return lax.all_gather(after(own, *others), "fsdp", axis=axis, tiled=True)


def fsdp_reduce(partial, axis):
    return lax.psum_scatter(partial, "fsdp", scatter_dimension=axis, tiled=True)


def shift(values, step):
    size = lax.axis_size("fsdp")
    return lax.ppermute(values, "fsdp", [(place, (place + step) % size) for place in range(size)])


def line_gather(own):
    size = lax.axis_size("fsdp")
    return [own] + [shift(own, -step) for step in range(1, size)]


def place_kernel(index, *refs):
    shards, out = refs[:-1], refs[-1]
    size, width = len(shards), shards[0].shape[1]
    for place, shard in enumerate(shards):
        to = lax.rem(index[0] + place, size) * width
        out[:, pl.ds(pl.multiple_of(to, width), width)] = shard[...]


def placed(shards):
    size = len(shards)
    rows, width = shards[0].shape
    vmem = pl.BlockSpec(memory_space=pltpu.VMEM)
    return pl.pallas_call(
        place_kernel,
        in_specs=[pl.BlockSpec(memory_space=pltpu.SMEM)] + [vmem] * size,
        out_specs=vmem,
        out_shape=jax.ShapeDtypeStruct((rows, size * width), low),
        cost_estimate=estimate(10**8),
        name="placed",
    )(lax.axis_index("fsdp")[None], *shards)


def add_low(left_side, right_side):
    return (left_side.astype(jnp.float32) + right_side.astype(jnp.float32)).astype(low)


def near_rows(own):
    return swap(own, "head", 1), swap(own, "head", 2)


def group_rows(own, near):
    half = own.shape[0] // 2
    first, second = near
    third_low = swap(second[:half], "head", 1)
    third_high = swap(first[half:], "head", 2)
    return jnp.concatenate([own, first, second, third_low, third_high], axis=0)


def join_kernel(start, near, to_first, to_second, first, second):
    rows = first.shape[0]
    half = rows // 2
    middle = start + rows
    first[:half] = near[start : start + half]
    first[half:] = add_low(near[start + half : middle], to_second[...])
    second[:half] = add_low(near[middle : middle + half], to_first[...])
    second[half:] = near[middle + half : middle + rows]


def group_reduce(near, start, third, own_part):
    rows, width = third.shape
    half = rows // 2
    to_first = swap(third[:half], "head", 1)
    to_second = swap(third[half:], "head", 2)
    own = own_part(to_first, to_second)
    vmem = pl.BlockSpec(memory_space=pltpu.VMEM)
    first, second = pl.pallas_call(
        functools.partial(join_kernel, start),
        in_specs=[vmem] * 3,
        out_specs=[vmem] * 2,
        out_shape=[jax.ShapeDtypeStruct((rows, width), low)] * 2,
        compiler_params=pltpu.CompilerParams(vmem_limit_bytes=24 * 2**20),
        cost_estimate=estimate(10**9),
        name="join",
    )(near, to_first, to_second)
    from_first = swap(first, "head", 1)
    from_second = swap(second, "head", 2)
    return (own, from_first, from_second), (first, second)


def summed(parts):
    return sum(part.astype(jnp.float32) for part in parts)


def total_over_all(values):
    for axis in ("tensor", "fsdp", "head"):
        mask = 1
        while mask < lax.axis_size(axis):
            values = values + swap(values, axis, mask)
            mask *= 2
    return values


def rolled(values, start):
    twice = jnp.concatenate([values, values], axis=-1)
    return lax.dynamic_slice_in_dim(twice, start, values.shape[-1], values.ndim - 1)


def slot_layout(lengths, slots):
    first_end = lengths[0, 0]
    second_end = first_end + lengths[0, 1]
    segment = (slots >= first_end).astype(jnp.int32) + (slots >= second_end).astype(jnp.int32)
    start = jnp.where(segment == 0, 0, jnp.where(segment == 1, first_end, second_end))
    return segment, slots - start


def estimate(flops):
    return pl.CostEstimate(
        flops=int(flops * cost_share), bytes_accessed=2**20, transcendentals=0
    )


def store_block(block, ints, values, kept, sent, columns):
    rows = values.shape[0]
    at = pl.ds(pl.multiple_of(((block >> 1) ^ ints[0]) * rows, rows), rows)

    @pl.when(ints[1] == (block & 1))
    def _():
        kept[at, columns] = values

    @pl.when(ints[1] != (block & 1))
    def _():
        sent[at, columns] = values


def row_starts(slots, first_end, second_end):
    return jnp.where(slots >= second_end, second_end, jnp.where(slots >= first_end, first_end, 0))


def attention_forward_kernel(
    ints,
    floats,
    kept_first,
    kept_second,
    received_first,
    received_second,
    gain,
    head_out_kept,
    head_out_sent,
    ordered,
    outs,
    log_totals,
):
    head_index, core, first_end, second_end = (ints[place] for place in range(4))
    rows = kept_first.shape[0] // 4
    slots = 8 * rows
    width = gain.shape[1]
    e = width // 2
    for parts, other in (
        ((kept_first, kept_second), 0),
        ((received_first, received_second), 1),
    ):
        for j in range(4):
            block = (head_index ^ j) * 2 + (core ^ other)
            at = pl.ds(pl.multiple_of(block * rows, rows), rows)
            for m in range(2):
                for kind in range(3):
                    to = (2 * kind + m) * e
                    ordered[at, to : to + e] = parts[m][
                        j * rows : (j + 1) * rows, kind * e : (kind + 1) * e
                    ]
    for start in range(0, slots, tile):
        stop = start + tile
        row = start + lax.broadcasted_iota(jnp.int32, (tile, 1), 0)
        begin = row_starts(row, first_end, second_end)
        value = ordered[:stop, 4 * e :]
        results = []
        for m in range(2):
            scores = contract(
                ordered[start:stop, m * e : (m + 1) * e],
                ordered[:stop, (2 + m) * e : (3 + m) * e],
                1,
                1,
            )
            column = lax.broadcasted_iota(jnp.int32, (tile, stop), 1)
            scores = jnp.where((column >= begin) & (column <= row), scores, -1e30)
            row_max = jnp.max(scores, axis=1, keepdims=True)
            expanded = jnp.exp(scores - row_max)
            row_total = jnp.sum(expanded, axis=1, keepdims=True)
            result = contract(expanded.astype(low), value, 1, 0) / row_total
            outs[m, start:stop, :] = result
            results.append(result)
            wide = jnp.broadcast_to(row_max + jnp.log(row_total), (tile, 128))
            log_totals[m : m + 1, start:stop] = jnp.transpose(wide)[:1]
        mixed = results[0] * floats[0] + results[1] * floats[1]
        scale = lax.rsqrt(jnp.mean(mixed * mixed, axis=1, keepdims=True) + 1e-05)
        normed = (mixed * scale * gain[...]).astype(low)
        for piece in range(tile // rows):
            store_block(
                start // rows + piece,
                ints,
                normed[piece * rows : (piece + 1) * rows],
                head_out_kept,
                head_out_sent,
                slice(None),
            )


def attention_forward(ints, floats, kept, received, gain):
    rows = kept[0].shape[0] // 4
    slots = 8 * rows
    width = gain.shape[1]
    vmem = pl.BlockSpec(memory_space=pltpu.VMEM)
    smem = pl.BlockSpec(memory_space=pltpu.SMEM)
    return pl.pallas_call(
        attention_forward_kernel,
        in_specs=[smem, smem] + [vmem] * 5,
        out_specs=[vmem] * 5,
        out_shape=[
            jax.ShapeDtypeStruct((slots // 2, width), low),
            jax.ShapeDtypeStruct((slots // 2, width), low),
            jax.ShapeDtypeStruct((slots, 3 * width), low),
            jax.ShapeDtypeStruct((2, slots, width), jnp.float32),
            jax.ShapeDtypeStruct((2, slots), jnp.float32),
        ],
        compiler_params=pltpu.CompilerParams(vmem_limit_bytes=40 * 2**20),
        cost_estimate=estimate(5 * 10**9),
        name="attention_forward",
    )(ints, floats, *kept, *received, gain)


def attention_backward_kernel(
    ints,
    floats,
    ordered,
    grads_kept,
    grads_received,
    outs,
    log_totals,
    gain,
    cosine,
    sine,
    kept_first,
    kept_second,
    sent_first,
    sent_second,
    gain_grad,
    lambda_grad,
    map_grads,
    deltas,
    query_grads,
    key_grads,
    value_grads,
):
    head_index, core, first_end, second_end = (ints[place] for place in range(4))
    rows = grads_kept.shape[0] // 4
    slots = 8 * rows
    width = gain.shape[1]
    e = width // 2
    gain_total = jnp.zeros((1, width), jnp.float32)
    lambda_total = jnp.zeros((1, width), jnp.float32)
    for part, other in ((grads_kept, 0), (grads_received, 1)):
        for j in range(4):
            block = (head_index ^ j) * 2 + (core ^ other)
            at = pl.ds(pl.multiple_of(block * rows, rows), rows)
            grad = part[j * rows : (j + 1) * rows, :].astype(jnp.float32)
            first, second = outs[0, at, :], outs[1, at, :]
            mixed = first * floats[0] + second * floats[1]
            scale = lax.rsqrt(jnp.mean(mixed * mixed, axis=1, keepdims=True) + 1e-05)
            gain_total += jnp.sum(grad * (mixed * scale), axis=0, keepdims=True)
            weighted = grad * gain[...]
            inner = jnp.mean(weighted * mixed, axis=1, keepdims=True)
            mixed_grad = scale * weighted - mixed * (scale * scale * scale * inner)
            lambda_total += jnp.sum(
                mixed_grad * jnp.where(core == 1, first, second), axis=0, keepdims=True
            )
            for m, out in ((0, first), (1, second)):
                map_grad = (mixed_grad * floats[m]).astype(low)
                map_grads[m, at, :] = map_grad
                delta = jnp.sum(map_grad.astype(jnp.float32) * out, axis=1, keepdims=True)
                deltas[m, :, at] = jnp.transpose(jnp.broadcast_to(delta, (rows, 128)))[:8]
    gain_grad[...] = gain_total * (1.0 - lambda_base)
    lambda_grad[...] = lambda_total
    query_grads[...] = jnp.zeros_like(query_grads)

    def pair(key_start, query_start, diagonal):
        at_keys = pl.ds(key_start, tile)
        at_queries = pl.ds(query_start, tile)
        column = query_start + lax.broadcasted_iota(jnp.int32, (1, tile), 1)
        begin = row_starts(column, first_end, second_end)
        row = key_start + lax.broadcasted_iota(jnp.int32, (tile, tile), 0)
        allowed = row >= begin
        if diagonal:
            allowed = allowed & (row <= column)
        value = ordered[at_keys, 4 * e :]
        for m in range(2):
            query = ordered[at_queries, m * e : (m + 1) * e]
            key = ordered[at_keys, (2 + m) * e : (3 + m) * e]
            map_grad = map_grads[m, at_queries, :]
            scores = contract(key, query, 1, 1)
            probability = jnp.where(
                allowed, jnp.exp(scores - log_totals[m : m + 1, at_queries]), 0.0
            )
            prob_grad = contract(value, map_grad, 1, 1)
            score_grad = (probability * (prob_grad - deltas[m, 0:1, at_queries])).astype(low)
            value_term = contract(probability.astype(low), map_grad, 1, 0)
            key_term = contract(score_grad, query, 1, 0)
            query_grads[m, at_queries, :] += contract(score_grad, key, 0, 0)
            if diagonal:
                key_grads[m, at_keys, :] = key_term
                if m == 0:
                    value_grads[at_keys, :] = value_term
                else:
                    value_grads[at_keys, :] += value_term
            else:
                key_grads[m, at_keys, :] += key_term
                value_grads[at_keys, :] += value_term

    for key_start in range(0, slots, tile):
        pair(key_start, key_start, True)

        def step(at, carry, key_start=key_start):
            pair(key_start, pl.multiple_of(at * tile, tile), False)
            return carry

        lax.fori_loop(key_start // tile + 1, slots // tile, step, 0)

    def turn_back(values, at):
        return values * cosine[at, :] - pltpu.roll(values, e // 2, 1) * sine[at, :]

    for block in range(8):
        at = slice(block * rows, (block + 1) * rows)
        for m, kept, sent in ((0, kept_first, sent_first), (1, kept_second, sent_second)):
            query = (turn_back(query_grads[m, at, :], at) * e ** (-0.5)).astype(low)
            key = turn_back(key_grads[m, at, :], at).astype(low)
            value = value_grads[at, m * e : (m + 1) * e].astype(low)
            store_block(
                block, ints, jnp.concatenate([query, key, value], axis=1), kept, sent, slice(None)
            )


def attention_backward(
    ints, floats, ordered, grads_kept, grads_received, outs, log_totals, gain, cosine, sine
):
    slots, width = outs.shape[1:]
    vmem = pl.BlockSpec(memory_space=pltpu.VMEM)
    smem = pl.BlockSpec(memory_space=pltpu.SMEM)
    return pl.pallas_call(
        attention_backward_kernel,
        in_specs=[smem, smem] + [vmem] * 8,
        out_specs=[vmem] * 6,
        out_shape=[jax.ShapeDtypeStruct((slots // 2, 3 * width // 2), low)] * 4
        + [jax.ShapeDtypeStruct((1, width), jnp.float32)] * 2,
        scratch_shapes=[
            pltpu.VMEM((2, slots, width), low),
            pltpu.VMEM((2, 8, slots), jnp.float32),
            pltpu.VMEM((2, slots, width // 2), jnp.float32),
            pltpu.VMEM((2, slots, width // 2), jnp.float32),
            pltpu.VMEM((slots, width), jnp.float32),
        ],
        compiler_params=pltpu.CompilerParams(vmem_limit_bytes=48 * 2**20),
        cost_estimate=estimate(20 * 10**9),
        name="attention_backward",
    )(ints, floats, ordered, grads_kept, grads_received, outs, log_totals, gain, cosine, sine)


def norm_back_kernel(one, two, three, values, gain, added, out, out_low, gain_grad):
    wide = values[...].astype(jnp.float32)
    grad = (
        one[...].astype(jnp.float32) + two[...].astype(jnp.float32) + three[...].astype(jnp.float32)
    )
    scale = lax.rsqrt(jnp.mean(wide * wide, axis=1, keepdims=True) + 1e-06)
    gained = grad * gain[...]
    inner = jnp.mean(gained * wide, axis=1, keepdims=True)
    result = added[...] + scale * gained - wide * (scale * scale * scale * inner)
    out[...] = result
    out_low[...] = result.astype(low)

    @pl.when(pl.program_id(0) == 0)
    def _():
        gain_grad[...] = jnp.zeros_like(gain_grad)

    gain_grad[...] += jnp.sum(grad * (wide * scale), axis=0, keepdims=True)


def norm_back(parts, values, gain, added):
    rows, width = values.shape
    block = rows // 4
    down = pl.BlockSpec((block, width), lambda i: (i, 0))
    once = pl.BlockSpec((1, width), lambda i: (0, 0))
    return pl.pallas_call(
        norm_back_kernel,
        grid=(4,),
        in_specs=[down] * 4 + [once, down],
        out_specs=[down, down, once],
        out_shape=[
            jax.ShapeDtypeStruct((rows, width), jnp.float32),
            jax.ShapeDtypeStruct((rows, width), low),
            jax.ShapeDtypeStruct((1, width), jnp.float32),
        ],
        compiler_params=pltpu.CompilerParams(vmem_limit_bytes=24 * 2**20),
        cost_estimate=estimate(10**9),
        name="norm_back",
    )(*parts, values, gain[None], added)


def project_kernel(inputs, weight, cosine, sine, first, second):
    e = cosine.shape[1]
    product = contract(inputs[...], weight[...], 1, 0)

    def turned(start):
        part = product[:, start : start + e]
        return part * cosine[...] + pltpu.roll(part, e // 2, 1) * sine[...]

    for out, start in ((first, 0), (second, 3 * e)):
        out[:, :e] = (turned(start) * e ** (-0.5)).astype(low)
        out[:, e : 2 * e] = turned(start + e).astype(low)
        out[:, 2 * e :] = product[:, start + 2 * e : start + 3 * e].astype(low)


def project(inputs, weight, cosine, sine):
    slots, width = inputs.shape
    columns = weight.shape[1]
    block = slots // 4
    down = lambda size: pl.BlockSpec((block, size), lambda i: (i, 0))
    return pl.pallas_call(
        project_kernel,
        grid=(4,),
        in_specs=[
            down(width),
            pl.BlockSpec((width, columns), lambda i: (0, 0)),
            down(cosine.shape[1]),
            down(cosine.shape[1]),
        ],
        out_specs=[down(columns // 2)] * 2,
        out_shape=[jax.ShapeDtypeStruct((slots, columns // 2), low)] * 2,
        compiler_params=pltpu.CompilerParams(vmem_limit_bytes=32 * 2**20),
        cost_estimate=estimate(2 * slots * width * columns),
        name="project",
    )(inputs, weight, cosine, sine)


def project_back_kernel(one, two, three, four, own, other, normed, out, gain):
    half = one.shape[1]
    total = contract(one[...], own[:, :half], 1, 1)
    total += contract(two[...], own[:, half:], 1, 1)
    total += contract(three[...], other[:, :half], 1, 1)
    total += contract(four[...], other[:, half:], 1, 1)
    out[...] = total.astype(low)
    part = jnp.sum(total * normed[...].astype(jnp.float32), axis=0, keepdims=True)

    @pl.when(pl.program_id(0) == 0)
    def _():
        gain[...] = jnp.zeros_like(gain)

    gain[...] += part


def project_back(parts, own, other, normed, first, count, rows):
    width, columns = own.shape
    down = lambda size: pl.BlockSpec((rows, size), lambda i: (first + i, 0))
    whole = pl.BlockSpec((width, columns), lambda i: (0, 0))
    return pl.pallas_call(
        project_back_kernel,
        grid=(count,),
        in_specs=[down(columns // 2)] * 4 + [whole, whole, down(width)],
        out_specs=[
            pl.BlockSpec((rows, width), lambda i: (i, 0)),
            pl.BlockSpec((1, width), lambda i: (0, 0)),
        ],
        out_shape=[
            jax.ShapeDtypeStruct((count * rows, width), low),
            jax.ShapeDtypeStruct((1, width), jnp.float32),
        ],
        compiler_params=pltpu.CompilerParams(vmem_limit_bytes=40 * 2**20),
        cost_estimate=estimate(4 * count * rows * width * columns),
        name="project_back",
    )(*parts, own, other, normed)


def gate_kernel(inputs, gate, up, hidden, gate_factor, up_factor):
    gate_pre = contract(gate[...], inputs[...], 1, 1)
    upward = contract(up[...], inputs[...], 1, 1)
    sigmoid = 1.0 / (1.0 + jnp.exp(-gate_pre))
    silu = gate_pre * sigmoid
    hidden[...] = (silu * upward).astype(low)
    gate_factor[...] = (upward * (sigmoid * (1.0 + gate_pre * (1.0 - sigmoid)))).astype(low)
    up_factor[...] = silu.astype(low)


def gate_units(inputs, gate, up):
    slots, width = inputs.shape
    units = gate.shape[0]
    block = slots // 4
    whole = pl.BlockSpec((units, width), lambda i: (0, 0))
    across = pl.BlockSpec((units, block), lambda i: (0, i))
    return pl.pallas_call(
        gate_kernel,
        grid=(4,),
        in_specs=[pl.BlockSpec((block, width), lambda i: (i, 0)), whole, whole],
        out_specs=[across] * 3,
        out_shape=[jax.ShapeDtypeStruct((units, slots), low)] * 3,
        compiler_params=pltpu.CompilerParams(vmem_limit_bytes=40 * 2**20),
        cost_estimate=estimate(4 * slots * width * units),
        name="gate_units",
    )(inputs, gate, up)


def gate_grad_kernel(grads, down, gate_factor, up_factor, gate_grad, up_grad):
    hidden_grad = contract(down[...], grads[...], 1, 1)
    gate_grad[...] = (hidden_grad * gate_factor[...].astype(jnp.float32)).astype(low)
    up_grad[...] = (hidden_grad * up_factor[...].astype(jnp.float32)).astype(low)


def gate_grads(grads, down, gate_factor, up_factor):
    slots, width = grads.shape
    units = down.shape[0]
    block = slots // 4
    across = pl.BlockSpec((units, block), lambda i: (0, i))
    return pl.pallas_call(
        gate_grad_kernel,
        grid=(4,),
        in_specs=[
            pl.BlockSpec((block, width), lambda i: (i, 0)),
            pl.BlockSpec((units, width), lambda i: (0, 0)),
            across,
            across,
        ],
        out_specs=[across] * 2,
        out_shape=[jax.ShapeDtypeStruct((units, slots), low)] * 2,
        compiler_params=pltpu.CompilerParams(vmem_limit_bytes=40 * 2**20),
        cost_estimate=estimate(2 * slots * width * units),
        name="gate_grads",
    )(grads, down, gate_factor, up_factor)


def sum_kernel(terms, *refs):
    out = refs[-1]
    total = contract(refs[0][...], refs[terms][...], 0, 0)
    for place in range(1, terms):
        total += contract(refs[place][...], refs[terms + place][...], 0, 0)
    out[...] = total.astype(out.dtype)


def sum_over_units(factors, weights, first, count, rows):
    units, width = weights[0].shape
    terms = len(factors)
    return pl.pallas_call(
        functools.partial(sum_kernel, terms),
        grid=(count,),
        in_specs=[pl.BlockSpec((units, rows), lambda i: (0, first + i))] * terms
        + [pl.BlockSpec((units, width), lambda i: (0, 0))] * terms,
        out_specs=pl.BlockSpec((rows, width), lambda i: (i, 0)),
        out_shape=jax.ShapeDtypeStruct((count * rows, width), low),
        compiler_params=pltpu.CompilerParams(vmem_limit_bytes=48 * 2**20),
        cost_estimate=estimate(2 * count * rows * width * units * terms),
        name="sum_over_units",
    )(*factors, *weights)


def body(
    tokens,
    lengths,
    attention_gain,
    query_weight,
    key_weight,
    value_weight,
    output_weight,
    lambda_vectors,
    head_gain,
    feedforward_gain,
    gate_weight,
    up_weight,
    down_weight,
    cotangent,
):
    rows, width = tokens.shape
    head_index = lax.axis_index("head")
    core = lax.axis_index("tensor")
    shard = query_weight.shape[0]
    qk_width = query_weight.shape[3]
    value_half = value_weight.shape[2]
    slots = rows * 8

    def in_order(mine, other):
        return jnp.where(core == 0, mine, other), jnp.where(core == 0, other, mine)

    own_slots = (
        (jnp.arange(4, dtype=jnp.int32) ^ head_index)[:, None] * (2 * rows)
        + core * rows
        + jnp.arange(rows, dtype=jnp.int32)[None, :]
    ).reshape(-1)
    segment_own, position_own = slot_layout(lengths, own_slots)
    valid = (segment_own[:rows] < 2).astype(jnp.float32)[:, None]
    half_width = qk_width // 2
    frequency = 10000.0 ** (-jnp.arange(half_width, dtype=jnp.float32) / half_width)

    def turn_tables(positions):
        angles = positions.astype(jnp.float32)[:, None] * frequency[None, :]
        cosine, sine = jnp.cos(angles), jnp.sin(angles)
        return jnp.concatenate([cosine, cosine], axis=1), jnp.concatenate([-sine, sine], axis=1)

    cosine, sine = turn_tables(position_own)
    cosine_all, sine_all = turn_tables(
        slot_layout(lengths, jnp.arange(slots, dtype=jnp.int32))[1]
    )
    own_head = head_index * 2 + core
    vectors = lax.dynamic_slice_in_dim(lambda_vectors, own_head, 1, 0)[0]
    first_exp = jnp.exp(jnp.sum(vectors[0] * vectors[1]))
    second_exp = jnp.exp(jnp.sum(vectors[2] * vectors[3]))
    lambda_value = first_exp - second_exp + lambda_base
    floats = jnp.stack(in_order(1.0, -lambda_value))
    ints = jnp.stack([head_index, core, lengths[0, 0], lengths[0, 0] + lengths[0, 1]])
    gain_own = rolled(
        lax.dynamic_slice_in_dim(head_gain, own_head, 1, 0), core * value_half
    ) * (1.0 - lambda_base)

    tokens_wide = tokens.astype(jnp.float32)
    attention_scale = lax.rsqrt(jnp.mean(tokens_wide * tokens_wide, axis=-1, keepdims=True) + 1e-06)
    normed_own = (tokens_wide * attention_scale * attention_gain).astype(low)
    output_local = jnp.concatenate(in_order(output_weight[0], output_weight[1]), axis=0)
    output_shards = line_gather(output_local)
    ffn_out_grad = valid * cotangent.astype(jnp.float32)
    ffn_out_grad_own = ffn_out_grad.astype(low)
    normed_near = [
        after(
            near,
            *(cosine, sine, cosine_all, sine_all),
            *(ffn_out_grad_own, ints, floats, gain_own, *output_shards),
        )
        for near in near_rows(normed_own)
    ]
    normed = group_rows(normed_own, normed_near)

    third = 3 * qk_width
    heads = [
        jnp.concatenate(
            [
                weight[:, place].reshape(shard, -1)
                for weight in (query_weight, key_weight, value_weight)
            ],
            axis=1,
        )
        for place in range(2)
    ]
    qkv_own = after(fsdp_gather(jnp.concatenate(in_order(*heads), axis=1), 0), normed)
    qkv_other = swap(qkv_own, "tensor", 1)
    gate_own = fsdp_gather(jnp.transpose(gate_weight), 1)
    up_own = fsdp_gather(jnp.transpose(up_weight), 1, normed)

    ffn_out_grad_own = after(ffn_out_grad_own, normed)
    ffn_out_grad_near = near_rows(ffn_out_grad_own)
    output_own = placed(output_shards)
    kept_first, sent_second = project(after(normed, output_own), qkv_own, cosine, sine)
    sent_first, kept_second = project(after(normed, kept_first), qkv_other, cosine, sine)
    ffn_out_grad_near = [after(near, sent_first) for near in ffn_out_grad_near]
    output_all = jnp.concatenate(
        [output_own, swap(after(output_own, sent_first), "tensor", 1)], axis=0
    )
    kept, sent, ordered, outs, log_totals = attention_forward(
        ints,
        floats,
        (after(kept_first, *ffn_out_grad_near), kept_second),
        (swap(sent_first, "tensor", 1), swap(sent_second, "tensor", 1)),
        gain_own,
    )
    received = swap(sent, "tensor", 1)
    head_out = jnp.concatenate(
        [
            kept[:, :value_half],
            received[:, value_half:],
            received[:, :value_half],
            kept[:, value_half:],
        ],
        axis=1,
    )

    ffn_out_grad_all = group_rows(ffn_out_grad_own, ffn_out_grad_near)
    third_out = contract(head_out[3 * rows :], output_all, 1, 0).astype(low)
    third_out = after(third_out, ffn_out_grad_all)
    down_own = fsdp_gather(down_weight, 1, third_out)
    nearer_out = contract(after(head_out, third_out)[: 3 * rows], output_all, 1, 0).astype(low)
    attention_out, _ = group_reduce(
        nearer_out,
        rows,
        third_out,
        lambda *arrived: nearer_out[:rows],
    )
    residual = tokens_wide + summed([after(part, gate_own) for part in attention_out])
    ffn_scale = lax.rsqrt(jnp.mean(residual * residual, axis=-1, keepdims=True) + 1e-06)
    ffn_in_own = (residual * ffn_scale * feedforward_gain).astype(low)
    ffn_in_near = near_rows(ffn_in_own)
    ffn_in = group_rows(ffn_in_own, ffn_in_near)
    gate_own, up_own = after(gate_own, ffn_in), after(up_own, ffn_in)
    gate_other, up_other = swap(gate_own, "tensor", 1), swap(up_own, "tensor", 1)
    hidden_own, gate_factor_own, up_factor_own = gate_units(ffn_in, gate_own, up_own)
    hidden_other, gate_factor_other, up_factor_other = gate_units(
        after(ffn_in, hidden_own), gate_other, up_other
    )

    down_own = after(down_own, hidden_other)
    down_other = swap(down_own, "tensor", 1)

    def weight_grad(own_side, other_side, right_side, *events):
        other = contract(other_side, right_side, 1, 0).astype(low)
        own = contract(after(own_side, other, *events), right_side, 1, 0)
        total = add_low(own, swap(other, "tensor", 1))
        return total, fsdp_reduce(total, 1)

    down_terms, down_grad = weight_grad(hidden_own, hidden_other, ffn_out_grad_all)
    gate_grad_own, up_grad_own = gate_grads(
        after(ffn_out_grad_all, down_terms), down_own, gate_factor_own, up_factor_own
    )
    gate_grad_other, up_grad_other = gate_grads(
        ffn_out_grad_all, down_other, gate_factor_other, up_factor_other
    )
    factors = [gate_grad_own, up_grad_own, gate_grad_other, up_grad_other]
    weights = [gate_own, up_own, gate_other, up_other]
    third_grad = sum_over_units(factors, weights, 3, 1, rows)
    gate_other_part = contract(after(gate_grad_other, third_grad), ffn_in, 1, 0).astype(low)
    near_grad = sum_over_units(
        [after(factors[0], gate_other_part)] + factors[1:], weights, 1, 2, rows
    )
    gate_terms = add_low(
        contract(after(gate_grad_own, near_grad), ffn_in, 1, 0),
        swap(gate_other_part, "tensor", 1),
    )
    gate_weight_grad = fsdp_reduce(gate_terms, 1)
    own_grads = []

    def own_grad(*arrived):
        own_grads.append(
            sum_over_units(
                [after(factors[0], gate_terms, down_grad, *arrived)] + factors[1:],
                weights,
                0,
                1,
                rows,
            )
        )
        return own_grads[0]

    ffn_in_sum, near_sent = group_reduce(near_grad, 0, third_grad, own_grad)
    up_terms, up_weight_grad = weight_grad(
        after(up_grad_own, own_grads[0]), after(up_grad_other, own_grads[0], *near_sent), ffn_in
    )
    residual_grad, residual_grad_low, feedforward_gain_part = norm_back(
        [after(part, up_terms) for part in ffn_in_sum],
        residual,
        feedforward_gain,
        ffn_out_grad,
    )
    feedforward_gain_part = feedforward_gain_part[0]

    ffn_out = sum_over_units(
        [after(hidden_own, residual_grad_low), hidden_other], [down_own, down_other], 0, 4, rows
    )
    residual_grad_near = [
        after(near, ffn_out, gate_weight_grad) for near in near_rows(residual_grad_low)
    ]
    attention_out_grad = group_rows(residual_grad_low, residual_grad_near)
    output_terms = contract(head_out, attention_out_grad, 0, 0).astype(low)
    head_out_grad = contract(after(attention_out_grad, output_terms), output_all, 1, 1).astype(low)
    pieces = [
        head_out_grad[:, place * value_half : (place + 1) * value_half] for place in range(4)
    ]
    ffn_arrived = []

    def ffn_own(*arrived):
        ffn_arrived.extend(arrived)
        return ffn_out[:rows]

    ffn_here, _ = group_reduce(
        ffn_out,
        rows,
        after(ffn_out[3 * rows :], attention_out_grad),
        ffn_own,
    )
    output_sum = add_low(
        output_terms[: 2 * value_half], swap(output_terms[2 * value_half :], "tensor", 1)
    )
    output_grad = fsdp_reduce(output_sum, 1)
    kept_first, kept_second, sent_first, sent_second, head_gain_part, lambda_part = (
        attention_backward(
            ints,
            floats,
            ordered,
            after(jnp.concatenate([pieces[0], pieces[3]], axis=1), output_sum, up_weight_grad),
            swap(jnp.concatenate([pieces[2], pieces[1]], axis=1), "tensor", 1),
            outs,
            log_totals,
            gain_own,
            cosine_all,
            sine_all,
        )
    )

    received_first = swap(after(sent_first, *ffn_arrived, output_grad), "tensor", 1)
    received_second = swap(sent_second, "tensor", 1)
    others_second = contract(normed, kept_second, 0, 0).astype(low)
    others_first = contract(after(normed, others_second), received_first, 0, 0).astype(low)
    parts = (kept_first, received_second, received_first, kept_second)
    own_first = add_low(
        contract(after(normed, others_first), kept_first, 0, 0), swap(others_first, "tensor", 1)
    )
    own_second = add_low(
        contract(after(normed, others_first), received_second, 0, 0),
        swap(others_second, "tensor", 1),
    )
    third_terms, third_gain = project_back(
        (after(kept_first, own_first, own_second, output_grad),) + parts[1:],
        qkv_own,
        qkv_other,
        normed,
        3,
        1,
        rows,
    )
    qkv_weight_grad = in_order(
        fsdp_reduce(own_first, 0).astype(jnp.float32),
        fsdp_reduce(own_second, 0).astype(jnp.float32),
    )
    output_grad = output_grad.astype(jnp.float32)
    output_grad = jnp.stack(in_order(output_grad[:value_half], output_grad[value_half:]))
    nearer_terms, nearer_gain = project_back(
        (after(kept_first, third_terms, own_first, own_second),) + parts[1:],
        qkv_own,
        qkv_other,
        normed,
        0,
        3,
        rows,
    )
    normed_grad, _ = group_reduce(
        nearer_terms,
        rows,
        after(third_terms, *ffn_here),
        lambda *arrived: nearer_terms[:rows],
    )
    attention_gain_part = (third_gain + nearer_gain)[0]
    ffn_here = [after(part, nearer_gain) for part in ffn_here]
    block_output = (valid * (residual + summed(ffn_here))).astype(low)
    tokens_grad, _, _ = norm_back(normed_grad, tokens, attention_gain, residual_grad)

    lambda_grad = -jnp.sum(lambda_part)
    vector_grads = lambda_grad * jnp.stack(
        [
            first_exp * vectors[1],
            first_exp * vectors[0],
            -second_exp * vectors[3],
            -second_exp * vectors[2],
        ]
    )
    lambda_full = lax.dynamic_update_slice(
        jnp.zeros(lambda_vectors.shape, jnp.float32), vector_grads[None], (own_head, 0, 0)
    )
    gain_full = lax.dynamic_update_slice(
        jnp.zeros(head_gain.shape, jnp.float32),
        rolled(head_gain_part, core * value_half),
        (own_head, 0),
    )
    small = total_over_all(
        jnp.concatenate(
            [
                attention_gain_part / attention_gain,
                feedforward_gain_part,
                lambda_full.reshape(-1),
                gain_full.reshape(-1),
            ]
        )
    )
    lambda_end = 2 * width + lambda_full.size
    return (
        block_output,
        tokens_grad,
        small[:width],
        *(
            jnp.stack(
                [part[:, kind * qk_width : (kind + 1) * qk_width] for part in qkv_weight_grad],
                axis=1,
            ).reshape(weight.shape)
            for kind, weight in enumerate((query_weight, key_weight, value_weight))
        ),
        output_grad.reshape(output_weight.shape),
        small[2 * width : lambda_end].reshape(lambda_full.shape),
        small[lambda_end:].reshape(gain_full.shape),
        small[width : 2 * width],
        jnp.transpose(gate_weight_grad).astype(jnp.float32),
        jnp.transpose(up_weight_grad).astype(jnp.float32),
        down_grad.astype(jnp.float32),
    )


def solution(mesh):
    placed = (
        P(("fsdp", "head", "tensor"), None),
        P("fsdp", None),
        P(),
        P("fsdp", "head", "tensor", None),
        P("fsdp", "head", "tensor", None),
        P("fsdp", "head", "tensor"),
        P("head", "tensor", "fsdp"),
        P(),
        P(),
        P(),
        P("fsdp", ("head", "tensor")),
        P("fsdp", ("head", "tensor")),
        P(("head", "tensor"), "fsdp"),
        P(("fsdp", "head", "tensor"), None),
    )
    return jax.shard_map(
        body,
        mesh=mesh,
        in_specs=placed,
        out_specs=(
            P(("fsdp", "head", "tensor"), None),
            P(("fsdp", "head", "tensor"), None),
            P(),
            P("fsdp", "head", "tensor", None),
            P("fsdp", "head", "tensor", None),
            P("fsdp", "head", "tensor"),
            P("head", "tensor", "fsdp"),
            P(),
            P(),
            P(),
            P("fsdp", ("head", "tensor")),
            P("fsdp", ("head", "tensor")),
            P(("head", "tensor"), "fsdp"),
        ),
        check_vma=False,
    )
```

time: 689 us -> 628 us (0.911)
  starting transfers between devices: 94.4 us -> 51.4 us
  Pallas kernels: 105 us -> 147 us
  other arithmetic: 70.6 us -> 36.5 us
  matrix products: 81.3 us -> 55.4 us
  waiting for transfers between devices: 246 us -> 229 us
  between operations: 6.07 us -> 19.2 us
    ppermute x30 -> x3, waiting for transfers between devices: 169 us -> 7.28 us  [shift(): lax.ppermute(values, 'fsdp', [(place, (place + step) % size) for place in...]
    ppermute x51 -> x54, waiting for transfers between devices: 77 us -> 167 us  [swap(): lax.ppermute(values, axis, [(place, place ^ mask) for place in range(size)])]
    all_gather x0 -> x4, waiting for transfers between devices: none -> 53.8 us  [fsdp_gather(): return lax.all_gather(after(own, *others), 'fsdp', axis=axis, tiled=True)]
    ppermute x30 -> x3, starting transfers between devices: 53.1 us -> 6.11 us  [shift(): lax.ppermute(values, 'fsdp', [(place, (place + step) % size) for place in...]
    pallas_call x1 -> x12, Pallas kernels: 11.1 us -> 52.5 us  [the longest x1 13.2 us: attention_forward(): pl.pallas_call(attention_forward_kernel, in_specs=[smem, smem] + [vmem] *...]
    unnamed x186 -> x215, local copies, waits for them, and re-layouts: 31.7 us -> 60.8 us
    slice x28 -> x16, local copies, waits for them, and re-layouts: 36.4 us -> 10.1 us  [the longest x4 4.93 us: group_reduce(): to_second = swap(third[half:], 'head', 2)]
    dot_general x15 -> x14, matrix products: 81.3 us -> 55.4 us  [contract(): lax.dot_general(left_side, right_side, (((left_dim,), (right_dim,)), ((),...]
  transfers between devices with their start and end apart: 81 -> 67, of which waited for: 30 -> 28; matrix products, arithmetic and copies ran while one was open for 31% -> 18% of each run, Pallas kernels for 13% -> 24%
where the time goes in v3:
time: 628 us; the launch traced here: 618 us
  waiting for transfers between devices  229 us (36%)
  Pallas kernels  147 us (23%)
  local copies, waits for them, and re-layouts  79.7 us (13%)
  matrix products  55.4 us (9%)
  starting transfers between devices  51.4 us (8%)
  other arithmetic  36.5 us (6%)
  between operations  19.2 us (3%)
    ppermute x54, waiting for transfers between devices, swap(): lax.ppermute(values, axis, [(place, place ^ mask) for place in range(size)])  167 us
    unnamed x215, local copies, waits for them, and re-layouts  60.8 us
    dot_general x14, matrix products, contract(): lax.dot_general(left_side, right_side, (((left_dim,), (right_dim,)), ((),...  55.4 us
    all_gather x4, waiting for transfers between devices, fsdp_gather(): return lax.all_gather(after(own, *others), 'fsdp', axis=axis, tiled=True)  53.8 us
    ppermute x54, starting transfers between devices, swap(): lax.ppermute(values, axis, [(place, place ^ mask) for place in range(size)])  43.4 us
    pallas_call x4, Pallas kernels, sum_over_units(): pl.pallas_call(functools.partial(sum_kernel, terms), grid=(count,), in_sp...  39.5 us
    pallas_call x1, Pallas kernels, attention_backward(): pl.pallas_call(attention_backward_kernel, in_specs=[smem, smem] + [vmem]...  25.2 us
    pallas_call x2, Pallas kernels, gate_units(): pl.pallas_call(gate_kernel, grid=(4,), in_specs=[pl.BlockSpec((block, wid...  19 us
  transfers between devices with their start and end apart: 67, of which 28 were waited for; matrix products, arithmetic and copies ran while one was open for 18% of the time, Pallas kernels for 24%

profile of v3, /device:TPU:0, one launch (start us, length us, event | category | flops | bytes accessed | tf_op | source)
XLA Modules:
  0.0 618.0 jit_solution(849247334728799463)
XLA Ops:
  8.3 5.1 collective-permute-start.1
  34.3 3.7 fusion.4
  42.1 7.3 %collective-permute-done.2.refs_2_ = bf16[256,512]{1,0:T(8,128)(2,1)} collective-permute-done((bf16[256,512]{1,0:T(8,128)(2,1)S(1)}, bf16[256,512]{1,0:T(8,128)(2,1)}, u32[]{:S(2)}, u32[]{:S(2)}) %collective-permute-start.2) | collective-permute-done | bytes 262176 | tf_op jit(solution)/shard_map/ppermute | solution.py:46
  54.9 3.8 collective-permute-done.5
  61.1 26.1 %all-gather.5.cloned.1.call-done.weight.own = bf16[2048,768]{1,0:T(8,128)(2,1)} async-done(((bf16[512,768]{1,0:T(8,128)(2,1)}), bf16[2048,768]{1,0:T(8,128)(2,1)}) %all-gather.5.cloned.1.call-update) | async-done | bytes 3145744 | tf_op jit(solution)/shard_map/all_gather | solution.py:37
  99.5 4.2 project.2
  103.9 4.2 project.3
  108.8 4.9 collective-permute-done.7
  121.9 13.2 %attention_forward.1 = (bf16[1024,256]{1,0:T(8,128)(2,1)S(1)}, bf16[1024,256]{1,0:T(8,128)(2,1)S(1)}, bf16[2048,768]{1,0:T(8,128)(2,1)S(1)}, f32[2,2048,256]{2,1,0:T(8,128)S(1)}, f32[2,2048]{1,0:T(2,128)S(1)}) custom-call(s32[4]{0:T(128)S(1)} %pad_add_fusion.ints, f32[2]{0:T(128)S(1)} %pad_maximum_fusion.18.floats, ...), custom_call_target="tpu_custom_call" | custom-call | flops 2000000000 | bytes 1048576 | tf_op jit(solution)/shard_map/attention_forward/pallas_call | solution.py:247
  146.5 8.9 %collective-permute-done.16.to_first = bf16[128,2048]{1,0:T(8,128)(2,1)S(1)} collective-permute-done((bf16[128,2048]{1,0:T(8,128)(2,1)}, bf16[128,2048]{1,0:T(8,128)(2,1)S(1)}, u32[]{:S(2)}, u32[]{:S(2)}) %collective-permute-start.16) | collective-permute-done | bytes 524320 | tf_op jit(solution)/shard_map/ppermute | solution.py:33
  158.9 23.0 %collective-permute-done.19 = bf16[256,2048]{1,0:T(8,128)(2,1)} collective-permute-done((bf16[256,2048]{1,0:T(8,128)(2,1)}, bf16[256,2048]{1,0:T(8,128)(2,1)}, u32[]{:S(2)}, u32[]{:S(2)}) %collective-permute-start.19) | collective-permute-done | bytes 1048608 | tf_op jit(solution)/shard_map/ppermute | solution.py:33
  186.6 20.8 %collective-permute-done.21 = bf16[256,2048]{1,0:T(8,128)(2,1)S(1)} collective-permute-done((bf16[256,2048]{1,0:T(8,128)(2,1)S(1)}, bf16[256,2048]{1,0:T(8,128)(2,1)S(1)}, u32[]{:S(2)}, u32[]{:S(2)}) %collective-permute-start.21) | collective-permute-done | bytes 1048608 | tf_op jit(solution)/shard_map/ppermute | solution.py:33
  210.4 9.2 %collective-permute-done.22 = bf16[128,2048]{1,0:T(8,128)(2,1)S(1)} collective-permute-done((bf16[128,2048]{1,0:T(8,128)(2,1)S(1)}, bf16[128,2048]{1,0:T(8,128)(2,1)S(1)}, u32[]{:S(2)}, u32[]{:S(2)}) %collective-permute-start.22) | collective-permute-done | bytes 524320 | tf_op jit(solution)/shard_map/ppermute | solution.py:33
  226.3 8.0 %gate_units.2 = (bf16[704,1024]{1,0:T(8,128)(2,1)S(1)}, bf16[704,1024]{1,0:T(8,128)(2,1)S(1)}, bf16[704,1024]{1,0:T(8,128)(2,1)S(1)}) custom-call(bf16[1024,2048]{1,0:T(8,128)(2,1)S(1)} %copy-done.18, bf16[704,2048]{1,0:T(8,128)(2,1)S(1)} %copy-done.6, bf16[704,2048]{1,0:T(8,128)(2,1)S(1)} %copy-done.7), custom_call_target="tpu_custom_call" | custom-call | flops 2362232064 | bytes 1048576 | tf_op jit(solution)/shard_map/gate_units/pallas_call | solution.py:529
  237.7 10.9 %gate_units.3 = (bf16[704,1024]{1,0:T(8,128)(2,1)S(1)}, bf16[704,1024]{1,0:T(8,128)(2,1)S(1)}, bf16[704,1024]{1,0:T(8,128)(2,1)S(1)}) custom-call(bf16[1024,2048]{1,0:T(8,128)(2,1)S(1)} %copy-done.18, bf16[704,2048]{1,0:T(8,128)(2,1)} %collective-permute-done.24.gate.refs_6_, bf16[704,2048]{1,0:T(8,128)(2,1)} %collective-permute-done.25.up.refs_7_), custom_call_target="tpu_custom_call" | custom-call | flops 2362232064 | bytes 1048576 | tf_op jit(solution)/shard_map/gate_units/pallas_call | solution.py:529
  248.7 4.5 convolution_convert_fusion.3
  253.4 27.8 %all-gather.11.cloned.1.call-done.down.refs_2_ = bf16[704,2048]{1,0:T(8,128)(2,1)} async-done(((bf16[704,512]{1,0:T(8,128)(2,1)}), bf16[704,2048]{1,0:T(8,128)(2,1)}) %all-gather.11.cloned.1.call-update) | async-done | bytes 2883600 | tf_op jit(solution)/shard_map/all_gather | solution.py:37
  281.1 7.1 %add_convert_fusion.2 = bf16[704,2048]{1,0:T(8,128)(2,1)} fusion(bf16[704,2048]{1,0:T(8,128)(2,1)} %collective-permute-done.26, bf16[704,1024]{1,0:T(8,128)(2,1)S(1)} %copy-done.52, bf16[1024,2048]{1,0:T(8,128)(2,1)} %copy-done.21), kind=kOutput, calls=%fused_computation.2 | convolution fusion | flops 2957115392 | bytes 11403264 | tf_op jit(solution)/shard_map/dot_general | solution.py:17
  295.6 4.6 gate_grads.2
  300.2 6.4 %gate_grads.3 = (bf16[704,1024]{1,0:T(8,128)(2,1)S(1)}, bf16[704,1024]{1,0:T(8,128)(2,1)S(1)}) custom-call(bf16[1024,2048]{1,0:T(8,128)(2,1)S(1)} %copy-done.23, bf16[704,2048]{1,0:T(8,128)(2,1)} %collective-permute-done.27.down.refs_3_, bf16[704,1024]{1,0:T(8,128)(2,1)S(1)} %copy-done.61, bf16[704,1024]{1,0:T(8,128)(2,1)S(1)} %copy-done.63), custom_call_target="tpu_custom_call" | custom-call | flops 1181116032 | bytes 1048576 | tf_op jit(solution)/shard_map/gate_grads/pallas_call | solution.py:552
  307.7 8.5 %sum_over_units.4 = bf16[256,2048]{1,0:T(8,128)(2,1)S(1)} custom-call(bf16[704,1024]{1,0:T(8,128)(2,1)S(1)} %get-tuple-element.146.refs_0_, bf16[704,1024]{1,0:T(8,128)(2,1)S(1)} %get-tuple-element.151.refs_1_, bf16[704,1024]{1,0:T(8,128)(2,1)S(1)} %get-tuple-element.143.refs_2_, bf16[704,1024]{1,0:T(8,128)(2,1)} %copy-done.27, ...), custom_call_target="tpu_custom_call" | custom-call | flops 1181116032 | bytes 1048576 | tf_op jit(solution)/shard_map/sum_over_units/pallas_call | solution.py:580
  317.2 3.3 convolution_convert_fusion.2
  321.0 12.5 %sum_over_units.5.near = bf16[512,2048]{1,0:T(8,128)(2,1)} custom-call(bf16[704,1024]{1,0:T(8,128)(2,1)S(1)} %get-tuple-element.146.refs_0_, bf16[704,1024]{1,0:T(8,128)(2,1)S(1)} %get-tuple-element.151.refs_1_, bf16[704,1024]{1,0:T(8,128)(2,1)S(1)} %get-tuple-element.143.refs_2_, bf16[704,1024]{1,0:T(8,128)(2,1)S(1)} %copy-done.28, ...), custom_call_target="tpu_custom_call" | custom-call | flops 2362232064 | bytes 1048576 | tf_op jit(solution)/shard_map/sum_over_units/pallas_call | solution.py:580
  333.5 4.5 add_convert_fusion.1
  343.0 10.9 %collective-permute-done.29.to_first = bf16[128,2048]{1,0:T(8,128)(2,1)S(1)} collective-permute-done((bf16[128,2048]{1,0:T(8,128)(2,1)S(1)}, bf16[128,2048]{1,0:T(8,128)(2,1)S(1)}, u32[]{:S(2)}, u32[]{:S(2)}) %collective-permute-start.29) | collective-permute-done | bytes 524320 | tf_op jit(solution)/shard_map/ppermute | solution.py:33
  358.1 8.1 %sum_over_units.6.one = bf16[256,2048]{1,0:T(8,128)(2,1)S(1)} custom-call(bf16[704,1024]{1,0:T(8,128)(2,1)S(1)} %get-tuple-element.146.refs_0_, bf16[704,1024]{1,0:T(8,128)(2,1)S(1)} %get-tuple-element.151.refs_1_, bf16[704,1024]{1,0:T(8,128)(2,1)S(1)} %copy-done.31, bf16[704,1024]{1,0:T(8,128)(2,1)} %copy-done.27, ...), custom_call_target="tpu_custom_call" | custom-call | flops 1181116032 | bytes 1048576 | tf_op jit(solution)/shard_map/sum_over_units/pallas_call | solution.py:580
  366.2 3.4 convolution_convert_fusion.1
  375.0 4.5 add_convert_fusion
  379.7 15.9 %collective-permute-done.32.two = bf16[256,2048]{1,0:T(8,128)(2,1)} collective-permute-done((bf16[256,2048]{1,0:T(8,128)(2,1)}, bf16[256,2048]{1,0:T(8,128)(2,1)}, u32[]{:S(2)}, u32[]{:S(2)}) %collective-permute-start.32) | collective-permute-done | bytes 1048608 | tf_op jit(solution)/shard_map/ppermute | solution.py:33
  397.5 4.8 norm_back.2
  406.5 10.4 %sum_over_units.7.near = bf16[1024,2048]{1,0:T(8,128)(2,1)} custom-call(bf16[704,1024]{1,0:T(8,128)(2,1)S(1)} %copy-done.53, bf16[704,1024]{1,0:T(8,128)(2,1)S(1)} %copy-done.55, bf16[704,2048]{1,0:T(8,128)(2,1)S(1)} %copy-done.33, bf16[704,2048]{1,0:T(8,128)(2,1)} %collective-permute-done.27.down.refs_3_), custom_call_target="tpu_custom_call" | custom-call | flops 2362232064 | bytes 1048576 | tf_op jit(solution)/shard_map/sum_over_units/pallas_call | solution.py:580
  416.9 11.3 %collective-permute-done.35 = bf16[256,2048]{1,0:T(8,128)(2,1)S(1)} collective-permute-done((bf16[256,2048]{1,0:T(8,128)(2,1)}, bf16[256,2048]{1,0:T(8,128)(2,1)S(1)}, u32[]{:S(2)}, u32[]{:S(2)}) %collective-permute-start.35) | collective-permute-done | bytes 1048608 | tf_op jit(solution)/shard_map/ppermute | solution.py:33
  435.2 5.6 collective-permute-done.36
  440.8 3.6 collective-permute-done.37
  465.2 25.2 %attention_backward.1 = (bf16[1024,384]{1,0:T(8,128)(2,1)S(1)}, bf16[1024,384]{1,0:T(8,128)(2,1)S(1)}, bf16[1024,384]{1,0:T(8,128)(2,1)S(1)}, bf16[1024,384]{1,0...) custom-call(s32[4]{0:T(128)S(1)} %pad_add_fusion.ints, f32[2]{0:T(128)S(1)} %pad_maximum_fusion.18.floats, ...), custom_call_target="tpu_custom_call" | custom-call | flops 8000000000 | bytes 1048576 | tf_op jit(solution)/shard_map/attention_backward/pallas_call | solution.py:380
  490.5 3.5 convolution_convert_fusion.6
  494.8 4.1 collective-permute-done.42.three
  498.8 6.0 convolution_convert_fusion.5
  504.9 5.0 add_convert_fusion.3
  522.5 5.0 add_convert_fusion.4
  536.3 3.7 project_back.2
  540.0 4.1 collective-permute-done.47
  544.4 8.5 %project_back.3 = (bf16[768,2048]{1,0:T(8,128)(2,1)S(1)}, f32[1,2048]{1,0:T(1,128)S(1)}) custom-call(bf16[1024,384]{1,0:T(8,128)(2,1)S(1)} %get-tuple-element.174.one, bf16[1024,384]{1,0:T(8,128)(2,1)S(1)} %copy-done.48, bf16[1024,384]{1,0:T(8,128)(2,1)S(1)} %copy-done.46, bf16[1024,384]{1,0:T(8,128)(2,1)S(1)} %copy-done.43, ...), custom_call_target="tpu_custom_call" | custom-call | flops 1932735232 | bytes 1048576 | tf_op jit(solution)/shard_map/project_back/pallas_call | solution.py:495
  556.3 6.0 collective-permute-done.53
  563.2 6.8 %collective-permute-done.54 = f32[10240]{0:T(1024)S(1)} collective-permute-done((f32[10240]{0:T(1024)S(1)}, f32[10240]{0:T(1024)S(1)}, u32[]{:S(2)}, u32[]{:S(2)}) %collective-permute-start.54) | collective-permute-done | bytes 40992 | tf_op jit(solution)/shard_map/ppermute | solution.py:33
  577.1 3.2 multiply_convert_fusion
  580.4 17.2 %collective-permute-done.56 = f32[10240]{0:T(1024)S(1)} collective-permute-done((f32[10240]{0:T(1024)S(1)}, f32[10240]{0:T(1024)S(1)}, u32[]{:S(2)}, u32[]{:S(2)}) %collective-permute-start.56) | collective-permute-done | bytes 40992 | tf_op jit(solution)/shard_map/ppermute | solution.py:33
  601.0 4.6 norm_back.3
  (438 shorter events, 185.0 us)
Async XLA Ops:
  7.2 80.0 %all-gather.5.cloned.1.call-start = ((), (), s32[]{:S(2)}) async-start(), calls=%async_computation.6 | async-start | bytes 3932160 | tf_op jit(solution)/shard_map/all_gather | solution.py:37
  8.3 33.7 %collective-permute-start.1 = (bf16[256,512]{1,0:T(8,128)(2,1)S(1)}, bf16[256,512]{1,0:T(8,128)(2,1)}, u32[]{:S(2)}, u32[]{:S(2)}) collective-permute-start(bf16[256,512]{1,0:T(8,128)(2,1)S(1)} %pad_maximum_fusion.16.refs_0_), channel_id=1, source_target_pairs={{0,24},{8,0},{16,8},{24,16},{1,25},{9,1},{17,9},{25,17},{2,26},{10... | collective-permute-start | bytes 786440 | tf_op jit(solution)/shard_map/ppermute | solution.py:46
  13.4 35.9 %collective-permute-start.2 = (bf16[256,512]{1,0:T(8,128)(2,1)S(1)}, bf16[256,512]{1,0:T(8,128)(2,1)}, u32[]{:S(2)}, u32[]{:S(2)}) collective-permute-start(bf16[256,512]{1,0:T(8,128)(2,1)S(1)} %pad_maximum_fusion.16.refs_0_), channel_id=1, source_target_pairs={{0,16},{8,24},{16,0},{24,8},{1,17},{9,25},{17,1},{25,9},{2,18},{10... | collective-permute-start | bytes 786440 | tf_op jit(solution)/shard_map/ppermute | solution.py:46
  13.4 35.9 %collective-permute-start.3 = (bf16[256,512]{1,0:T(8,128)(2,1)S(1)}, bf16[256,512]{1,0:T(8,128)(2,1)}, u32[]{:S(2)}, u32[]{:S(2)}) collective-permute-start(bf16[256,512]{1,0:T(8,128)(2,1)S(1)} %pad_maximum_fusion.16.refs_0_), channel_id=1, source_target_pairs={{0,8},{8,16},{16,24},{24,0},{1,9},{9,17},{17,25},{25,1},{2,10},{10... | collective-permute-start | bytes 786440 | tf_op jit(solution)/shard_map/ppermute | solution.py:46
  19.2 139.6 %all-gather.7.cloned.1.call-start = ((), (), s32[]{:S(2)}) async-start(), calls=%async_computation.7 | async-start | bytes 3604480 | tf_op jit(solution)/shard_map/all_gather | solution.py:37
  21.2 29.8 %collective-permute-start = (bf16[256,2048]{1,0:T(8,128)(2,1)}, bf16[256,2048]{1,0:T(8,128)(2,1)S(1)}, u32[]{:S(2)}, u32[]{:S(2)}) collective-permute-start(bf16[256,2048]{1,0:T(8,128)(2,1)} %get-tuple-element.211), channel_id=1, source_target_pairs={{0,2},{2,0},{4,6},{6,4},{1,3},{3,1},{5,7},{7,5},{8,10},{10,8},{12,... | collective-permute-start | bytes 3145736 | tf_op jit(solution)/shard_map/ppermute | solution.py:33
  22.7 26.6 %collective-permute-start.4 = (bf16[256,2048]{1,0:T(8,128)(2,1)}, bf16[256,2048]{1,0:T(8,128)(2,1)S(1)}, u32[]{:S(2)}, u32[]{:S(2)}) collective-permute-start(bf16[256,2048]{1,0:T(8,128)(2,1)} %get-tuple-element.211), channel_id=1, source_target_pairs={{0,4},{2,6},{4,0},{6,2},{1,5},{3,7},{5,1},{7,3},{8,12},{10,14},{12... | collective-permute-start | bytes 3145736 | tf_op jit(solution)/shard_map/ppermute | solution.py:33
  87.2 16.7 %collective-permute-start.8 = (bf16[2048,768]{1,0:T(8,128)(2,1)}, bf16[2048,768]{1,0:T(8,128)(2,1)S(1)}, u32[]{:S(2)}, u32[]{:S(2)}) collective-permute-start(bf16[2048,768]{1,0:T(8,128)(2,1)} %all-gather.5.cloned.1.call-done.weight.own), channel_id=1, source_target_pairs={{0,1},{1,0},{2,3},{3,2},{4,5},{5,4},{6,7},{7,6},{8,9},{9,8},{10,11... | collective-permute-start | bytes 9437192 | tf_op jit(solution)/shard_map/ppermute | solution.py:33
  87.3 134.5 %all-gather.9.cloned.1.call-start = ((), (), s32[]{:S(2)}) async-start(), calls=%async_computation.8 | async-start | bytes 3604480 | tf_op jit(solution)/shard_map/all_gather | solution.py:37
  87.8 25.9 %collective-permute-start.7 = (bf16[256,2048]{1,0:T(8,128)(2,1)}, bf16[256,2048]{1,0:T(8,128)(2,1)}, u32[]{:S(2)}, u32[]{:S(2)}) collective-permute-start(bf16[256,2048]{1,0:T(8,128)(2,1)} %get-tuple-element.107), channel_id=1, source_target_pairs={{0,2},{2,0},{4,6},{6,4},{1,3},{3,1},{5,7},{7,5},{8,10},{10,8},{12,... | collective-permute-start | bytes 3145736 | tf_op jit(solution)/shard_map/ppermute | solution.py:33
  89.3 25.6 %collective-permute-start.9 = (bf16[256,2048]{1,0:T(8,128)(2,1)}, bf16[256,2048]{1,0:T(8,128)(2,1)}, u32[]{:S(2)}, u32[]{:S(2)}) collective-permute-start(bf16[256,2048]{1,0:T(8,128)(2,1)} %get-tuple-element.107), channel_id=1, source_target_pairs={{0,4},{2,6},{4,0},{6,2},{1,5},{3,7},{5,1},{7,3},{8,12},{10,14},{12... | collective-permute-start | bytes 3145736 | tf_op jit(solution)/shard_map/ppermute | solution.py:33
  103.8 18.0 %collective-permute-start.11 = (bf16[1024,384]{1,0:T(8,128)(2,1)S(1)}, bf16[1024,384]{1,0:T(8,128)(2,1)S(1)}, u32[]{:S(2)}, u32[]{:S(2)}) collective-permute-start(bf16[1024,384]{1,0:T(8,128)(2,1)S(1)} %get-tuple-element.114), channel_id=1, source_target_pairs={{0,1},{1,0},{2,3},{3,2},{4,5},{5,4},{6,7},{7,6},{8,9},{9,8},{10,11... | collective-permute-start | bytes 2359304 | tf_op jit(solution)/shard_map/ppermute | solution.py:33
  108.2 13.7 %collective-permute-start.10 = (bf16[1024,384]{1,0:T(8,128)(2,1)S(1)}, bf16[1024,384]{1,0:T(8,128)(2,1)S(1)}, u32[]{:S(2)}, u32[]{:S(2)}) collective-permute-start(bf16[1024,384]{1,0:T(8,128)(2,1)S(1)} %get-tuple-element.109), channel_id=1, source_target_pairs={{0,1},{1,0},{2,3},{3,2},{4,5},{5,4},{6,7},{7,6},{8,9},{9,8},{10,11... | collective-permute-start | bytes 2359304 | tf_op jit(solution)/shard_map/ppermute | solution.py:33
  114.9 24.0 %collective-permute-start.13 = (bf16[256,2048]{1,0:T(8,128)(2,1)S(1)}, bf16[256,2048]{1,0:T(8,128)(2,1)S(1)}, u32[]{:S(2)}, u32[]{:S(2)}) collective-permute-start(bf16[256,2048]{1,0:T(8,128)(2,1)S(1)} %copy-done.79), channel_id=1, source_target_pairs={{0,1},{1,0},{2,3},{3,2},{4,5},{5,4},{6,7},{7,6},{8,9},{9,8},{10,11... | collective-permute-start | bytes 3145736 | tf_op jit(solution)/shard_map/ppermute | solution.py:33
  116.0 20.8 %collective-permute-start.14 = (bf16[128,2048]{1,0:T(8,128)(2,1)S(1)}, bf16[128,2048]{1,0:T(8,128)(2,1)S(1)}, u32[]{:S(2)}, u32[]{:S(2)}) collective-permute-start(bf16[128,2048]{1,0:T(8,128)(2,1)S(1)} %slice.232), channel_id=1, source_target_pairs={{0,2},{2,0},{4,6},{6,4},{1,3},{3,1},{5,7},{7,5},{8,10},{10,8},{12,... | collective-permute-start | bytes 1572872 | tf_op jit(solution)/shard_map/ppermute | solution.py:33
  118.9 17.9 %collective-permute-start.15 = (bf16[128,2048]{1,0:T(8,128)(2,1)S(1)}, bf16[128,2048]{1,0:T(8,128)(2,1)S(1)}, u32[]{:S(2)}, u32[]{:S(2)}) collective-permute-start(bf16[128,2048]{1,0:T(8,128)(2,1)S(1)} %slice.233), channel_id=1, source_target_pairs={{0,4},{2,6},{4,0},{6,2},{1,5},{3,7},{5,1},{7,3},{8,12},{10,14},{12... | collective-permute-start | bytes 1572872 | tf_op jit(solution)/shard_map/ppermute | solution.py:33
  141.3 14.0 %collective-permute-start.16 = (bf16[128,2048]{1,0:T(8,128)(2,1)}, bf16[128,2048]{1,0:T(8,128)(2,1)S(1)}, u32[]{:S(2)}, u32[]{:S(2)}) collective-permute-start(bf16[128,2048]{1,0:T(8,128)(2,1)} %get-tuple-element.227), channel_id=1, source_target_pairs={{0,2},{2,0},{4,6},{6,4},{1,3},{3,1},{5,7},{7,5},{8,10},{10,8},{12,... | collective-permute-start | bytes 1572872 | tf_op jit(solution)/shard_map/ppermute | solution.py:33
  142.8 13.7 %collective-permute-start.17 = (bf16[128,2048]{1,0:T(8,128)(2,1)}, bf16[128,2048]{1,0:T(8,128)(2,1)S(1)}, u32[]{:S(2)}, u32[]{:S(2)}) collective-permute-start(bf16[128,2048]{1,0:T(8,128)(2,1)} %get-tuple-element.226), channel_id=1, source_target_pairs={{0,4},{2,6},{4,0},{6,2},{1,5},{3,7},{5,1},{7,3},{8,12},{10,14},{12... | collective-permute-start | bytes 1572872 | tf_op jit(solution)/shard_map/ppermute | solution.py:33
  143.4 137.8 %all-gather.11.cloned.1.call-start = ((), (), s32[]{:S(2)}) async-start(), calls=%async_computation.9 | async-start | bytes 3604480 | tf_op jit(solution)/shard_map/all_gather | solution.py:37
  157.7 24.1 %collective-permute-start.19 = (bf16[256,2048]{1,0:T(8,128)(2,1)}, bf16[256,2048]{1,0:T(8,128)(2,1)}, u32[]{:S(2)}, u32[]{:S(2)}) collective-permute-start(bf16[256,2048]{1,0:T(8,128)(2,1)} %get-tuple-element.123), channel_id=1, source_target_pairs={{0,4},{2,6},{4,0},{6,2},{1,5},{3,7},{5,1},{7,3},{8,12},{10,14},{12... | collective-permute-start | bytes 3145736 | tf_op jit(solution)/shard_map/ppermute | solution.py:33
  158.2 23.6 %collective-permute-start.18 = (bf16[256,2048]{1,0:T(8,128)(2,1)S(1)}, bf16[256,2048]{1,0:T(8,128)(2,1)}, u32[]{:S(2)}, u32[]{:S(2)}) collective-permute-start(bf16[256,2048]{1,0:T(8,128)(2,1)S(1)} %get-tuple-element.121), channel_id=1, source_target_pairs={{0,2},{2,0},{4,6},{6,4},{1,3},{3,1},{5,7},{7,5},{8,10},{10,8},{12,... | collective-permute-start | bytes 3145736 | tf_op jit(solution)/shard_map/ppermute | solution.py:33
  184.4 22.9 %collective-permute-start.21 = (bf16[256,2048]{1,0:T(8,128)(2,1)S(1)}, bf16[256,2048]{1,0:T(8,128)(2,1)S(1)}, u32[]{:S(2)}, u32[]{:S(2)}) collective-permute-start(bf16[256,2048]{1,0:T(8,128)(2,1)S(1)} %get-tuple-element.207), channel_id=1, source_target_pairs={{0,4},{2,6},{4,0},{6,2},{1,5},{3,7},{5,1},{7,3},{8,12},{10,14},{12... | collective-permute-start | bytes 3145736 | tf_op jit(solution)/shard_map/ppermute | solution.py:33
  186.0 23.5 %collective-permute-start.20 = (bf16[256,2048]{1,0:T(8,128)(2,1)S(1)}, bf16[256,2048]{1,0:T(8,128)(2,1)S(1)}, u32[]{:S(2)}, u32[]{:S(2)}) collective-permute-start(bf16[256,2048]{1,0:T(8,128)(2,1)S(1)} %get-tuple-element.207), channel_id=1, source_target_pairs={{0,2},{2,0},{4,6},{6,4},{1,3},{3,1},{5,7},{7,5},{8,10},{10,8},{12,... | collective-permute-start | bytes 3145736 | tf_op jit(solution)/shard_map/ppermute | solution.py:33
  221.7 16.0 %collective-permute-start.24 = (bf16[704,2048]{1,0:T(8,128)(2,1)S(1)}, bf16[704,2048]{1,0:T(8,128)(2,1)}, u32[]{:S(2)}, u32[]{:S(2)}) collective-permute-start(bf16[704,2048]{1,0:T(8,128)(2,1)S(1)} %copy-done.6), channel_id=1, source_target_pairs={{0,1},{1,0},{2,3},{3,2},{4,5},{5,4},{6,7},{7,6},{8,9},{9,8},{10,11... | collective-permute-start | bytes 8650760 | tf_op jit(solution)/shard_map/ppermute | solution.py:33
  221.8 16.0 %collective-permute-start.25 = (bf16[704,2048]{1,0:T(8,128)(2,1)}, bf16[704,2048]{1,0:T(8,128)(2,1)}, u32[]{:S(2)}, u32[]{:S(2)}) collective-permute-start(bf16[704,2048]{1,0:T(8,128)(2,1)} %all-gather.9.cloned.1.call-done.up.refs_5_), channel_id=1, source_target_pairs={{0,1},{1,0},{2,3},{3,2},{4,5},{5,4},{6,7},{7,6},{8,9},{9,8},{10,11... | collective-permute-start | bytes 8650760 | tf_op jit(solution)/shard_map/ppermute | solution.py:33
  222.3 134.4 %reduce-scatter.7.cloned.1.call-start = ((), (), s32[]{:S(2)}) async-start(), calls=%async_computation.10 | async-start | bytes 3604480 | tf_op jit(solution)/shard_map/reduce_scatter | solution.py:41
  253.2 27.9 %collective-permute-start.26 = (bf16[704,2048]{1,0:T(8,128)(2,1)}, bf16[704,2048]{1,0:T(8,128)(2,1)}, u32[]{:S(2)}, u32[]{:S(2)}) collective-permute-start(bf16[704,2048]{1,0:T(8,128)(2,1)} %convolution_convert_fusion.3), channel_id=1, source_target_pairs={{0,1},{1,0},{2,3},{3,2},{4,5},{5,4},{6,7},{7,6},{8,9},{9,8},{10,11... | collective-permute-start | bytes 8650760 | tf_op jit(solution)/shard_map/ppermute | solution.py:33
  281.1 19.1 %collective-permute-start.27 = (bf16[704,2048]{1,0:T(8,128)(2,1)}, bf16[704,2048]{1,0:T(8,128)(2,1)}, u32[]{:S(2)}, u32[]{:S(2)}) collective-permute-start(bf16[704,2048]{1,0:T(8,128)(2,1)} %all-gather.11.cloned.1.call-done.down.refs_2_), channel_id=1, source_target_pairs={{0,1},{1,0},{2,3},{3,2},{4,5},{5,4},{6,7},{7,6},{8,9},{9,8},{10,11... | collective-permute-start | bytes 8650760 | tf_op jit(solution)/shard_map/ppermute | solution.py:33
  288.2 128.7 %reduce-scatter.9.cloned.1.call-start = ((), (), s32[]{:S(2)}) async-start(), calls=%async_computation.11 | async-start | bytes 3604480 | tf_op jit(solution)/shard_map/reduce_scatter | solution.py:41
  338.0 123.1 %reduce-scatter.11.cloned.1.call-start = ((), (), s32[]{:S(2)}) async-start(), calls=%async_computation.12 | async-start | bytes 3604480 | tf_op jit(solution)/shard_map/reduce_scatter | solution.py:41
  339.9 14.0 %collective-permute-start.29 = (bf16[128,2048]{1,0:T(8,128)(2,1)S(1)}, bf16[128,2048]{1,0:T(8,128)(2,1)S(1)}, u32[]{:S(2)}, u32[]{:S(2)}) collective-permute-start(bf16[128,2048]{1,0:T(8,128)(2,1)S(1)} %get-tuple-element.225), channel_id=1, source_target_pairs={{0,2},{2,0},{4,6},{6,4},{1,3},{3,1},{5,7},{7,5},{8,10},{10,8},{12,... | collective-permute-start | bytes 1572872 | tf_op jit(solution)/shard_map/ppermute | solution.py:33
  341.5 13.6 %collective-permute-start.30 = (bf16[128,2048]{1,0:T(8,128)(2,1)S(1)}, bf16[128,2048]{1,0:T(8,128)(2,1)S(1)}, u32[]{:S(2)}, u32[]{:S(2)}) collective-permute-start(bf16[128,2048]{1,0:T(8,128)(2,1)S(1)} %get-tuple-element.224), channel_id=1, source_target_pairs={{0,4},{2,6},{4,0},{6,2},{1,5},{3,7},{5,1},{7,3},{8,12},{10,14},{12... | collective-permute-start | bytes 1572872 | tf_op jit(solution)/shard_map/ppermute | solution.py:33
  369.7 25.9 %collective-permute-start.32 = (bf16[256,2048]{1,0:T(8,128)(2,1)}, bf16[256,2048]{1,0:T(8,128)(2,1)}, u32[]{:S(2)}, u32[]{:S(2)}) collective-permute-start(bf16[256,2048]{1,0:T(8,128)(2,1)} %get-tuple-element.148), channel_id=1, source_target_pairs={{0,2},{2,0},{4,6},{6,4},{1,3},{3,1},{5,7},{7,5},{8,10},{10,8},{12,... | collective-permute-start | bytes 3145736 | tf_op jit(solution)/shard_map/ppermute | solution.py:33
  370.3 25.5 %collective-permute-start.33 = (bf16[256,2048]{1,0:T(8,128)(2,1)}, bf16[256,2048]{1,0:T(8,128)(2,1)}, u32[]{:S(2)}, u32[]{:S(2)}) collective-permute-start(bf16[256,2048]{1,0:T(8,128)(2,1)} %get-tuple-element.149), channel_id=1, source_target_pairs={{0,4},{2,6},{4,0},{6,2},{1,5},{3,7},{5,1},{7,3},{8,12},{10,14},{12... | collective-permute-start | bytes 3145736 | tf_op jit(solution)/shard_map/ppermute | solution.py:33
  379.4 114.7 %reduce-scatter.13.cloned.1.call-start = ((), (), s32[]{:S(2)}) async-start(), calls=%async_computation.13 | async-start | bytes 1310720 | tf_op jit(solution)/shard_map/reduce_scatter | solution.py:41
  403.6 24.7 %collective-permute-start.35 = (bf16[256,2048]{1,0:T(8,128)(2,1)}, bf16[256,2048]{1,0:T(8,128)(2,1)S(1)}, u32[]{:S(2)}, u32[]{:S(2)}) collective-permute-start(bf16[256,2048]{1,0:T(8,128)(2,1)} %get-tuple-element.155), channel_id=1, source_target_pairs={{0,4},{2,6},{4,0},{6,2},{1,5},{3,7},{5,1},{7,3},{8,12},{10,14},{12... | collective-permute-start | bytes 3145736 | tf_op jit(solution)/shard_map/ppermute | solution.py:33
  405.1 26.1 %collective-permute-start.34 = (bf16[256,2048]{1,0:T(8,128)(2,1)}, bf16[256,2048]{1,0:T(8,128)(2,1)}, u32[]{:S(2)}, u32[]{:S(2)}) collective-permute-start(bf16[256,2048]{1,0:T(8,128)(2,1)} %get-tuple-element.155), channel_id=1, source_target_pairs={{0,2},{2,0},{4,6},{6,4},{1,3},{3,1},{5,7},{7,5},{8,10},{10,8},{12,... | collective-permute-start | bytes 3145736 | tf_op jit(solution)/shard_map/ppermute | solution.py:33
  454.7 150.9 %reduce-scatter.17.cloned.1.call-start = ((), (), s32[]{:S(2)}) async-start(), calls=%async_computation.15 | async-start | bytes 1966080 | tf_op jit(solution)/shard_map/reduce_scatter | solution.py:41
  457.2 36.9 %collective-permute-start.40 = (bf16[128,2048]{1,0:T(8,128)(2,1)}, bf16[128,2048]{1,0:T(8,128)(2,1)S(1)}, u32[]{:S(2)}, u32[]{:S(2)}) collective-permute-start(bf16[128,2048]{1,0:T(8,128)(2,1)} %get-tuple-element.223), channel_id=1, source_target_pairs={{0,2},{2,0},{4,6},{6,4},{1,3},{3,1},{5,7},{7,5},{8,10},{10,8},{12,... | collective-permute-start | bytes 1572872 | tf_op jit(solution)/shard_map/ppermute | solution.py:33
  457.8 36.3 %collective-permute-start.41 = (bf16[128,2048]{1,0:T(8,128)(2,1)}, bf16[128,2048]{1,0:T(8,128)(2,1)}, u32[]{:S(2)}, u32[]{:S(2)}) collective-permute-start(bf16[128,2048]{1,0:T(8,128)(2,1)} %get-tuple-element.222), channel_id=1, source_target_pairs={{0,4},{2,6},{4,0},{6,2},{1,5},{3,7},{5,1},{7,3},{8,12},{10,14},{12... | collective-permute-start | bytes 1572872 | tf_op jit(solution)/shard_map/ppermute | solution.py:33
  510.8 94.8 %reduce-scatter.15.cloned.1.call-start = ((), (), s32[]{:S(2)}) async-start(), calls=%async_computation.14 | async-start | bytes 1966080 | tf_op jit(solution)/shard_map/reduce_scatter | solution.py:41
  518.4 25.8 %collective-permute-start.47 = (bf16[256,2048]{1,0:T(8,128)(2,1)}, bf16[256,2048]{1,0:T(8,128)(2,1)}, u32[]{:S(2)}, u32[]{:S(2)}) collective-permute-start(bf16[256,2048]{1,0:T(8,128)(2,1)} %get-tuple-element.179), channel_id=1, source_target_pairs={{0,4},{2,6},{4,0},{6,2},{1,5},{3,7},{5,1},{7,3},{8,12},{10,14},{12... | collective-permute-start | bytes 3145736 | tf_op jit(solution)/shard_map/ppermute | solution.py:33
  518.9 25.5 %collective-permute-start.46 = (bf16[256,2048]{1,0:T(8,128)(2,1)}, bf16[256,2048]{1,0:T(8,128)(2,1)}, u32[]{:S(2)}, u32[]{:S(2)}) collective-permute-start(bf16[256,2048]{1,0:T(8,128)(2,1)} %get-tuple-element.177), channel_id=1, source_target_pairs={{0,2},{2,0},{4,6},{6,4},{1,3},{3,1},{5,7},{7,5},{8,10},{10,8},{12,... | collective-permute-start | bytes 3145736 | tf_op jit(solution)/shard_map/ppermute | solution.py:33
  553.2 16.8 %collective-permute-start.48 = (bf16[128,2048]{1,0:T(8,128)(2,1)S(1)}, bf16[128,2048]{1,0:T(8,128)(2,1)S(1)}, u32[]{:S(2)}, u32[]{:S(2)}) collective-permute-start(bf16[128,2048]{1,0:T(8,128)(2,1)S(1)} %get-tuple-element.217), channel_id=1, source_target_pairs={{0,2},{2,0},{4,6},{6,4},{1,3},{3,1},{5,7},{7,5},{8,10},{10,8},{12,... | collective-permute-start | bytes 1572872 | tf_op jit(solution)/shard_map/ppermute | solution.py:33
  554.7 15.4 %collective-permute-start.49 = (bf16[128,2048]{1,0:T(8,128)(2,1)S(1)}, bf16[128,2048]{1,0:T(8,128)(2,1)S(1)}, u32[]{:S(2)}, u32[]{:S(2)}) collective-permute-start(bf16[128,2048]{1,0:T(8,128)(2,1)S(1)} %get-tuple-element.216), channel_id=1, source_target_pairs={{0,4},{2,6},{4,0},{6,2},{1,5},{3,7},{5,1},{7,3},{8,12},{10,14},{12... | collective-permute-start | bytes 1572872 | tf_op jit(solution)/shard_map/ppermute | solution.py:33
  571.6 27.8 %collective-permute-start.50 = (bf16[256,2048]{1,0:T(8,128)(2,1)}, bf16[256,2048]{1,0:T(8,128)(2,1)}, u32[]{:S(2)}, u32[]{:S(2)}) collective-permute-start(bf16[256,2048]{1,0:T(8,128)(2,1)} %get-tuple-element.183), channel_id=1, source_target_pairs={{0,2},{2,0},{4,6},{6,4},{1,3},{3,1},{5,7},{7,5},{8,10},{10,8},{12,... | collective-permute-start | bytes 3145736 | tf_op jit(solution)/shard_map/ppermute | solution.py:33
  573.6 25.8 %collective-permute-start.51 = (bf16[256,2048]{1,0:T(8,128)(2,1)}, bf16[256,2048]{1,0:T(8,128)(2,1)}, u32[]{:S(2)}, u32[]{:S(2)}) collective-permute-start(bf16[256,2048]{1,0:T(8,128)(2,1)} %get-tuple-element.184), channel_id=1, source_target_pairs={{0,4},{2,6},{4,0},{6,2},{1,5},{3,7},{5,1},{7,3},{8,12},{10,14},{12... | collective-permute-start | bytes 3145736 | tf_op jit(solution)/shard_map/ppermute | solution.py:33
  575.2 22.4 %collective-permute-start.56 = (f32[10240]{0:T(1024)S(1)}, f32[10240]{0:T(1024)S(1)}, u32[]{:S(2)}, u32[]{:S(2)}) collective-permute-start(f32[10240]{0:T(1024)S(1)} %add.180), channel_id=1, source_target_pairs={{0,4},{2,6},{4,0},{6,2},{1,5},{3,7},{5,1},{7,3},{8,12},{10,14},{12... | collective-permute-start | bytes 122888 | tf_op jit(solution)/shard_map/ppermute | solution.py:33
  (117 other events, 810.1 us)
Sparse Core Ops, SparseCore 0:
  19.3 67.7 all-gather.4
  88.7 60.0 all-gather.6
  150.5 57.8 all-gather.8
  222.4 58.6 all-gather.10
  288.4 55.0 reduce-scatter.6
  345.6 56.0 reduce-scatter.8
  404.0 56.0 reduce-scatter.10
  462.9 26.9 reduce-scatter.12
  510.9 34.0 reduce-scatter.16
  547.3 36.0 reduce-scatter.14

commit v4 on v3

--- a/solution.py
+++ b/solution.py
@@ -9,7 +9,7 @@
 
 lambda_base = 0.2
 tile = 512
-cost_share = 0.4
+cost_share = 0.02
 low = jnp.bfloat16
 
 
@@ -81,12 +81,13 @@
     return swap(own, "head", 1), swap(own, "head", 2)
 
 
-def group_rows(own, near):
+def group_rows(own, near, *events):
     half = own.shape[0] // 2
     first, second = near
     third_low = swap(second[:half], "head", 1)
     third_high = swap(first[half:], "head", 2)
-    return jnp.concatenate([own, first, second, third_low, third_high], axis=0)
+    far = [after(part, *events) for part in (third_low, third_high)]
+    return jnp.concatenate([after(own, *events), first, second, *far], axis=0)
 
 
 def join_kernel(start, near, to_first, to_second, first, second):
@@ -99,11 +100,11 @@
     second[half:] = near[middle + half : middle + rows]
 
 
-def group_reduce(near, start, third, own_part):
-    rows, width = third.shape
-    half = rows // 2
-    to_first = swap(third[:half], "head", 1)
-    to_second = swap(third[half:], "head", 2)
+def group_reduce(near, start, halves, own_part, hold=()):
+    half, width = halves[0].shape
+    rows = 2 * half
+    to_first = swap(halves[0], "head", 1)
+    to_second = swap(halves[1], "head", 2)
     own = own_part(to_first, to_second)
     vmem = pl.BlockSpec(memory_space=pltpu.VMEM)
     first, second = pl.pallas_call(
@@ -114,7 +115,7 @@
         compiler_params=pltpu.CompilerParams(vmem_limit_bytes=24 * 2**20),
         cost_estimate=estimate(10**9),
         name="join",
-    )(near, to_first, to_second)
+    )(after(near, *hold), to_first, to_second)
     from_first = swap(first, "head", 1)
     from_second = swap(second, "head", 2)
     return (own, from_first, from_second), (first, second)
@@ -144,6 +145,12 @@
     segment = (slots >= first_end).astype(jnp.int32) + (slots >= second_end).astype(jnp.int32)
     start = jnp.where(segment == 0, 0, jnp.where(segment == 1, first_end, second_end))
     return segment, slots - start
+
+
+def store_parts(values, outs):
+    size = values.shape[0] // len(outs)
+    for place, out in enumerate(outs):
+        out[...] = values[place * size : (place + 1) * size].astype(out.dtype)
 
 
 def estimate(flops):
@@ -472,13 +479,13 @@
     )(inputs, weight, cosine, sine)
 
 
-def project_back_kernel(one, two, three, four, own, other, normed, out, gain):
+def project_back_kernel(one, two, three, four, own, other, normed, gain, *outs):
     half = one.shape[1]
     total = contract(one[...], own[:, :half], 1, 1)
     total += contract(two[...], own[:, half:], 1, 1)
     total += contract(three[...], other[:, :half], 1, 1)
     total += contract(four[...], other[:, half:], 1, 1)
-    out[...] = total.astype(low)
+    store_parts(total, outs)
     part = jnp.sum(total * normed[...].astype(jnp.float32), axis=0, keepdims=True)
 
     @pl.when(pl.program_id(0) == 0)
@@ -488,7 +495,7 @@
     gain[...] += part
 
 
-def project_back(parts, own, other, normed, first, count, rows):
+def project_back(grads, own, other, normed, first, count, rows, parts=1):
     width, columns = own.shape
     down = lambda size: pl.BlockSpec((rows, size), lambda i: (first + i, 0))
     whole = pl.BlockSpec((width, columns), lambda i: (0, 0))
@@ -496,18 +503,14 @@
         project_back_kernel,
         grid=(count,),
         in_specs=[down(columns // 2)] * 4 + [whole, whole, down(width)],
-        out_specs=[
-            pl.BlockSpec((rows, width), lambda i: (i, 0)),
-            pl.BlockSpec((1, width), lambda i: (0, 0)),
-        ],
-        out_shape=[
-            jax.ShapeDtypeStruct((count * rows, width), low),
-            jax.ShapeDtypeStruct((1, width), jnp.float32),
-        ],
+        out_specs=[pl.BlockSpec((1, width), lambda i: (0, 0))]
+        + [pl.BlockSpec((rows // parts, width), lambda i: (i, 0))] * parts,
+        out_shape=[jax.ShapeDtypeStruct((1, width), jnp.float32)]
+        + [jax.ShapeDtypeStruct((count * rows // parts, width), low)] * parts,
         compiler_params=pltpu.CompilerParams(vmem_limit_bytes=40 * 2**20),
         cost_estimate=estimate(4 * count * rows * width * columns),
         name="project_back",
-    )(*parts, own, other, normed)
+    )(*grads, own, other, normed)
 
 
 def gate_kernel(inputs, gate, up, hidden, gate_factor, up_factor):
@@ -567,14 +570,13 @@
 
 
 def sum_kernel(terms, *refs):
-    out = refs[-1]
     total = contract(refs[0][...], refs[terms][...], 0, 0)
     for place in range(1, terms):
         total += contract(refs[place][...], refs[terms + place][...], 0, 0)
-    out[...] = total.astype(out.dtype)
-
-
-def sum_over_units(factors, weights, first, count, rows):
+    store_parts(total, refs[2 * terms :])
+
+
+def sum_over_units(factors, weights, first, count, rows, parts=1):
     units, width = weights[0].shape
     terms = len(factors)
     return pl.pallas_call(
@@ -582,8 +584,8 @@
         grid=(count,),
         in_specs=[pl.BlockSpec((units, rows), lambda i: (0, first + i))] * terms
         + [pl.BlockSpec((units, width), lambda i: (0, 0))] * terms,
-        out_specs=pl.BlockSpec((rows, width), lambda i: (i, 0)),
-        out_shape=jax.ShapeDtypeStruct((count * rows, width), low),
+        out_specs=[pl.BlockSpec((rows // parts, width), lambda i: (i, 0))] * parts,
+        out_shape=[jax.ShapeDtypeStruct((count * rows // parts, width), low)] * parts,
         compiler_params=pltpu.CompilerParams(vmem_limit_bytes=48 * 2**20),
         cost_estimate=estimate(2 * count * rows * width * units * terms),
         name="sum_over_units",
@@ -647,23 +649,6 @@
         lax.dynamic_slice_in_dim(head_gain, own_head, 1, 0), core * value_half
     ) * (1.0 - lambda_base)
 
-    tokens_wide = tokens.astype(jnp.float32)
-    attention_scale = lax.rsqrt(jnp.mean(tokens_wide * tokens_wide, axis=-1, keepdims=True) + 1e-06)
-    normed_own = (tokens_wide * attention_scale * attention_gain).astype(low)
-    output_local = jnp.concatenate(in_order(output_weight[0], output_weight[1]), axis=0)
-    output_shards = line_gather(output_local)
-    ffn_out_grad = valid * cotangent.astype(jnp.float32)
-    ffn_out_grad_own = ffn_out_grad.astype(low)
-    normed_near = [
-        after(
-            near,
-            *(cosine, sine, cosine_all, sine_all),
-            *(ffn_out_grad_own, ints, floats, gain_own, *output_shards),
-        )
-        for near in near_rows(normed_own)
-    ]
-    normed = group_rows(normed_own, normed_near)
-
     third = 3 * qk_width
     heads = [
         jnp.concatenate(
@@ -675,20 +660,40 @@
         )
         for place in range(2)
     ]
-    qkv_own = after(fsdp_gather(jnp.concatenate(in_order(*heads), axis=1), 0), normed)
+    qkv_local = jnp.concatenate(in_order(*heads), axis=1)
+
+    output_local = jnp.concatenate(in_order(output_weight[0], output_weight[1]), axis=0)
+
+    tokens_wide = after(tokens, output_local).astype(jnp.float32)
+    attention_scale = lax.rsqrt(jnp.mean(tokens_wide * tokens_wide, axis=-1, keepdims=True) + 1e-06)
+    normed_own = (tokens_wide * attention_scale * attention_gain).astype(low)
+    output_own = placed(line_gather(output_local))
+    ffn_out_grad = valid * cotangent.astype(jnp.float32)
+    ffn_out_grad_own = ffn_out_grad.astype(low)
+    normed_near = [
+        after(
+            near,
+            *(cosine, sine, cosine_all, sine_all),
+            *(ffn_out_grad_own, ints, floats, gain_own, output_own),
+        )
+        for near in near_rows(normed_own)
+    ]
+    normed = group_rows(normed_own, normed_near)
+
+    qkv_own = after(fsdp_gather(qkv_local, 0), normed)
     qkv_other = swap(qkv_own, "tensor", 1)
     gate_own = fsdp_gather(jnp.transpose(gate_weight), 1)
     up_own = fsdp_gather(jnp.transpose(up_weight), 1, normed)
 
     ffn_out_grad_own = after(ffn_out_grad_own, normed)
     ffn_out_grad_near = near_rows(ffn_out_grad_own)
-    output_own = placed(output_shards)
-    kept_first, sent_second = project(after(normed, output_own), qkv_own, cosine, sine)
+    kept_first, sent_second = project(normed, qkv_own, cosine, sine)
     sent_first, kept_second = project(after(normed, kept_first), qkv_other, cosine, sine)
     ffn_out_grad_near = [after(near, sent_first) for near in ffn_out_grad_near]
-    output_all = jnp.concatenate(
-        [output_own, swap(after(output_own, sent_first), "tensor", 1)], axis=0
-    )
+    output_other = swap(after(output_own, sent_first), "tensor", 1)
+    output_kept = jnp.concatenate([output_own[:value_half], output_other[value_half:]], axis=0)
+    output_sent = jnp.concatenate([output_other[:value_half], output_own[value_half:]], axis=0)
+    output_all = jnp.concatenate([output_kept, output_sent], axis=0)
     kept, sent, ordered, outs, log_totals = attention_forward(
         ints,
         floats,
@@ -696,22 +701,14 @@
         (swap(sent_first, "tensor", 1), swap(sent_second, "tensor", 1)),
         gain_own,
     )
-    received = swap(sent, "tensor", 1)
-    head_out = jnp.concatenate(
-        [
-            kept[:, :value_half],
-            received[:, value_half:],
-            received[:, :value_half],
-            kept[:, value_half:],
-        ],
-        axis=1,
-    )
-
-    ffn_out_grad_all = group_rows(ffn_out_grad_own, ffn_out_grad_near)
-    third_out = contract(head_out[3 * rows :], output_all, 1, 0).astype(low)
-    third_out = after(third_out, ffn_out_grad_all)
-    down_own = fsdp_gather(down_weight, 1, third_out)
-    nearer_out = contract(after(head_out, third_out)[: 3 * rows], output_all, 1, 0).astype(low)
+    head_out = jnp.concatenate([kept, swap(sent, "tensor", 1)], axis=1)
+
+    third_out = [
+        contract(head_out[start : start + rows // 2], output_all, 1, 0).astype(low)
+        for start in (3 * rows, 7 * rows // 2)
+    ]
+    down_own = fsdp_gather(down_weight, 1, *third_out)
+    nearer_out = contract(after(head_out, *third_out)[: 3 * rows], output_all, 1, 0).astype(low)
     attention_out, _ = group_reduce(
         nearer_out,
         rows,
@@ -733,6 +730,8 @@
     down_own = after(down_own, hidden_other)
     down_other = swap(down_own, "tensor", 1)
 
+    ffn_out_grad_all = group_rows(ffn_out_grad_own, ffn_out_grad_near, hidden_own)
+
     def weight_grad(own_side, other_side, right_side, *events):
         other = contract(other_side, right_side, 1, 0).astype(low)
         own = contract(after(own_side, other, *events), right_side, 1, 0)
@@ -748,20 +747,20 @@
     )
     factors = [gate_grad_own, up_grad_own, gate_grad_other, up_grad_other]
     weights = [gate_own, up_own, gate_other, up_other]
-    third_grad = sum_over_units(factors, weights, 3, 1, rows)
-    gate_other_part = contract(after(gate_grad_other, third_grad), ffn_in, 1, 0).astype(low)
-    near_grad = sum_over_units(
+    third_grad = sum_over_units(factors, weights, 3, 1, rows, 2)
+    gate_other_part = contract(after(gate_grad_other, *third_grad), ffn_in, 1, 0).astype(low)
+    (near_grad,) = sum_over_units(
         [after(factors[0], gate_other_part)] + factors[1:], weights, 1, 2, rows
     )
-    gate_terms = add_low(
-        contract(after(gate_grad_own, near_grad), ffn_in, 1, 0),
-        swap(gate_other_part, "tensor", 1),
-    )
-    gate_weight_grad = fsdp_reduce(gate_terms, 1)
-    own_grads = []
+    own_grads, gate_sums = [], []
 
     def own_grad(*arrived):
-        own_grads.append(
+        gate_terms = add_low(
+            contract(after(gate_grad_own, near_grad, *arrived), ffn_in, 1, 0),
+            swap(gate_other_part, "tensor", 1),
+        )
+        gate_sums.append(fsdp_reduce(gate_terms, 1))
+        own_grads.extend(
             sum_over_units(
                 [after(factors[0], gate_terms, down_grad, *arrived)] + factors[1:],
                 weights,
@@ -773,6 +772,7 @@
         return own_grads[0]
 
     ffn_in_sum, near_sent = group_reduce(near_grad, 0, third_grad, own_grad)
+    gate_weight_grad = gate_sums[0]
     up_terms, up_weight_grad = weight_grad(
         after(up_grad_own, own_grads[0]), after(up_grad_other, own_grads[0], *near_sent), ffn_in
     )
@@ -784,32 +784,22 @@
     )
     feedforward_gain_part = feedforward_gain_part[0]
 
-    ffn_out = sum_over_units(
+    (ffn_out,) = sum_over_units(
         [after(hidden_own, residual_grad_low), hidden_other], [down_own, down_other], 0, 4, rows
     )
     residual_grad_near = [
         after(near, ffn_out, gate_weight_grad) for near in near_rows(residual_grad_low)
     ]
     attention_out_grad = group_rows(residual_grad_low, residual_grad_near)
-    output_terms = contract(head_out, attention_out_grad, 0, 0).astype(low)
-    head_out_grad = contract(after(attention_out_grad, output_terms), output_all, 1, 1).astype(low)
-    pieces = [
-        head_out_grad[:, place * value_half : (place + 1) * value_half] for place in range(4)
+    head_grad_sent = contract(attention_out_grad, output_sent, 1, 1).astype(low)
+    head_grad_kept = contract(after(attention_out_grad, head_grad_sent), output_kept, 1, 1)
+    output_terms = contract(head_out, after(attention_out_grad, head_grad_sent), 0, 0).astype(low)
+    output_terms = [
+        output_terms[place * value_half : (place + 1) * value_half] for place in range(4)
     ]
-    ffn_arrived = []
-
-    def ffn_own(*arrived):
-        ffn_arrived.extend(arrived)
-        return ffn_out[:rows]
-
-    ffn_here, _ = group_reduce(
-        ffn_out,
-        rows,
-        after(ffn_out[3 * rows :], attention_out_grad),
-        ffn_own,
-    )
     output_sum = add_low(
-        output_terms[: 2 * value_half], swap(output_terms[2 * value_half :], "tensor", 1)
+        jnp.concatenate([output_terms[0], output_terms[3]], axis=0),
+        swap(jnp.concatenate([output_terms[2], output_terms[1]], axis=0), "tensor", 1),
     )
     output_grad = fsdp_reduce(output_sum, 1)
     kept_first, kept_second, sent_first, sent_second, head_gain_part, lambda_part = (
@@ -817,8 +807,8 @@
             ints,
             floats,
             ordered,
-            after(jnp.concatenate([pieces[0], pieces[3]], axis=1), output_sum, up_weight_grad),
-            swap(jnp.concatenate([pieces[2], pieces[1]], axis=1), "tensor", 1),
+            after(head_grad_kept.astype(low), output_sum, up_weight_grad),
+            swap(head_grad_sent, "tensor", 1),
             outs,
             log_totals,
             gain_own,
@@ -827,10 +817,29 @@
         )
     )
 
+    ffn_arrived = []
+
+    def ffn_own(*arrived):
+        ffn_arrived.extend(arrived)
+        return ffn_out[:rows]
+
+    ffn_here, ffn_sent = group_reduce(
+        ffn_out,
+        rows,
+        [
+            after(ffn_out[start : start + rows // 2], attention_out_grad)
+            for start in (3 * rows, 7 * rows // 2)
+        ],
+        ffn_own,
+        (kept_first,),
+    )
+
     received_first = swap(after(sent_first, *ffn_arrived, output_grad), "tensor", 1)
     received_second = swap(sent_second, "tensor", 1)
     others_second = contract(normed, kept_second, 0, 0).astype(low)
-    others_first = contract(after(normed, others_second), received_first, 0, 0).astype(low)
+    others_first = contract(
+        after(normed, others_second, *ffn_sent), received_first, 0, 0
+    ).astype(low)
     parts = (kept_first, received_second, received_first, kept_second)
     own_first = add_low(
         contract(after(normed, others_first), kept_first, 0, 0), swap(others_first, "tensor", 1)
@@ -839,7 +848,7 @@
         contract(after(normed, others_first), received_second, 0, 0),
         swap(others_second, "tensor", 1),
     )
-    third_terms, third_gain = project_back(
+    third_gain, *third_terms = project_back(
         (after(kept_first, own_first, own_second, output_grad),) + parts[1:],
         qkv_own,
         qkv_other,
@@ -847,6 +856,7 @@
         3,
         1,
         rows,
+        2,
     )
     qkv_weight_grad = in_order(
         fsdp_reduce(own_first, 0).astype(jnp.float32),
@@ -854,8 +864,8 @@
     )
     output_grad = output_grad.astype(jnp.float32)
     output_grad = jnp.stack(in_order(output_grad[:value_half], output_grad[value_half:]))
-    nearer_terms, nearer_gain = project_back(
-        (after(kept_first, third_terms, own_first, own_second),) + parts[1:],
+    nearer_gain, nearer_terms = project_back(
+        (after(kept_first, third_gain),) + parts[1:],
         qkv_own,
         qkv_other,
         normed,
@@ -866,7 +876,7 @@
     normed_grad, _ = group_reduce(
         nearer_terms,
         rows,
-        after(third_terms, *ffn_here),
+        [after(terms, *ffn_here) for terms in third_terms],
         lambda *arrived: nearer_terms[:rows],
     )
     attention_gain_part = (third_gain + nearer_gain)[0]

time: 628 us -> 613 us (0.976)
  waiting for transfers between devices: 229 us -> 215 us
  local copies, waits for them, and re-layouts: 79.7 us -> 71.4 us
  matrix products: 55.4 us -> 61.7 us
    ppermute x54, waiting for transfers between devices: 167 us -> 150 us  [swap(): lax.ppermute(values, axis, [(place, place ^ mask) for place in range(size)])]
    reduce_scatter x6, waiting for transfers between devices: 0.05 us -> 7.46 us  [fsdp_reduce(): return lax.psum_scatter(partial, 'fsdp', scatter_dimension=axis, tiled=True)]
    dot_general x14 -> x16, matrix products: 55.4 us -> 61.7 us  [contract(): lax.dot_general(left_side, right_side, (((left_dim,), (right_dim,)), ((),...]
    unnamed x215 -> x208, local copies, waits for them, and re-layouts: 60.8 us -> 54.5 us
  transfers between devices with their start and end apart: 67 -> 67, of which waited for: 28 -> 28; matrix products, arithmetic and copies ran while one was open for 18% -> 18% of each run, Pallas kernels for 24% -> 25%
where the time goes in v4:
time: 613 us; the launch traced here: 603 us
  waiting for transfers between devices  215 us (35%)
  Pallas kernels  148 us (24%)
  local copies, waits for them, and re-layouts  71.4 us (12%)
  matrix products  61.7 us (10%)
  starting transfers between devices  54.8 us (9%)
  other arithmetic  33 us (5%)
  between operations  19.5 us (3%)
    ppermute x54, waiting for transfers between devices, swap(): lax.ppermute(values, axis, [(place, place ^ mask) for place in range(size)])  150 us
    dot_general x16, matrix products, contract(): lax.dot_general(left_side, right_side, (((left_dim,), (right_dim,)), ((),...  61.7 us
    unnamed x208, local copies, waits for them, and re-layouts  54.5 us
    all_gather x4, waiting for transfers between devices, fsdp_gather(): return lax.all_gather(after(own, *others), 'fsdp', axis=axis, tiled=True)  49.7 us
    ppermute x54, starting transfers between devices, swap(): lax.ppermute(values, axis, [(place, place ^ mask) for place in range(size)])  46.5 us
    pallas_call x4, Pallas kernels, sum_over_units(): pl.pallas_call(functools.partial(sum_kernel, terms), grid=(count,), in_sp...  40 us
    pallas_call x1, Pallas kernels, attention_backward(): pl.pallas_call(attention_backward_kernel, in_specs=[smem, smem] + [vmem]...  25.3 us
    pallas_call x2, Pallas kernels, gate_units(): pl.pallas_call(gate_kernel, grid=(4,), in_specs=[pl.BlockSpec((block, wid...  20.3 us
  transfers between devices with their start and end apart: 67, of which 28 were waited for; matrix products, arithmetic and copies ran while one was open for 18% of the time, Pallas kernels for 25%

profile of v4, /device:TPU:0, one launch (start us, length us, event | category | flops | bytes accessed | tf_op | source)
XLA Modules:
  0.0 603.3 jit_solution(17078744369647445942)
XLA Ops:
  8.3 5.1 collective-permute-start.1
  34.3 3.7 fusion.10
  42.0 7.3 %collective-permute-done.2.refs_2_ = bf16[256,512]{1,0:T(8,128)(2,1)} collective-permute-done((bf16[256,512]{1,0:T(8,128)(2,1)S(1)}, bf16[256,512]{1,0:T(8,128)(2,1)}, u32[]{:S(2)}, u32[]{:S(2)}) %collective-permute-start.2) | collective-permute-done | bytes 262176 | tf_op jit(solution)/shard_map/ppermute | solution.py:46
  57.1 3.8 collective-permute-done.5
  63.4 23.8 %all-gather.5.cloned.1.call-done.weight.own = bf16[2048,768]{1,0:T(8,128)(2,1)} async-done(((bf16[512,768]{1,0:T(8,128)(2,1)}), bf16[2048,768]{1,0:T(8,128)(2,1)}) %all-gather.5.cloned.1.call-update) | async-done | bytes 3145744 | tf_op jit(solution)/shard_map/all_gather | solution.py:37
  96.8 4.2 project.2
  101.1 4.3 project.3
  106.1 7.2 %collective-permute-done.7 = bf16[256,2048]{1,0:T(8,128)(2,1)S(1)} collective-permute-done((bf16[256,2048]{1,0:T(8,128)(2,1)}, bf16[256,2048]{1,0:T(8,128)(2,1)S(1)}, u32[]{:S(2)}, u32[]{:S(2)}) %collective-permute-start.7) | collective-permute-done | bytes 1048608 | tf_op jit(solution)/shard_map/ppermute | solution.py:33
  115.5 13.3 %attention_forward.1 = (bf16[1024,256]{1,0:T(8,128)(2,1)S(1)}, bf16[1024,256]{1,0:T(8,128)(2,1)S(1)}, bf16[2048,768]{1,0:T(8,128)(2,1)S(1)}, f32[2,2048,256]{2,1,0:T(8,128)S(1)}, f32[2,2048]{1,0:T(2,128)S(1)}) custom-call(s32[4]{0:T(128)S(1)} %pad_add_fusion.ints, f32[2]{0:T(128)S(1)} %pad_maximum_fusion.13.floats, ...), custom_call_target="tpu_custom_call" | custom-call | flops 100000000 | bytes 1048576 | tf_op jit(solution)/shard_map/attention_forward/pallas_call | solution.py:254
  139.2 8.3 %collective-permute-done.14.to_first = bf16[128,2048]{1,0:T(8,128)(2,1)S(1)} collective-permute-done((bf16[128,2048]{1,0:T(8,128)(2,1)}, bf16[128,2048]{1,0:T(8,128)(2,1)S(1)}, u32[]{:S(2)}, u32[]{:S(2)}) %collective-permute-start.14) | collective-permute-done | bytes 524320 | tf_op jit(solution)/shard_map/ppermute | solution.py:33
  152.1 21.1 %collective-permute-done.17 = bf16[256,2048]{1,0:T(8,128)(2,1)} collective-permute-done((bf16[256,2048]{1,0:T(8,128)(2,1)}, bf16[256,2048]{1,0:T(8,128)(2,1)}, u32[]{:S(2)}, u32[]{:S(2)}) %collective-permute-start.17) | collective-permute-done | bytes 1048608 | tf_op jit(solution)/shard_map/ppermute | solution.py:33
  178.6 20.8 %collective-permute-done.19 = bf16[256,2048]{1,0:T(8,128)(2,1)S(1)} collective-permute-done((bf16[256,2048]{1,0:T(8,128)(2,1)S(1)}, bf16[256,2048]{1,0:T(8,128)(2,1)S(1)}, u32[]{:S(2)}, u32[]{:S(2)}) %collective-permute-start.19) | collective-permute-done | bytes 1048608 | tf_op jit(solution)/shard_map/ppermute | solution.py:33
  202.7 8.4 %collective-permute-done.20 = bf16[128,2048]{1,0:T(8,128)(2,1)S(1)} collective-permute-done((bf16[128,2048]{1,0:T(8,128)(2,1)S(1)}, bf16[128,2048]{1,0:T(8,128)(2,1)S(1)}, u32[]{:S(2)}, u32[]{:S(2)}) %collective-permute-start.20) | collective-permute-done | bytes 524320 | tf_op jit(solution)/shard_map/ppermute | solution.py:33
  224.5 8.1 %gate_units.2 = (bf16[704,1024]{1,0:T(8,128)(2,1)S(1)}, bf16[704,1024]{1,0:T(8,128)(2,1)S(1)}, bf16[704,1024]{1,0:T(8,128)(2,1)S(1)}) custom-call(bf16[1024,2048]{1,0:T(8,128)(2,1)S(1)} %copy-done.16, bf16[704,2048]{1,0:T(8,128)(2,1)S(1)} %copy-done.5, bf16[704,2048]{1,0:T(8,128)(2,1)S(1)} %copy-done.6), custom_call_target="tpu_custom_call" | custom-call | flops 118111600 | bytes 1048576 | tf_op jit(solution)/shard_map/gate_units/pallas_call | solution.py:532
  235.9 12.3 %gate_units.3 = (bf16[704,1024]{1,0:T(8,128)(2,1)S(1)}, bf16[704,1024]{1,0:T(8,128)(2,1)S(1)}, bf16[704,1024]{1,0:T(8,128)(2,1)S(1)}) custom-call(bf16[1024,2048]{1,0:T(8,128)(2,1)S(1)} %copy-done.16, bf16[704,2048]{1,0:T(8,128)(2,1)} %collective-permute-done.24.gate.refs_6_, bf16[704,2048]{1,0:T(8,128)(2,1)} %collective-permute-done.25.up.refs_7_), custom_call_target="tpu_custom_call" | custom-call | flops 118111600 | bytes 1048576 | tf_op jit(solution)/shard_map/gate_units/pallas_call | solution.py:532
  248.2 4.5 convolution_convert_fusion.3
  252.8 25.8 %all-gather.11.cloned.1.call-done.down.refs_2_ = bf16[704,2048]{1,0:T(8,128)(2,1)} async-done(((bf16[704,512]{1,0:T(8,128)(2,1)}), bf16[704,2048]{1,0:T(8,128)(2,1)}) %all-gather.11.cloned.1.call-update) | async-done | bytes 2883600 | tf_op jit(solution)/shard_map/all_gather | solution.py:37
  278.7 7.1 %add_convert_fusion.2 = bf16[704,2048]{1,0:T(8,128)(2,1)} fusion(bf16[704,2048]{1,0:T(8,128)(2,1)} %collective-permute-done.26, bf16[704,1024]{1,0:T(8,128)(2,1)S(1)} %copy-done.51, bf16[1024,2048]{1,0:T(8,128)(2,1)} %copy-done.19), kind=kOutput, calls=%fused_computation.2 | convolution fusion | flops 2957115392 | bytes 11403264 | tf_op jit(solution)/shard_map/dot_general | solution.py:17
  293.1 4.6 gate_grads.2
  297.7 6.4 %gate_grads.3 = (bf16[704,1024]{1,0:T(8,128)(2,1)S(1)}, bf16[704,1024]{1,0:T(8,128)(2,1)S(1)}) custom-call(bf16[1024,2048]{1,0:T(8,128)(2,1)S(1)} %copy-done.20, bf16[704,2048]{1,0:T(8,128)(2,1)} %collective-permute-done.27.down.refs_3_, bf16[704,1024]{1,0:T(8,128)(2,1)S(1)} %copy-done.60, bf16[704,1024]{1,0:T(8,128)(2,1)S(1)} %copy-done.62), custom_call_target="tpu_custom_call" | custom-call | flops 59055800 | bytes 1048576 | tf_op jit(solution)/shard_map/gate_grads/pallas_call | solution.py:555
  305.2 8.5 %sum_over_units.4 = (bf16[128,2048]{1,0:T(8,128)(2,1)S(1)}, bf16[128,2048]{1,0:T(8,128)(2,1)S(1)}) custom-call(bf16[704,1024]{1,0:T(8,128)(2,1)S(1)} %get-tuple-element.158.refs_0_, bf16[704,1024]{1,0:T(8,128)(2,1)S(1)} %get-tuple-element.163.refs_1_, bf16[704,1024]{1,0:T(8,128)(2,1)S(1)} %get-tuple-element.155.refs_2_, bf16[704,1024]{1,0:T(8,128)(2,1)} %copy-done.24, ...), custom_call_target="tpu_custom_call" | custom-call | flops 59055800 | bytes 1048576 | tf_op jit(solution)/shard_map/sum_over_units/pallas_call | solution.py:582
  313.7 4.6 convolution_convert_fusion.2
  321.7 12.5 %sum_over_units.5.near = bf16[512,2048]{1,0:T(8,128)(2,1)} custom-call(bf16[704,1024]{1,0:T(8,128)(2,1)S(1)} %get-tuple-element.158.refs_0_, bf16[704,1024]{1,0:T(8,128)(2,1)S(1)} %get-tuple-element.163.refs_1_, bf16[704,1024]{1,0:T(8,128)(2,1)S(1)} %get-tuple-element.155.refs_2_, bf16[704,1024]{1,0:T(8,128)(2,1)S(1)} %copy-done.25, ...), custom_call_target="tpu_custom_call" | custom-call | flops 118111600 | bytes 1048576 | tf_op jit(solution)/shard_map/sum_over_units/pallas_call | solution.py:582
  335.0 4.6 add_convert_fusion.1
  345.5 8.6 %sum_over_units.6.one = bf16[256,2048]{1,0:T(8,128)(2,1)S(1)} custom-call(bf16[704,1024]{1,0:T(8,128)(2,1)S(1)} %get-tuple-element.158.refs_0_, bf16[704,1024]{1,0:T(8,128)(2,1)S(1)} %get-tuple-element.163.refs_1_, bf16[704,1024]{1,0:T(8,128)(2,1)S(1)} %copy-done.28, bf16[704,1024]{1,0:T(8,128)(2,1)} %copy-done.24, ...), custom_call_target="tpu_custom_call" | custom-call | flops 59055800 | bytes 1048576 | tf_op jit(solution)/shard_map/sum_over_units/pallas_call | solution.py:582
  354.1 3.4 convolution_convert_fusion.1
  358.6 4.2 collective-permute-done.31
  362.8 4.5 add_convert_fusion
  367.7 15.8 %collective-permute-done.32.two = bf16[256,2048]{1,0:T(8,128)(2,1)} collective-permute-done((bf16[256,2048]{1,0:T(8,128)(2,1)}, bf16[256,2048]{1,0:T(8,128)(2,1)}, u32[]{:S(2)}, u32[]{:S(2)}) %collective-permute-start.32) | collective-permute-done | bytes 1048608 | tf_op jit(solution)/shard_map/ppermute | solution.py:33
  385.1 4.8 norm_back.2
  393.5 10.4 %sum_over_units.7.near = bf16[1024,2048]{1,0:T(8,128)(2,1)} custom-call(bf16[704,1024]{1,0:T(8,128)(2,1)S(1)} %copy-done.52, bf16[704,1024]{1,0:T(8,128)(2,1)S(1)} %copy-done.54, bf16[704,2048]{1,0:T(8,128)(2,1)S(1)} %copy-done.30, bf16[704,2048]{1,0:T(8,128)(2,1)} %collective-permute-done.27.down.refs_3_), custom_call_target="tpu_custom_call" | custom-call | flops 118111600 | bytes 1048576 | tf_op jit(solution)/shard_map/sum_over_units/pallas_call | solution.py:582
  403.9 12.2 %collective-permute-done.35 = bf16[256,2048]{1,0:T(8,128)(2,1)S(1)} collective-permute-done((bf16[256,2048]{1,0:T(8,128)(2,1)}, bf16[256,2048]{1,0:T(8,128)(2,1)S(1)}, u32[]{:S(2)}, u32[]{:S(2)}) %collective-permute-start.35) | collective-permute-done | bytes 1048608 | tf_op jit(solution)/shard_map/ppermute | solution.py:33
  422.1 6.9 %collective-permute-done.36 = bf16[128,2048]{1,0:T(8,128)(2,1)S(1)} collective-permute-done((bf16[128,2048]{1,0:T(8,128)(2,1)S(1)}, bf16[128,2048]{1,0:T(8,128)(2,1)S(1)}, u32[]{:S(2)}, u32[]{:S(2)}) %collective-permute-start.36) | collective-permute-done | bytes 524320 | tf_op jit(solution)/shard_map/ppermute | solution.py:33
  429.0 3.2 collective-permute-done.37
  445.6 4.5 convolution_convert_fusion.9.grads_kept
  450.2 7.4 %reduce-scatter.11.cloned.1.call-done = bf16[704,512]{1,0:T(8,128)(2,1)} async-done(((bf16[704,2048]{1,0:T(8,128)(2,1)}), bf16[704,512]{1,0:T(8,128)(2,1)}) %reduce-scatter.11.cloned.1.call-update) | async-done | bytes 720912 | tf_op jit(solution)/shard_map/reduce_scatter | solution.py:41
  458.6 25.3 %attention_backward.1 = (bf16[1024,384]{1,0:T(8,128)(2,1)S(1)}, bf16[1024,384]{1,0:T(8,128)(2,1)S(1)}, bf16[1024,384]{1,0:T(8,128)(2,1)S(1)}, bf16[1024,384]{1,0...) custom-call(s32[4]{0:T(128)S(1)} %pad_add_fusion.ints, f32[2]{0:T(128)S(1)} %pad_maximum_fusion.13.floats, ...), custom_call_target="tpu_custom_call" | custom-call | flops 400000000 | bytes 1048576 | tf_op jit(solution)/shard_map/attention_backward/pallas_call | solution.py:387
  484.0 3.5 convolution_convert_fusion.6
  492.4 3.6 convolution_convert_fusion.5
  496.0 5.0 add_convert_fusion.3
  502.4 3.2 collective-permute-done.43
  505.7 5.8 add_convert_fusion.4
  525.7 3.8 project_back.2
  529.5 8.5 %project_back.3 = (f32[1,2048]{1,0:T(1,128)S(1)}, bf16[768,2048]{1,0:T(8,128)(2,1)S(1)}) custom-call(bf16[1024,384]{1,0:T(8,128)(2,1)S(1)} %copy-done.41, bf16[1024,384]{1,0:T(8,128)(2,1)S(1)} %copy-done.47, bf16[1024,384]{1,0:T(8,128)(2,1)S(1)} %copy-done.45, bf16[1024,384]{1,0:T(8,128)(2,1)S(1)} %copy-done.43, bf16[2048,768]{1,0:T(8,128)(2,1)S(1)} %copy-done.11, ...), custom_call_target="tpu_custom_call" | custom-call | flops 96636768 | bytes 1048576 | tf_op jit(solution)/shard_map/project_back/pallas_call | solution.py:502
  547.9 4.5 collective-permute-done.54
  560.6 3.2 multiply_convert_fusion
  564.0 18.6 %collective-permute-done.56 = f32[10240]{0:T(1024)S(1)} collective-permute-done((f32[10240]{0:T(1024)S(1)}, f32[10240]{0:T(1024)S(1)}, u32[]{:S(2)}, u32[]{:S(2)}) %collective-permute-start.56) | collective-permute-done | bytes 40992 | tf_op jit(solution)/shard_map/ppermute | solution.py:33
  586.0 4.6 norm_back.3
  (429 shorter events, 178.0 us)
Async XLA Ops:
  7.2 80.0 %all-gather.5.cloned.1.call-start = ((), (), s32[]{:S(2)}) async-start(), calls=%async_computation.6 | async-start | bytes 3932160 | tf_op jit(solution)/shard_map/all_gather | solution.py:37
  8.3 33.7 %collective-permute-start.1 = (bf16[256,512]{1,0:T(8,128)(2,1)S(1)}, bf16[256,512]{1,0:T(8,128)(2,1)}, u32[]{:S(2)}, u32[]{:S(2)}) collective-permute-start(bf16[256,512]{1,0:T(8,128)(2,1)S(1)} %pad_maximum_fusion.11.refs_0_), channel_id=1, source_target_pairs={{0,24},{8,0},{16,8},{24,16},{1,25},{9,1},{17,9},{25,17},{2,26},{10... | collective-permute-start | bytes 786440 | tf_op jit(solution)/shard_map/ppermute | solution.py:46
  13.4 35.9 %collective-permute-start.2 = (bf16[256,512]{1,0:T(8,128)(2,1)S(1)}, bf16[256,512]{1,0:T(8,128)(2,1)}, u32[]{:S(2)}, u32[]{:S(2)}) collective-permute-start(bf16[256,512]{1,0:T(8,128)(2,1)S(1)} %pad_maximum_fusion.11.refs_0_), channel_id=1, source_target_pairs={{0,16},{8,24},{16,0},{24,8},{1,17},{9,25},{17,1},{25,9},{2,18},{10... | collective-permute-start | bytes 786440 | tf_op jit(solution)/shard_map/ppermute | solution.py:46
  13.4 35.9 %collective-permute-start.3 = (bf16[256,512]{1,0:T(8,128)(2,1)S(1)}, bf16[256,512]{1,0:T(8,128)(2,1)}, u32[]{:S(2)}, u32[]{:S(2)}) collective-permute-start(bf16[256,512]{1,0:T(8,128)(2,1)S(1)} %pad_maximum_fusion.11.refs_0_), channel_id=1, source_target_pairs={{0,8},{8,16},{16,24},{24,0},{1,9},{9,17},{17,25},{25,1},{2,10},{10... | collective-permute-start | bytes 786440 | tf_op jit(solution)/shard_map/ppermute | solution.py:46
  19.2 132.8 %all-gather.7.cloned.1.call-start = ((), (), s32[]{:S(2)}) async-start(), calls=%async_computation.7 | async-start | bytes 3604480 | tf_op jit(solution)/shard_map/all_gather | solution.py:37
  21.2 32.0 %collective-permute-start = (bf16[256,2048]{1,0:T(8,128)(2,1)}, bf16[256,2048]{1,0:T(8,128)(2,1)S(1)}, u32[]{:S(2)}, u32[]{:S(2)}) collective-permute-start(bf16[256,2048]{1,0:T(8,128)(2,1)} %get-tuple-element.227), channel_id=1, source_target_pairs={{0,2},{2,0},{4,6},{6,4},{1,3},{3,1},{5,7},{7,5},{8,10},{10,8},{12,... | collective-permute-start | bytes 3145736 | tf_op jit(solution)/shard_map/ppermute | solution.py:33
  22.7 28.9 %collective-permute-start.4 = (bf16[256,2048]{1,0:T(8,128)(2,1)}, bf16[256,2048]{1,0:T(8,128)(2,1)S(1)}, u32[]{:S(2)}, u32[]{:S(2)}) collective-permute-start(bf16[256,2048]{1,0:T(8,128)(2,1)} %get-tuple-element.227), channel_id=1, source_target_pairs={{0,4},{2,6},{4,0},{6,2},{1,5},{3,7},{5,1},{7,3},{8,12},{10,14},{12... | collective-permute-start | bytes 3145736 | tf_op jit(solution)/shard_map/ppermute | solution.py:33
  87.2 13.9 %collective-permute-start.8 = (bf16[2048,768]{1,0:T(8,128)(2,1)}, bf16[2048,768]{1,0:T(8,128)(2,1)S(1)}, u32[]{:S(2)}, u32[]{:S(2)}) collective-permute-start(bf16[2048,768]{1,0:T(8,128)(2,1)} %all-gather.5.cloned.1.call-done.weight.own), channel_id=1, source_target_pairs={{0,1},{1,0},{2,3},{3,2},{4,5},{5,4},{6,7},{7,6},{8,9},{9,8},{10,11... | collective-permute-start | bytes 9437192 | tf_op jit(solution)/shard_map/ppermute | solution.py:33
  87.3 126.0 %all-gather.9.cloned.1.call-start = ((), (), s32[]{:S(2)}) async-start(), calls=%async_computation.8 | async-start | bytes 3604480 | tf_op jit(solution)/shard_map/all_gather | solution.py:37
  87.5 25.8 %collective-permute-start.7 = (bf16[256,2048]{1,0:T(8,128)(2,1)}, bf16[256,2048]{1,0:T(8,128)(2,1)S(1)}, u32[]{:S(2)}, u32[]{:S(2)}) collective-permute-start(bf16[256,2048]{1,0:T(8,128)(2,1)} %get-tuple-element.136), channel_id=1, source_target_pairs={{0,2},{2,0},{4,6},{6,4},{1,3},{3,1},{5,7},{7,5},{8,10},{10,8},{12,... | collective-permute-start | bytes 3145736 | tf_op jit(solution)/shard_map/ppermute | solution.py:33
  89.1 25.4 %collective-permute-start.9 = (bf16[256,2048]{1,0:T(8,128)(2,1)}, bf16[256,2048]{1,0:T(8,128)(2,1)S(1)}, u32[]{:S(2)}, u32[]{:S(2)}) collective-permute-start(bf16[256,2048]{1,0:T(8,128)(2,1)} %get-tuple-element.136), channel_id=1, source_target_pairs={{0,4},{2,6},{4,0},{6,2},{1,5},{3,7},{5,1},{7,3},{8,12},{10,14},{12... | collective-permute-start | bytes 3145736 | tf_op jit(solution)/shard_map/ppermute | solution.py:33
  105.3 23.6 %collective-permute-start.13 = (bf16[256,2048]{1,0:T(8,128)(2,1)S(1)}, bf16[256,2048]{1,0:T(8,128)(2,1)S(1)}, u32[]{:S(2)}, u32[]{:S(2)}) collective-permute-start(bf16[256,2048]{1,0:T(8,128)(2,1)S(1)} %copy-done.73), channel_id=1, source_target_pairs={{0,1},{1,0},{2,3},{3,2},{4,5},{5,4},{6,7},{7,6},{8,9},{9,8},{10,11... | collective-permute-start | bytes 3145736 | tf_op jit(solution)/shard_map/ppermute | solution.py:33
  133.8 13.7 %collective-permute-start.14 = (bf16[128,2048]{1,0:T(8,128)(2,1)}, bf16[128,2048]{1,0:T(8,128)(2,1)S(1)}, u32[]{:S(2)}, u32[]{:S(2)}) collective-permute-start(bf16[128,2048]{1,0:T(8,128)(2,1)} %convolution_convert_fusion.8), channel_id=1, source_target_pairs={{0,2},{2,0},{4,6},{6,4},{1,3},{3,1},{5,7},{7,5},{8,10},{10,8},{12,... | collective-permute-start | bytes 1572872 | tf_op jit(solution)/shard_map/ppermute | solution.py:33
  134.4 13.5 %collective-permute-start.15 = (bf16[128,2048]{1,0:T(8,128)(2,1)}, bf16[128,2048]{1,0:T(8,128)(2,1)S(1)}, u32[]{:S(2)}, u32[]{:S(2)}) collective-permute-start(bf16[128,2048]{1,0:T(8,128)(2,1)} %convolution_convert_fusion.7), channel_id=1, source_target_pairs={{0,4},{2,6},{4,0},{6,2},{1,5},{3,7},{5,1},{7,3},{8,12},{10,14},{12... | collective-permute-start | bytes 1572872 | tf_op jit(solution)/shard_map/ppermute | solution.py:33
  136.0 142.7 %all-gather.11.cloned.1.call-start = ((), (), s32[]{:S(2)}) async-start(), calls=%async_computation.9 | async-start | bytes 3604480 | tf_op jit(solution)/shard_map/all_gather | solution.py:37
  149.1 24.1 %collective-permute-start.17 = (bf16[256,2048]{1,0:T(8,128)(2,1)}, bf16[256,2048]{1,0:T(8,128)(2,1)}, u32[]{:S(2)}, u32[]{:S(2)}) collective-permute-start(bf16[256,2048]{1,0:T(8,128)(2,1)} %get-tuple-element.130), channel_id=1, source_target_pairs={{0,4},{2,6},{4,0},{6,2},{1,5},{3,7},{5,1},{7,3},{8,12},{10,14},{12... | collective-permute-start | bytes 3145736 | tf_op jit(solution)/shard_map/ppermute | solution.py:33
  150.7 23.6 %collective-permute-start.16 = (bf16[256,2048]{1,0:T(8,128)(2,1)S(1)}, bf16[256,2048]{1,0:T(8,128)(2,1)}, u32[]{:S(2)}, u32[]{:S(2)}) collective-permute-start(bf16[256,2048]{1,0:T(8,128)(2,1)S(1)} %get-tuple-element.128), channel_id=1, source_target_pairs={{0,2},{2,0},{4,6},{6,4},{1,3},{3,1},{5,7},{7,5},{8,10},{10,8},{12,... | collective-permute-start | bytes 3145736 | tf_op jit(solution)/shard_map/ppermute | solution.py:33
  176.8 22.6 %collective-permute-start.19 = (bf16[256,2048]{1,0:T(8,128)(2,1)S(1)}, bf16[256,2048]{1,0:T(8,128)(2,1)S(1)}, u32[]{:S(2)}, u32[]{:S(2)}) collective-permute-start(bf16[256,2048]{1,0:T(8,128)(2,1)S(1)} %get-tuple-element.223), channel_id=1, source_target_pairs={{0,4},{2,6},{4,0},{6,2},{1,5},{3,7},{5,1},{7,3},{8,12},{10,14},{12... | collective-permute-start | bytes 3145736 | tf_op jit(solution)/shard_map/ppermute | solution.py:33
  177.4 23.6 %collective-permute-start.18 = (bf16[256,2048]{1,0:T(8,128)(2,1)S(1)}, bf16[256,2048]{1,0:T(8,128)(2,1)S(1)}, u32[]{:S(2)}, u32[]{:S(2)}) collective-permute-start(bf16[256,2048]{1,0:T(8,128)(2,1)S(1)} %get-tuple-element.223), channel_id=1, source_target_pairs={{0,2},{2,0},{4,6},{6,4},{1,3},{3,1},{5,7},{7,5},{8,10},{10,8},{12,... | collective-permute-start | bytes 3145736 | tf_op jit(solution)/shard_map/ppermute | solution.py:33
  213.3 22.6 %collective-permute-start.24 = (bf16[704,2048]{1,0:T(8,128)(2,1)S(1)}, bf16[704,2048]{1,0:T(8,128)(2,1)}, u32[]{:S(2)}, u32[]{:S(2)}) collective-permute-start(bf16[704,2048]{1,0:T(8,128)(2,1)S(1)} %copy-done.5), channel_id=1, source_target_pairs={{0,1},{1,0},{2,3},{3,2},{4,5},{5,4},{6,7},{7,6},{8,9},{9,8},{10,11... | collective-permute-start | bytes 8650760 | tf_op jit(solution)/shard_map/ppermute | solution.py:33
  213.3 22.6 %collective-permute-start.25 = (bf16[704,2048]{1,0:T(8,128)(2,1)}, bf16[704,2048]{1,0:T(8,128)(2,1)}, u32[]{:S(2)}, u32[]{:S(2)}) collective-permute-start(bf16[704,2048]{1,0:T(8,128)(2,1)} %all-gather.9.cloned.1.call-done.up.refs_5_), channel_id=1, source_target_pairs={{0,1},{1,0},{2,3},{3,2},{4,5},{5,4},{6,7},{7,6},{8,9},{9,8},{10,11... | collective-permute-start | bytes 8650760 | tf_op jit(solution)/shard_map/ppermute | solution.py:33
  215.7 16.9 %collective-permute-start.22 = (bf16[128,2048]{1,0:T(8,128)(2,1)}, bf16[128,2048]{1,0:T(8,128)(2,1)S(1)}, u32[]{:S(2)}, u32[]{:S(2)}) collective-permute-start(bf16[128,2048]{1,0:T(8,128)(2,1)} %slice.213), channel_id=1, source_target_pairs={{0,2},{2,0},{4,6},{6,4},{1,3},{3,1},{5,7},{7,5},{8,10},{10,8},{12,... | collective-permute-start | bytes 1572872 | tf_op jit(solution)/shard_map/ppermute | solution.py:33
  218.7 13.9 %collective-permute-start.23 = (bf16[128,2048]{1,0:T(8,128)(2,1)}, bf16[128,2048]{1,0:T(8,128)(2,1)}, u32[]{:S(2)}, u32[]{:S(2)}) collective-permute-start(bf16[128,2048]{1,0:T(8,128)(2,1)} %slice.214), channel_id=1, source_target_pairs={{0,4},{2,6},{4,0},{6,2},{1,5},{3,7},{5,1},{7,3},{8,12},{10,14},{12... | collective-permute-start | bytes 1572872 | tf_op jit(solution)/shard_map/ppermute | solution.py:33
  220.0 124.1 %reduce-scatter.7.cloned.1.call-start = ((), (), s32[]{:S(2)}) async-start(), calls=%async_computation.10 | async-start | bytes 3604480 | tf_op jit(solution)/shard_map/reduce_scatter | solution.py:41
  252.7 25.9 %collective-permute-start.26 = (bf16[704,2048]{1,0:T(8,128)(2,1)}, bf16[704,2048]{1,0:T(8,128)(2,1)}, u32[]{:S(2)}, u32[]{:S(2)}) collective-permute-start(bf16[704,2048]{1,0:T(8,128)(2,1)} %convolution_convert_fusion.3), channel_id=1, source_target_pairs={{0,1},{1,0},{2,3},{3,2},{4,5},{5,4},{6,7},{7,6},{8,9},{9,8},{10,11... | collective-permute-start | bytes 8650760 | tf_op jit(solution)/shard_map/ppermute | solution.py:33
  278.7 19.0 %collective-permute-start.27 = (bf16[704,2048]{1,0:T(8,128)(2,1)}, bf16[704,2048]{1,0:T(8,128)(2,1)}, u32[]{:S(2)}, u32[]{:S(2)}) collective-permute-start(bf16[704,2048]{1,0:T(8,128)(2,1)} %all-gather.11.cloned.1.call-done.down.refs_2_), channel_id=1, source_target_pairs={{0,1},{1,0},{2,3},{3,2},{4,5},{5,4},{6,7},{7,6},{8,9},{9,8},{10,11... | collective-permute-start | bytes 8650760 | tf_op jit(solution)/shard_map/ppermute | solution.py:33
  285.8 118.2 %reduce-scatter.9.cloned.1.call-start = ((), (), s32[]{:S(2)}) async-start(), calls=%async_computation.11 | async-start | bytes 3604480 | tf_op jit(solution)/shard_map/reduce_scatter | solution.py:41
  318.3 16.7 %collective-permute-start.30 = (bf16[704,2048]{1,0:T(8,128)(2,1)}, bf16[704,2048]{1,0:T(8,128)(2,1)S(1)}, u32[]{:S(2)}, u32[]{:S(2)}) collective-permute-start(bf16[704,2048]{1,0:T(8,128)(2,1)} %convolution_convert_fusion.2), channel_id=1, source_target_pairs={{0,1},{1,0},{2,3},{3,2},{4,5},{5,4},{6,7},{7,6},{8,9},{9,8},{10,11... | collective-permute-start | bytes 8650760 | tf_op jit(solution)/shard_map/ppermute | solution.py:33
  318.7 15.5 %collective-permute-start.28 = (bf16[128,2048]{1,0:T(8,128)(2,1)S(1)}, bf16[128,2048]{1,0:T(8,128)(2,1)S(1)}, u32[]{:S(2)}, u32[]{:S(2)}) collective-permute-start(bf16[128,2048]{1,0:T(8,128)(2,1)S(1)} %get-tuple-element.153), channel_id=1, source_target_pairs={{0,2},{2,0},{4,6},{6,4},{1,3},{3,1},{5,7},{7,5},{8,10},{10,8},{12,... | collective-permute-start | bytes 1572872 | tf_op jit(solution)/shard_map/ppermute | solution.py:33
  320.2 14.0 %collective-permute-start.29 = (bf16[128,2048]{1,0:T(8,128)(2,1)S(1)}, bf16[128,2048]{1,0:T(8,128)(2,1)S(1)}, u32[]{:S(2)}, u32[]{:S(2)}) collective-permute-start(bf16[128,2048]{1,0:T(8,128)(2,1)S(1)} %get-tuple-element.154), channel_id=1, source_target_pairs={{0,4},{2,6},{4,0},{6,2},{1,5},{3,7},{5,1},{7,3},{8,12},{10,14},{12... | collective-permute-start | bytes 1572872 | tf_op jit(solution)/shard_map/ppermute | solution.py:33
  339.6 118.0 %reduce-scatter.11.cloned.1.call-start = ((), (), s32[]{:S(2)}) async-start(), calls=%async_computation.12 | async-start | bytes 3604480 | tf_op jit(solution)/shard_map/reduce_scatter | solution.py:41
  357.6 25.9 %collective-permute-start.32 = (bf16[256,2048]{1,0:T(8,128)(2,1)}, bf16[256,2048]{1,0:T(8,128)(2,1)}, u32[]{:S(2)}, u32[]{:S(2)}) collective-permute-start(bf16[256,2048]{1,0:T(8,128)(2,1)} %get-tuple-element.160), channel_id=1, source_target_pairs={{0,2},{2,0},{4,6},{6,4},{1,3},{3,1},{5,7},{7,5},{8,10},{10,8},{12,... | collective-permute-start | bytes 3145736 | tf_op jit(solution)/shard_map/ppermute | solution.py:33
  357.6 25.8 %collective-permute-start.33 = (bf16[256,2048]{1,0:T(8,128)(2,1)}, bf16[256,2048]{1,0:T(8,128)(2,1)}, u32[]{:S(2)}, u32[]{:S(2)}) collective-permute-start(bf16[256,2048]{1,0:T(8,128)(2,1)} %get-tuple-element.161), channel_id=1, source_target_pairs={{0,4},{2,6},{4,0},{6,2},{1,5},{3,7},{5,1},{7,3},{8,12},{10,14},{12... | collective-permute-start | bytes 3145736 | tf_op jit(solution)/shard_map/ppermute | solution.py:33
  367.4 120.3 %reduce-scatter.13.cloned.1.call-start = ((), (), s32[]{:S(2)}) async-start(), calls=%async_computation.13 | async-start | bytes 1310720 | tf_op jit(solution)/shard_map/reduce_scatter | solution.py:41
  391.2 24.9 %collective-permute-start.35 = (bf16[256,2048]{1,0:T(8,128)(2,1)}, bf16[256,2048]{1,0:T(8,128)(2,1)S(1)}, u32[]{:S(2)}, u32[]{:S(2)}) collective-permute-start(bf16[256,2048]{1,0:T(8,128)(2,1)} %get-tuple-element.167), channel_id=1, source_target_pairs={{0,4},{2,6},{4,0},{6,2},{1,5},{3,7},{5,1},{7,3},{8,12},{10,14},{12... | collective-permute-start | bytes 3145736 | tf_op jit(solution)/shard_map/ppermute | solution.py:33
  391.9 27.1 %collective-permute-start.34 = (bf16[256,2048]{1,0:T(8,128)(2,1)}, bf16[256,2048]{1,0:T(8,128)(2,1)}, u32[]{:S(2)}, u32[]{:S(2)}) collective-permute-start(bf16[256,2048]{1,0:T(8,128)(2,1)} %get-tuple-element.167), channel_id=1, source_target_pairs={{0,2},{2,0},{4,6},{6,4},{1,3},{3,1},{5,7},{7,5},{8,10},{10,8},{12,... | collective-permute-start | bytes 3145736 | tf_op jit(solution)/shard_map/ppermute | solution.py:33
  441.3 149.3 %reduce-scatter.17.cloned.1.call-start = ((), (), s32[]{:S(2)}) async-start(), calls=%async_computation.15 | async-start | bytes 1966080 | tf_op jit(solution)/shard_map/reduce_scatter | solution.py:41
  441.8 15.8 %collective-permute-start.39 = (bf16[1024,256]{1,0:T(8,128)(2,1)}, bf16[1024,256]{1,0:T(8,128)(2,1)}, u32[]{:S(2)}, u32[]{:S(2)}) collective-permute-start(bf16[1024,256]{1,0:T(8,128)(2,1)} %convolution_convert_fusion.10), channel_id=1, source_target_pairs={{0,1},{1,0},{2,3},{3,2},{4,5},{5,4},{6,7},{7,6},{8,9},{9,8},{10,11... | collective-permute-start | bytes 1572872 | tf_op jit(solution)/shard_map/ppermute | solution.py:33
  444.3 43.4 %collective-permute-start.40 = (bf16[128,2048]{1,0:T(8,128)(2,1)}, bf16[128,2048]{1,0:T(8,128)(2,1)}, u32[]{:S(2)}, u32[]{:S(2)}) collective-permute-start(bf16[128,2048]{1,0:T(8,128)(2,1)} %get-tuple-element.179), channel_id=1, source_target_pairs={{0,2},{2,0},{4,6},{6,4},{1,3},{3,1},{5,7},{7,5},{8,10},{10,8},{12,... | collective-permute-start | bytes 1572872 | tf_op jit(solution)/shard_map/ppermute | solution.py:33
  445.3 42.4 %collective-permute-start.41 = (bf16[128,2048]{1,0:T(8,128)(2,1)}, bf16[128,2048]{1,0:T(8,128)(2,1)}, u32[]{:S(2)}, u32[]{:S(2)}) collective-permute-start(bf16[128,2048]{1,0:T(8,128)(2,1)} %get-tuple-element.180), channel_id=1, source_target_pairs={{0,4},{2,6},{4,0},{6,2},{1,5},{3,7},{5,1},{7,3},{8,12},{10,14},{12... | collective-permute-start | bytes 1572872 | tf_op jit(solution)/shard_map/ppermute | solution.py:33
  501.9 88.7 %reduce-scatter.15.cloned.1.call-start = ((), (), s32[]{:S(2)}) async-start(), calls=%async_computation.14 | async-start | bytes 1966080 | tf_op jit(solution)/shard_map/reduce_scatter | solution.py:41
  511.5 28.0 %collective-permute-start.47 = (bf16[256,2048]{1,0:T(8,128)(2,1)}, bf16[256,2048]{1,0:T(8,128)(2,1)}, u32[]{:S(2)}, u32[]{:S(2)}) collective-permute-start(bf16[256,2048]{1,0:T(8,128)(2,1)} %copy-done.69), channel_id=1, source_target_pairs={{0,4},{2,6},{4,0},{6,2},{1,5},{3,7},{5,1},{7,3},{8,12},{10,14},{12... | collective-permute-start | bytes 3145736 | tf_op jit(solution)/shard_map/ppermute | solution.py:33
  513.0 26.5 %collective-permute-start.46 = (bf16[256,2048]{1,0:T(8,128)(2,1)}, bf16[256,2048]{1,0:T(8,128)(2,1)}, u32[]{:S(2)}, u32[]{:S(2)}) collective-permute-start(bf16[256,2048]{1,0:T(8,128)(2,1)} %copy-done.68), channel_id=1, source_target_pairs={{0,2},{2,0},{4,6},{6,4},{1,3},{3,1},{5,7},{7,5},{8,10},{10,8},{12,... | collective-permute-start | bytes 3145736 | tf_op jit(solution)/shard_map/ppermute | solution.py:33
  539.5 14.4 %collective-permute-start.48 = (bf16[128,2048]{1,0:T(8,128)(2,1)S(1)}, bf16[128,2048]{1,0:T(8,128)(2,1)S(1)}, u32[]{:S(2)}, u32[]{:S(2)}) collective-permute-start(bf16[128,2048]{1,0:T(8,128)(2,1)S(1)} %get-tuple-element.197), channel_id=1, source_target_pairs={{0,2},{2,0},{4,6},{6,4},{1,3},{3,1},{5,7},{7,5},{8,10},{10,8},{12,... | collective-permute-start | bytes 1572872 | tf_op jit(solution)/shard_map/ppermute | solution.py:33
  540.2 14.0 %collective-permute-start.49 = (bf16[128,2048]{1,0:T(8,128)(2,1)S(1)}, bf16[128,2048]{1,0:T(8,128)(2,1)S(1)}, u32[]{:S(2)}, u32[]{:S(2)}) collective-permute-start(bf16[128,2048]{1,0:T(8,128)(2,1)S(1)} %get-tuple-element.199), channel_id=1, source_target_pairs={{0,4},{2,6},{4,0},{6,2},{1,5},{3,7},{5,1},{7,3},{8,12},{10,14},{12... | collective-permute-start | bytes 1572872 | tf_op jit(solution)/shard_map/ppermute | solution.py:33
  555.8 28.6 %collective-permute-start.50 = (bf16[256,2048]{1,0:T(8,128)(2,1)}, bf16[256,2048]{1,0:T(8,128)(2,1)}, u32[]{:S(2)}, u32[]{:S(2)}) collective-permute-start(bf16[256,2048]{1,0:T(8,128)(2,1)} %get-tuple-element.200), channel_id=1, source_target_pairs={{0,2},{2,0},{4,6},{6,4},{1,3},{3,1},{5,7},{7,5},{8,10},{10,8},{12,... | collective-permute-start | bytes 3145736 | tf_op jit(solution)/shard_map/ppermute | solution.py:33
  557.2 27.2 %collective-permute-start.51 = (bf16[256,2048]{1,0:T(8,128)(2,1)}, bf16[256,2048]{1,0:T(8,128)(2,1)}, u32[]{:S(2)}, u32[]{:S(2)}) collective-permute-start(bf16[256,2048]{1,0:T(8,128)(2,1)} %get-tuple-element.201), channel_id=1, source_target_pairs={{0,4},{2,6},{4,0},{6,2},{1,5},{3,7},{5,1},{7,3},{8,12},{10,14},{12... | collective-permute-start | bytes 3145736 | tf_op jit(solution)/shard_map/ppermute | solution.py:33
  559.1 23.5 %collective-permute-start.56 = (f32[10240]{0:T(1024)S(1)}, f32[10240]{0:T(1024)S(1)}, u32[]{:S(2)}, u32[]{:S(2)}) collective-permute-start(f32[10240]{0:T(1024)S(1)} %add.180), channel_id=1, source_target_pairs={{0,4},{2,6},{4,0},{6,2},{1,5},{3,7},{5,1},{7,3},{8,12},{10,14},{12... | collective-permute-start | bytes 122888 | tf_op jit(solution)/shard_map/ppermute | solution.py:33
  (114 other events, 801.0 us)
Sparse Core Ops, SparseCore 0:
  19.4 67.7 all-gather.4
  88.7 60.1 all-gather.6
  150.5 57.8 all-gather.8
  220.1 58.5 all-gather.10
  285.9 55.0 reduce-scatter.6
  343.1 56.0 reduce-scatter.8
  401.5 56.0 reduce-scatter.10
  460.5 26.9 reduce-scatter.12
  502.0 35.1 reduce-scatter.16
  539.5 34.6 reduce-scatter.14

commit v5 on v4

--- a/solution.py
+++ b/solution.py
@@ -112,7 +112,7 @@
         in_specs=[vmem] * 3,
         out_specs=[vmem] * 2,
         out_shape=[jax.ShapeDtypeStruct((rows, width), low)] * 2,
-        compiler_params=pltpu.CompilerParams(vmem_limit_bytes=24 * 2**20),
+        compiler_params=pltpu.CompilerParams(vmem_limit_bytes=10 * 2**20),
         cost_estimate=estimate(10**9),
         name="join",
     )(after(near, *hold), to_first, to_second)
@@ -151,6 +151,10 @@
     size = values.shape[0] // len(outs)
     for place, out in enumerate(outs):
         out[...] = values[place * size : (place + 1) * size].astype(out.dtype)
+
+
+def kept_block(shape):
+    return pl.BlockSpec(shape, lambda i: (0,) * len(shape), pipeline_mode=pl.Buffered(1))
 
 
 def estimate(flops):
@@ -262,7 +266,7 @@
             jax.ShapeDtypeStruct((2, slots, width), jnp.float32),
             jax.ShapeDtypeStruct((2, slots), jnp.float32),
         ],
-        compiler_params=pltpu.CompilerParams(vmem_limit_bytes=40 * 2**20),
+        compiler_params=pltpu.CompilerParams(vmem_limit_bytes=32 * 2**20),
         cost_estimate=estimate(5 * 10**9),
         name="attention_forward",
     )(ints, floats, *kept, *received, gain)
@@ -397,7 +401,7 @@
             pltpu.VMEM((2, slots, width // 2), jnp.float32),
             pltpu.VMEM((slots, width), jnp.float32),
         ],
-        compiler_params=pltpu.CompilerParams(vmem_limit_bytes=48 * 2**20),
+        compiler_params=pltpu.CompilerParams(vmem_limit_bytes=40 * 2**20),
         cost_estimate=estimate(20 * 10**9),
         name="attention_backward",
     )(ints, floats, ordered, grads_kept, grads_received, outs, log_totals, gain, cosine, sine)
@@ -437,7 +441,7 @@
             jax.ShapeDtypeStruct((rows, width), low),
             jax.ShapeDtypeStruct((1, width), jnp.float32),
         ],
-        compiler_params=pltpu.CompilerParams(vmem_limit_bytes=24 * 2**20),
+        compiler_params=pltpu.CompilerParams(vmem_limit_bytes=12 * 2**20),
         cost_estimate=estimate(10**9),
         name="norm_back",
     )(*parts, values, gain[None], added)
@@ -467,13 +471,13 @@
         grid=(4,),
         in_specs=[
             down(width),
-            pl.BlockSpec((width, columns), lambda i: (0, 0)),
+            kept_block((width, columns)),
             down(cosine.shape[1]),
             down(cosine.shape[1]),
         ],
         out_specs=[down(columns // 2)] * 2,
         out_shape=[jax.ShapeDtypeStruct((slots, columns // 2), low)] * 2,
-        compiler_params=pltpu.CompilerParams(vmem_limit_bytes=32 * 2**20),
+        compiler_params=pltpu.CompilerParams(vmem_limit_bytes=14 * 2**20),
         cost_estimate=estimate(2 * slots * width * columns),
         name="project",
     )(inputs, weight, cosine, sine)
@@ -498,7 +502,7 @@
 def project_back(grads, own, other, normed, first, count, rows, parts=1):
     width, columns = own.shape
     down = lambda size: pl.BlockSpec((rows, size), lambda i: (first + i, 0))
-    whole = pl.BlockSpec((width, columns), lambda i: (0, 0))
+    whole = kept_block((width, columns))
     return pl.pallas_call(
         project_back_kernel,
         grid=(count,),
@@ -507,7 +511,7 @@
         + [pl.BlockSpec((rows // parts, width), lambda i: (i, 0))] * parts,
         out_shape=[jax.ShapeDtypeStruct((1, width), jnp.float32)]
         + [jax.ShapeDtypeStruct((count * rows // parts, width), low)] * parts,
-        compiler_params=pltpu.CompilerParams(vmem_limit_bytes=40 * 2**20),
+        compiler_params=pltpu.CompilerParams(vmem_limit_bytes=22 * 2**20),
         cost_estimate=estimate(4 * count * rows * width * columns),
         name="project_back",
     )(*grads, own, other, normed)
@@ -527,7 +531,7 @@
     slots, width = inputs.shape
     units = gate.shape[0]
     block = slots // 4
-    whole = pl.BlockSpec((units, width), lambda i: (0, 0))
+    whole = kept_block((units, width))
     across = pl.BlockSpec((units, block), lambda i: (0, i))
     return pl.pallas_call(
         gate_kernel,
@@ -535,7 +539,7 @@
         in_specs=[pl.BlockSpec((block, width), lambda i: (i, 0)), whole, whole],
         out_specs=[across] * 3,
         out_shape=[jax.ShapeDtypeStruct((units, slots), low)] * 3,
-        compiler_params=pltpu.CompilerParams(vmem_limit_bytes=40 * 2**20),
+        compiler_params=pltpu.CompilerParams(vmem_limit_bytes=22 * 2**20),
         cost_estimate=estimate(4 * slots * width * units),
         name="gate_units",
     )(inputs, gate, up)
@@ -557,13 +561,13 @@
         grid=(4,),
         in_specs=[
             pl.BlockSpec((block, width), lambda i: (i, 0)),
-            pl.BlockSpec((units, width), lambda i: (0, 0)),
+            kept_block((units, width)),
             across,
             across,
         ],
         out_specs=[across] * 2,
         out_shape=[jax.ShapeDtypeStruct((units, slots), low)] * 2,
-        compiler_params=pltpu.CompilerParams(vmem_limit_bytes=40 * 2**20),
+        compiler_params=pltpu.CompilerParams(vmem_limit_bytes=16 * 2**20),
         cost_estimate=estimate(2 * slots * width * units),
         name="gate_grads",
     )(grads, down, gate_factor, up_factor)
@@ -583,10 +587,10 @@
         functools.partial(sum_kernel, terms),
         grid=(count,),
         in_specs=[pl.BlockSpec((units, rows), lambda i: (0, first + i))] * terms
-        + [pl.BlockSpec((units, width), lambda i: (0, 0))] * terms,
+        + [kept_block((units, width))] * terms,
         out_specs=[pl.BlockSpec((rows // parts, width), lambda i: (i, 0))] * parts,
         out_shape=[jax.ShapeDtypeStruct((count * rows // parts, width), low)] * parts,
-        compiler_params=pltpu.CompilerParams(vmem_limit_bytes=48 * 2**20),
+        compiler_params=pltpu.CompilerParams(vmem_limit_bytes=26 * 2**20),
         cost_estimate=estimate(2 * count * rows * width * units * terms),
         name="sum_over_units",
     )(*factors, *weights)
@@ -727,9 +731,6 @@
         after(ffn_in, hidden_own), gate_other, up_other
     )
 
-    down_own = after(down_own, hidden_other)
-    down_other = swap(down_own, "tensor", 1)
-
     ffn_out_grad_all = group_rows(ffn_out_grad_own, ffn_out_grad_near, hidden_own)
 
     def weight_grad(own_side, other_side, right_side, *events):
@@ -739,6 +740,8 @@
         return total, fsdp_reduce(total, 1)
 
     down_terms, down_grad = weight_grad(hidden_own, hidden_other, ffn_out_grad_all)
+    down_own = after(down_own, down_terms)
+    down_other = swap(down_own, "tensor", 1)
     gate_grad_own, up_grad_own = gate_grads(
         after(ffn_out_grad_all, down_terms), down_own, gate_factor_own, up_factor_own
     )
@@ -862,8 +865,6 @@
         fsdp_reduce(own_first, 0).astype(jnp.float32),
         fsdp_reduce(own_second, 0).astype(jnp.float32),
     )
-    output_grad = output_grad.astype(jnp.float32)
-    output_grad = jnp.stack(in_order(output_grad[:value_half], output_grad[value_half:]))
     nearer_gain, nearer_terms = project_back(
         (after(kept_first, third_gain),) + parts[1:],
         qkv_own,
@@ -879,6 +880,11 @@
         [after(terms, *ffn_here) for terms in third_terms],
         lambda *arrived: nearer_terms[:rows],
     )
+    output_grad, gate_weight_grad, up_weight_grad, down_grad = (
+        after(grad, nearer_gain).astype(jnp.float32)
+        for grad in (output_grad, gate_weight_grad, up_weight_grad, down_grad)
+    )
+    output_grad = jnp.stack(in_order(output_grad[:value_half], output_grad[value_half:]))
     attention_gain_part = (third_gain + nearer_gain)[0]
     ffn_here = [after(part, nearer_gain) for part in ffn_here]
     block_output = (valid * (residual + summed(ffn_here))).astype(low)
@@ -927,9 +933,9 @@
         small[2 * width : lambda_end].reshape(lambda_full.shape),
         small[lambda_end:].reshape(gain_full.shape),
         small[width : 2 * width],
-        jnp.transpose(gate_weight_grad).astype(jnp.float32),
-        jnp.transpose(up_weight_grad).astype(jnp.float32),
-        down_grad.astype(jnp.float32),
+        jnp.transpose(gate_weight_grad),
+        jnp.transpose(up_weight_grad),
+        down_grad,
     )
 
 

time: 613 us -> 608 us (level)
  local copies, waits for them, and re-layouts: 71.4 us -> 88.9 us
  Pallas kernels: 148 us -> 137 us
  waiting for transfers between devices: 215 us -> 208 us
    unnamed x208 -> x230, local copies, waits for them, and re-layouts: 54.5 us -> 73.1 us
    ppermute x54, waiting for transfers between devices: 150 us -> 158 us  [swap(): lax.ppermute(values, axis, [(place, place ^ mask) for place in range(size)])]
    ppermute x3, waiting for transfers between devices: 7.33 us -> 0.01 us  [shift(): lax.ppermute(values, 'fsdp', [(place, (place + step) % size) for place in...]
    all_gather x4, waiting for transfers between devices: 49.7 us -> 43.1 us  [fsdp_gather(): return lax.all_gather(after(own, *others), 'fsdp', axis=axis, tiled=True)]
    pallas_call x4, Pallas kernels: 40 us -> 33.6 us  [sum_over_units(): pl.pallas_call(functools.partial(sum_kernel, terms), grid=(count,), in_sp...]
  transfers between devices with their start and end apart: 67 -> 67, of which waited for: 28 -> 32; matrix products, arithmetic and copies ran while one was open for 18% -> 17% of each run, Pallas kernels for 25% -> 23%
where the time goes in v5:
time: 608 us; the launch traced here: 598 us
  waiting for transfers between devices  208 us (34%)
  Pallas kernels  137 us (23%)
  local copies, waits for them, and re-layouts  88.9 us (15%)
  matrix products  57 us (9%)
  starting transfers between devices  55.7 us (9%)
  other arithmetic  31.8 us (5%)
  between operations  19.6 us (3%)
    ppermute x54, waiting for transfers between devices, swap(): lax.ppermute(values, axis, [(place, place ^ mask) for place in range(size)])  158 us
    unnamed x230, local copies, waits for them, and re-layouts  73.1 us
    dot_general x16, matrix products, contract(): lax.dot_general(left_side, right_side, (((left_dim,), (right_dim,)), ((),...  57 us
    ppermute x54, starting transfers between devices, swap(): lax.ppermute(values, axis, [(place, place ^ mask) for place in range(size)])  46.5 us
    all_gather x4, waiting for transfers between devices, fsdp_gather(): return lax.all_gather(after(own, *others), 'fsdp', axis=axis, tiled=True)  43.1 us
    pallas_call x4, Pallas kernels, sum_over_units(): pl.pallas_call(functools.partial(sum_kernel, terms), grid=(count,), in_sp...  33.6 us
    pallas_call x1, Pallas kernels, attention_backward(): pl.pallas_call(attention_backward_kernel, in_specs=[smem, smem] + [vmem]...  22.8 us
    pallas_call x2, Pallas kernels, gate_units(): pl.pallas_call(gate_kernel, grid=(4,), in_specs=[pl.BlockSpec((block, wid...  20.3 us
  transfers between devices with their start and end apart: 67, of which 32 were waited for; matrix products, arithmetic and copies ran while one was open for 17% of the time, Pallas kernels for 23%

profile of v5, /device:TPU:0, one launch (start us, length us, event | category | flops | bytes accessed | tf_op | source)
XLA Modules:
  0.0 598.0 jit_solution(519818604851267318)
XLA Ops:
  8.3 3.1 collective-permute-start.3
  35.2 3.7 fusion.10
  51.8 7.0 %collective-permute-done.5 = bf16[128,2048]{1,0:T(8,128)(2,1)S(1)} collective-permute-done((bf16[128,2048]{1,0:T(8,128)(2,1)S(1)}, bf16[128,2048]{1,0:T(8,128)(2,1)S(1)}, u32[]{:S(2)}, u32[]{:S(2)}) %collective-permute-start.5) | collective-permute-done | bytes 524320 | tf_op jit(solution)/shard_map/ppermute | solution.py:33
  60.7 27.1 %all-gather.5.cloned.1.call-done.weight.own = bf16[2048,768]{1,0:T(8,128)(2,1)} async-done(((bf16[512,768]{1,0:T(8,128)(2,1)}), bf16[2048,768]{1,0:T(8,128)(2,1)}) %all-gather.5.cloned.1.call-update) | async-done | bytes 3145744 | tf_op jit(solution)/shard_map/all_gather | solution.py:37
  97.4 4.2 project.2
  101.7 4.3 project.3
  106.7 7.1 %collective-permute-done.9 = bf16[256,2048]{1,0:T(8,128)(2,1)S(1)} collective-permute-done((bf16[256,2048]{1,0:T(8,128)(2,1)}, bf16[256,2048]{1,0:T(8,128)(2,1)S(1)}, u32[]{:S(2)}, u32[]{:S(2)}) %collective-permute-start.9) | collective-permute-done | bytes 1048608 | tf_op jit(solution)/shard_map/ppermute | solution.py:33
  116.1 13.3 %attention_forward.1 = (bf16[1024,256]{1,0:T(8,128)(2,1)S(1)}, bf16[1024,256]{1,0:T(8,128)(2,1)S(1)}, bf16[2048,768]{1,0:T(8,128)(2,1)S(1)}, f32[2,2048,256]{2,1,0:T(8,128)S(1)}, f32[2,2048]{1,0:T(2,128)S(1)}) custom-call(s32[4]{0:T(128)S(1)} %pad_add_fusion.ints, f32[2]{0:T(128)S(1)} %pad_maximum_fusion.13.floats, ...), custom_call_target="tpu_custom_call" | custom-call | flops 100000000 | bytes 1048576 | tf_op jit(solution)/shard_map/attention_forward/pallas_call | solution.py:258
  136.7 3.1 convolution_convert_fusion.near
  139.8 8.4 %collective-permute-done.14.to_first = bf16[128,2048]{1,0:T(8,128)(2,1)S(1)} collective-permute-done((bf16[128,2048]{1,0:T(8,128)(2,1)}, bf16[128,2048]{1,0:T(8,128)(2,1)S(1)}, u32[]{:S(2)}, u32[]{:S(2)}) %collective-permute-start.14) | collective-permute-done | bytes 524320 | tf_op jit(solution)/shard_map/ppermute | solution.py:33
  151.9 22.5 %collective-permute-done.16 = bf16[256,2048]{1,0:T(8,128)(2,1)} collective-permute-done((bf16[256,2048]{1,0:T(8,128)(2,1)}, bf16[256,2048]{1,0:T(8,128)(2,1)}, u32[]{:S(2)}, u32[]{:S(2)}) %collective-permute-start.16) | collective-permute-done | bytes 1048608 | tf_op jit(solution)/shard_map/ppermute | solution.py:33
  179.5 20.3 %collective-permute-done.19 = bf16[256,2048]{1,0:T(8,128)(2,1)S(1)} collective-permute-done((bf16[256,2048]{1,0:T(8,128)(2,1)S(1)}, bf16[256,2048]{1,0:T(8,128)(2,1)S(1)}, u32[]{:S(2)}, u32[]{:S(2)}) %collective-permute-start.19) | collective-permute-done | bytes 1048608 | tf_op jit(solution)/shard_map/ppermute | solution.py:33
  203.0 8.8 %collective-permute-done.20 = bf16[128,2048]{1,0:T(8,128)(2,1)S(1)} collective-permute-done((bf16[128,2048]{1,0:T(8,128)(2,1)S(1)}, bf16[128,2048]{1,0:T(8,128)(2,1)S(1)}, u32[]{:S(2)}, u32[]{:S(2)}) %collective-permute-start.20) | collective-permute-done | bytes 524320 | tf_op jit(solution)/shard_map/ppermute | solution.py:33
  224.9 8.1 %gate_units.2 = (bf16[704,1024]{1,0:T(8,128)(2,1)S(1)}, bf16[704,1024]{1,0:T(8,128)(2,1)S(1)}, bf16[704,1024]{1,0:T(8,128)(2,1)S(1)}) custom-call(bf16[1024,2048]{1,0:T(8,128)(2,1)S(1)} %copy-done.20, bf16[704,2048]{1,0:T(8,128)(2,1)S(1)} %copy-done.6, bf16[704,2048]{1,0:T(8,128)(2,1)S(1)} %copy-done.7), custom_call_target="tpu_custom_call" | custom-call | flops 118111600 | bytes 1048576 | tf_op jit(solution)/shard_map/gate_units/pallas_call | solution.py:536
  236.3 12.3 %gate_units.3 = (bf16[704,1024]{1,0:T(8,128)(2,1)S(1)}, bf16[704,1024]{1,0:T(8,128)(2,1)S(1)}, bf16[704,1024]{1,0:T(8,128)(2,1)S(1)}) custom-call(bf16[1024,2048]{1,0:T(8,128)(2,1)S(1)} %copy-done.20, bf16[704,2048]{1,0:T(8,128)(2,1)} %collective-permute-done.24.gate.refs_6_, bf16[704,2048]{1,0:T(8,128)(2,1)} %collective-permute-done.25.up.refs_7_), custom_call_target="tpu_custom_call" | custom-call | flops 118111600 | bytes 1048576 | tf_op jit(solution)/shard_map/gate_units/pallas_call | solution.py:536
  248.6 3.4 convolution_convert_fusion.3
  252.1 5.3 collective-permute-done.26
  257.4 4.5 add_convert_fusion.2
  261.8 16.0 %all-gather.11.cloned.1.call-done.down.refs_2_ = bf16[704,2048]{1,0:T(8,128)(2,1)} async-done(((bf16[704,512]{1,0:T(8,128)(2,1)}), bf16[704,2048]{1,0:T(8,128)(2,1)}) %all-gather.11.cloned.1.call-update) | async-done | bytes 2883600 | tf_op jit(solution)/shard_map/all_gather | solution.py:37
  284.9 4.6 gate_grads.2
  289.6 7.4 %gate_grads.3 = (bf16[704,1024]{1,0:T(8,128)(2,1)S(1)}, bf16[704,1024]{1,0:T(8,128)(2,1)S(1)}) custom-call(bf16[1024,2048]{1,0:T(8,128)(2,1)S(1)} %copy-done.24, bf16[704,2048]{1,0:T(8,128)(2,1)} %collective-permute-done.27.down.refs_3_, bf16[704,1024]{1,0:T(8,128)(2,1)S(1)} %copy-done.70, bf16[704,1024]{1,0:T(8,128)(2,1)S(1)} %copy-done.72), custom_call_target="tpu_custom_call" | custom-call | flops 59055800 | bytes 1048576 | tf_op jit(solution)/shard_map/gate_grads/pallas_call | solution.py:559
  297.1 7.5 %sum_over_units.4 = (bf16[128,2048]{1,0:T(8,128)(2,1)S(1)}, bf16[128,2048]{1,0:T(8,128)(2,1)S(1)}) custom-call(bf16[704,1024]{1,0:T(8,128)(2,1)S(1)} %get-tuple-element.162.refs_0_, bf16[704,1024]{1,0:T(8,128)(2,1)S(1)} %get-tuple-element.167.refs_1_, bf16[704,1024]{1,0:T(8,128)(2,1)S(1)} %get-tuple-element.159.refs_2_, ...), custom_call_target="tpu_custom_call" | custom-call | flops 59055800 | bytes 1048576 | tf_op jit(solution)/shard_map/sum_over_units/pallas_call | solution.py:586
  304.6 3.4 convolution_convert_fusion.2
  311.4 9.9 %sum_over_units.5.near = bf16[512,2048]{1,0:T(8,128)(2,1)S(1)} custom-call(bf16[704,1024]{1,0:T(8,128)(2,1)S(1)} %get-tuple-element.162.refs_0_, bf16[704,1024]{1,0:T(8,128)(2,1)S(1)} %get-tuple-element.167.refs_1_, bf16[704,1024]{1,0:T(8,128)(2,1)S(1)} %get-tuple-element.159.refs_2_, bf16[704,1024]{1,0:T(8,128)(2,1)S(1)} %get-tuple-element.166.refs_3_, ...), custom_call_target="tpu_custom_call" | custom-call | flops 118111600 | bytes 1048576 | tf_op jit(solution)/shard_map/sum_over_units/pallas_call | solution.py:586
  324.4 4.5 add_convert_fusion.1
  342.2 6.8 %sum_over_units.6.one = bf16[256,2048]{1,0:T(8,128)(2,1)S(1)} custom-call(bf16[704,1024]{1,0:T(8,128)(2,1)S(1)} %copy-done.31, bf16[704,1024]{1,0:T(8,128)(2,1)S(1)} %copy-done.29, bf16[704,1024]{1,0:T(8,128)(2,1)S(1)} %copy-done.35, bf16[704,1024]{1,0:T(8,128)(2,1)S(1)} %copy-done.33, bf16[704,2048]{1,0:T(8,128)(2,1)S(1)} %copy-done.6, ...), custom_call_target="tpu_custom_call" | custom-call | flops 59055800 | bytes 1048576 | tf_op jit(solution)/shard_map/sum_over_units/pallas_call | solution.py:586
  349.1 3.4 convolution_convert_fusion.1
  357.8 4.5 add_convert_fusion
  362.6 15.8 %collective-permute-done.33.three = bf16[256,2048]{1,0:T(8,128)(2,1)} collective-permute-done((bf16[256,2048]{1,0:T(8,128)(2,1)}, bf16[256,2048]{1,0:T(8,128)(2,1)}, u32[]{:S(2)}, u32[]{:S(2)}) %collective-permute-start.33) | collective-permute-done | bytes 1048608 | tf_op jit(solution)/shard_map/ppermute | solution.py:33
  381.3 4.8 norm_back.2
  389.5 9.4 %sum_over_units.7.near = bf16[1024,2048]{1,0:T(8,128)(2,1)S(1)} custom-call(bf16[704,1024]{1,0:T(8,128)(2,1)S(1)} %copy-done.62, bf16[704,1024]{1,0:T(8,128)(2,1)S(1)} %copy-done.64, bf16[704,2048]{1,0:T(8,128)(2,1)S(1)} %copy-done.37, bf16[704,2048]{1,0:T(8,128)(2,1)} %collective-permute-done.27.down.refs_3_), custom_call_target="tpu_custom_call" | custom-call | flops 118111600 | bytes 1048576 | tf_op jit(solution)/shard_map/sum_over_units/pallas_call | solution.py:586
  401.0 11.1 %collective-permute-done.35 = bf16[256,2048]{1,0:T(8,128)(2,1)S(1)} collective-permute-done((bf16[256,2048]{1,0:T(8,128)(2,1)}, bf16[256,2048]{1,0:T(8,128)(2,1)S(1)}, u32[]{:S(2)}, u32[]{:S(2)}) %collective-permute-start.35) | collective-permute-done | bytes 1048608 | tf_op jit(solution)/shard_map/ppermute | solution.py:33
  418.2 6.4 %collective-permute-done.36 = bf16[128,2048]{1,0:T(8,128)(2,1)S(1)} collective-permute-done((bf16[128,2048]{1,0:T(8,128)(2,1)S(1)}, bf16[128,2048]{1,0:T(8,128)(2,1)S(1)}, u32[]{:S(2)}, u32[]{:S(2)}) %collective-permute-start.36) | collective-permute-done | bytes 524320 | tf_op jit(solution)/shard_map/ppermute | solution.py:33
  424.6 3.6 collective-permute-done.37
  433.3 2.6 collective-permute-done.38
  441.7 4.6 convolution_convert_fusion.9.grads_kept
  446.3 5.3 reduce-scatter.11.cloned.1.call-done
  457.9 22.8 %attention_backward.1 = (bf16[1024,384]{1,0:T(8,128)(2,1)S(1)}, bf16[1024,384]{1,0:T(8,128)(2,1)S(1)}, bf16[1024,384]{1,0:T(8,128)(2,1)S(1)}, bf16[1024,384]{1,0...) custom-call(s32[4]{0:T(128)S(1)} %pad_add_fusion.ints, f32[2]{0:T(128)S(1)} %pad_maximum_fusion.13.floats, ...), custom_call_target="tpu_custom_call" | custom-call | flops 400000000 | bytes 1048576 | tf_op jit(solution)/shard_map/attention_backward/pallas_call | solution.py:391
  480.8 3.6 convolution_convert_fusion.6
  491.1 3.6 convolution_convert_fusion.5
  494.7 5.1 add_convert_fusion.3
  504.5 5.8 add_convert_fusion.4
  523.9 7.2 %project_back.3 = (f32[1,2048]{1,0:T(1,128)S(1)}, bf16[768,2048]{1,0:T(8,128)(2,1)S(1)}) custom-call(bf16[1024,384]{1,0:T(8,128)(2,1)S(1)} %copy-done.52, bf16[1024,384]{1,0:T(8,128)(2,1)S(1)} %copy-done.58, bf16[1024,384]{1,0:T(8,128)(2,1)S(1)} %copy-done.56, bf16[1024,384]{1,0:T(8,128)(2,1)S(1)} %copy-done.54, bf16[2048,768]{1,0:T(8,128)(2,1)S(1)} %copy-done.14, ...), custom_call_target="tpu_custom_call" | custom-call | flops 96636768 | bytes 1048576 | tf_op jit(solution)/shard_map/project_back/pallas_call | solution.py:506
  534.5 3.2 multiply_convert_fusion
  538.6 6.9 %collective-permute-done.49.to_second = bf16[128,2048]{1,0:T(8,128)(2,1)S(1)} collective-permute-done((bf16[128,2048]{1,0:T(8,128)(2,1)S(1)}, bf16[128,2048]{1,0:T(8,128)(2,1)S(1)}, u32[]{:S(2)}, u32[]{:S(2)}) %collective-permute-start.49) | collective-permute-done | bytes 524320 | tf_op jit(solution)/shard_map/ppermute | solution.py:33
  555.3 4.7 collective-permute-done.54
  560.1 13.4 %collective-permute-done.55 = f32[10240]{0:T(1024)S(1)} collective-permute-done((f32[10240]{0:T(1024)S(1)}, f32[10240]{0:T(1024)S(1)}, u32[]{:S(2)}, u32[]{:S(2)}) %collective-permute-start.55) | collective-permute-done | bytes 40992 | tf_op jit(solution)/shard_map/ppermute | solution.py:33
  580.9 4.4 norm_back.3
  (451 shorter events, 199.8 us)
Async XLA Ops:
  7.2 80.5 %all-gather.5.cloned.1.call-start = ((), (), s32[]{:S(2)}) async-start(), calls=%async_computation.6 | async-start | bytes 3932160 | tf_op jit(solution)/shard_map/all_gather | solution.py:37
  8.3 34.5 %collective-permute-start.3 = (bf16[256,512]{1,0:T(8,128)(2,1)S(1)}, bf16[256,512]{1,0:T(8,128)(2,1)}, u32[]{:S(2)}, u32[]{:S(2)}) collective-permute-start(bf16[256,512]{1,0:T(8,128)(2,1)S(1)} %pad_maximum_fusion.11.refs_0_), channel_id=1, source_target_pairs={{0,8},{8,16},{16,24},{24,0},{1,9},{9,17},{17,25},{25,1},{2,10},{10... | collective-permute-start | bytes 786440 | tf_op jit(solution)/shard_map/ppermute | solution.py:46
  11.4 31.4 %collective-permute-start.2 = (bf16[256,512]{1,0:T(8,128)(2,1)S(1)}, bf16[256,512]{1,0:T(8,128)(2,1)}, u32[]{:S(2)}, u32[]{:S(2)}) collective-permute-start(bf16[256,512]{1,0:T(8,128)(2,1)S(1)} %pad_maximum_fusion.11.refs_0_), channel_id=1, source_target_pairs={{0,16},{8,24},{16,0},{24,8},{1,17},{9,25},{17,1},{25,9},{2,18},{10... | collective-permute-start | bytes 786440 | tf_op jit(solution)/shard_map/ppermute | solution.py:46
  14.0 28.8 %collective-permute-start.1 = (bf16[256,512]{1,0:T(8,128)(2,1)S(1)}, bf16[256,512]{1,0:T(8,128)(2,1)}, u32[]{:S(2)}, u32[]{:S(2)}) collective-permute-start(bf16[256,512]{1,0:T(8,128)(2,1)S(1)} %pad_maximum_fusion.11.refs_0_), channel_id=1, source_target_pairs={{0,24},{8,0},{16,8},{24,16},{1,25},{9,1},{17,9},{25,17},{2,26},{10... | collective-permute-start | bytes 786440 | tf_op jit(solution)/shard_map/ppermute | solution.py:46
  20.1 131.9 %all-gather.7.cloned.1.call-start = ((), (), s32[]{:S(2)}) async-start(), calls=%async_computation.7 | async-start | bytes 3604480 | tf_op jit(solution)/shard_map/all_gather | solution.py:37
  22.1 24.3 %collective-permute-start.4 = (bf16[256,2048]{1,0:T(8,128)(2,1)}, bf16[256,2048]{1,0:T(8,128)(2,1)S(1)}, u32[]{:S(2)}, u32[]{:S(2)}) collective-permute-start(bf16[256,2048]{1,0:T(8,128)(2,1)} %get-tuple-element.235), channel_id=1, source_target_pairs={{0,4},{2,6},{4,0},{6,2},{1,5},{3,7},{5,1},{7,3},{8,12},{10,14},{12... | collective-permute-start | bytes 3145736 | tf_op jit(solution)/shard_map/ppermute | solution.py:33
  23.6 24.4 %collective-permute-start = (bf16[256,2048]{1,0:T(8,128)(2,1)}, bf16[256,2048]{1,0:T(8,128)(2,1)S(1)}, u32[]{:S(2)}, u32[]{:S(2)}) collective-permute-start(bf16[256,2048]{1,0:T(8,128)(2,1)} %get-tuple-element.235), channel_id=1, source_target_pairs={{0,2},{2,0},{4,6},{6,4},{1,3},{3,1},{5,7},{7,5},{8,10},{10,8},{12,... | collective-permute-start | bytes 3145736 | tf_op jit(solution)/shard_map/ppermute | solution.py:33
  87.7 13.9 %collective-permute-start.8 = (bf16[2048,768]{1,0:T(8,128)(2,1)}, bf16[2048,768]{1,0:T(8,128)(2,1)S(1)}, u32[]{:S(2)}, u32[]{:S(2)}) collective-permute-start(bf16[2048,768]{1,0:T(8,128)(2,1)} %all-gather.5.cloned.1.call-done.weight.own), channel_id=1, source_target_pairs={{0,1},{1,0},{2,3},{3,2},{4,5},{5,4},{6,7},{7,6},{8,9},{9,8},{10,11... | collective-permute-start | bytes 9437192 | tf_op jit(solution)/shard_map/ppermute | solution.py:33
  87.8 126.1 %all-gather.9.cloned.1.call-start = ((), (), s32[]{:S(2)}) async-start(), calls=%async_computation.8 | async-start | bytes 3604480 | tf_op jit(solution)/shard_map/all_gather | solution.py:37
  88.1 25.8 %collective-permute-start.9 = (bf16[256,2048]{1,0:T(8,128)(2,1)}, bf16[256,2048]{1,0:T(8,128)(2,1)S(1)}, u32[]{:S(2)}, u32[]{:S(2)}) collective-permute-start(bf16[256,2048]{1,0:T(8,128)(2,1)} %get-tuple-element.140), channel_id=1, source_target_pairs={{0,4},{2,6},{4,0},{6,2},{1,5},{3,7},{5,1},{7,3},{8,12},{10,14},{12... | collective-permute-start | bytes 3145736 | tf_op jit(solution)/shard_map/ppermute | solution.py:33
  89.7 25.4 %collective-permute-start.7 = (bf16[256,2048]{1,0:T(8,128)(2,1)}, bf16[256,2048]{1,0:T(8,128)(2,1)S(1)}, u32[]{:S(2)}, u32[]{:S(2)}) collective-permute-start(bf16[256,2048]{1,0:T(8,128)(2,1)} %get-tuple-element.140), channel_id=1, source_target_pairs={{0,2},{2,0},{4,6},{6,4},{1,3},{3,1},{5,7},{7,5},{8,10},{10,8},{12,... | collective-permute-start | bytes 3145736 | tf_op jit(solution)/shard_map/ppermute | solution.py:33
  106.0 23.6 %collective-permute-start.13 = (bf16[256,2048]{1,0:T(8,128)(2,1)S(1)}, bf16[256,2048]{1,0:T(8,128)(2,1)S(1)}, u32[]{:S(2)}, u32[]{:S(2)}) collective-permute-start(bf16[256,2048]{1,0:T(8,128)(2,1)S(1)} %copy-done.83), channel_id=1, source_target_pairs={{0,1},{1,0},{2,3},{3,2},{4,5},{5,4},{6,7},{7,6},{8,9},{9,8},{10,11... | collective-permute-start | bytes 3145736 | tf_op jit(solution)/shard_map/ppermute | solution.py:33
  134.5 13.7 %collective-permute-start.14 = (bf16[128,2048]{1,0:T(8,128)(2,1)}, bf16[128,2048]{1,0:T(8,128)(2,1)S(1)}, u32[]{:S(2)}, u32[]{:S(2)}) collective-permute-start(bf16[128,2048]{1,0:T(8,128)(2,1)} %convolution_convert_fusion.8), channel_id=1, source_target_pairs={{0,2},{2,0},{4,6},{6,4},{1,3},{3,1},{5,7},{7,5},{8,10},{10,8},{12,... | collective-permute-start | bytes 1572872 | tf_op jit(solution)/shard_map/ppermute | solution.py:33
  135.9 13.4 %collective-permute-start.15 = (bf16[128,2048]{1,0:T(8,128)(2,1)}, bf16[128,2048]{1,0:T(8,128)(2,1)S(1)}, u32[]{:S(2)}, u32[]{:S(2)}) collective-permute-start(bf16[128,2048]{1,0:T(8,128)(2,1)} %convolution_convert_fusion.7), channel_id=1, source_target_pairs={{0,4},{2,6},{4,0},{6,2},{1,5},{3,7},{5,1},{7,3},{8,12},{10,14},{12... | collective-permute-start | bytes 1572872 | tf_op jit(solution)/shard_map/ppermute | solution.py:33
  136.6 141.3 %all-gather.11.cloned.1.call-start = ((), (), s32[]{:S(2)}) async-start(), calls=%async_computation.9 | async-start | bytes 3604480 | tf_op jit(solution)/shard_map/all_gather | solution.py:37
  150.6 23.9 %collective-permute-start.16 = (bf16[256,2048]{1,0:T(8,128)(2,1)}, bf16[256,2048]{1,0:T(8,128)(2,1)}, u32[]{:S(2)}, u32[]{:S(2)}) collective-permute-start(bf16[256,2048]{1,0:T(8,128)(2,1)} %get-tuple-element.132), channel_id=1, source_target_pairs={{0,2},{2,0},{4,6},{6,4},{1,3},{3,1},{5,7},{7,5},{8,10},{10,8},{12,... | collective-permute-start | bytes 3145736 | tf_op jit(solution)/shard_map/ppermute | solution.py:33
  151.1 23.5 %collective-permute-start.17 = (bf16[256,2048]{1,0:T(8,128)(2,1)S(1)}, bf16[256,2048]{1,0:T(8,128)(2,1)}, u32[]{:S(2)}, u32[]{:S(2)}) collective-permute-start(bf16[256,2048]{1,0:T(8,128)(2,1)S(1)} %get-tuple-element.134), channel_id=1, source_target_pairs={{0,4},{2,6},{4,0},{6,2},{1,5},{3,7},{5,1},{7,3},{8,12},{10,14},{12... | collective-permute-start | bytes 3145736 | tf_op jit(solution)/shard_map/ppermute | solution.py:33
  177.2 22.6 %collective-permute-start.19 = (bf16[256,2048]{1,0:T(8,128)(2,1)S(1)}, bf16[256,2048]{1,0:T(8,128)(2,1)S(1)}, u32[]{:S(2)}, u32[]{:S(2)}) collective-permute-start(bf16[256,2048]{1,0:T(8,128)(2,1)S(1)} %get-tuple-element.231), channel_id=1, source_target_pairs={{0,4},{2,6},{4,0},{6,2},{1,5},{3,7},{5,1},{7,3},{8,12},{10,14},{12... | collective-permute-start | bytes 3145736 | tf_op jit(solution)/shard_map/ppermute | solution.py:33
  178.1 23.8 %collective-permute-start.18 = (bf16[256,2048]{1,0:T(8,128)(2,1)S(1)}, bf16[256,2048]{1,0:T(8,128)(2,1)S(1)}, u32[]{:S(2)}, u32[]{:S(2)}) collective-permute-start(bf16[256,2048]{1,0:T(8,128)(2,1)S(1)} %get-tuple-element.231), channel_id=1, source_target_pairs={{0,2},{2,0},{4,6},{6,4},{1,3},{3,1},{5,7},{7,5},{8,10},{10,8},{12,... | collective-permute-start | bytes 3145736 | tf_op jit(solution)/shard_map/ppermute | solution.py:33
  213.9 22.4 %collective-permute-start.24 = (bf16[704,2048]{1,0:T(8,128)(2,1)S(1)}, bf16[704,2048]{1,0:T(8,128)(2,1)}, u32[]{:S(2)}, u32[]{:S(2)}) collective-permute-start(bf16[704,2048]{1,0:T(8,128)(2,1)S(1)} %copy-done.6), channel_id=1, source_target_pairs={{0,1},{1,0},{2,3},{3,2},{4,5},{5,4},{6,7},{7,6},{8,9},{9,8},{10,11... | collective-permute-start | bytes 8650760 | tf_op jit(solution)/shard_map/ppermute | solution.py:33
  213.9 22.5 %collective-permute-start.25 = (bf16[704,2048]{1,0:T(8,128)(2,1)}, bf16[704,2048]{1,0:T(8,128)(2,1)}, u32[]{:S(2)}, u32[]{:S(2)}) collective-permute-start(bf16[704,2048]{1,0:T(8,128)(2,1)} %all-gather.9.cloned.1.call-done.up.refs_5_), channel_id=1, source_target_pairs={{0,1},{1,0},{2,3},{3,2},{4,5},{5,4},{6,7},{7,6},{8,9},{9,8},{10,11... | collective-permute-start | bytes 8650760 | tf_op jit(solution)/shard_map/ppermute | solution.py:33
  216.3 16.8 %collective-permute-start.23 = (bf16[128,2048]{1,0:T(8,128)(2,1)}, bf16[128,2048]{1,0:T(8,128)(2,1)S(1)}, u32[]{:S(2)}, u32[]{:S(2)}) collective-permute-start(bf16[128,2048]{1,0:T(8,128)(2,1)} %slice.214), channel_id=1, source_target_pairs={{0,4},{2,6},{4,0},{6,2},{1,5},{3,7},{5,1},{7,3},{8,12},{10,14},{12... | collective-permute-start | bytes 1572872 | tf_op jit(solution)/shard_map/ppermute | solution.py:33
  219.1 13.9 %collective-permute-start.22 = (bf16[128,2048]{1,0:T(8,128)(2,1)}, bf16[128,2048]{1,0:T(8,128)(2,1)}, u32[]{:S(2)}, u32[]{:S(2)}) collective-permute-start(bf16[128,2048]{1,0:T(8,128)(2,1)} %slice.213), channel_id=1, source_target_pairs={{0,2},{2,0},{4,6},{6,4},{1,3},{3,1},{5,7},{7,5},{8,10},{10,8},{12,... | collective-permute-start | bytes 1572872 | tf_op jit(solution)/shard_map/ppermute | solution.py:33
  220.4 114.6 %reduce-scatter.7.cloned.1.call-start = ((), (), s32[]{:S(2)}) async-start(), calls=%async_computation.10 | async-start | bytes 3604480 | tf_op jit(solution)/shard_map/reduce_scatter | solution.py:41
  277.9 134.2 %reduce-scatter.9.cloned.1.call-start = ((), (), s32[]{:S(2)}) async-start(), calls=%async_computation.11 | async-start | bytes 3604480 | tf_op jit(solution)/shard_map/reduce_scatter | solution.py:41
  308.0 16.4 %collective-permute-start.30 = (bf16[704,2048]{1,0:T(8,128)(2,1)S(1)}, bf16[704,2048]{1,0:T(8,128)(2,1)S(1)}, u32[]{:S(2)}, u32[]{:S(2)}) collective-permute-start(bf16[704,2048]{1,0:T(8,128)(2,1)S(1)} %convolution_convert_fusion.2), channel_id=1, source_target_pairs={{0,1},{1,0},{2,3},{3,2},{4,5},{5,4},{6,7},{7,6},{8,9},{9,8},{10,11... | collective-permute-start | bytes 8650760 | tf_op jit(solution)/shard_map/ppermute | solution.py:33
  308.6 14.0 %collective-permute-start.28 = (bf16[128,2048]{1,0:T(8,128)(2,1)S(1)}, bf16[128,2048]{1,0:T(8,128)(2,1)S(1)}, u32[]{:S(2)}, u32[]{:S(2)}) collective-permute-start(bf16[128,2048]{1,0:T(8,128)(2,1)S(1)} %get-tuple-element.157), channel_id=1, source_target_pairs={{0,2},{2,0},{4,6},{6,4},{1,3},{3,1},{5,7},{7,5},{8,10},{10,8},{12,... | collective-permute-start | bytes 1572872 | tf_op jit(solution)/shard_map/ppermute | solution.py:33
  309.9 13.6 %collective-permute-start.29 = (bf16[128,2048]{1,0:T(8,128)(2,1)S(1)}, bf16[128,2048]{1,0:T(8,128)(2,1)S(1)}, u32[]{:S(2)}, u32[]{:S(2)}) collective-permute-start(bf16[128,2048]{1,0:T(8,128)(2,1)S(1)} %get-tuple-element.158), channel_id=1, source_target_pairs={{0,4},{2,6},{4,0},{6,2},{1,5},{3,7},{5,1},{7,3},{8,12},{10,14},{12... | collective-permute-start | bytes 1572872 | tf_op jit(solution)/shard_map/ppermute | solution.py:33
  328.9 122.7 %reduce-scatter.11.cloned.1.call-start = ((), (), s32[]{:S(2)}) async-start(), calls=%async_computation.12 | async-start | bytes 3604480 | tf_op jit(solution)/shard_map/reduce_scatter | solution.py:41
  352.5 25.9 %collective-permute-start.33 = (bf16[256,2048]{1,0:T(8,128)(2,1)}, bf16[256,2048]{1,0:T(8,128)(2,1)}, u32[]{:S(2)}, u32[]{:S(2)}) collective-permute-start(bf16[256,2048]{1,0:T(8,128)(2,1)} %get-tuple-element.165), channel_id=1, source_target_pairs={{0,4},{2,6},{4,0},{6,2},{1,5},{3,7},{5,1},{7,3},{8,12},{10,14},{12... | collective-permute-start | bytes 3145736 | tf_op jit(solution)/shard_map/ppermute | solution.py:33
  354.2 25.5 %collective-permute-start.32 = (bf16[256,2048]{1,0:T(8,128)(2,1)}, bf16[256,2048]{1,0:T(8,128)(2,1)}, u32[]{:S(2)}, u32[]{:S(2)}) collective-permute-start(bf16[256,2048]{1,0:T(8,128)(2,1)} %get-tuple-element.164), channel_id=1, source_target_pairs={{0,2},{2,0},{4,6},{6,4},{1,3},{3,1},{5,7},{7,5},{8,10},{10,8},{12,... | collective-permute-start | bytes 3145736 | tf_op jit(solution)/shard_map/ppermute | solution.py:33
  362.3 122.2 %reduce-scatter.13.cloned.1.call-start = ((), (), s32[]{:S(2)}) async-start(), calls=%async_computation.13 | async-start | bytes 1310720 | tf_op jit(solution)/shard_map/reduce_scatter | solution.py:41
  387.4 24.6 %collective-permute-start.35 = (bf16[256,2048]{1,0:T(8,128)(2,1)}, bf16[256,2048]{1,0:T(8,128)(2,1)S(1)}, u32[]{:S(2)}, u32[]{:S(2)}) collective-permute-start(bf16[256,2048]{1,0:T(8,128)(2,1)} %get-tuple-element.171), channel_id=1, source_target_pairs={{0,4},{2,6},{4,0},{6,2},{1,5},{3,7},{5,1},{7,3},{8,12},{10,14},{12... | collective-permute-start | bytes 3145736 | tf_op jit(solution)/shard_map/ppermute | solution.py:33
  387.9 27.0 %collective-permute-start.34 = (bf16[256,2048]{1,0:T(8,128)(2,1)}, bf16[256,2048]{1,0:T(8,128)(2,1)}, u32[]{:S(2)}, u32[]{:S(2)}) collective-permute-start(bf16[256,2048]{1,0:T(8,128)(2,1)} %get-tuple-element.171), channel_id=1, source_target_pairs={{0,2},{2,0},{4,6},{6,4},{1,3},{3,1},{5,7},{7,5},{8,10},{10,8},{12,... | collective-permute-start | bytes 3145736 | tf_op jit(solution)/shard_map/ppermute | solution.py:33
  412.1 12.4 %collective-permute-start.36 = (bf16[128,2048]{1,0:T(8,128)(2,1)S(1)}, bf16[128,2048]{1,0:T(8,128)(2,1)S(1)}, u32[]{:S(2)}, u32[]{:S(2)}) collective-permute-start(bf16[128,2048]{1,0:T(8,128)(2,1)S(1)} %slice.216), channel_id=1, source_target_pairs={{0,2},{2,0},{4,6},{6,4},{1,3},{3,1},{5,7},{7,5},{8,10},{10,8},{12,... | collective-permute-start | bytes 1572872 | tf_op jit(solution)/shard_map/ppermute | solution.py:33
  437.3 148.0 %reduce-scatter.17.cloned.1.call-start = ((), (), s32[]{:S(2)}) async-start(), calls=%async_computation.15 | async-start | bytes 1966080 | tf_op jit(solution)/shard_map/reduce_scatter | solution.py:41
  437.8 13.7 %collective-permute-start.39 = (bf16[1024,256]{1,0:T(8,128)(2,1)}, bf16[1024,256]{1,0:T(8,128)(2,1)}, u32[]{:S(2)}, u32[]{:S(2)}) collective-permute-start(bf16[1024,256]{1,0:T(8,128)(2,1)} %convolution_convert_fusion.10), channel_id=1, source_target_pairs={{0,1},{1,0},{2,3},{3,2},{4,5},{5,4},{6,7},{7,6},{8,9},{9,8},{10,11... | collective-permute-start | bytes 1572872 | tf_op jit(solution)/shard_map/ppermute | solution.py:33
  440.3 44.2 %collective-permute-start.40 = (bf16[128,2048]{1,0:T(8,128)(2,1)}, bf16[128,2048]{1,0:T(8,128)(2,1)}, u32[]{:S(2)}, u32[]{:S(2)}) collective-permute-start(bf16[128,2048]{1,0:T(8,128)(2,1)} %get-tuple-element.183), channel_id=1, source_target_pairs={{0,2},{2,0},{4,6},{6,4},{1,3},{3,1},{5,7},{7,5},{8,10},{10,8},{12,... | collective-permute-start | bytes 1572872 | tf_op jit(solution)/shard_map/ppermute | solution.py:33
  440.9 43.6 %collective-permute-start.41 = (bf16[128,2048]{1,0:T(8,128)(2,1)}, bf16[128,2048]{1,0:T(8,128)(2,1)}, u32[]{:S(2)}, u32[]{:S(2)}) collective-permute-start(bf16[128,2048]{1,0:T(8,128)(2,1)} %get-tuple-element.184), channel_id=1, source_target_pairs={{0,4},{2,6},{4,0},{6,2},{1,5},{3,7},{5,1},{7,3},{8,12},{10,14},{12... | collective-permute-start | bytes 1572872 | tf_op jit(solution)/shard_map/ppermute | solution.py:33
  500.7 84.6 %reduce-scatter.15.cloned.1.call-start = ((), (), s32[]{:S(2)}) async-start(), calls=%async_computation.14 | async-start | bytes 1966080 | tf_op jit(solution)/shard_map/reduce_scatter | solution.py:41
  501.3 29.8 %collective-permute-start.46 = (bf16[256,2048]{1,0:T(8,128)(2,1)}, bf16[256,2048]{1,0:T(8,128)(2,1)}, u32[]{:S(2)}, u32[]{:S(2)}) collective-permute-start(bf16[256,2048]{1,0:T(8,128)(2,1)} %copy-done.79), channel_id=1, source_target_pairs={{0,2},{2,0},{4,6},{6,4},{1,3},{3,1},{5,7},{7,5},{8,10},{10,8},{12,... | collective-permute-start | bytes 3145736 | tf_op jit(solution)/shard_map/ppermute | solution.py:33
  502.7 28.4 %collective-permute-start.47 = (bf16[256,2048]{1,0:T(8,128)(2,1)}, bf16[256,2048]{1,0:T(8,128)(2,1)}, u32[]{:S(2)}, u32[]{:S(2)}) collective-permute-start(bf16[256,2048]{1,0:T(8,128)(2,1)} %copy-done.78), channel_id=1, source_target_pairs={{0,4},{2,6},{4,0},{6,2},{1,5},{3,7},{5,1},{7,3},{8,12},{10,14},{12... | collective-permute-start | bytes 3145736 | tf_op jit(solution)/shard_map/ppermute | solution.py:33
  531.5 14.0 %collective-permute-start.49 = (bf16[128,2048]{1,0:T(8,128)(2,1)S(1)}, bf16[128,2048]{1,0:T(8,128)(2,1)S(1)}, u32[]{:S(2)}, u32[]{:S(2)}) collective-permute-start(bf16[128,2048]{1,0:T(8,128)(2,1)S(1)} %get-tuple-element.203), channel_id=1, source_target_pairs={{0,4},{2,6},{4,0},{6,2},{1,5},{3,7},{5,1},{7,3},{8,12},{10,14},{12... | collective-permute-start | bytes 1572872 | tf_op jit(solution)/shard_map/ppermute | solution.py:33
  533.0 13.7 %collective-permute-start.48 = (bf16[128,2048]{1,0:T(8,128)(2,1)S(1)}, bf16[128,2048]{1,0:T(8,128)(2,1)S(1)}, u32[]{:S(2)}, u32[]{:S(2)}) collective-permute-start(bf16[128,2048]{1,0:T(8,128)(2,1)S(1)} %get-tuple-element.201), channel_id=1, source_target_pairs={{0,2},{2,0},{4,6},{6,4},{1,3},{3,1},{5,7},{7,5},{8,10},{10,8},{12,... | collective-permute-start | bytes 1572872 | tf_op jit(solution)/shard_map/ppermute | solution.py:33
  537.7 13.9 %collective-permute-start.53 = (f32[10240]{0:T(1024)S(1)}, f32[10240]{0:T(1024)S(1)}, u32[]{:S(2)}, u32[]{:S(2)}) collective-permute-start(f32[10240]{0:T(1024)S(1)} %fusion.22), channel_id=1, source_target_pairs={{0,8},{8,0},{16,24},{24,16},{1,9},{9,1},{17,25},{25,17},{2,10},{10... | collective-permute-start | bytes 122888 | tf_op jit(solution)/shard_map/ppermute | solution.py:33
  548.3 31.0 %collective-permute-start.50 = (bf16[256,2048]{1,0:T(8,128)(2,1)}, bf16[256,2048]{1,0:T(8,128)(2,1)S(1)}, u32[]{:S(2)}, u32[]{:S(2)}) collective-permute-start(bf16[256,2048]{1,0:T(8,128)(2,1)} %get-tuple-element.204), channel_id=1, source_target_pairs={{0,2},{2,0},{4,6},{6,4},{1,3},{3,1},{5,7},{7,5},{8,10},{10,8},{12,... | collective-permute-start | bytes 3145736 | tf_op jit(solution)/shard_map/ppermute | solution.py:33
  549.7 29.6 %collective-permute-start.51 = (bf16[256,2048]{1,0:T(8,128)(2,1)}, bf16[256,2048]{1,0:T(8,128)(2,1)}, u32[]{:S(2)}, u32[]{:S(2)}) collective-permute-start(bf16[256,2048]{1,0:T(8,128)(2,1)} %get-tuple-element.205), channel_id=1, source_target_pairs={{0,4},{2,6},{4,0},{6,2},{1,5},{3,7},{5,1},{7,3},{8,12},{10,14},{12... | collective-permute-start | bytes 3145736 | tf_op jit(solution)/shard_map/ppermute | solution.py:33
  559.9 13.5 %collective-permute-start.55 = (f32[10240]{0:T(1024)S(1)}, f32[10240]{0:T(1024)S(1)}, u32[]{:S(2)}, u32[]{:S(2)}) collective-permute-start(f32[10240]{0:T(1024)S(1)} %add.179), channel_id=1, source_target_pairs={{0,2},{2,0},{4,6},{6,4},{1,3},{3,1},{5,7},{7,5},{8,10},{10,8},{12,... | collective-permute-start | bytes 122888 | tf_op jit(solution)/shard_map/ppermute | solution.py:33
  (125 other events, 899.4 us)
Sparse Core Ops, SparseCore 0:
  20.2 67.4 all-gather.4
  89.3 58.6 all-gather.6
  149.5 57.8 all-gather.8
  220.5 57.2 all-gather.10
  280.0 54.9 reduce-scatter.6
  337.1 56.0 reduce-scatter.8
  395.5 56.0 reduce-scatter.10
  454.4 26.9 reduce-scatter.12
  500.8 35.1 reduce-scatter.16
  538.3 35.1 reduce-scatter.14

commit v6 on v5

--- a/solution.py
+++ b/solution.py
@@ -693,7 +693,6 @@
     ffn_out_grad_near = near_rows(ffn_out_grad_own)
     kept_first, sent_second = project(normed, qkv_own, cosine, sine)
     sent_first, kept_second = project(after(normed, kept_first), qkv_other, cosine, sine)
-    ffn_out_grad_near = [after(near, sent_first) for near in ffn_out_grad_near]
     output_other = swap(after(output_own, sent_first), "tensor", 1)
     output_kept = jnp.concatenate([output_own[:value_half], output_other[value_half:]], axis=0)
     output_sent = jnp.concatenate([output_other[:value_half], output_own[value_half:]], axis=0)
@@ -701,10 +700,11 @@
     kept, sent, ordered, outs, log_totals = attention_forward(
         ints,
         floats,
-        (after(kept_first, *ffn_out_grad_near), kept_second),
+        (kept_first, kept_second),
         (swap(sent_first, "tensor", 1), swap(sent_second, "tensor", 1)),
         gain_own,
     )
+    sent = after(sent, *ffn_out_grad_near)
     head_out = jnp.concatenate([kept, swap(sent, "tensor", 1)], axis=1)
 
     third_out = [
@@ -731,6 +731,7 @@
         after(ffn_in, hidden_own), gate_other, up_other
     )
 
+    ffn_out_grad_near = [after(near, hidden_own) for near in ffn_out_grad_near]
     ffn_out_grad_all = group_rows(ffn_out_grad_own, ffn_out_grad_near, hidden_own)
 
     def weight_grad(own_side, other_side, right_side, *events):

time: 608 us -> 598 us (0.984)
  local copies, waits for them, and re-layouts: 88.9 us -> 81.4 us
    all_gather x4, waiting for transfers between devices: 43.1 us -> 32.3 us  [fsdp_gather(): return lax.all_gather(after(own, *others), 'fsdp', axis=axis, tiled=True)]
    ppermute x54, waiting for transfers between devices: 158 us -> 166 us  [swap(): lax.ppermute(values, axis, [(place, place ^ mask) for place in range(size)])]
  transfers between devices with their start and end apart: 67 -> 67, of which waited for: 32 -> 35; matrix products, arithmetic and copies ran while one was open for 17% -> 17% of each run, Pallas kernels for 23% -> 23%
where the time goes in v6:
time: 598 us; the launch traced here: 589 us
  waiting for transfers between devices  206 us (34%)
  Pallas kernels  137 us (23%)
  local copies, waits for them, and re-layouts  81.4 us (14%)
  matrix products  57.3 us (10%)
  starting transfers between devices  55.3 us (9%)
  other arithmetic  31.8 us (5%)
  between operations  19.6 us (3%)
    ppermute x54, waiting for transfers between devices, swap(): lax.ppermute(values, axis, [(place, place ^ mask) for place in range(size)])  166 us
    unnamed x230, local copies, waits for them, and re-layouts  69.3 us
    dot_general x16, matrix products, contract(): lax.dot_general(left_side, right_side, (((left_dim,), (right_dim,)), ((),...  57.3 us
    ppermute x54, starting transfers between devices, swap(): lax.ppermute(values, axis, [(place, place ^ mask) for place in range(size)])  46.1 us
    pallas_call x4, Pallas kernels, sum_over_units(): pl.pallas_call(functools.partial(sum_kernel, terms), grid=(count,), in_sp...  33.6 us
    all_gather x4, waiting for transfers between devices, fsdp_gather(): return lax.all_gather(after(own, *others), 'fsdp', axis=axis, tiled=True)  32.3 us
    pallas_call x1, Pallas kernels, attention_backward(): pl.pallas_call(attention_backward_kernel, in_specs=[smem, smem] + [vmem]...  22.8 us
    pallas_call x2, Pallas kernels, gate_units(): pl.pallas_call(gate_kernel, grid=(4,), in_specs=[pl.BlockSpec((block, wid...  20.3 us
  transfers between devices with their start and end apart: 67, of which 35 were waited for; matrix products, arithmetic and copies ran while one was open for 17% of the time, Pallas kernels for 23%

profile of v6, /device:TPU:0, one launch (start us, length us, event | category | flops | bytes accessed | tf_op | source)
XLA Modules:
  0.0 588.6 jit_solution(7682564228777317020)
XLA Ops:
  8.3 3.1 collective-permute-start.3
  35.2 3.7 fusion.10
  51.8 7.0 %collective-permute-done.5 = bf16[128,2048]{1,0:T(8,128)(2,1)S(1)} collective-permute-done((bf16[128,2048]{1,0:T(8,128)(2,1)S(1)}, bf16[128,2048]{1,0:T(8,128)(2,1)S(1)}, u32[]{:S(2)}, u32[]{:S(2)}) %collective-permute-start.5) | collective-permute-done | bytes 524320 | tf_op jit(solution)/shard_map/ppermute | solution.py:33
  60.7 27.1 %all-gather.5.cloned.1.call-done.weight.own = bf16[2048,768]{1,0:T(8,128)(2,1)} async-done(((bf16[512,768]{1,0:T(8,128)(2,1)}), bf16[2048,768]{1,0:T(8,128)(2,1)}) %all-gather.5.cloned.1.call-update) | async-done | bytes 3145744 | tf_op jit(solution)/shard_map/all_gather | solution.py:37
  97.4 4.2 project.2
  101.7 4.3 project.3
  106.7 3.1 collective-permute-done.9.received_second
  110.9 13.3 %attention_forward.1 = (bf16[1024,256]{1,0:T(8,128)(2,1)S(1)}, bf16[1024,256]{1,0:T(8,128)(2,1)S(1)}, bf16[2048,768]{1,0:T(8,128)(2,1)S(1)}, f32[2,2048,256]{2,1,0:T(8,128)S(1)}, f32[2,2048]{1,0:T(2,128)S(1)}) custom-call(s32[4]{0:T(128)S(1)} %pad_add_fusion.ints, f32[2]{0:T(128)S(1)} %pad_maximum_fusion.13.floats, ...), custom_call_target="tpu_custom_call" | custom-call | flops 100000000 | bytes 1048576 | tf_op jit(solution)/shard_map/attention_forward/pallas_call | solution.py:258
  130.7 3.1 convolution_convert_fusion.near
  133.9 9.9 %collective-permute-done.14.to_first = bf16[128,2048]{1,0:T(8,128)(2,1)S(1)} collective-permute-done((bf16[128,2048]{1,0:T(8,128)(2,1)}, bf16[128,2048]{1,0:T(8,128)(2,1)S(1)}, u32[]{:S(2)}, u32[]{:S(2)}) %collective-permute-start.14) | collective-permute-done | bytes 524320 | tf_op jit(solution)/shard_map/ppermute | solution.py:33
  148.0 21.8 %collective-permute-done.16 = bf16[256,2048]{1,0:T(8,128)(2,1)} collective-permute-done((bf16[256,2048]{1,0:T(8,128)(2,1)}, bf16[256,2048]{1,0:T(8,128)(2,1)}, u32[]{:S(2)}, u32[]{:S(2)}) %collective-permute-start.16) | collective-permute-done | bytes 1048608 | tf_op jit(solution)/shard_map/ppermute | solution.py:33
  174.4 21.9 %collective-permute-done.19 = bf16[256,2048]{1,0:T(8,128)(2,1)S(1)} collective-permute-done((bf16[256,2048]{1,0:T(8,128)(2,1)S(1)}, bf16[256,2048]{1,0:T(8,128)(2,1)S(1)}, u32[]{:S(2)}, u32[]{:S(2)}) %collective-permute-start.19) | collective-permute-done | bytes 1048608 | tf_op jit(solution)/shard_map/ppermute | solution.py:33
  199.9 7.8 %collective-permute-done.20 = bf16[128,2048]{1,0:T(8,128)(2,1)S(1)} collective-permute-done((bf16[128,2048]{1,0:T(8,128)(2,1)S(1)}, bf16[128,2048]{1,0:T(8,128)(2,1)S(1)}, u32[]{:S(2)}, u32[]{:S(2)}) %collective-permute-start.20) | collective-permute-done | bytes 524320 | tf_op jit(solution)/shard_map/ppermute | solution.py:33
  215.2 8.0 %gate_units.2 = (bf16[704,1024]{1,0:T(8,128)(2,1)S(1)}, bf16[704,1024]{1,0:T(8,128)(2,1)S(1)}, bf16[704,1024]{1,0:T(8,128)(2,1)S(1)}) custom-call(bf16[1024,2048]{1,0:T(8,128)(2,1)S(1)} %copy-done.20, bf16[704,2048]{1,0:T(8,128)(2,1)S(1)} %copy-done.6, bf16[704,2048]{1,0:T(8,128)(2,1)S(1)} %copy-done.7), custom_call_target="tpu_custom_call" | custom-call | flops 118111600 | bytes 1048576 | tf_op jit(solution)/shard_map/gate_units/pallas_call | solution.py:536
  225.8 11.5 %collective-permute-done.22 = bf16[128,2048]{1,0:T(8,128)(2,1)S(1)} collective-permute-done((bf16[128,2048]{1,0:T(8,128)(2,1)S(1)}, bf16[128,2048]{1,0:T(8,128)(2,1)S(1)}, u32[]{:S(2)}, u32[]{:S(2)}) %collective-permute-start.22) | collective-permute-done | bytes 524320 | tf_op jit(solution)/shard_map/ppermute | solution.py:33
  238.3 12.3 %gate_units.3 = (bf16[704,1024]{1,0:T(8,128)(2,1)S(1)}, bf16[704,1024]{1,0:T(8,128)(2,1)S(1)}, bf16[704,1024]{1,0:T(8,128)(2,1)S(1)}) custom-call(bf16[1024,2048]{1,0:T(8,128)(2,1)S(1)} %copy-done.20, bf16[704,2048]{1,0:T(8,128)(2,1)} %collective-permute-done.24.gate.refs_6_, bf16[704,2048]{1,0:T(8,128)(2,1)} %collective-permute-done.25.up.refs_7_), custom_call_target="tpu_custom_call" | custom-call | flops 118111600 | bytes 1048576 | tf_op jit(solution)/shard_map/gate_units/pallas_call | solution.py:536
  250.6 3.4 convolution_convert_fusion.3
  254.1 5.3 collective-permute-done.26
  259.3 4.5 add_convert_fusion.2
  263.8 4.6 all-gather.11.cloned.1.call-done.down.refs_2_
  275.5 4.6 gate_grads.2
  280.2 7.4 %gate_grads.3 = (bf16[704,1024]{1,0:T(8,128)(2,1)S(1)}, bf16[704,1024]{1,0:T(8,128)(2,1)S(1)}) custom-call(bf16[1024,2048]{1,0:T(8,128)(2,1)S(1)} %copy-done.24, bf16[704,2048]{1,0:T(8,128)(2,1)} %collective-permute-done.27.down.refs_3_, bf16[704,1024]{1,0:T(8,128)(2,1)S(1)} %copy-done.70, bf16[704,1024]{1,0:T(8,128)(2,1)S(1)} %copy-done.72), custom_call_target="tpu_custom_call" | custom-call | flops 59055800 | bytes 1048576 | tf_op jit(solution)/shard_map/gate_grads/pallas_call | solution.py:559
  287.6 7.5 %sum_over_units.4 = (bf16[128,2048]{1,0:T(8,128)(2,1)S(1)}, bf16[128,2048]{1,0:T(8,128)(2,1)S(1)}) custom-call(bf16[704,1024]{1,0:T(8,128)(2,1)S(1)} %get-tuple-element.162.refs_0_, bf16[704,1024]{1,0:T(8,128)(2,1)S(1)} %get-tuple-element.167.refs_1_, bf16[704,1024]{1,0:T(8,128)(2,1)S(1)} %get-tuple-element.159.refs_2_, ...), custom_call_target="tpu_custom_call" | custom-call | flops 59055800 | bytes 1048576 | tf_op jit(solution)/shard_map/sum_over_units/pallas_call | solution.py:586
  295.2 3.4 convolution_convert_fusion.2
  302.0 9.9 %sum_over_units.5.near = bf16[512,2048]{1,0:T(8,128)(2,1)S(1)} custom-call(bf16[704,1024]{1,0:T(8,128)(2,1)S(1)} %get-tuple-element.162.refs_0_, bf16[704,1024]{1,0:T(8,128)(2,1)S(1)} %get-tuple-element.167.refs_1_, bf16[704,1024]{1,0:T(8,128)(2,1)S(1)} %get-tuple-element.159.refs_2_, bf16[704,1024]{1,0:T(8,128)(2,1)S(1)} %get-tuple-element.166.refs_3_, ...), custom_call_target="tpu_custom_call" | custom-call | flops 118111600 | bytes 1048576 | tf_op jit(solution)/shard_map/sum_over_units/pallas_call | solution.py:586
  314.9 4.5 add_convert_fusion.1
  332.8 6.8 %sum_over_units.6.one = bf16[256,2048]{1,0:T(8,128)(2,1)S(1)} custom-call(bf16[704,1024]{1,0:T(8,128)(2,1)S(1)} %copy-done.31, bf16[704,1024]{1,0:T(8,128)(2,1)S(1)} %copy-done.29, bf16[704,1024]{1,0:T(8,128)(2,1)S(1)} %copy-done.35, bf16[704,1024]{1,0:T(8,128)(2,1)S(1)} %copy-done.33, bf16[704,2048]{1,0:T(8,128)(2,1)S(1)} %copy-done.6, ...), custom_call_target="tpu_custom_call" | custom-call | flops 59055800 | bytes 1048576 | tf_op jit(solution)/shard_map/sum_over_units/pallas_call | solution.py:586
  339.6 3.4 convolution_convert_fusion.1
  348.4 4.5 add_convert_fusion
  353.2 15.8 %collective-permute-done.33.three = bf16[256,2048]{1,0:T(8,128)(2,1)} collective-permute-done((bf16[256,2048]{1,0:T(8,128)(2,1)}, bf16[256,2048]{1,0:T(8,128)(2,1)}, u32[]{:S(2)}, u32[]{:S(2)}) %collective-permute-start.33) | collective-permute-done | bytes 1048608 | tf_op jit(solution)/shard_map/ppermute | solution.py:33
  371.9 4.8 norm_back.2
  380.1 9.4 %sum_over_units.7.near = bf16[1024,2048]{1,0:T(8,128)(2,1)S(1)} custom-call(bf16[704,1024]{1,0:T(8,128)(2,1)S(1)} %copy-done.62, bf16[704,1024]{1,0:T(8,128)(2,1)S(1)} %copy-done.64, bf16[704,2048]{1,0:T(8,128)(2,1)S(1)} %copy-done.37, bf16[704,2048]{1,0:T(8,128)(2,1)} %collective-permute-done.27.down.refs_3_), custom_call_target="tpu_custom_call" | custom-call | flops 118111600 | bytes 1048576 | tf_op jit(solution)/shard_map/sum_over_units/pallas_call | solution.py:586
  391.5 11.1 %collective-permute-done.35 = bf16[256,2048]{1,0:T(8,128)(2,1)S(1)} collective-permute-done((bf16[256,2048]{1,0:T(8,128)(2,1)}, bf16[256,2048]{1,0:T(8,128)(2,1)S(1)}, u32[]{:S(2)}, u32[]{:S(2)}) %collective-permute-start.35) | collective-permute-done | bytes 1048608 | tf_op jit(solution)/shard_map/ppermute | solution.py:33
  408.7 6.4 %collective-permute-done.36 = bf16[128,2048]{1,0:T(8,128)(2,1)S(1)} collective-permute-done((bf16[128,2048]{1,0:T(8,128)(2,1)S(1)}, bf16[128,2048]{1,0:T(8,128)(2,1)S(1)}, u32[]{:S(2)}, u32[]{:S(2)}) %collective-permute-start.36) | collective-permute-done | bytes 524320 | tf_op jit(solution)/shard_map/ppermute | solution.py:33
  415.2 3.6 collective-permute-done.37
  432.2 4.6 convolution_convert_fusion.9.grads_kept
  436.8 5.3 reduce-scatter.11.cloned.1.call-done
  448.5 22.8 %attention_backward.1 = (bf16[1024,384]{1,0:T(8,128)(2,1)S(1)}, bf16[1024,384]{1,0:T(8,128)(2,1)S(1)}, bf16[1024,384]{1,0:T(8,128)(2,1)S(1)}, bf16[1024,384]{1,0...) custom-call(s32[4]{0:T(128)S(1)} %pad_add_fusion.ints, f32[2]{0:T(128)S(1)} %pad_maximum_fusion.13.floats, ...), custom_call_target="tpu_custom_call" | custom-call | flops 400000000 | bytes 1048576 | tf_op jit(solution)/shard_map/attention_backward/pallas_call | solution.py:391
  471.4 3.5 convolution_convert_fusion.6
  481.6 3.7 convolution_convert_fusion.5
  485.3 5.1 add_convert_fusion.3
  495.0 5.9 add_convert_fusion.4
  514.5 7.2 %project_back.3 = (f32[1,2048]{1,0:T(1,128)S(1)}, bf16[768,2048]{1,0:T(8,128)(2,1)S(1)}) custom-call(bf16[1024,384]{1,0:T(8,128)(2,1)S(1)} %copy-done.52, bf16[1024,384]{1,0:T(8,128)(2,1)S(1)} %copy-done.58, bf16[1024,384]{1,0:T(8,128)(2,1)S(1)} %copy-done.56, bf16[1024,384]{1,0:T(8,128)(2,1)S(1)} %copy-done.54, bf16[2048,768]{1,0:T(8,128)(2,1)S(1)} %copy-done.14, ...), custom_call_target="tpu_custom_call" | custom-call | flops 96636768 | bytes 1048576 | tf_op jit(solution)/shard_map/project_back/pallas_call | solution.py:506
  525.0 3.2 multiply_convert_fusion
  529.2 6.9 %collective-permute-done.49.to_second = bf16[128,2048]{1,0:T(8,128)(2,1)S(1)} collective-permute-done((bf16[128,2048]{1,0:T(8,128)(2,1)S(1)}, bf16[128,2048]{1,0:T(8,128)(2,1)S(1)}, u32[]{:S(2)}, u32[]{:S(2)}) %collective-permute-start.49) | collective-permute-done | bytes 524320 | tf_op jit(solution)/shard_map/ppermute | solution.py:33
  545.9 4.6 collective-permute-done.54
  550.7 13.4 %collective-permute-done.55 = f32[10240]{0:T(1024)S(1)} collective-permute-done((f32[10240]{0:T(1024)S(1)}, f32[10240]{0:T(1024)S(1)}, u32[]{:S(2)}, u32[]{:S(2)}) %collective-permute-start.55) | collective-permute-done | bytes 40992 | tf_op jit(solution)/shard_map/ppermute | solution.py:33
  571.5 4.4 norm_back.3
  (451 shorter events, 195.5 us)
Async XLA Ops:
  7.2 80.5 %all-gather.5.cloned.1.call-start = ((), (), s32[]{:S(2)}) async-start(), calls=%async_computation.6 | async-start | bytes 3932160 | tf_op jit(solution)/shard_map/all_gather | solution.py:37
  8.3 34.5 %collective-permute-start.3 = (bf16[256,512]{1,0:T(8,128)(2,1)S(1)}, bf16[256,512]{1,0:T(8,128)(2,1)}, u32[]{:S(2)}, u32[]{:S(2)}) collective-permute-start(bf16[256,512]{1,0:T(8,128)(2,1)S(1)} %pad_maximum_fusion.11.refs_0_), channel_id=1, source_target_pairs={{0,8},{8,16},{16,24},{24,0},{1,9},{9,17},{17,25},{25,1},{2,10},{10... | collective-permute-start | bytes 786440 | tf_op jit(solution)/shard_map/ppermute | solution.py:46
  11.4 31.4 %collective-permute-start.2 = (bf16[256,512]{1,0:T(8,128)(2,1)S(1)}, bf16[256,512]{1,0:T(8,128)(2,1)}, u32[]{:S(2)}, u32[]{:S(2)}) collective-permute-start(bf16[256,512]{1,0:T(8,128)(2,1)S(1)} %pad_maximum_fusion.11.refs_0_), channel_id=1, source_target_pairs={{0,16},{8,24},{16,0},{24,8},{1,17},{9,25},{17,1},{25,9},{2,18},{10... | collective-permute-start | bytes 786440 | tf_op jit(solution)/shard_map/ppermute | solution.py:46
  14.0 28.8 %collective-permute-start.1 = (bf16[256,512]{1,0:T(8,128)(2,1)S(1)}, bf16[256,512]{1,0:T(8,128)(2,1)}, u32[]{:S(2)}, u32[]{:S(2)}) collective-permute-start(bf16[256,512]{1,0:T(8,128)(2,1)S(1)} %pad_maximum_fusion.11.refs_0_), channel_id=1, source_target_pairs={{0,24},{8,0},{16,8},{24,16},{1,25},{9,1},{17,9},{25,17},{2,26},{10... | collective-permute-start | bytes 786440 | tf_op jit(solution)/shard_map/ppermute | solution.py:46
  20.1 127.9 %all-gather.7.cloned.1.call-start = ((), (), s32[]{:S(2)}) async-start(), calls=%async_computation.7 | async-start | bytes 3604480 | tf_op jit(solution)/shard_map/all_gather | solution.py:37
  22.1 24.3 %collective-permute-start.4 = (bf16[256,2048]{1,0:T(8,128)(2,1)}, bf16[256,2048]{1,0:T(8,128)(2,1)S(1)}, u32[]{:S(2)}, u32[]{:S(2)}) collective-permute-start(bf16[256,2048]{1,0:T(8,128)(2,1)} %get-tuple-element.235), channel_id=1, source_target_pairs={{0,4},{2,6},{4,0},{6,2},{1,5},{3,7},{5,1},{7,3},{8,12},{10,14},{12... | collective-permute-start | bytes 3145736 | tf_op jit(solution)/shard_map/ppermute | solution.py:33
  23.6 24.4 %collective-permute-start = (bf16[256,2048]{1,0:T(8,128)(2,1)}, bf16[256,2048]{1,0:T(8,128)(2,1)S(1)}, u32[]{:S(2)}, u32[]{:S(2)}) collective-permute-start(bf16[256,2048]{1,0:T(8,128)(2,1)} %get-tuple-element.235), channel_id=1, source_target_pairs={{0,2},{2,0},{4,6},{6,4},{1,3},{3,1},{5,7},{7,5},{8,10},{10,8},{12,... | collective-permute-start | bytes 3145736 | tf_op jit(solution)/shard_map/ppermute | solution.py:33
  87.7 13.9 %collective-permute-start.7 = (bf16[2048,768]{1,0:T(8,128)(2,1)}, bf16[2048,768]{1,0:T(8,128)(2,1)S(1)}, u32[]{:S(2)}, u32[]{:S(2)}) collective-permute-start(bf16[2048,768]{1,0:T(8,128)(2,1)} %all-gather.5.cloned.1.call-done.weight.own), channel_id=1, source_target_pairs={{0,1},{1,0},{2,3},{3,2},{4,5},{5,4},{6,7},{7,6},{8,9},{9,8},{10,11... | collective-permute-start | bytes 9437192 | tf_op jit(solution)/shard_map/ppermute | solution.py:33
  87.8 122.3 %all-gather.9.cloned.1.call-start = ((), (), s32[]{:S(2)}) async-start(), calls=%async_computation.8 | async-start | bytes 3604480 | tf_op jit(solution)/shard_map/all_gather | solution.py:37
  88.1 36.2 %collective-permute-start.11 = (bf16[256,2048]{1,0:T(8,128)(2,1)}, bf16[256,2048]{1,0:T(8,128)(2,1)S(1)}, u32[]{:S(2)}, u32[]{:S(2)}) collective-permute-start(bf16[256,2048]{1,0:T(8,128)(2,1)} %get-tuple-element.138), channel_id=1, source_target_pairs={{0,4},{2,6},{4,0},{6,2},{1,5},{3,7},{5,1},{7,3},{8,12},{10,14},{12... | collective-permute-start | bytes 3145736 | tf_op jit(solution)/shard_map/ppermute | solution.py:33
  89.7 34.6 %collective-permute-start.10 = (bf16[256,2048]{1,0:T(8,128)(2,1)}, bf16[256,2048]{1,0:T(8,128)(2,1)S(1)}, u32[]{:S(2)}, u32[]{:S(2)}) collective-permute-start(bf16[256,2048]{1,0:T(8,128)(2,1)} %get-tuple-element.138), channel_id=1, source_target_pairs={{0,2},{2,0},{4,6},{6,4},{1,3},{3,1},{5,7},{7,5},{8,10},{10,8},{12,... | collective-permute-start | bytes 3145736 | tf_op jit(solution)/shard_map/ppermute | solution.py:33
  106.0 18.6 %collective-permute-start.13 = (bf16[256,2048]{1,0:T(8,128)(2,1)S(1)}, bf16[256,2048]{1,0:T(8,128)(2,1)S(1)}, u32[]{:S(2)}, u32[]{:S(2)}) collective-permute-start(bf16[256,2048]{1,0:T(8,128)(2,1)S(1)} %copy-done.83), channel_id=1, source_target_pairs={{0,1},{1,0},{2,3},{3,2},{4,5},{5,4},{6,7},{7,6},{8,9},{9,8},{10,11... | collective-permute-start | bytes 3145736 | tf_op jit(solution)/shard_map/ppermute | solution.py:33
  129.6 14.2 %collective-permute-start.14 = (bf16[128,2048]{1,0:T(8,128)(2,1)}, bf16[128,2048]{1,0:T(8,128)(2,1)S(1)}, u32[]{:S(2)}, u32[]{:S(2)}) collective-permute-start(bf16[128,2048]{1,0:T(8,128)(2,1)} %convolution_convert_fusion.8), channel_id=1, source_target_pairs={{0,2},{2,0},{4,6},{6,4},{1,3},{3,1},{5,7},{7,5},{8,10},{10,8},{12,... | collective-permute-start | bytes 1572872 | tf_op jit(solution)/shard_map/ppermute | solution.py:33
  130.1 13.9 %collective-permute-start.15 = (bf16[128,2048]{1,0:T(8,128)(2,1)}, bf16[128,2048]{1,0:T(8,128)(2,1)S(1)}, u32[]{:S(2)}, u32[]{:S(2)}) collective-permute-start(bf16[128,2048]{1,0:T(8,128)(2,1)} %convolution_convert_fusion.7), channel_id=1, source_target_pairs={{0,4},{2,6},{4,0},{6,2},{1,5},{3,7},{5,1},{7,3},{8,12},{10,14},{12... | collective-permute-start | bytes 1572872 | tf_op jit(solution)/shard_map/ppermute | solution.py:33
  130.6 137.8 %all-gather.11.cloned.1.call-start = ((), (), s32[]{:S(2)}) async-start(), calls=%async_computation.9 | async-start | bytes 3604480 | tf_op jit(solution)/shard_map/all_gather | solution.py:37
  145.2 24.6 %collective-permute-start.16 = (bf16[256,2048]{1,0:T(8,128)(2,1)}, bf16[256,2048]{1,0:T(8,128)(2,1)}, u32[]{:S(2)}, u32[]{:S(2)}) collective-permute-start(bf16[256,2048]{1,0:T(8,128)(2,1)} %get-tuple-element.130), channel_id=1, source_target_pairs={{0,2},{2,0},{4,6},{6,4},{1,3},{3,1},{5,7},{7,5},{8,10},{10,8},{12,... | collective-permute-start | bytes 3145736 | tf_op jit(solution)/shard_map/ppermute | solution.py:33
  146.8 24.0 %collective-permute-start.17 = (bf16[256,2048]{1,0:T(8,128)(2,1)S(1)}, bf16[256,2048]{1,0:T(8,128)(2,1)}, u32[]{:S(2)}, u32[]{:S(2)}) collective-permute-start(bf16[256,2048]{1,0:T(8,128)(2,1)S(1)} %get-tuple-element.132), channel_id=1, source_target_pairs={{0,4},{2,6},{4,0},{6,2},{1,5},{3,7},{5,1},{7,3},{8,12},{10,14},{12... | collective-permute-start | bytes 3145736 | tf_op jit(solution)/shard_map/ppermute | solution.py:33
  173.3 23.0 %collective-permute-start.19 = (bf16[256,2048]{1,0:T(8,128)(2,1)S(1)}, bf16[256,2048]{1,0:T(8,128)(2,1)S(1)}, u32[]{:S(2)}, u32[]{:S(2)}) collective-permute-start(bf16[256,2048]{1,0:T(8,128)(2,1)S(1)} %get-tuple-element.231), channel_id=1, source_target_pairs={{0,4},{2,6},{4,0},{6,2},{1,5},{3,7},{5,1},{7,3},{8,12},{10,14},{12... | collective-permute-start | bytes 3145736 | tf_op jit(solution)/shard_map/ppermute | solution.py:33
  173.8 23.4 %collective-permute-start.18 = (bf16[256,2048]{1,0:T(8,128)(2,1)S(1)}, bf16[256,2048]{1,0:T(8,128)(2,1)S(1)}, u32[]{:S(2)}, u32[]{:S(2)}) collective-permute-start(bf16[256,2048]{1,0:T(8,128)(2,1)S(1)} %get-tuple-element.231), channel_id=1, source_target_pairs={{0,2},{2,0},{4,6},{6,4},{1,3},{3,1},{5,7},{7,5},{8,10},{10,8},{12,... | collective-permute-start | bytes 3145736 | tf_op jit(solution)/shard_map/ppermute | solution.py:33
  210.1 28.2 %collective-permute-start.24 = (bf16[704,2048]{1,0:T(8,128)(2,1)S(1)}, bf16[704,2048]{1,0:T(8,128)(2,1)}, u32[]{:S(2)}, u32[]{:S(2)}) collective-permute-start(bf16[704,2048]{1,0:T(8,128)(2,1)S(1)} %copy-done.6), channel_id=1, source_target_pairs={{0,1},{1,0},{2,3},{3,2},{4,5},{5,4},{6,7},{7,6},{8,9},{9,8},{10,11... | collective-permute-start | bytes 8650760 | tf_op jit(solution)/shard_map/ppermute | solution.py:33
  210.1 28.2 %collective-permute-start.25 = (bf16[704,2048]{1,0:T(8,128)(2,1)}, bf16[704,2048]{1,0:T(8,128)(2,1)}, u32[]{:S(2)}, u32[]{:S(2)}) collective-permute-start(bf16[704,2048]{1,0:T(8,128)(2,1)} %all-gather.9.cloned.1.call-done.up.refs_5_), channel_id=1, source_target_pairs={{0,1},{1,0},{2,3},{3,2},{4,5},{5,4},{6,7},{7,6},{8,9},{9,8},{10,11... | collective-permute-start | bytes 8650760 | tf_op jit(solution)/shard_map/ppermute | solution.py:33
  210.6 114.9 %reduce-scatter.7.cloned.1.call-start = ((), (), s32[]{:S(2)}) async-start(), calls=%async_computation.10 | async-start | bytes 3604480 | tf_op jit(solution)/shard_map/reduce_scatter | solution.py:41
  223.4 14.0 %collective-permute-start.22 = (bf16[128,2048]{1,0:T(8,128)(2,1)S(1)}, bf16[128,2048]{1,0:T(8,128)(2,1)S(1)}, u32[]{:S(2)}, u32[]{:S(2)}) collective-permute-start(bf16[128,2048]{1,0:T(8,128)(2,1)S(1)} %slice.213), channel_id=1, source_target_pairs={{0,2},{2,0},{4,6},{6,4},{1,3},{3,1},{5,7},{7,5},{8,10},{10,8},{12,... | collective-permute-start | bytes 1572872 | tf_op jit(solution)/shard_map/ppermute | solution.py:33
  224.5 13.6 %collective-permute-start.23 = (bf16[128,2048]{1,0:T(8,128)(2,1)S(1)}, bf16[128,2048]{1,0:T(8,128)(2,1)S(1)}, u32[]{:S(2)}, u32[]{:S(2)}) collective-permute-start(bf16[128,2048]{1,0:T(8,128)(2,1)S(1)} %slice.214), channel_id=1, source_target_pairs={{0,4},{2,6},{4,0},{6,2},{1,5},{3,7},{5,1},{7,3},{8,12},{10,14},{12... | collective-permute-start | bytes 1572872 | tf_op jit(solution)/shard_map/ppermute | solution.py:33
  268.4 134.2 %reduce-scatter.9.cloned.1.call-start = ((), (), s32[]{:S(2)}) async-start(), calls=%async_computation.11 | async-start | bytes 3604480 | tf_op jit(solution)/shard_map/reduce_scatter | solution.py:41
  298.5 16.4 %collective-permute-start.30 = (bf16[704,2048]{1,0:T(8,128)(2,1)S(1)}, bf16[704,2048]{1,0:T(8,128)(2,1)S(1)}, u32[]{:S(2)}, u32[]{:S(2)}) collective-permute-start(bf16[704,2048]{1,0:T(8,128)(2,1)S(1)} %convolution_convert_fusion.2), channel_id=1, source_target_pairs={{0,1},{1,0},{2,3},{3,2},{4,5},{5,4},{6,7},{7,6},{8,9},{9,8},{10,11... | collective-permute-start | bytes 8650760 | tf_op jit(solution)/shard_map/ppermute | solution.py:33
  299.2 14.0 %collective-permute-start.28 = (bf16[128,2048]{1,0:T(8,128)(2,1)S(1)}, bf16[128,2048]{1,0:T(8,128)(2,1)S(1)}, u32[]{:S(2)}, u32[]{:S(2)}) collective-permute-start(bf16[128,2048]{1,0:T(8,128)(2,1)S(1)} %get-tuple-element.157), channel_id=1, source_target_pairs={{0,2},{2,0},{4,6},{6,4},{1,3},{3,1},{5,7},{7,5},{8,10},{10,8},{12,... | collective-permute-start | bytes 1572872 | tf_op jit(solution)/shard_map/ppermute | solution.py:33
  300.5 13.6 %collective-permute-start.29 = (bf16[128,2048]{1,0:T(8,128)(2,1)S(1)}, bf16[128,2048]{1,0:T(8,128)(2,1)S(1)}, u32[]{:S(2)}, u32[]{:S(2)}) collective-permute-start(bf16[128,2048]{1,0:T(8,128)(2,1)S(1)} %get-tuple-element.158), channel_id=1, source_target_pairs={{0,4},{2,6},{4,0},{6,2},{1,5},{3,7},{5,1},{7,3},{8,12},{10,14},{12... | collective-permute-start | bytes 1572872 | tf_op jit(solution)/shard_map/ppermute | solution.py:33
  319.5 122.7 %reduce-scatter.11.cloned.1.call-start = ((), (), s32[]{:S(2)}) async-start(), calls=%async_computation.12 | async-start | bytes 3604480 | tf_op jit(solution)/shard_map/reduce_scatter | solution.py:41
  343.1 25.9 %collective-permute-start.33 = (bf16[256,2048]{1,0:T(8,128)(2,1)}, bf16[256,2048]{1,0:T(8,128)(2,1)}, u32[]{:S(2)}, u32[]{:S(2)}) collective-permute-start(bf16[256,2048]{1,0:T(8,128)(2,1)} %get-tuple-element.165), channel_id=1, source_target_pairs={{0,4},{2,6},{4,0},{6,2},{1,5},{3,7},{5,1},{7,3},{8,12},{10,14},{12... | collective-permute-start | bytes 3145736 | tf_op jit(solution)/shard_map/ppermute | solution.py:33
  344.7 25.5 %collective-permute-start.32 = (bf16[256,2048]{1,0:T(8,128)(2,1)}, bf16[256,2048]{1,0:T(8,128)(2,1)}, u32[]{:S(2)}, u32[]{:S(2)}) collective-permute-start(bf16[256,2048]{1,0:T(8,128)(2,1)} %get-tuple-element.164), channel_id=1, source_target_pairs={{0,2},{2,0},{4,6},{6,4},{1,3},{3,1},{5,7},{7,5},{8,10},{10,8},{12,... | collective-permute-start | bytes 3145736 | tf_op jit(solution)/shard_map/ppermute | solution.py:33
  352.9 122.2 %reduce-scatter.13.cloned.1.call-start = ((), (), s32[]{:S(2)}) async-start(), calls=%async_computation.13 | async-start | bytes 1310720 | tf_op jit(solution)/shard_map/reduce_scatter | solution.py:41
  378.0 24.6 %collective-permute-start.35 = (bf16[256,2048]{1,0:T(8,128)(2,1)}, bf16[256,2048]{1,0:T(8,128)(2,1)S(1)}, u32[]{:S(2)}, u32[]{:S(2)}) collective-permute-start(bf16[256,2048]{1,0:T(8,128)(2,1)} %get-tuple-element.171), channel_id=1, source_target_pairs={{0,4},{2,6},{4,0},{6,2},{1,5},{3,7},{5,1},{7,3},{8,12},{10,14},{12... | collective-permute-start | bytes 3145736 | tf_op jit(solution)/shard_map/ppermute | solution.py:33
  378.5 27.0 %collective-permute-start.34 = (bf16[256,2048]{1,0:T(8,128)(2,1)}, bf16[256,2048]{1,0:T(8,128)(2,1)}, u32[]{:S(2)}, u32[]{:S(2)}) collective-permute-start(bf16[256,2048]{1,0:T(8,128)(2,1)} %get-tuple-element.171), channel_id=1, source_target_pairs={{0,2},{2,0},{4,6},{6,4},{1,3},{3,1},{5,7},{7,5},{8,10},{10,8},{12,... | collective-permute-start | bytes 3145736 | tf_op jit(solution)/shard_map/ppermute | solution.py:33
  402.7 12.4 %collective-permute-start.36 = (bf16[128,2048]{1,0:T(8,128)(2,1)S(1)}, bf16[128,2048]{1,0:T(8,128)(2,1)S(1)}, u32[]{:S(2)}, u32[]{:S(2)}) collective-permute-start(bf16[128,2048]{1,0:T(8,128)(2,1)S(1)} %slice.216), channel_id=1, source_target_pairs={{0,2},{2,0},{4,6},{6,4},{1,3},{3,1},{5,7},{7,5},{8,10},{10,8},{12,... | collective-permute-start | bytes 1572872 | tf_op jit(solution)/shard_map/ppermute | solution.py:33
  427.9 148.0 %reduce-scatter.17.cloned.1.call-start = ((), (), s32[]{:S(2)}) async-start(), calls=%async_computation.15 | async-start | bytes 1966080 | tf_op jit(solution)/shard_map/reduce_scatter | solution.py:41
  428.4 13.7 %collective-permute-start.39 = (bf16[1024,256]{1,0:T(8,128)(2,1)}, bf16[1024,256]{1,0:T(8,128)(2,1)}, u32[]{:S(2)}, u32[]{:S(2)}) collective-permute-start(bf16[1024,256]{1,0:T(8,128)(2,1)} %convolution_convert_fusion.10), channel_id=1, source_target_pairs={{0,1},{1,0},{2,3},{3,2},{4,5},{5,4},{6,7},{7,6},{8,9},{9,8},{10,11... | collective-permute-start | bytes 1572872 | tf_op jit(solution)/shard_map/ppermute | solution.py:33
  430.9 44.1 %collective-permute-start.40 = (bf16[128,2048]{1,0:T(8,128)(2,1)}, bf16[128,2048]{1,0:T(8,128)(2,1)}, u32[]{:S(2)}, u32[]{:S(2)}) collective-permute-start(bf16[128,2048]{1,0:T(8,128)(2,1)} %get-tuple-element.183), channel_id=1, source_target_pairs={{0,2},{2,0},{4,6},{6,4},{1,3},{3,1},{5,7},{7,5},{8,10},{10,8},{12,... | collective-permute-start | bytes 1572872 | tf_op jit(solution)/shard_map/ppermute | solution.py:33
  431.4 43.6 %collective-permute-start.41 = (bf16[128,2048]{1,0:T(8,128)(2,1)}, bf16[128,2048]{1,0:T(8,128)(2,1)}, u32[]{:S(2)}, u32[]{:S(2)}) collective-permute-start(bf16[128,2048]{1,0:T(8,128)(2,1)} %get-tuple-element.184), channel_id=1, source_target_pairs={{0,4},{2,6},{4,0},{6,2},{1,5},{3,7},{5,1},{7,3},{8,12},{10,14},{12... | collective-permute-start | bytes 1572872 | tf_op jit(solution)/shard_map/ppermute | solution.py:33
  491.3 84.7 %reduce-scatter.15.cloned.1.call-start = ((), (), s32[]{:S(2)}) async-start(), calls=%async_computation.14 | async-start | bytes 1966080 | tf_op jit(solution)/shard_map/reduce_scatter | solution.py:41
  491.8 29.9 %collective-permute-start.46 = (bf16[256,2048]{1,0:T(8,128)(2,1)}, bf16[256,2048]{1,0:T(8,128)(2,1)}, u32[]{:S(2)}, u32[]{:S(2)}) collective-permute-start(bf16[256,2048]{1,0:T(8,128)(2,1)} %copy-done.79), channel_id=1, source_target_pairs={{0,2},{2,0},{4,6},{6,4},{1,3},{3,1},{5,7},{7,5},{8,10},{10,8},{12,... | collective-permute-start | bytes 3145736 | tf_op jit(solution)/shard_map/ppermute | solution.py:33
  493.3 28.4 %collective-permute-start.47 = (bf16[256,2048]{1,0:T(8,128)(2,1)}, bf16[256,2048]{1,0:T(8,128)(2,1)}, u32[]{:S(2)}, u32[]{:S(2)}) collective-permute-start(bf16[256,2048]{1,0:T(8,128)(2,1)} %copy-done.78), channel_id=1, source_target_pairs={{0,4},{2,6},{4,0},{6,2},{1,5},{3,7},{5,1},{7,3},{8,12},{10,14},{12... | collective-permute-start | bytes 3145736 | tf_op jit(solution)/shard_map/ppermute | solution.py:33
  522.1 14.0 %collective-permute-start.49 = (bf16[128,2048]{1,0:T(8,128)(2,1)S(1)}, bf16[128,2048]{1,0:T(8,128)(2,1)S(1)}, u32[]{:S(2)}, u32[]{:S(2)}) collective-permute-start(bf16[128,2048]{1,0:T(8,128)(2,1)S(1)} %get-tuple-element.203), channel_id=1, source_target_pairs={{0,4},{2,6},{4,0},{6,2},{1,5},{3,7},{5,1},{7,3},{8,12},{10,14},{12... | collective-permute-start | bytes 1572872 | tf_op jit(solution)/shard_map/ppermute | solution.py:33
  523.5 13.7 %collective-permute-start.48 = (bf16[128,2048]{1,0:T(8,128)(2,1)S(1)}, bf16[128,2048]{1,0:T(8,128)(2,1)S(1)}, u32[]{:S(2)}, u32[]{:S(2)}) collective-permute-start(bf16[128,2048]{1,0:T(8,128)(2,1)S(1)} %get-tuple-element.201), channel_id=1, source_target_pairs={{0,2},{2,0},{4,6},{6,4},{1,3},{3,1},{5,7},{7,5},{8,10},{10,8},{12,... | collective-permute-start | bytes 1572872 | tf_op jit(solution)/shard_map/ppermute | solution.py:33
  528.3 13.9 %collective-permute-start.53 = (f32[10240]{0:T(1024)S(1)}, f32[10240]{0:T(1024)S(1)}, u32[]{:S(2)}, u32[]{:S(2)}) collective-permute-start(f32[10240]{0:T(1024)S(1)} %fusion.22), channel_id=1, source_target_pairs={{0,8},{8,0},{16,24},{24,16},{1,9},{9,1},{17,25},{25,17},{2,10},{10... | collective-permute-start | bytes 122888 | tf_op jit(solution)/shard_map/ppermute | solution.py:33
  538.9 31.0 %collective-permute-start.50 = (bf16[256,2048]{1,0:T(8,128)(2,1)}, bf16[256,2048]{1,0:T(8,128)(2,1)S(1)}, u32[]{:S(2)}, u32[]{:S(2)}) collective-permute-start(bf16[256,2048]{1,0:T(8,128)(2,1)} %get-tuple-element.204), channel_id=1, source_target_pairs={{0,2},{2,0},{4,6},{6,4},{1,3},{3,1},{5,7},{7,5},{8,10},{10,8},{12,... | collective-permute-start | bytes 3145736 | tf_op jit(solution)/shard_map/ppermute | solution.py:33
  540.4 29.5 %collective-permute-start.51 = (bf16[256,2048]{1,0:T(8,128)(2,1)}, bf16[256,2048]{1,0:T(8,128)(2,1)}, u32[]{:S(2)}, u32[]{:S(2)}) collective-permute-start(bf16[256,2048]{1,0:T(8,128)(2,1)} %get-tuple-element.205), channel_id=1, source_target_pairs={{0,4},{2,6},{4,0},{6,2},{1,5},{3,7},{5,1},{7,3},{8,12},{10,14},{12... | collective-permute-start | bytes 3145736 | tf_op jit(solution)/shard_map/ppermute | solution.py:33
  550.5 13.5 %collective-permute-start.55 = (f32[10240]{0:T(1024)S(1)}, f32[10240]{0:T(1024)S(1)}, u32[]{:S(2)}, u32[]{:S(2)}) collective-permute-start(f32[10240]{0:T(1024)S(1)} %add.179), channel_id=1, source_target_pairs={{0,2},{2,0},{4,6},{6,4},{1,3},{3,1},{5,7},{7,5},{8,10},{10,8},{12,... | collective-permute-start | bytes 122888 | tf_op jit(solution)/shard_map/ppermute | solution.py:33
  (125 other events, 905.2 us)
Sparse Core Ops, SparseCore 0:
  20.2 67.4 all-gather.4
  89.3 58.6 all-gather.6
  149.5 57.8 all-gather.8
  210.8 57.6 all-gather.10
  270.6 54.9 reduce-scatter.6
  327.7 56.0 reduce-scatter.8
  386.0 56.0 reduce-scatter.10
  445.0 26.9 reduce-scatter.12
  491.4 35.1 reduce-scatter.16
  528.9 35.1 reduce-scatter.14
